TPU v7x, 32 devices: a whole 2x2x4 slice. The times are simulated.
32 devices in a mesh: dp: 8 (over y, x, core), expert: 4 (over z).
Axes of the slice: x: 2, y: 2, z: 4, core: 2. Of those that a mesh axis runs over, the one named last changes fastest.
Arguments:
- acts: float32 [8192, 1024], P(('dp', 'expert')), may hold values from -18 to 18, as said below
- grads_out: float32 [8192, 1024], P(('dp', 'expert')), may hold values from -18 to 18, as said below
- routes: int32 [8192, 2], P(('dp', 'expert')), may hold values from 0 to 3, all different within a row; in each aligned block of 256 rows (0 to 255, 256 to 511, ...) at most 192 rows name the same one
- counts: int32 [32, 4], P(('dp', 'expert')), may hold values from 96 to 192
- old_act_factor: float32 [4, 1024, 1024], P('expert', 'dp'), may hold values from -1 to 4, as said below
- old_grad_factor: float32 [4, 1024, 1024], P('expert', 'dp'), may hold values from -1 to 4, as said below
- momentum: float32 [4, 1024, 1024], P('expert', 'dp'), may hold values from -0.0018 to 0.0018
- weights: float32 [4, 1024, 1024], P('expert', 'dp'), may hold values from -0.1875 to 0.1875
Outputs:
- act_factor: float32 [4, 1024, 1024], P('expert', 'dp')
- grad_factor: float32 [4, 1024, 1024], P('expert', 'dp')
- new_momentum: float32 [4, 1024, 1024], P('expert', 'dp')
- new_weights: float32 [4, 1024, 1024], P('expert', 'dp')
Inputs may be any that keep to these rules, and one draw needn't show every extreme that they name: `acts`: entries are independent across rows; each feature has its own scale. `grads_out`: entries are independent across rows; each feature has its own scale. `old_act_factor`: each expert's matrix is symmetric, and each diagonal entry exceeds the sum of the magnitudes of the other entries of its row. `old_grad_factor`: each expert's matrix is symmetric, and each diagonal entry exceeds the sum of the magnitudes of the other entries of its row. `routes`: within the rows of one device no expert is named by more than 192 rows.
All inputs are finite; a program needn't handle non-finite values. Where the computation divides by a largest or mean magnitude, that divisor is 1e-20 or more.
Results may differ from a plain program's by a relative error of at most 0.00013.
Values sent between devices are 32-bit elements; how exact they have to be, the bound alone decides.
No kernel may reach another device: no remote copies, remote signals or barrier semaphores. Data moves between devices by JAX's collectives and lax.ppermute only.
A program may use at most 128 MiB of HBM per device.

v0:
```python
import jax
import jax.numpy as jnp
from jax import lax
from jax.sharding import PartitionSpec as P


def product(left, right):
    return jnp.dot(left, right, precision=lax.Precision.HIGHEST, preferred_element_type=jnp.float32)


def inner_rows(left, right):
    return jnp.einsum(
        "rc,rf->cf",
        left,
        right,
        precision=lax.Precision.HIGHEST,
        preferred_element_type=jnp.float32,
    )


def first_iterate(factor):
    size = factor.shape[0]
    unit = jnp.eye(size, dtype=jnp.float32)
    damp = 0.1 * jnp.trace(factor) / size
    shifted = factor + damp * unit
    alpha = 1.0 / jnp.max(jnp.sum(jnp.abs(shifted), axis=1))
    return (shifted, alpha * (2.0 * unit - alpha * shifted))


def on_device(acts, grads_out, routes, counts, old_act_factor, old_grad_factor, momentum, weights):
    n_expert = lax.axis_size("expert")
    exp_dev = weights.shape[0]
    n_all = n_expert * exp_dev
    samples = routes.shape[0]
    feat = acts.shape[1]
    block = weights.shape[1]
    capacity = min(samples, 3 * samples * routes.shape[1] // (2 * n_all))
    experts = jnp.arange(n_all, dtype=jnp.int32)
    hit = jnp.sum(
        (routes[:, :, None] == experts[None, None, :]).astype(jnp.int32), axis=1, dtype=jnp.int32
    )
    rank = jnp.cumsum(hit, axis=0, dtype=jnp.int32) - hit
    keep = hit * (rank < counts[0][None, :]).astype(jnp.int32)
    slot_ids = jnp.arange(capacity, dtype=jnp.int32)
    match = hit[:, :, None] * (rank[:, :, None] == slot_ids[None, None, :]).astype(jnp.int32)
    row_ids = jnp.arange(samples, dtype=jnp.int32)
    source = jnp.sum(match * row_ids[:, None, None], axis=0, dtype=jnp.int32)
    present = jnp.sum(match * keep[:, :, None], axis=0, dtype=jnp.int32).astype(jnp.float32)
    sent_acts = jnp.take(acts, source, axis=0) * present[:, :, None]
    sent_grads = jnp.take(grads_out, source, axis=0) * present[:, :, None]
    got_acts, got_grads, got_present = (
        lax.all_to_all(sent_acts, "expert", split_axis=0, concat_axis=1, tiled=True),
        lax.all_to_all(sent_grads, "expert", split_axis=0, concat_axis=1, tiled=True),
        lax.all_to_all(present, "expert", split_axis=0, concat_axis=1, tiled=True),
    )
    mine = lax.psum(jnp.sum(got_present, axis=1), "dp")
    total = jnp.maximum(mine, jnp.float32(1.0))
    pieces = []
    local = 0
    act_cols = got_acts[local]
    grad_cols = got_grads[local]
    pieces.append(inner_rows(act_cols, got_acts[local]))
    pieces.append(inner_rows(grad_cols, got_grads[local]))
    pieces.append(inner_rows(grad_cols, got_acts[local]))
    stats = lax.psum_scatter(jnp.concatenate(pieces, axis=1), "dp", scatter_dimension=0, tiled=True)
    act_new = jnp.stack([stats[:, 0:feat] / total[0]])
    grad_new = jnp.stack([stats[:, feat : 2 * feat] / total[0]])
    act_factor = 0.5 * old_act_factor + 0.5 * act_new
    grad_factor = 0.5 * old_grad_factor + 0.5 * grad_new
    gradient_rows = jnp.stack([stats[:, 2 * feat : 3 * feat] / total[0]])
    full_act, full_grad, gradient_full = (
        lax.all_gather(act_factor, "dp", axis=1, tiled=True),
        lax.all_gather(grad_factor, "dp", axis=1, tiled=True),
        lax.all_gather(gradient_rows, "dp", axis=1, tiled=True),
    )
    offset = lax.axis_index("dp") * block
    local = 0
    shifted_act, first_act = first_iterate(full_act[local])
    shifted_grad, first_grad = first_iterate(full_grad[local])
    first_rows = lax.dynamic_slice_in_dim(first_grad, offset, block, 0)
    inverse_rows = 2.0 * first_rows - product(product(first_rows, shifted_grad), first_grad)
    left_side = product(inverse_rows, gradient_full[local])
    half_way = product(left_side, first_act)
    precond = 2.0 * half_way - product(product(half_way, shifted_act), first_act)
    moment_new = 0.9 * momentum[local] + precond
    moments = [moment_new]
    updates = [weights[local] - 0.5 * moment_new]
    return (act_factor, grad_factor, jnp.stack(moments), jnp.stack(updates))


def solution(mesh):
    in_specs = (
        P(("dp", "expert"), None),
        P(("dp", "expert"), None),
        P(("dp", "expert"), None),
        P(("dp", "expert"), None),
        P("expert", "dp", None),
        P("expert", "dp", None),
        P("expert", "dp", None),
        P("expert", "dp", None),
    )
    out_specs = (
        P("expert", "dp", None),
        P("expert", "dp", None),
        P("expert", "dp", None),
        P("expert", "dp", None),
    )
    return jax.shard_map(
        on_device, mesh=mesh, in_specs=in_specs, out_specs=out_specs, check_vma=False
    )
```

profile of v0, /device:TPU:25, one launch (start us, length us, event | category | flops | bytes accessed | tf_op | source)
XLA Modules:
  0.0 447.1 jit_solution(2143074122829102825)
XLA Ops:
  10.8 3.6 gather_fusion
  14.5 3.6 gather_fusion.1
  18.1 5.1 %select_multiply_fusion.1 = (f32[4,192,1024]{2,1,0:T(8,128)}, f32[4,192,1024]{2,1,0:T(8,128)S(1)}) fusion(f32[4,192,1024]{2,1,0:T(8,128)} %bitcast.89, f32[4,192]{1,0:T(4,128)S(1)} %get-tuple-element.26, pred[4,192]{1,0:T(4,128)(4,1)S(1)} %compare_and_fusion, f32[4,192,1024]{2,1,0:T(8,128)} %bitcast.90), kind=kLoop, calls=%fused_computation.17 | loop fusion | flops 3145728 | bytes 12586752 | tf_op jit(solution)/shard_map/mul | solution.py:49
  23.2 73.0 %all_to_all.13 = f32[4,192,1024]{2,1,0:T(8,128)} all-to-all(f32[4,192,1024]{2,1,0:T(8,128)S(1)} %get-tuple-element.24), channel_id=1, replica_groups=mesh['dp'=8,'expert'=4] {'expert'}, dimensions={0} | all-to-all | bytes 6291456 | tf_op jit(solution)/shard_map/all_to_all | solution.py:53
  96.2 5.8 %all-to-all-start = ((f32[4,192,1024]{2,1,0:T(8,128)}), f32[4,192,1024]{2,1,0:T(8,128)}, u32[]{:S(2)}, u32[]{:S(2)}) async-start(f32[4,192,1024]{2,1,0:T(8,128)} %get-tuple-element.23), calls=%async_computation | async-start | bytes 6291456 | tf_op jit(solution)/shard_map/all_to_all | solution.py:52
  102.0 14.4 %convolution_bitcast_fusion.1 = f32[1024,1024]{0,1:T(8,128)} fusion(f32[4,192,1024]{2,1,0:T(8,128)} %all_to_all.13), kind=kOutput, calls=%fused_computation.22 | convolution fusion | flops 9663676416 | bytes 7340032 | tf_op jit(solution)/shard_map/rc,rf->cf/dot_general | solution.py:12
  116.5 52.5 %all-to-all-done = f32[4,192,1024]{2,1,0:T(8,128)} async-done(((f32[4,192,1024]{2,1,0:T(8,128)}), f32[4,192,1024]{2,1,0:T(8,128)}, u32[]{:S(2)}, u32[]{:S(2)}) %all-to-all-start) | async-done | bytes 3145760 | tf_op jit(solution)/shard_map/all_to_all | solution.py:52
  169.0 13.0 %convolution_bitcast_fusion = f32[1024,1024]{0,1:T(8,128)S(1)} fusion(f32[4,192,1024]{2,1,0:T(8,128)} %all_to_all.13, f32[4,192,1024]{2,1,0:T(8,128)} %all-to-all-done), kind=kOutput, calls=%fused_computation.21 | convolution fusion | flops 9663676416 | bytes 10485760 | tf_op jit(solution)/shard_map/rc,rf->cf/dot_general | solution.py:12
  182.0 13.4 %convolution_bitcast_fusion.2 = f32[1024,1024]{0,1:T(8,128)S(1)} fusion(f32[4,192,1024]{2,1,0:T(8,128)} %all-to-all-done), kind=kOutput, calls=%fused_computation.23 | convolution fusion | flops 9663676416 | bytes 7340032 | tf_op jit(solution)/shard_map/rc,rf->cf/dot_general | solution.py:12
  195.4 5.6 %pad_maximum_fusion = f32[1024,3072]{0,1:T(8,128)} fusion(f32[1024,1024]{0,1:T(8,128)S(1)} %convolution_bitcast_fusion, f32[1024,1024]{0,1:T(8,128)S(1)} %copy-done.8, f32[1024,1024]{0,1:T(8,128)S(1)} %convolution_bitcast_fusion.2), kind=kLoop, calls=%fused_computation.2 | loop fusion | flops 6291456 | bytes 25165824 | tf_op jit(solution)/shard_map/concatenate | solution.py:65
  201.6 6.6 %all-to-all-start.2 = ((f32[4,1,192]{2,1,0:T(1,128)}), f32[4,1,192]{2,1,0:T(1,128)S(1)}, u32[]{:S(2)}, u32[]{:S(2)}) async-start(f32[4,1,192]{2,1,0:T(1,128)} %copy.46), calls=%async_computation.3 | async-start | bytes 8192 | tf_op jit(solution)/shard_map/all_to_all | solution.py:54
  210.3 14.4 %psum.7 = f32[1]{0:T(128)} all-reduce(f32[1]{0:T(128)} %bitcast.10), channel_id=1, replica_groups=mesh['dp'=8,'expert'=4] {'dp'}, use_global_device_ids=true, to_apply=%region_7.9 | all-reduce | flops 1 | bytes 8 | tf_op jit(solution)/shard_map/psum | solution.py:56
  225.3 71.3 %reduce-scatter.2.cloned.1.call-done = f32[128,3072]{0,1:T(8,128)} async-done(((f32[1024,3072]{0,1:T(8,128)}), f32[128,3072]{0,1:T(8,128)}) %reduce-scatter.2.cloned.1.call-update) | async-done | bytes 1572880 | tf_op jit(solution)/shard_map/reduce_scatter | solution.py:65
  304.3 32.7 %all-gather.7.cloned.1.call-done = f32[1,1024,1024]{1,2,0:T(8,128)} async-done(((f32[1,128,1024]{1,2,0:T(8,128)}), f32[1,1024,1024]{1,2,0:T(8,128)}) %all-gather.7.cloned.1.call-update) | async-done | bytes 4194320 | tf_op jit(solution)/shard_map/all_gather | solution.py:72
  337.0 2.9 fusion.2
  340.5 36.3 %all-gather.5.cloned.1.call-done = f32[1,1024,1024]{1,2,0:T(8,128)} async-done(((f32[1,128,1024]{1,2,0:T(8,128)}), f32[1,1024,1024]{1,2,0:T(8,128)}) %all-gather.5.cloned.1.call-update) | async-done | bytes 4194320 | tf_op jit(solution)/shard_map/all_gather | solution.py:73
  388.4 3.0 fusion
  391.9 4.6 %fusion.8 = f32[128,1024]{1,0:T(8,128)S(1)} fusion(f32[1,1024,1024]{1,2,0:T(8,128)S(1)} %copy-done.3, f32[]{:T(128)S(6)} %div.29, f32[1024,1024]{0,1:T(8,128)S(1)} %fusion, s32[]{:T(128)S(6)} %select_n.19), kind=kOutput, calls=%fused_computation.20 | convolution fusion | flops 1613758464 | bytes 5242888 | tf_op jit(solution)/shard_map/dot_general | solution.py:8
  396.5 3.4 convolution_subtract_fusion
  399.9 16.1 %all-gather.9.cloned.1.call-done = f32[1024,1024]{0,1:T(8,128)} async-done(((f32[128,1024]{0,1:T(8,128)}), f32[1024,1024]{0,1:T(8,128)}) %all-gather.9.cloned.1.call-update) | async-done | bytes 4194320 | tf_op jit(solution)/shard_map/all_gather | solution.py:74
  416.1 7.1 %fusion.43 = f32[128,1024]{1,0:T(8,128)S(1)} fusion(f32[128,1024]{0,1:T(8,128)S(1)} %convolution_subtract_fusion, f32[1024,1024]{0,1:T(8,128)} %all-gather.9.cloned.1.call-done), kind=kOutput, calls=%fused_computation.70 | convolution fusion | flops 1610612736 | bytes 5242880 | tf_op jit(solution)/shard_map/dot_general | solution.py:8
  423.2 4.6 %fusion.6 = f32[128,1024]{1,0:T(8,128)S(1)} fusion(f32[128,1024]{1,0:T(8,128)S(1)} %fusion.43, f32[]{:T(128)S(6)} %div.33, f32[1,1024,1024]{1,2,0:T(8,128)S(1)} %copy-done.4, f32[]{:T(128)S(6)} %div.32), kind=kOutput, calls=%fused_computation.19 | convolution fusion | flops 1617952768 | bytes 5242888 | tf_op jit(solution)/shard_map/dot_general | solution.py:8
  427.9 6.7 %fusion.17 = f32[128,1024]{1,0:T(8,128)S(1)} fusion(f32[128,1024]{1,0:T(8,128)S(1)} %fusion.6, f32[1,1024,1024]{1,2,0:T(8,128)} %all-gather.7.cloned.1.call-done, f32[]{:T(128)S(6)} %div.32), kind=kOutput, calls=%fused_computation.32 | convolution fusion | flops 1613758464 | bytes 5242884 | tf_op jit(solution)/shard_map/dot_general | solution.py:8
  434.6 3.4 fusion.21
  (69 shorter events, 26.1 us)
Async XLA Ops:
  7.2 3.7 copy-start
  10.8 3.7 copy-start.2
  96.2 72.7 %all-to-all-start = ((f32[4,192,1024]{2,1,0:T(8,128)}), f32[4,192,1024]{2,1,0:T(8,128)}, u32[]{:S(2)}, u32[]{:S(2)}) async-start(f32[4,192,1024]{2,1,0:T(8,128)} %get-tuple-element.23), calls=%async_computation | async-start | bytes 6291456 | tf_op jit(solution)/shard_map/all_to_all | solution.py:52
  102.0 194.6 %reduce-scatter.2.cloned.1.call-start = ((), (), s32[]{:S(2)}) async-start(), calls=%async_computation.4 | async-start | bytes 14155776 | tf_op jit(solution)/shard_map/reduce_scatter | solution.py:65
  182.0 13.4 %copy-start.8 = (f32[1024,1024]{0,1:T(8,128)S(1)}, f32[1024,1024]{0,1:T(8,128)}, u32[]{:S(2)}) copy-start(f32[1024,1024]{0,1:T(8,128)} %convolution_bitcast_fusion.1) | copy-start | bytes 12582916
  201.0 7.2 %copy-start.9 = (f32[1,128,1024]{2,1,0:T(8,128)S(1)}, f32[1,128,1024]{2,1,0:T(8,128)}, u32[]{:S(2)}) copy-start(f32[1,128,1024]{2,1,0:T(8,128)} %param.14) | copy-start | bytes 1572868
  201.0 7.4 %copy-start.10 = (f32[1,128,1024]{2,1,0:T(8,128)S(1)}, f32[1,128,1024]{2,1,0:T(8,128)}, u32[]{:S(2)}) copy-start(f32[1,128,1024]{2,1,0:T(8,128)} %param.15) | copy-start | bytes 1572868
  201.0 100.8 %copy-start.11 = (f32[1,128,1024]{2,1,0:T(8,128)S(1)}, f32[1,128,1024]{2,1,0:T(8,128)}, u32[]{:S(2)}) copy-start(f32[1,128,1024]{2,1,0:T(8,128)} %param.16) | copy-start | bytes 1572868
  201.6 8.0 %all-to-all-start.2 = ((f32[4,1,192]{2,1,0:T(1,128)}), f32[4,1,192]{2,1,0:T(1,128)S(1)}, u32[]{:S(2)}, u32[]{:S(2)}) async-start(f32[4,1,192]{2,1,0:T(1,128)} %copy.46), calls=%async_computation.3 | async-start | bytes 8192 | tf_op jit(solution)/shard_map/all_to_all | solution.py:54
  208.2 128.8 %all-gather.7.cloned.1.call-start = ((), (), s32[]{:S(2)}) async-start(), calls=%async_computation.6 | async-start | bytes 4718592 | tf_op jit(solution)/shard_map/all_gather | solution.py:72
  208.4 93.6 %copy-start.12 = (f32[1,128,1024]{2,1,0:T(8,128)S(1)}, f32[1,128,1024]{2,1,0:T(8,128)}, u32[]{:S(2)}) copy-start(f32[1,128,1024]{2,1,0:T(8,128)} %param.17) | copy-start | bytes 1572868
  298.9 3.4 copy-start.7
  298.9 4.4 copy-start.6
  298.9 78.0 %all-gather.5.cloned.1.call-start = ((), (), s32[]{:S(2)}) async-start(), calls=%async_computation.5 | async-start | bytes 4718592 | tf_op jit(solution)/shard_map/all_gather | solution.py:73
  299.7 116.4 %all-gather.9.cloned.1.call-start = ((), (), s32[]{:S(2)}) async-start(), calls=%async_computation.7 | async-start | bytes 4718592 | tf_op jit(solution)/shard_map/all_gather | solution.py:74
  388.4 3.5 copy-start.3
  416.1 7.1 %copy-start.4 = (f32[1,1024,1024]{1,2,0:T(8,128)S(1)}, f32[1,1024,1024]{1,2,0:T(8,128)}, u32[]{:S(2)}) copy-start(f32[1,1024,1024]{1,2,0:T(8,128)} %all-gather.7.cloned.1.call-done) | copy-start | bytes 12582916
  427.9 6.7 %copy-start.5 = (f32[1,1024,1024]{1,2,0:T(8,128)S(1)}, f32[1,1024,1024]{1,2,0:T(8,128)}, u32[]{:S(2)}) copy-start(f32[1,1024,1024]{1,2,0:T(8,128)} %all-gather.7.cloned.1.call-done) | copy-start | bytes 12582916
  434.6 5.5 %copy-start.1 = (f32[256,1024]{1,0:T(8,128)S(1)}, f32[256,1024]{1,0:T(8,128)}, u32[]{:S(2)}) copy-start(f32[256,1024]{1,0:T(8,128)} %param.10) | copy-start | bytes 3145732
Sparse Core Ops, SparseCore 0:
  201.1 95.4 reduce-scatter.1
  299.1 37.8 all-gather.6
  339.4 37.4 all-gather.4
  378.6 37.4 all-gather.8
where the time goes:
time: 455 us; the launch traced here: 447 us
  waiting for transfers between devices  211 us (46%)
  blocking collectives  87.4 us (19%)
  matrix products  70.6 us (16%)
  other arithmetic  34.2 us (8%)
  between operations  17.8 us (4%)
  local copies, waits for them, and re-layouts  13.7 us (3%)
  starting transfers between devices  12.7 us (3%)
    all_to_all x1, blocking collectives, on_device(): lax.all_to_all(sent_grads, 'expert', split_axis=0, concat_axis=1, tiled=T...  73 us
    reduce_scatter x1, waiting for transfers between devices, on_device(): lax.psum_scatter(jnp.concatenate(pieces, axis=1), 'dp', scatter_dimension...  71.3 us
    all_to_all x1, waiting for transfers between devices, on_device(): lax.all_to_all(sent_acts, 'expert', split_axis=0, concat_axis=1, tiled=True)  52.5 us
    dot_general x3, matrix products, inner_rows(): jnp.einsum('rc,rf->cf', left, right, precision=lax.Precision.HIGHEST, pre...  40.8 us
    all_gather x1, waiting for transfers between devices, on_device(): lax.all_gather(grad_factor, 'dp', axis=1, tiled=True)  36.3 us
    all_gather x1, waiting for transfers between devices, on_device(): lax.all_gather(act_factor, 'dp', axis=1, tiled=True)  32.7 us
    dot_general x6, matrix products, product(): jnp.dot(left, right, precision=lax.Precision.HIGHEST, preferred_element_t...  29.8 us
    all_gather x1, waiting for transfers between devices, on_device(): lax.all_gather(gradient_rows, 'dp', axis=1, tiled=True)  16.1 us
  transfers between devices with their start and end apart: 6, of which 6 were waited for; matrix products, arithmetic and copies ran while one was open for 10% of the time, Pallas kernels for 0%

commit v1 on v0

v1 whole, which is shorter than its diff:
```python
import functools

import jax
import jax.numpy as jnp
from jax import lax
from jax.experimental import pallas as pl
from jax.experimental.pallas import tpu as pltpu
from jax.sharding import PartitionSpec as P

F32 = jnp.float32
BF16 = jnp.bfloat16
TILE = 128
VMEM_LIMIT = 56 * 1024 * 1024


def split(value):
    high = value.astype(BF16)
    return high, (value - high.astype(F32)).astype(BF16)


def dot(left, right):
    return jnp.dot(left, right, preferred_element_type=F32)


def band_place(owner, block):
    per_tile = TILE // block
    if per_tile == 1:
        return pl.multiple_of(owner * TILE, TILE), 0
    return (
        pl.multiple_of(lax.div(owner, per_tile) * TILE, TILE),
        pl.multiple_of(lax.rem(owner, per_tile) * block, block),
    )


def split_rows(parts, high, low, feat):
    extra = high.shape[1] - feat
    for number, part in enumerate(parts):
        rows = part.shape[0]
        here = slice(number * rows, (number + 1) * rows)
        top, rest = split(part[...])
        high[here, 0:feat] = top
        low[here, 0:feat] = rest
        if extra:
            high[here, feat : feat + extra] = top[:, 0:extra]
            low[here, feat : feat + extra] = rest[:, 0:extra]


def left_rows(parts, turned, column, row, block):
    for number, part in enumerate(parts):
        rows = part.shape[0]
        turned[:, number * rows : (number + 1) * rows] = part[:, pl.ds(column, TILE)].T
    return turned[pl.ds(row, block), :]


def weighted(rows, weights, lanes):
    halves = [split(rows * weights[pl.ds(lane, 1), :]) for lane in lanes]
    tops = [half[0] for half in halves]
    return jnp.concatenate(tops + [half[1] for half in halves], axis=0), jnp.concatenate(tops, axis=0)


def act_kernel(turns, block, place, weights, *refs):
    parts, outs, (high, low, turned) = refs[:4], refs[4:-3], refs[-3:]
    feat = parts[0].shape[1]
    width = outs[0].shape[2]
    mine, expert = place[0], place[1]
    split_rows(parts, high, low, feat)
    lanes = [expert ^ (2 * turn) for turn in turns]
    for k, out in enumerate(outs):
        column, row = band_place(mine ^ (2 * k), block)
        both, tops = weighted(left_rows(parts, turned, column, row, block), weights, lanes)
        first = dot(both, high[:, pl.ds(column, width)])
        second = dot(tops, low[:, pl.ds(column, width)])
        half = len(turns) * block
        total = first[0:half] + first[half : 2 * half] + second
        for number in range(len(turns)):
            out[number] = total[number * block : (number + 1) * block]


def grad_kernel(turns, block, place, weights, *refs):
    grads, acts, outs = refs[:4], refs[4:8], refs[8:-5]
    high, low, act_high, act_low, turned = refs[-5:]
    feat = grads[0].shape[1]
    width = outs[0].shape[2] - feat
    mine, expert = place[0], place[1]
    split_rows(grads, high, low, feat)
    split_rows(acts, act_high, act_low, feat)
    lanes = [expert ^ (2 * turn) for turn in turns]
    half = len(turns) * block
    for k, out in enumerate(outs):
        column, row = band_place(mine ^ (2 * k), block)
        both, tops = weighted(left_rows(grads, turned, column, row, block), weights, lanes)
        first = dot(both, high[:, pl.ds(column, width)])
        second = dot(tops, low[:, pl.ds(column, width)])
        total = first[0:half] + first[half : 2 * half] + second
        first = dot(both, act_high[...])
        second = dot(tops, act_low[...])
        mixed = first[0:half] + first[half : 2 * half] + second
        for number in range(len(turns)):
            here = slice(number * block, (number + 1) * block)
            out[number, :, 0:width] = total[here]
            out[number, :, width : width + feat] = mixed[here]


def whole_in_vmem(count):
    return [pl.BlockSpec(memory_space=pltpu.VMEM)] * count


def act_bands(turns, place, weights, parts, chips, block, width):
    rows, feat = parts[0].shape
    return pl.pallas_call(
        functools.partial(act_kernel, turns, block),
        out_shape=[jax.ShapeDtypeStruct((len(turns), block, width), F32)] * chips,
        in_specs=[pl.BlockSpec(memory_space=pltpu.SMEM)] + whole_in_vmem(5),
        out_specs=whole_in_vmem(chips),
        scratch_shapes=[
            pltpu.VMEM((4 * rows, feat + width - TILE), BF16),
            pltpu.VMEM((4 * rows, feat + width - TILE), BF16),
            pltpu.VMEM((TILE, 4 * rows), F32),
        ],
        compiler_params=pltpu.CompilerParams(vmem_limit_bytes=VMEM_LIMIT),
    )(place, weights, *parts)


def grad_bands(turns, place, weights, grads, acts, chips, block, width):
    rows, feat = grads[0].shape
    return pl.pallas_call(
        functools.partial(grad_kernel, turns, block),
        out_shape=[jax.ShapeDtypeStruct((len(turns), block, width + feat), F32)] * chips,
        in_specs=[pl.BlockSpec(memory_space=pltpu.SMEM)] + whole_in_vmem(9),
        out_specs=whole_in_vmem(chips),
        scratch_shapes=[
            pltpu.VMEM((4 * rows, feat + width - TILE), BF16),
            pltpu.VMEM((4 * rows, feat + width - TILE), BF16),
            pltpu.VMEM((4 * rows, feat), BF16),
            pltpu.VMEM((4 * rows, feat), BF16),
            pltpu.VMEM((TILE, 4 * rows), F32),
        ],
        compiler_params=pltpu.CompilerParams(vmem_limit_bytes=VMEM_LIMIT),
    )(place, weights, *grads, *acts)


def unfold(bands, full):
    tiles = full.shape[0] // TILE
    for i in range(tiles):
        for step in range(tiles // 2 + 1):
            j = (i + step) % tiles
            here = bands[i * TILE : (i + 1) * TILE, step * TILE : (step + 1) * TILE]
            full[i * TILE : (i + 1) * TILE, j * TILE : (j + 1) * TILE] = here
            if 0 < step < tiles // 2:
                full[j * TILE : (j + 1) * TILE, i * TILE : (i + 1) * TILE] = here.T


def damping(full):
    size = full.shape[0]
    value = full[...]
    lanes = lax.broadcasted_iota(jnp.int32, (size, size), 1)
    sublanes = lax.broadcasted_iota(jnp.int32, (size, size), 0)
    trace = jnp.sum(jnp.sum(jnp.where(lanes == sublanes, value, 0.0), axis=0, keepdims=True), axis=1, keepdims=True)
    largest = jnp.max(jnp.sum(jnp.abs(value), axis=0, keepdims=True), axis=1, keepdims=True)
    damp = trace * (0.1 / size)
    return damp, 1.0 / (largest + damp)


def times(left, high, low):
    rows = left.shape[0]
    top, rest = split(left)
    first = dot(jnp.concatenate([top, rest], axis=0), high[...])
    return first[0:rows] + first[rows : 2 * rows] + dot(top, low[...])


def chain_kernel(devices, place, *refs):
    act_blocks, mixed_blocks = refs[:devices], refs[devices : 2 * devices]
    momentum, weights, act_out, grad_out, moment_out, weight_out = refs[2 * devices : 2 * devices + 6]
    bands, full, act_high, act_low, high, low, mid_high, mid_low = refs[2 * devices + 6 :]
    block, feat = momentum.shape
    width = act_blocks[0].shape[1]
    mine = place[0]
    own = pl.ds(pl.multiple_of(mine * block, block), block)
    here = [pl.ds(pl.multiple_of((mine ^ k) * block, block), block) for k in range(devices)]
    for k in range(devices):
        bands[here[k], :] = act_blocks[k][...]
    unfold(bands, full)
    act_out[...] = full[own, :]
    act_damp, act_alpha = damping(full)
    top, rest = split(full[...])
    act_high[...] = top
    act_low[...] = rest
    for k in range(devices):
        bands[here[k], :] = mixed_blocks[k][:, 0:width]
    unfold(bands, full)
    rows = full[own, :]
    grad_out[...] = rows
    damp, alpha = damping(full)
    top, rest = split(full[...])
    high[...] = top
    low[...] = rest
    for k in range(devices):
        top, rest = split(mixed_blocks[k][:, width : width + feat])
        mid_high[here[k], :] = top
        mid_low[here[k], :] = rest
    lanes = lax.broadcasted_iota(jnp.int32, (block, feat), 1)
    sublanes = lax.broadcasted_iota(jnp.int32, (block, feat), 0)
    unit = jnp.where(lanes == sublanes + mine * block, 1.0, 0.0).astype(F32)
    rest_rows = unit - alpha * (rows + damp * unit)
    once = 2.0 * rest_rows - alpha * (times(rest_rows, high, low) + damp * rest_rows)
    left = alpha * (unit + rest_rows + once - alpha * (times(once, high, low) + damp * once))
    half_way = times(left, mid_high, mid_low)
    value = half_way
    for _ in range(3):
        value = half_way + value - act_alpha * (times(value, act_high, act_low) + act_damp * value)
    moment = 0.9 * momentum[...] + act_alpha * value
    moment_out[...] = moment
    weight_out[...] = weights[...] - 0.5 * moment


def chain(place, act_blocks, mixed_blocks, momentum, weights):
    devices = len(act_blocks)
    block, feat = momentum.shape
    width = act_blocks[0].shape[1]
    square = (feat, feat)
    return pl.pallas_call(
        functools.partial(chain_kernel, devices),
        out_shape=[jax.ShapeDtypeStruct((block, feat), F32)] * 4,
        in_specs=[pl.BlockSpec(memory_space=pltpu.SMEM)] + whole_in_vmem(2 * devices + 2),
        out_specs=whole_in_vmem(4),
        scratch_shapes=[pltpu.VMEM((feat, width), F32), pltpu.VMEM(square, F32)]
        + [pltpu.VMEM(square, BF16)] * 6,
        compiler_params=pltpu.CompilerParams(vmem_limit_bytes=VMEM_LIMIT),
    )(place, *act_blocks, *mixed_blocks, momentum, weights)


def swap(value, axis, step):
    size = lax.axis_size(axis)
    return lax.ppermute(value, axis, [(i, i ^ step) for i in range(size)])


def kept_rows(routes, counts, experts):
    samples = routes.shape[0]
    ids = jnp.arange(experts, dtype=jnp.int32)
    hit = jnp.sum((routes.T[None, :, :] == ids[:, None, None]).astype(jnp.int32), axis=1, dtype=jnp.int32)
    before = jnp.triu(jnp.ones((samples, samples), BF16), 1)
    rank = dot(hit.astype(BF16), before)
    return jnp.where(rank < counts[0].astype(F32)[:, None], hit, 0).astype(F32)


def on_device(acts, grads_out, routes, counts, old_act_factor, old_grad_factor, momentum, weights):
    devices, experts = lax.axis_size("dp"), lax.axis_size("expert")
    chips = devices // 2
    feat, block = acts.shape[1], weights.shape[1]
    width = feat // 2 + TILE
    mine = lax.axis_index("dp")
    place = jnp.stack([mine, lax.axis_index("expert")]).astype(jnp.int32)

    keep = kept_rows(routes, counts, experts)
    acts_far, grads_far = swap(acts, "expert", 1), swap(grads_out, "expert", 1)
    keep = jnp.concatenate([keep, swap(keep, "expert", 1)], axis=1)
    keep = jnp.concatenate([keep, swap(keep, "dp", 1)], axis=1)
    total = lax.psum(jnp.sum(keep[:, 0 : acts.shape[0]], axis=1), ("dp", "expert"))
    total = jnp.maximum(lax.dynamic_slice_in_dim(total, lax.axis_index("expert"), 1), 1.0)
    act_parts = (acts, acts_far, swap(acts, "dp", 1), swap(acts_far, "dp", 1))
    grad_parts = (grads_out, grads_far, swap(grads_out, "dp", 1), swap(grads_far, "dp", 1))

    def to_owners(bands):
        total = bands[0]
        for k in range(1, chips):
            total = total + swap(bands[k], "dp", 2 * k)
        return total

    def own_band(old):
        start = mine * block // TILE * TILE
        wide = jnp.concatenate([old[0], old[0][:, 0 : width - TILE]], axis=1)
        return lax.dynamic_slice_in_dim(wide, start, width, 1)

    def across(near, far):
        for number in range(far.shape[0]):
            near = near + swap(far[number], "expert", 2 * (number + 1))
        return near

    def to_all(value):
        blocks = []
        for k in range(chips):
            blocks.append(swap(value, "dp", 2 * k) if k else value)
            blocks.append(swap(blocks[-1], "dp", 1))
        return blocks

    turns = tuple(range(experts // 2))
    act_sums = to_owners(act_bands(turns, place, keep, act_parts, chips, block, width))
    far_sums = to_owners(grad_bands(turns[1:], place, keep, grad_parts, act_parts, chips, block, width))
    near_sums = to_owners(grad_bands(turns[:1], place, keep, grad_parts, act_parts, chips, block, width))
    act_band = 0.5 * own_band(old_act_factor) + 0.5 * (across(act_sums[0], act_sums[1:]) / total[0])
    mixed = across(near_sums[0], far_sums) / total[0]
    mixed = jnp.concatenate(
        [0.5 * own_band(old_grad_factor) + 0.5 * mixed[:, 0:width], mixed[:, width:]], axis=1
    )
    outs = chain(place, to_all(act_band), to_all(mixed), momentum[0], weights[0])
    return tuple(out[None] for out in outs)


def solution(mesh):
    rows = P(("dp", "expert"), None)
    matrix = P("expert", "dp", None)
    return jax.shard_map(
        on_device,
        mesh=mesh,
        in_specs=(rows,) * 4 + (matrix,) * 4,
        out_specs=(matrix,) * 4,
        check_vma=False,
    )
```

time: 455 us -> 292 us (0.64); the launches traced: 447 us -> 290 us
  waiting for transfers between devices: 211 us -> 100 us
  matrix products: 70.6 us -> 0.25 us
  Pallas kernels: 0 us -> 45.5 us
  starting transfers between devices: 12.7 us -> 49.7 us
  other arithmetic: 34.2 us -> 6.8 us
  between operations: 17.8 us -> 1.58 us
  local copies, waits for them, and re-layouts: 13.7 us -> 3.83 us
  blocking collectives: 87.4 us -> 81.5 us
    ppermute x0 -> x33, waiting for transfers between devices: none -> 100 us  [swap(): return lax.ppermute(value, axis, [(i, i ^ step) for i in range(size)])]
    all_gather x3 -> x0, waiting for transfers between devices: 85.2 us -> none  [the longest x1 36.3 us: on_device(): lax.all_gather(grad_factor, 'dp', axis=1, tiled=True)]
    all_to_all x1 -> x0, blocking collectives: 73 us -> none  [on_device(): lax.all_to_all(sent_grads, 'expert', split_axis=0, concat_axis=1, tiled=T...]
    reduce_scatter x1 -> x0, waiting for transfers between devices: 71.3 us -> none  [on_device(): lax.psum_scatter(jnp.concatenate(pieces, axis=1), 'dp', scatter_dimension...]
    dot_general x9 -> x1, matrix products: 70.6 us -> 0.25 us  [dot(): return jnp.dot(left, right, preferred_element_type=F32)]
    psum x1, blocking collectives: 14.4 us -> 81.5 us  [on_device(): lax.psum(jnp.sum(keep[:, 0:acts.shape[0]], axis=1), ('dp', 'expert'))]
    all_to_all x2 -> x0, waiting for transfers between devices: 53.5 us -> none  [the longest x1 52.5 us: on_device(): lax.all_to_all(sent_acts, 'expert', split_axis=0, concat_axis=1, tiled=True)]
    ppermute x0 -> x33, starting transfers between devices: none -> 49.7 us  [swap(): return lax.ppermute(value, axis, [(i, i ^ step) for i in range(size)])]
  transfers between devices with their start and end apart: 6 -> 33, of which waited for: 6 -> 10; matrix products, arithmetic and copies ran while one was open for 10% -> 3% of each run, Pallas kernels for 0% -> 7%
where the time goes in v1:
time: 292 us; the launch traced here: 290 us
  waiting for transfers between devices  100 us (34%)
  blocking collectives  81.5 us (28%)
  starting transfers between devices  49.7 us (17%)
  Pallas kernels  45.5 us (16%)
  other arithmetic  6.8 us (2%)
  local copies, waits for them, and re-layouts  3.83 us (1%)
    ppermute x33, waiting for transfers between devices, swap(): return lax.ppermute(value, axis, [(i, i ^ step) for i in range(size)])  100 us
    psum x1, blocking collectives, on_device(): lax.psum(jnp.sum(keep[:, 0:acts.shape[0]], axis=1), ('dp', 'expert'))  81.5 us
    ppermute x33, starting transfers between devices, swap(): return lax.ppermute(value, axis, [(i, i ^ step) for i in range(size)])  49.7 us
    pallas_call x2, Pallas kernels, grad_bands(): pl.pallas_call(functools.partial(grad_kernel, turns, block), out_shape=[j...  22.6 us
    pallas_call x1, Pallas kernels, chain(): pl.pallas_call(functools.partial(chain_kernel, devices), out_shape=[jax.S...  13.6 us
    pallas_call x1, Pallas kernels, act_bands(): pl.pallas_call(functools.partial(act_kernel, turns, block), out_shape=[ja...  9.29 us
  transfers between devices with their start and end apart: 33, of which 10 were waited for; matrix products, arithmetic and copies ran while one was open for 3% of the time, Pallas kernels for 7%

profile of v1, /device:TPU:25, one launch (start us, length us, event | category | flops | bytes accessed | tf_op | source)
XLA Modules:
  0.0 289.6 jit_solution(3754637390590395345)
XLA Ops:
  0.9 1.3 collective-permute-start.16
  3.4 21.5 %collective-permute-done.2.refs_1_.refs_5_ = f32[256,1024]{1,0:T(8,128)S(1)} collective-permute-done((f32[256,1024]{1,0:T(8,128)}, f32[256,1024]{1,0:T(8,128)S(1)}, u32[]{:S(2)}, u32[]{:S(2)}) %collective-permute-start.2) | collective-permute-done | bytes 1048608 | tf_op jit(solution)/shard_map/ppermute | solution.py:234
  24.9 2.7 collective-permute-start.4
  27.6 19.9 %collective-permute-done.16.refs_1_ = f32[256,1024]{1,0:T(8,128)} collective-permute-done((f32[256,1024]{1,0:T(8,128)}, f32[256,1024]{1,0:T(8,128)}, u32[]{:S(2)}, u32[]{:S(2)}) %collective-permute-start.16) | collective-permute-done | bytes 1048608 | tf_op jit(solution)/shard_map/ppermute | solution.py:234
  47.5 1.5 collective-permute-start.18
  50.3 2.3 collective-permute-done
  56.5 11.3 %shard_map.113 = (f32[1,128,1664]{2,1,0:T(8,128)}, f32[1,128,1664]{2,1,0:T(8,128)}, f32[1,128,1664]{2,1,0:T(8,128)}, f32[1,128,1664]{2,1,0:T(8,128)}) custom-call(s32[2]{0:T(128)} %pad_add_fusion.place, f32[4,1024]{1,0:T(4,128)} %pad_maximum_fusion.1.weights, f32[256,1024]{1,0:T(8,128)} %refs_0_.5, f32[256,1024]{1,0:T(8,128)} %collective-permute-done.16.refs_1_, ...), custom_call_target="tpu_custom_call" | custom-call | tf_op jit(solution)/shard_map/pallas_call | solution.py:126
  70.5 9.3 %shard_map.111 = (f32[2,128,640]{2,1,0:T(8,128)}, f32[2,128,640]{2,1,0:T(8,128)}, f32[2,128,640]{2,1,0:T(8,128)}, f32[2,128,640]{2,1,0:T(8,128)}) custom-call(s32[2]{0:T(128)} %pad_add_fusion.place, f32[4,1024]{1,0:T(4,128)} %pad_maximum_fusion.1.weights, f32[256,1024]{1,0:T(8,128)} %refs_4_.3, f32[256,1024]{1,0:T(8,128)} %copy-done, f32[256,1024]{1,0:T(8,128)} %copy-done.1, ...), custom_call_target="tpu_custom_call" | custom-call | tf_op jit(solution)/shard_map/pallas_call | solution.py:110
  82.2 11.3 %shard_map.112 = (f32[1,128,1664]{2,1,0:T(8,128)}, f32[1,128,1664]{2,1,0:T(8,128)}, f32[1,128,1664]{2,1,0:T(8,128)}, f32[1,128,1664]{2,1,0:T(8,128)}) custom-call(s32[2]{0:T(128)} %pad_add_fusion.place, f32[4,1024]{1,0:T(4,128)} %pad_maximum_fusion.1.weights, f32[256,1024]{1,0:T(8,128)} %refs_0_.5, f32[256,1024]{1,0:T(8,128)} %collective-permute-done.16.refs_1_, ...), custom_call_target="tpu_custom_call" | custom-call | tf_op jit(solution)/shard_map/pallas_call | solution.py:126
  93.7 14.2 %collective-permute-start.20 = (f32[1,128,1664]{2,1,0:T(8,128)}, f32[1,128,1664]{2,1,0:T(8,128)S(1)}, u32[]{:S(2)}, u32[]{:S(2)}) collective-permute-start(f32[1,128,1664]{2,1,0:T(8,128)} %get-tuple-element.26), channel_id=1, source_target_pairs={{0,16},{4,20},{8,24},{12,28},{16,0},{20,4},{24,8},{28,12},{1,17},{... | collective-permute-start | bytes 2555912 | tf_op jit(solution)/shard_map/ppermute | solution.py:234
  109.7 11.0 %collective-permute-done.5 = f32[2,128,640]{2,1,0:T(8,128)} collective-permute-done((f32[2,128,640]{2,1,0:T(8,128)}, f32[2,128,640]{2,1,0:T(8,128)}, u32[]{:S(2)}, u32[]{:S(2)}) %collective-permute-start.5) | collective-permute-done | bytes 655392 | tf_op jit(solution)/shard_map/ppermute | solution.py:234
  120.7 2.1 collective-permute-start.21
  122.9 81.5 %psum.7 = f32[4]{0:T(128)S(1)} all-reduce(f32[4]{0:T(128)S(1)} %get-tuple-element.36), channel_id=1, replica_groups=mesh['dp'=8,'expert'=4] {'dp','expert'}, use_global_device_ids=true, to_apply=%region_2.3 | all-reduce | flops 4 | bytes 32 | tf_op jit(solution)/shard_map/psum | solution.py:258
  205.7 1.9 add_add_fusion
  208.7 1.7 fusion.2
  211.8 1.2 collective-permute-start.29
  213.4 11.8 %collective-permute-done.8 = f32[128,640]{1,0:T(8,128)S(1)} collective-permute-done((f32[128,640]{1,0:T(8,128)S(1)}, f32[128,640]{1,0:T(8,128)S(1)}, u32[]{:S(2)}, u32[]{:S(2)}) %collective-permute-start.8) | collective-permute-done | bytes 327712 | tf_op jit(solution)/shard_map/ppermute | solution.py:234
  226.4 1.2 collective-permute-start.12
  227.6 26.9 %collective-permute-done.10.refs_2_ = f32[128,640]{1,0:T(8,128)S(1)} collective-permute-done((f32[128,640]{1,0:T(8,128)S(1)}, f32[128,640]{1,0:T(8,128)S(1)}, u32[]{:S(2)}, u32[]{:S(2)}) %collective-permute-start.10) | collective-permute-done | bytes 327712 | tf_op jit(solution)/shard_map/ppermute | solution.py:234
  254.5 2.3 collective-permute-start.14
  256.8 7.7 %collective-permute-start.9 = (f32[128,640]{1,0:T(8,128)S(1)}, f32[128,640]{1,0:T(8,128)}, u32[]{:S(2)}, u32[]{:S(2)}) collective-permute-start(f32[128,640]{1,0:T(8,128)S(1)} %fusion.8.refs_0_), channel_id=1, source_target_pairs={{0,4},{4,0},{8,12},{12,8},{16,20},{20,16},{24,28},{28,24},{1,5},{5... | collective-permute-start | bytes 983048 | tf_op jit(solution)/shard_map/ppermute | solution.py:234
  267.3 5.1 %collective-permute-done.13.refs_5_ = f32[128,640]{1,0:T(8,128)S(1)} collective-permute-done((f32[128,640]{1,0:T(8,128)S(1)}, f32[128,640]{1,0:T(8,128)S(1)}, u32[]{:S(2)}, u32[]{:S(2)}) %collective-permute-start.13) | collective-permute-done | bytes 327712 | tf_op jit(solution)/shard_map/ppermute | solution.py:234
  272.8 1.3 collective-permute-done.15.refs_7_
  275.9 13.6 %shard_map.114 = (f32[128,1024]{1,0:T(8,128)}, f32[128,1024]{1,0:T(8,128)}, f32[128,1024]{1,0:T(8,128)}, f32[128,1024]{1,0:T(8,128)}) custom-call(s32[2]{0:T(128)} %pad_add_fusion.place, f32[128,640]{1,0:T(8,128)} %copy-done.4, f32[128,640]{1,0:T(8,128)} %collective-permute-done.9.refs_1_, f32[128,640]{1,0:T(8,128)} %copy-done.16, f32[128,640]{1,0:T(8,128)} %copy-done.19, ...), custom_call_target="tpu_custom_call" | custom-call | tf_op jit(solution)/shard_map/pallas_call | solution.py:221
  (110 shorter events, 23.3 us)
Async XLA Ops:
  0.6 24.3 %collective-permute-start.2 = (f32[256,1024]{1,0:T(8,128)}, f32[256,1024]{1,0:T(8,128)S(1)}, u32[]{:S(2)}, u32[]{:S(2)}) collective-permute-start(f32[256,1024]{1,0:T(8,128)} %refs_4_.3), channel_id=1, source_target_pairs={{0,1},{1,0},{2,3},{3,2},{4,5},{5,4},{6,7},{7,6},{8,9},{9,8},{10,11... | collective-permute-start | bytes 3145736 | tf_op jit(solution)/shard_map/ppermute | solution.py:234
  0.9 46.6 %collective-permute-start.16 = (f32[256,1024]{1,0:T(8,128)}, f32[256,1024]{1,0:T(8,128)}, u32[]{:S(2)}, u32[]{:S(2)}) collective-permute-start(f32[256,1024]{1,0:T(8,128)} %refs_0_.5), channel_id=1, source_target_pairs={{0,1},{1,0},{2,3},{3,2},{4,5},{5,4},{6,7},{7,6},{8,9},{9,8},{10,11... | collective-permute-start | bytes 3145736 | tf_op jit(solution)/shard_map/ppermute | solution.py:234
  2.2 53.0 %collective-permute-start.3 = (f32[256,1024]{1,0:T(8,128)}, f32[256,1024]{1,0:T(8,128)S(1)}, u32[]{:S(2)}, u32[]{:S(2)}) collective-permute-start(f32[256,1024]{1,0:T(8,128)} %refs_4_.3), channel_id=1, source_target_pairs={{0,4},{4,0},{8,12},{12,8},{16,20},{20,16},{24,28},{28,24},{1,5},{5... | collective-permute-start | bytes 3145736 | tf_op jit(solution)/shard_map/ppermute | solution.py:234
  3.4 51.8 %collective-permute-start.17 = (f32[256,1024]{1,0:T(8,128)}, f32[256,1024]{1,0:T(8,128)}, u32[]{:S(2)}, u32[]{:S(2)}) collective-permute-start(f32[256,1024]{1,0:T(8,128)} %refs_0_.5), channel_id=1, source_target_pairs={{0,4},{4,0},{8,12},{12,8},{16,20},{20,16},{24,28},{28,24},{1,5},{5... | collective-permute-start | bytes 3145736 | tf_op jit(solution)/shard_map/ppermute | solution.py:234
  24.9 30.2 %collective-permute-start.4 = (f32[256,1024]{1,0:T(8,128)S(1)}, f32[256,1024]{1,0:T(8,128)S(1)}, u32[]{:S(2)}, u32[]{:S(2)}) collective-permute-start(f32[256,1024]{1,0:T(8,128)S(1)} %collective-permute-done.2.refs_1_.refs_5_), channel_id=1, source_target_pairs={{0,4},{4,0},{8,12},{12,8},{16,20},{20,16},{24,28},{28,24},{1,5},{5... | collective-permute-start | bytes 3145736 | tf_op jit(solution)/shard_map/ppermute | solution.py:234
  67.8 25.7 %collective-permute-start.22 = (f32[1,128,1664]{2,1,0:T(8,128)}, f32[1,128,1664]{2,1,0:T(8,128)S(1)}, u32[]{:S(2)}, u32[]{:S(2)}) collective-permute-start(f32[1,128,1664]{2,1,0:T(8,128)} %get-tuple-element.29), channel_id=1, source_target_pairs={{0,8},{4,12},{8,0},{12,4},{16,24},{20,28},{24,16},{28,20},{1,9},{5... | collective-permute-start | bytes 2555912 | tf_op jit(solution)/shard_map/ppermute | solution.py:234
  69.0 24.7 %collective-permute-start.23 = (f32[1,128,1664]{2,1,0:T(8,128)}, f32[1,128,1664]{2,1,0:T(8,128)S(1)}, u32[]{:S(2)}, u32[]{:S(2)}) collective-permute-start(f32[1,128,1664]{2,1,0:T(8,128)} %get-tuple-element.30), channel_id=1, source_target_pairs={{0,16},{4,20},{8,24},{12,28},{16,0},{20,4},{24,8},{28,12},{1,17},{... | collective-permute-start | bytes 2555912 | tf_op jit(solution)/shard_map/ppermute | solution.py:234
  70.3 37.7 %collective-permute-start.24 = (f32[1,128,1664]{2,1,0:T(8,128)}, f32[1,128,1664]{2,1,0:T(8,128)S(1)}, u32[]{:S(2)}, u32[]{:S(2)}) collective-permute-start(f32[1,128,1664]{2,1,0:T(8,128)} %get-tuple-element.31), channel_id=1, source_target_pairs={{0,24},{4,28},{8,16},{12,20},{16,8},{20,12},{24,0},{28,4},{1,25},{... | collective-permute-start | bytes 2555912 | tf_op jit(solution)/shard_map/ppermute | solution.py:234
  79.8 40.9 %collective-permute-start.5 = (f32[2,128,640]{2,1,0:T(8,128)}, f32[2,128,640]{2,1,0:T(8,128)}, u32[]{:S(2)}, u32[]{:S(2)}) collective-permute-start(f32[2,128,640]{2,1,0:T(8,128)} %get-tuple-element.21), channel_id=1, source_target_pairs={{0,8},{4,12},{8,0},{12,4},{16,24},{20,28},{24,16},{28,20},{1,9},{5... | collective-permute-start | bytes 1966088 | tf_op jit(solution)/shard_map/ppermute | solution.py:234
  81.0 41.9 %collective-permute-start.6 = (f32[2,128,640]{2,1,0:T(8,128)}, f32[2,128,640]{2,1,0:T(8,128)}, u32[]{:S(2)}, u32[]{:S(2)}) collective-permute-start(f32[2,128,640]{2,1,0:T(8,128)} %get-tuple-element.22), channel_id=1, source_target_pairs={{0,16},{4,20},{8,24},{12,28},{16,0},{20,4},{24,8},{28,12},{1,17},{... | collective-permute-start | bytes 1966088 | tf_op jit(solution)/shard_map/ppermute | solution.py:234
  93.5 115.2 %collective-permute-start.19 = (f32[1,128,1664]{2,1,0:T(8,128)}, f32[1,128,1664]{2,1,0:T(8,128)S(1)}, u32[]{:S(2)}, u32[]{:S(2)}) collective-permute-start(f32[1,128,1664]{2,1,0:T(8,128)} %get-tuple-element.25), channel_id=1, source_target_pairs={{0,8},{4,12},{8,0},{12,4},{16,24},{20,28},{24,16},{28,20},{1,9},{5... | collective-permute-start | bytes 2555912 | tf_op jit(solution)/shard_map/ppermute | solution.py:234
  93.7 115.0 %collective-permute-start.20 = (f32[1,128,1664]{2,1,0:T(8,128)}, f32[1,128,1664]{2,1,0:T(8,128)S(1)}, u32[]{:S(2)}, u32[]{:S(2)}) collective-permute-start(f32[1,128,1664]{2,1,0:T(8,128)} %get-tuple-element.26), channel_id=1, source_target_pairs={{0,16},{4,20},{8,24},{12,28},{16,0},{20,4},{24,8},{28,12},{1,17},{... | collective-permute-start | bytes 2555912 | tf_op jit(solution)/shard_map/ppermute | solution.py:234
  108.0 97.7 %collective-permute-start.7 = (f32[2,128,640]{2,1,0:T(8,128)}, f32[2,128,640]{2,1,0:T(8,128)}, u32[]{:S(2)}, u32[]{:S(2)}) collective-permute-start(f32[2,128,640]{2,1,0:T(8,128)} %get-tuple-element.23), channel_id=1, source_target_pairs={{0,24},{4,28},{8,16},{12,20},{16,8},{20,12},{24,0},{28,4},{1,25},{... | collective-permute-start | bytes 1966088 | tf_op jit(solution)/shard_map/ppermute | solution.py:234
  120.7 88.0 %collective-permute-start.21 = (f32[1,128,1664]{2,1,0:T(8,128)}, f32[1,128,1664]{2,1,0:T(8,128)}, u32[]{:S(2)}, u32[]{:S(2)}) collective-permute-start(f32[1,128,1664]{2,1,0:T(8,128)} %get-tuple-element.27), channel_id=1, source_target_pairs={{0,24},{4,28},{8,16},{12,20},{16,8},{20,12},{24,0},{28,4},{1,25},{... | collective-permute-start | bytes 2555912 | tf_op jit(solution)/shard_map/ppermute | solution.py:234
  122.8 85.9 %collective-permute-start.25 = (f32[128,1664]{1,0:T(8,128)}, f32[128,1664]{1,0:T(8,128)}, u32[]{:S(2)}, u32[]{:S(2)}) collective-permute-start(f32[128,1664]{1,0:T(8,128)} %add_bitcast_fusion), channel_id=1, source_target_pairs={{0,2},{1,3},{2,0},{3,1},{4,6},{5,7},{6,4},{7,5},{8,10},{9,11},{10,... | collective-permute-start | bytes 2555912 | tf_op jit(solution)/shard_map/ppermute | solution.py:234
  207.7 17.5 %collective-permute-start.8 = (f32[128,640]{1,0:T(8,128)S(1)}, f32[128,640]{1,0:T(8,128)S(1)}, u32[]{:S(2)}, u32[]{:S(2)}) collective-permute-start(f32[128,640]{1,0:T(8,128)S(1)} %slice_bitcast_fusion), channel_id=1, source_target_pairs={{0,2},{1,3},{2,0},{3,1},{4,6},{5,7},{6,4},{7,5},{8,10},{9,11},{10,... | collective-permute-start | bytes 983048 | tf_op jit(solution)/shard_map/ppermute | solution.py:234
  210.7 55.6 %collective-permute-start.27 = (f32[128,1664]{1,0:T(8,128)S(1)}, f32[128,1664]{1,0:T(8,128)S(1)}, u32[]{:S(2)}, u32[]{:S(2)}) collective-permute-start(f32[128,1664]{1,0:T(8,128)S(1)} %pad_maximum_fusion.refs_8_), channel_id=1, source_target_pairs={{0,8},{4,12},{8,0},{12,4},{16,24},{20,28},{24,16},{28,20},{1,9},{5... | collective-permute-start | bytes 2555912 | tf_op jit(solution)/shard_map/ppermute | solution.py:234
  211.8 54.7 %collective-permute-start.29 = (f32[128,1664]{1,0:T(8,128)S(1)}, f32[128,1664]{1,0:T(8,128)S(1)}, u32[]{:S(2)}, u32[]{:S(2)}) collective-permute-start(f32[128,1664]{1,0:T(8,128)S(1)} %pad_maximum_fusion.refs_8_), channel_id=1, source_target_pairs={{0,16},{4,20},{8,24},{12,28},{16,0},{20,4},{24,8},{28,12},{1,17},{... | collective-permute-start | bytes 2555912 | tf_op jit(solution)/shard_map/ppermute | solution.py:234
  213.0 53.8 %collective-permute-start.31 = (f32[128,1664]{1,0:T(8,128)S(1)}, f32[128,1664]{1,0:T(8,128)S(1)}, u32[]{:S(2)}, u32[]{:S(2)}) collective-permute-start(f32[128,1664]{1,0:T(8,128)S(1)} %pad_maximum_fusion.refs_8_), channel_id=1, source_target_pairs={{0,24},{4,28},{8,16},{12,20},{16,8},{20,12},{24,0},{28,4},{1,25},{... | collective-permute-start | bytes 2555912 | tf_op jit(solution)/shard_map/ppermute | solution.py:234
  225.3 29.2 %collective-permute-start.10 = (f32[128,640]{1,0:T(8,128)S(1)}, f32[128,640]{1,0:T(8,128)S(1)}, u32[]{:S(2)}, u32[]{:S(2)}) collective-permute-start(f32[128,640]{1,0:T(8,128)S(1)} %fusion.8.refs_0_), channel_id=1, source_target_pairs={{0,8},{4,12},{8,0},{12,4},{16,24},{20,28},{24,16},{28,20},{1,9},{5... | collective-permute-start | bytes 983048 | tf_op jit(solution)/shard_map/ppermute | solution.py:234
  226.4 30.4 %collective-permute-start.12 = (f32[128,640]{1,0:T(8,128)S(1)}, f32[128,640]{1,0:T(8,128)S(1)}, u32[]{:S(2)}, u32[]{:S(2)}) collective-permute-start(f32[128,640]{1,0:T(8,128)S(1)} %fusion.8.refs_0_), channel_id=1, source_target_pairs={{0,16},{4,20},{8,24},{12,28},{16,0},{20,4},{24,8},{28,12},{1,17},{... | collective-permute-start | bytes 983048 | tf_op jit(solution)/shard_map/ppermute | solution.py:234
  254.5 10.0 %collective-permute-start.14 = (f32[128,640]{1,0:T(8,128)S(1)}, f32[128,640]{1,0:T(8,128)S(1)}, u32[]{:S(2)}, u32[]{:S(2)}) collective-permute-start(f32[128,640]{1,0:T(8,128)S(1)} %fusion.8.refs_0_), channel_id=1, source_target_pairs={{0,24},{4,28},{8,16},{12,20},{16,8},{20,12},{24,0},{28,4},{1,25},{... | collective-permute-start | bytes 983048 | tf_op jit(solution)/shard_map/ppermute | solution.py:234
  256.8 9.1 %collective-permute-start.9 = (f32[128,640]{1,0:T(8,128)S(1)}, f32[128,640]{1,0:T(8,128)}, u32[]{:S(2)}, u32[]{:S(2)}) collective-permute-start(f32[128,640]{1,0:T(8,128)S(1)} %fusion.8.refs_0_), channel_id=1, source_target_pairs={{0,4},{4,0},{8,12},{12,8},{16,20},{20,16},{24,28},{28,24},{1,5},{5... | collective-permute-start | bytes 983048 | tf_op jit(solution)/shard_map/ppermute | solution.py:234
  265.9 8.1 %collective-permute-start.26 = (f32[128,1664]{1,0:T(8,128)S(1)}, f32[128,1664]{1,0:T(8,128)S(1)}, u32[]{:S(2)}, u32[]{:S(2)}) collective-permute-start(f32[128,1664]{1,0:T(8,128)S(1)} %pad_maximum_fusion.refs_8_), channel_id=1, source_target_pairs={{0,4},{4,0},{8,12},{12,8},{16,20},{20,16},{24,28},{28,24},{1,5},{5... | collective-permute-start | bytes 2555912 | tf_op jit(solution)/shard_map/ppermute | solution.py:234
  (32 other events, 492.3 us)

commit v2 on v1

v2 whole, which is shorter than its diff:
```python
import functools
import math

import jax
import jax.numpy as jnp
from jax import lax
from jax.experimental import pallas as pl
from jax.experimental.pallas import tpu as pltpu
from jax.sharding import PartitionSpec as P

F32 = jnp.float32
BF16 = jnp.bfloat16
TILE = 128
VMEM_LIMIT = 56 * 1024 * 1024


def split(value):
    high = value.astype(BF16)
    return high, (value - high.astype(F32)).astype(BF16)


def dot(left, right):
    return jnp.dot(left, right, preferred_element_type=F32)


def band_place(owner, block):
    per_tile = TILE // block
    if per_tile == 1:
        return pl.multiple_of(owner * TILE, TILE), 0
    return (
        pl.multiple_of(lax.div(owner, per_tile) * TILE, TILE),
        pl.multiple_of(lax.rem(owner, per_tile) * block, block),
    )


def split_rows(parts, high, low, feat):
    extra = high.shape[1] - feat
    for number, part in enumerate(parts):
        rows = part.shape[0]
        here = slice(number * rows, (number + 1) * rows)
        top, rest = split(part[...])
        high[here, 0:feat] = top
        low[here, 0:feat] = rest
        if extra:
            high[here, feat : feat + extra] = top[:, 0:extra]
            low[here, feat : feat + extra] = rest[:, 0:extra]


def left_rows(parts, turned, column, row, block):
    for number, part in enumerate(parts):
        rows = part.shape[0]
        turned[:, number * rows : (number + 1) * rows] = part[:, pl.ds(column, TILE)].T
    return turned[pl.ds(row, block), :]


def weighted(rows, weights, lanes):
    halves = [split(rows * weights[pl.ds(lane, 1), :]) for lane in lanes]
    tops = [half[0] for half in halves]
    return jnp.concatenate(tops + [half[1] for half in halves], axis=0), jnp.concatenate(tops, axis=0)


def three(both, tops, high, low):
    half = tops.shape[0]
    first = dot(both, high)
    return first[0:half] + first[half : 2 * half] + dot(tops, low)


def orders(chips):
    bits = list(range(chips.bit_length() - 1))
    return bits, bits[1:] + bits[:1]


def held_and_sent(chips, order):
    if not order:
        return [0], []
    held = [k for k in range(chips) if not (k >> order[0]) & 1]
    return held, [k | (1 << order[0]) for k in held]


def slots(chips):
    places = {}
    for half, order in enumerate(orders(chips)):
        for which, group in enumerate(held_and_sent(chips, order)):
            for position, k in enumerate(group):
                places[k, half] = (2 * half + which, position)
    return places


def store(outs, seeds, place, number, columns, value):
    output, position = place
    if seeds:
        value = value + seeds[output][position, number, :, columns]
    outs[output][position, number, :, columns] = value


def act_kernel(turns, block, chips, seeded, place, weights, *refs):
    parts, refs = refs[:2], refs[2:]
    seeds, refs = (refs[:4], refs[4:]) if seeded else ((), refs)
    outs, (high, low, turned) = refs[:4], refs[4:]
    feat = parts[0].shape[1]
    width = outs[0].shape[3]
    mine, expert = place[0], place[1]
    split_rows(parts, high, low, feat)
    lanes = [expert ^ (2 * turn) for turn in turns]
    places = slots(chips)
    rows = lax.broadcasted_iota(jnp.int32, (block, width), 0)
    columns = lax.broadcasted_iota(jnp.int32, (block, width), 1)
    corner = jnp.logical_and(rows == block - 1, columns == 0)
    for k in range(chips):
        column, row = band_place(mine ^ (2 * k), block)
        both, tops = weighted(left_rows(parts, turned, column, row, block), weights, lanes)
        total = three(both, tops, high[:, pl.ds(column, width)], low[:, pl.ds(column, width)])
        for number, lane in enumerate(lanes):
            count = jnp.sum(weights[pl.ds(lane, 1), :], axis=1, keepdims=True)
            value = jnp.where(corner, count, total[number * block : (number + 1) * block])
            for half in range(2):
                here = value[half * (block // 2) : (half + 1) * (block // 2)]
                store(outs, seeds, places[k, half], number, slice(0, width), here)


def grad_kernel(turns, block, chips, seeded, place, weights, *refs):
    grads, acts, refs = refs[:2], refs[2:4], refs[4:]
    seeds, refs = (refs[:4], refs[4:]) if seeded else ((), refs)
    outs, (high, low, act_high, act_low, turned) = refs[:4], refs[4:]
    feat = grads[0].shape[1]
    width = outs[0].shape[3] - feat
    mine, expert = place[0], place[1]
    split_rows(grads, high, low, feat)
    split_rows(acts, act_high, act_low, feat)
    lanes = [expert ^ (2 * turn) for turn in turns]
    places = slots(chips)
    for k in range(chips):
        column, row = band_place(mine ^ (2 * k), block)
        both, tops = weighted(left_rows(grads, turned, column, row, block), weights, lanes)
        total = three(both, tops, high[:, pl.ds(column, width)], low[:, pl.ds(column, width)])
        mixed = three(both, tops, act_high[...], act_low[...])
        for number in range(len(lanes)):
            for half in range(2):
                first = number * block + half * (block // 2)
                here = slice(first, first + block // 2)
                store(outs, seeds, places[k, half], number, slice(0, width), total[here])
                store(outs, seeds, places[k, half], number, slice(width, width + feat), mixed[here])


def whole_in_vmem(count):
    return [pl.BlockSpec(memory_space=pltpu.VMEM)] * count


def cost(flops, *arrays):
    size = sum(4 * math.prod(array.shape) for array in arrays)
    return pl.CostEstimate(flops=flops, bytes_accessed=size, transcendentals=0)


def bands(body, turns, place, weights, parts, seeds, chips, block, width):
    rows, feat = parts[0].shape
    extended = pltpu.VMEM((2 * rows, feat + feat // 2), BF16)
    plain = pltpu.VMEM((2 * rows, feat), BF16)
    scratch = [extended, extended] + ([plain, plain] if len(parts) > 2 else [])
    shapes = [
        jax.ShapeDtypeStruct((len(group), len(turns), block // 2, width), F32)
        for order in orders(chips)
        for group in held_and_sent(chips, order)
    ]
    operands = (weights, *parts, *seeds)
    return pl.pallas_call(
        functools.partial(body, turns, block, chips, bool(seeds)),
        out_shape=shapes,
        in_specs=[pl.BlockSpec(memory_space=pltpu.SMEM)] + whole_in_vmem(len(operands)),
        out_specs=whole_in_vmem(4),
        scratch_shapes=scratch + [pltpu.VMEM((TILE, 2 * rows), F32)],
        cost_estimate=cost(12 * rows * chips * block * width * len(turns), *operands, *shapes),
        compiler_params=pltpu.CompilerParams(vmem_limit_bytes=VMEM_LIMIT),
    )(place, *operands)


def unfold(bands, full):
    tiles = full.shape[0] // TILE
    first_column = lax.broadcasted_iota(jnp.int32, (TILE, TILE), 1) == 0
    for i in range(tiles):
        for step in range(tiles // 2 + 1):
            j = (i + step) % tiles
            here = bands[i * TILE : (i + 1) * TILE, step * TILE : (step + 1) * TILE]
            if step == 0:
                here = jnp.where(first_column, here.T, here)
            full[i * TILE : (i + 1) * TILE, j * TILE : (j + 1) * TILE] = here
            if 0 < step < tiles // 2:
                full[j * TILE : (j + 1) * TILE, i * TILE : (i + 1) * TILE] = here.T


def damping(full):
    size = full.shape[0]
    value = full[...]
    lanes = lax.broadcasted_iota(jnp.int32, (size, size), 1)
    sublanes = lax.broadcasted_iota(jnp.int32, (size, size), 0)
    trace = jnp.sum(jnp.sum(jnp.where(lanes == sublanes, value, 0.0), axis=0, keepdims=True), axis=1, keepdims=True)
    largest = jnp.max(jnp.sum(jnp.abs(value), axis=0, keepdims=True), axis=1, keepdims=True)
    damp = trace * (0.1 / size)
    return damp, 1.0 / (largest + damp)


def times(left, high, low):
    rows = left.shape[0]
    top, rest = split(left)
    first = dot(jnp.concatenate([top, rest], axis=0), high[...])
    return first[0:rows] + first[rows : 2 * rows] + dot(top, low[...])


def chain_kernel(devices, place, *refs):
    pieces = 2 * devices
    act_blocks, mixed_blocks = refs[:pieces], refs[pieces : 2 * pieces]
    momentum, weights, act_out, grad_out, moment_out, weight_out = refs[2 * pieces : 2 * pieces + 6]
    bands, full, act_high, act_low, high, low, mid_high, mid_low = refs[2 * pieces + 6 :]
    block, feat = momentum.shape
    width = act_blocks[0].shape[1]
    mine = place[0]
    own = pl.ds(pl.multiple_of(mine * block, block), block)
    step = block // 2
    here = [
        pl.ds(pl.multiple_of((mine ^ k) * block + half * step, step), step)
        for k in range(devices)
        for half in range(2)
    ]
    for k in range(pieces):
        bands[here[k], :] = act_blocks[k][...]
    unfold(bands, full)
    act_out[...] = full[own, :]
    act_damp, act_alpha = damping(full)
    top, rest = split(full[...])
    act_high[...] = top
    act_low[...] = rest
    for k in range(pieces):
        bands[here[k], :] = mixed_blocks[k][:, 0:width]
    unfold(bands, full)
    rows = full[own, :]
    grad_out[...] = rows
    damp, alpha = damping(full)
    top, rest = split(full[...])
    high[...] = top
    low[...] = rest
    for k in range(pieces):
        top, rest = split(mixed_blocks[k][:, width : width + feat])
        mid_high[here[k], :] = top
        mid_low[here[k], :] = rest
    lanes = lax.broadcasted_iota(jnp.int32, (block, feat), 1)
    sublanes = lax.broadcasted_iota(jnp.int32, (block, feat), 0)
    unit = jnp.where(lanes == sublanes + mine * block, 1.0, 0.0).astype(F32)
    rest_rows = unit - alpha * (rows + damp * unit)
    once = 2.0 * rest_rows - alpha * (times(rest_rows, high, low) + damp * rest_rows)
    left = alpha * (unit + rest_rows + once - alpha * (times(once, high, low) + damp * once))
    half_way = times(left, mid_high, mid_low)
    value = half_way
    for _ in range(3):
        value = half_way + value - act_alpha * (times(value, act_high, act_low) + act_damp * value)
    moment = 0.9 * momentum[...] + act_alpha * value
    moment_out[...] = moment
    weight_out[...] = weights[...] - 0.5 * moment


def chain(place, act_blocks, mixed_blocks, momentum, weights):
    devices = len(act_blocks) // 2
    block, feat = momentum.shape
    width = act_blocks[0].shape[1]
    square = (feat, feat)
    return pl.pallas_call(
        functools.partial(chain_kernel, devices),
        out_shape=[jax.ShapeDtypeStruct((block, feat), F32)] * 4,
        in_specs=[pl.BlockSpec(memory_space=pltpu.SMEM)] + whole_in_vmem(4 * devices + 2),
        out_specs=whole_in_vmem(4),
        scratch_shapes=[pltpu.VMEM((feat, width), F32), pltpu.VMEM(square, F32)]
        + [pltpu.VMEM(square, BF16)] * 6,
        cost_estimate=cost(36 * block * feat * feat, *act_blocks, *mixed_blocks),
        compiler_params=pltpu.CompilerParams(vmem_limit_bytes=VMEM_LIMIT),
    )(place, *act_blocks, *mixed_blocks, momentum, weights)


def swap(value, axis, step):
    size = lax.axis_size(axis)
    return lax.ppermute(value, axis, [(i, i ^ step) for i in range(size)])


def kept_rows(routes, counts, experts):
    samples = routes.shape[0]
    ids = jnp.arange(experts, dtype=jnp.int32)
    hit = jnp.sum((routes.T[None, :, :] == ids[:, None, None]).astype(jnp.int32), axis=1, dtype=jnp.int32)
    before = jnp.triu(jnp.ones((samples, samples), BF16), 1)
    rank = dot(hit.astype(BF16), before)
    return jnp.where(rank < counts[0].astype(F32)[:, None], hit, 0).astype(F32)


def to_owner(pieces, chips):
    results = []
    for half, order in enumerate(orders(chips)):
        keep, leave = pieces[2 * half], pieces[2 * half + 1]
        held, _ = held_and_sent(chips, order)
        got = swap(leave, "dp", 2 << order[0])
        sums = {k: keep[i] + got[i] for i, k in enumerate(held)}
        for bit in order[1:]:
            low = [k for k in sums if not (k >> bit) & 1]
            high = [sums[k | (1 << bit)] for k in low]
            got = swap(jnp.stack(high), "dp", 2 << bit)
            sums = {k: sums[k] + got[i] for i, k in enumerate(low)}
        results.append(sums[0])
    return results


def across(near, far):
    for number in range(far.shape[0]):
        near = near + swap(far[number], "expert", 2 * (number + 1))
    return near


def to_all(halves, chips):
    pieces = {}
    for half, order in enumerate(orders(chips)):
        held = {0: halves[half]}
        for bit in order:
            for k in list(held):
                held[k | (1 << bit)] = swap(held[k], "dp", 2 << bit)
        for k in range(chips):
            pieces[2 * k, half] = held[k]
            pieces[2 * k + 1, half] = swap(held[k], "dp", 1)
    return [pieces[k, half] for k in range(2 * chips) for half in range(2)]


def on_device(acts, grads_out, routes, counts, old_act_factor, old_grad_factor, momentum, weights):
    devices, experts = lax.axis_size("dp"), lax.axis_size("expert")
    chips = devices // 2
    feat, block = acts.shape[1], weights.shape[1]
    width = feat // 2 + TILE
    mine = lax.axis_index("dp")
    place = jnp.stack([mine, lax.axis_index("expert")]).astype(jnp.int32)

    acts_far = swap(acts, "expert", 1)
    keep = kept_rows(routes, counts, experts)
    grads_out, keep = lax.optimization_barrier((grads_out, keep))
    keep_far = swap(keep, "expert", 1)
    grads_far = swap(grads_out, "expert", 1)
    near_keep = jnp.concatenate([keep, swap(keep, "dp", 1)], axis=1)
    far_keep = jnp.concatenate([keep_far, swap(keep_far, "dp", 1)], axis=1)
    near_acts = (acts, swap(acts, "dp", 1))
    near_grads = (grads_out, swap(grads_out, "dp", 1))

    def own_band(old):
        start = mine * block // TILE * TILE
        wide = jnp.concatenate([old[0], old[0][:, 0 : width - TILE]], axis=1)
        return 0.5 * lax.dynamic_slice_in_dim(wide, start, width, 1)

    old_act, old_grad = own_band(old_act_factor), own_band(old_grad_factor)
    turns = tuple(range(experts // 2))
    size = (chips, block, width)
    mixed_size = (chips, block, width + feat)
    act_seeds = bands(act_kernel, turns, place, near_keep, near_acts, (), *size)
    grad_parts = near_grads + near_acts
    far_seeds = bands(grad_kernel, turns[1:], place, near_keep, grad_parts, (), *mixed_size)
    near_seeds = bands(grad_kernel, turns[:1], place, near_keep, grad_parts, (), *mixed_size)

    far_acts = (acts_far, swap(acts_far, "dp", 1))
    act_pieces = bands(act_kernel, turns, place, far_keep, far_acts, act_seeds, *size)
    grads_far, act_pieces = lax.optimization_barrier((grads_far, act_pieces))
    grad_parts = (grads_far, swap(grads_far, "dp", 1)) + far_acts
    far_pieces = bands(grad_kernel, turns[1:], place, far_keep, grad_parts, far_seeds, *mixed_size)
    near_seeds, far_pieces = lax.optimization_barrier((near_seeds, far_pieces))
    near_pieces = bands(grad_kernel, turns[:1], place, far_keep, grad_parts, near_seeds, *mixed_size)

    act_sums = [across(total[0], total[1:]) for total in to_owner(act_pieces, chips)]
    far_sums = to_owner(far_pieces, chips)
    near_sums = to_owner(near_pieces, chips)
    total = jnp.maximum(act_sums[1][-1:, 0:1], 1.0)
    step = block // 2
    act_halves, mixed_halves = [], []
    for half in range(2):
        here = slice(half * step, (half + 1) * step)
        act_halves.append(old_act[here] + 0.5 * (act_sums[half] / total))
        mixed = across(near_sums[half][0], far_sums[half]) / total
        mixed = jnp.concatenate([old_grad[here] + 0.5 * mixed[:, 0:width], mixed[:, width:]], axis=1)
        mixed_halves.append(mixed)
    outs = chain(place, to_all(act_halves, chips), to_all(mixed_halves, chips), momentum[0], weights[0])
    return tuple(out[None] for out in outs)


def solution(mesh):
    rows = P(("dp", "expert"), None)
    matrix = P("expert", "dp", None)
    return jax.shard_map(
        on_device,
        mesh=mesh,
        in_specs=(rows,) * 4 + (matrix,) * 4,
        out_specs=(matrix,) * 4,
        check_vma=False,
    )
```

time: 292 us -> 292 us (level)
  blocking collectives: 81.5 us -> 0 us
  waiting for transfers between devices: 100 us -> 180 us
  Pallas kernels: 45.5 us -> 58.6 us
  starting transfers between devices: 49.7 us -> 39.6 us
  other arithmetic: 6.8 us -> 2.21 us
    psum x1 -> x0, blocking collectives: 81.5 us -> none  [on_device(): lax.psum(jnp.sum(keep[:, 0:acts.shape[0]], axis=1), ('dp', 'expert'))]
    ppermute x33 -> x53, waiting for transfers between devices: 100 us -> 180 us  [swap(): return lax.ppermute(value, axis, [(i, i ^ step) for i in range(size)])]
    pallas_call x3 -> x6, Pallas kernels: 31.9 us -> 44.5 us  [bands(): pl.pallas_call(functools.partial(body, turns, block, chips, bool(seeds)),...]
    ppermute x33 -> x53, starting transfers between devices: 49.7 us -> 39.6 us  [swap(): return lax.ppermute(value, axis, [(i, i ^ step) for i in range(size)])]
  transfers between devices with their start and end apart: 33 -> 53, of which waited for: 10 -> 21; matrix products, arithmetic and copies ran while one was open for 3% -> 1% of each run, Pallas kernels for 7% -> 15%
where the time goes in v2:
time: 292 us; the launch traced here: 288 us
  waiting for transfers between devices  180 us (62%)
  Pallas kernels  58.6 us (20%)
  starting transfers between devices  39.6 us (14%)
  local copies, waits for them, and re-layouts  5.31 us (2%)
    ppermute x53, waiting for transfers between devices, swap(): return lax.ppermute(value, axis, [(i, i ^ step) for i in range(size)])  180 us
    pallas_call x6, Pallas kernels, bands(): pl.pallas_call(functools.partial(body, turns, block, chips, bool(seeds)),...  44.5 us
    ppermute x53, starting transfers between devices, swap(): return lax.ppermute(value, axis, [(i, i ^ step) for i in range(size)])  39.6 us
    pallas_call x1, Pallas kernels, chain(): pl.pallas_call(functools.partial(chain_kernel, devices), out_shape=[jax.S...  14.1 us
  transfers between devices with their start and end apart: 53, of which 21 were waited for; matrix products, arithmetic and copies ran while one was open for 1% of the time, Pallas kernels for 15%

profile of v2, /device:TPU:25, one launch (start us, length us, event | category | flops | bytes accessed | tf_op | source)
XLA Modules:
  0.0 288.3 jit_solution(15064661688453527506)
XLA Ops:
  2.5 22.4 %collective-permute-done.3.refs_0_.refs_2_ = f32[256,1024]{1,0:T(8,128)S(1)} collective-permute-done((f32[256,1024]{1,0:T(8,128)}, f32[256,1024]{1,0:T(8,128)S(1)}, u32[]{:S(2)}, u32[]{:S(2)}) %collective-permute-start.3) | collective-permute-done | bytes 1048608 | tf_op jit(solution)/shard_map/ppermute | solution.py:278
  29.0 22.9 %collective-permute-done.1 = f32[4,256]{1,0:T(4,128)S(1)} collective-permute-done((f32[4,256]{1,0:T(4,128)S(1)}, f32[4,256]{1,0:T(4,128)S(1)}, u32[]{:S(2)}, u32[]{:S(2)}) %collective-permute-start.1) | collective-permute-done | bytes 4128 | tf_op jit(solution)/shard_map/ppermute | solution.py:278
  54.8 6.0 %shard_map.111 = (f32[2,2,64,640]{3,2,1,0:T(8,128)}, f32[2,2,64,640]{3,2,1,0:T(8,128)}, f32[2,2,64,640]{3,2,1,0:T(8,128)}, f32[2,2,64,640]{3,2,1,0:T(8,128)}) custom-call(s32[2]{0:T(128)} %pad_add_fusion.place, f32[4,512]{1,0:T(4,128)} %copy-done.14, f32[256,1024]{1,0:T(8,128)} %refs_2_.3, f32[256,1024]{1,0:T(8,128)} %collective-permute-done.6.refs_1_.refs_3_), custom_call_target="tpu_custom_call" | custom-call | flops 2013265920 | bytes 4726784 | tf_op jit(solution)/shard_map/pallas_call | solution.py:165
  61.8 6.9 %shard_map.112 = (f32[2,2,64,640]{3,2,1,0:T(8,128)}, f32[2,2,64,640]{3,2,1,0:T(8,128)}, f32[2,2,64,640]{3,2,1,0:T(8,128)}, f32[2,2,64,640]{3,2,1,0:T(8,128)}) custom-call(s32[2]{0:T(128)} %pad_add_fusion.place, f32[4,512]{1,0:T(4,128)} %copy-done.15, f32[256,1024]{1,0:T(8,128)} %copy-done.16, f32[256,1024]{1,0:T(8,128)} %copy-done.17, ...), custom_call_target="tpu_custom_call" | custom-call | flops 2013265920 | bytes 7348224 | tf_op jit(solution)/shard_map/pallas_call | solution.py:165
  72.5 7.3 %shard_map.114 = (f32[2,1,64,1664]{3,2,1,0:T(8,128)}, f32[2,1,64,1664]{3,2,1,0:T(8,128)}, f32[2,1,64,1664]{3,2,1,0:T(8,128)}, f32[2,1,64,1664]{3,2,1,0:T(8,128)}) custom-call(s32[2]{0:T(128)} %pad_add_fusion.place, f32[4,512]{1,0:T(4,128)} %copy-done.14, f32[256,1024]{1,0:T(8,128)} %refs_0_.3, f32[256,1024]{1,0:T(8,128)} %collective-permute-done.28.refs_1_, ...), custom_call_target="tpu_custom_call" | custom-call | flops 2617245696 | bytes 7610368 | tf_op jit(solution)/shard_map/pallas_call | solution.py:165
  80.4 4.8 %collective-permute-done.10 = f32[2,2,64,640]{3,2,1,0:T(8,128)S(1)} collective-permute-done((f32[2,2,64,640]{3,2,1,0:T(8,128)}, f32[2,2,64,640]{3,2,1,0:T(8,128)S(1)}, u32[]{:S(2)}, u32[]{:S(2)}) %collective-permute-start.10) | collective-permute-done | bytes 655392 | tf_op jit(solution)/shard_map/ppermute | solution.py:278
  86.5 7.6 %shard_map.113 = (f32[2,1,64,1664]{3,2,1,0:T(8,128)}, f32[2,1,64,1664]{3,2,1,0:T(8,128)}, f32[2,1,64,1664]{3,2,1,0:T(8,128)}, f32[2,1,64,1664]{3,2,1,0:T(8,128)}) custom-call(s32[2]{0:T(128)} %pad_add_fusion.place, f32[4,512]{1,0:T(4,128)} %copy-done.14, f32[256,1024]{1,0:T(8,128)} %refs_0_.3, f32[256,1024]{1,0:T(8,128)} %collective-permute-done.28.refs_1_, ...), custom_call_target="tpu_custom_call" | custom-call | flops 2617245696 | bytes 7610368 | tf_op jit(solution)/shard_map/pallas_call | solution.py:165
  96.7 8.3 %shard_map.115 = (f32[2,1,64,1664]{3,2,1,0:T(8,128)}, f32[2,1,64,1664]{3,2,1,0:T(8,128)}, f32[2,1,64,1664]{3,2,1,0:T(8,128)}, f32[2,1,64,1664]{3,2,1,0:T(8,128)}) custom-call(s32[2]{0:T(128)} %pad_add_fusion.place, f32[4,512]{1,0:T(4,128)} %copy-done.15, f32[256,1024]{1,0:T(8,128)} %collective-permute-done.refs_0_, f32[256,1024]{1,0:T(8,128)} %copy-done.18, ...), custom_call_target="tpu_custom_call" | custom-call | flops 2617245696 | bytes 11018240 | tf_op jit(solution)/shard_map/pallas_call | solution.py:165
  105.0 8.4 %shard_map.116 = (f32[2,1,64,1664]{3,2,1,0:T(8,128)}, f32[2,1,64,1664]{3,2,1,0:T(8,128)}, f32[2,1,64,1664]{3,2,1,0:T(8,128)}, f32[2,1,64,1664]{3,2,1,0:T(8,128)}) custom-call(s32[2]{0:T(128)} %pad_add_fusion.place, f32[4,512]{1,0:T(4,128)} %copy-done.15, f32[256,1024]{1,0:T(8,128)} %collective-permute-done.refs_0_, f32[256,1024]{1,0:T(8,128)} %copy-done.18, ...), custom_call_target="tpu_custom_call" | custom-call | flops 2617245696 | bytes 11018240 | tf_op jit(solution)/shard_map/pallas_call | solution.py:165
  120.0 3.4 %collective-permute-done.9 = f32[64,640]{1,0:T(8,128)S(1)} collective-permute-done((f32[64,640]{1,0:T(8,128)S(1)}, f32[64,640]{1,0:T(8,128)S(1)}, u32[]{:S(2)}, u32[]{:S(2)}) %collective-permute-start.9) | collective-permute-done | bytes 163872 | tf_op jit(solution)/shard_map/ppermute | solution.py:278
  124.8 7.5 %collective-permute-done.34 = f32[2,1,64,1664]{3,2,1,0:T(8,128)S(1)} collective-permute-done((f32[2,1,64,1664]{3,2,1,0:T(8,128)}, f32[2,1,64,1664]{3,2,1,0:T(8,128)S(1)}, u32[]{:S(2)}, u32[]{:S(2)}) %collective-permute-start.34) | collective-permute-done | bytes 852000 | tf_op jit(solution)/shard_map/ppermute | solution.py:278
  132.6 18.0 %collective-permute-done.36 = f32[2,1,64,1664]{3,2,1,0:T(8,128)S(1)} collective-permute-done((f32[2,1,64,1664]{3,2,1,0:T(8,128)S(1)}, f32[2,1,64,1664]{3,2,1,0:T(8,128)S(1)}, u32[]{:S(2)}, u32[]{:S(2)}) %collective-permute-start.36) | collective-permute-done | bytes 852000 | tf_op jit(solution)/shard_map/ppermute | solution.py:278
  153.8 25.1 %collective-permute-done.37 = f32[1,1,64,1664]{3,2,1,0:T(8,128)S(1)} collective-permute-done((f32[1,1,64,1664]{3,2,1,0:T(8,128)S(1)}, f32[1,1,64,1664]{3,2,1,0:T(8,128)S(1)}, u32[]{:S(2)}, u32[]{:S(2)}) %collective-permute-start.37) | collective-permute-done | bytes 426016 | tf_op jit(solution)/shard_map/ppermute | solution.py:278
  179.2 7.5 %collective-permute-done.32 = f32[1,1,64,1664]{3,2,1,0:T(8,128)S(1)} collective-permute-done((f32[1,1,64,1664]{3,2,1,0:T(8,128)S(1)}, f32[1,1,64,1664]{3,2,1,0:T(8,128)S(1)}, u32[]{:S(2)}, u32[]{:S(2)}) %collective-permute-start.32) | collective-permute-done | bytes 426016 | tf_op jit(solution)/shard_map/ppermute | solution.py:278
  187.3 19.8 %collective-permute-done.38 = f32[64,1664]{1,0:T(8,128)S(1)} collective-permute-done((f32[64,1664]{1,0:T(8,128)S(1)}, f32[64,1664]{1,0:T(8,128)S(1)}, u32[]{:S(2)}, u32[]{:S(2)}) %collective-permute-start.38) | collective-permute-done | bytes 426016 | tf_op jit(solution)/shard_map/ppermute | solution.py:278
  207.5 19.4 %collective-permute-done.33 = f32[64,1664]{1,0:T(8,128)S(1)} collective-permute-done((f32[64,1664]{1,0:T(8,128)S(1)}, f32[64,1664]{1,0:T(8,128)S(1)}, u32[]{:S(2)}, u32[]{:S(2)}) %collective-permute-start.33) | collective-permute-done | bytes 426016 | tf_op jit(solution)/shard_map/ppermute | solution.py:278
  230.1 3.7 %collective-permute-done.23.refs_12_ = f32[64,640]{1,0:T(8,128)S(1)} collective-permute-done((f32[64,640]{1,0:T(8,128)S(1)}, f32[64,640]{1,0:T(8,128)S(1)}, u32[]{:S(2)}, u32[]{:S(2)}) %collective-permute-start.23) | collective-permute-done | bytes 163872 | tf_op jit(solution)/shard_map/ppermute | solution.py:278
  243.0 2.8 collective-permute-done.46.refs_25_
  245.7 3.1 %collective-permute-start.39 = (f32[64,1664]{1,0:T(8,128)S(1)}, f32[64,1664]{1,0:T(8,128)S(1)}, u32[]{:S(2)}, u32[]{:S(2)}) collective-permute-start(f32[64,1664]{1,0:T(8,128)S(1)} %pad_maximum_fusion.refs_16_), channel_id=1, source_target_pairs={{0,4},{4,0},{8,12},{12,8},{16,20},{20,16},{24,28},{28,24},{1,5},{5... | collective-permute-start | bytes 1277960 | tf_op jit(solution)/shard_map/ppermute | solution.py:278
  248.9 6.9 %collective-permute-done.41.refs_20_ = f32[64,1664]{1,0:T(8,128)S(1)} collective-permute-done((f32[64,1664]{1,0:T(8,128)S(1)}, f32[64,1664]{1,0:T(8,128)S(1)}, u32[]{:S(2)}, u32[]{:S(2)}) %collective-permute-start.41) | collective-permute-done | bytes 426016 | tf_op jit(solution)/shard_map/ppermute | solution.py:278
  255.8 3.7 %collective-permute-start.44 = (f32[64,1664]{1,0:T(8,128)S(1)}, f32[64,1664]{1,0:T(8,128)S(1)}, u32[]{:S(2)}, u32[]{:S(2)}) collective-permute-start(f32[64,1664]{1,0:T(8,128)S(1)} %collective-permute-done.42.refs_21_), channel_id=1, source_target_pairs={{0,4},{4,0},{8,12},{12,8},{16,20},{20,16},{24,28},{28,24},{1,5},{5... | collective-permute-start | bytes 1277960 | tf_op jit(solution)/shard_map/ppermute | solution.py:278
  260.3 4.6 %collective-permute-done.50.refs_29_ = f32[64,1664]{1,0:T(8,128)S(1)} collective-permute-done((f32[64,1664]{1,0:T(8,128)S(1)}, f32[64,1664]{1,0:T(8,128)S(1)}, u32[]{:S(2)}, u32[]{:S(2)}) %collective-permute-start.50) | collective-permute-done | bytes 426016 | tf_op jit(solution)/shard_map/ppermute | solution.py:278
  267.1 3.9 %collective-permute-done.49.refs_28_ = f32[64,1664]{1,0:T(8,128)S(1)} collective-permute-done((f32[64,1664]{1,0:T(8,128)S(1)}, f32[64,1664]{1,0:T(8,128)S(1)}, u32[]{:S(2)}, u32[]{:S(2)}) %collective-permute-start.49) | collective-permute-done | bytes 426016 | tf_op jit(solution)/shard_map/ppermute | solution.py:278
  274.0 14.1 %shard_map.117 = (f32[128,1024]{1,0:T(8,128)}, f32[128,1024]{1,0:T(8,128)}, f32[128,1024]{1,0:T(8,128)}, f32[128,1024]{1,0:T(8,128)}) custom-call(s32[2]{0:T(128)} %pad_add_fusion.place, f32[64,640]{1,0:T(8,128)} %copy-done.12, f32[64,640]{1,0:T(8,128)} %copy-done.11, f32[64,640]{1,0:T(8,128)} %copy-done.40, f32[64,640]{1,0:T(8,128)} %copy-done.41, ...), custom_call_target="tpu_custom_call" | custom-call | flops 4831838208 | bytes 9437184 | tf_op jit(solution)/shard_map/pallas_call | solution.py:264
  (222 shorter events, 48.0 us)
Async XLA Ops:
  0.6 24.3 %collective-permute-start.3 = (f32[256,1024]{1,0:T(8,128)}, f32[256,1024]{1,0:T(8,128)S(1)}, u32[]{:S(2)}, u32[]{:S(2)}) collective-permute-start(f32[256,1024]{1,0:T(8,128)} %refs_2_.3), channel_id=1, source_target_pairs={{0,1},{1,0},{2,3},{3,2},{4,5},{5,4},{6,7},{7,6},{8,9},{9,8},{10,11... | collective-permute-start | bytes 3145736 | tf_op jit(solution)/shard_map/ppermute | solution.py:278
  0.9 53.9 %collective-permute-start.6 = (f32[256,1024]{1,0:T(8,128)}, f32[256,1024]{1,0:T(8,128)}, u32[]{:S(2)}, u32[]{:S(2)}) collective-permute-start(f32[256,1024]{1,0:T(8,128)} %refs_2_.3), channel_id=1, source_target_pairs={{0,4},{4,0},{8,12},{12,8},{16,20},{20,16},{24,28},{28,24},{1,5},{5... | collective-permute-start | bytes 3145736 | tf_op jit(solution)/shard_map/ppermute | solution.py:278
  24.9 35.8 %collective-permute-start.4 = (f32[256,1024]{1,0:T(8,128)S(1)}, f32[256,1024]{1,0:T(8,128)S(1)}, u32[]{:S(2)}, u32[]{:S(2)}) collective-permute-start(f32[256,1024]{1,0:T(8,128)S(1)} %collective-permute-done.3.refs_0_.refs_2_), channel_id=1, source_target_pairs={{0,4},{4,0},{8,12},{12,8},{16,20},{20,16},{24,28},{28,24},{1,5},{5... | collective-permute-start | bytes 3145736 | tf_op jit(solution)/shard_map/ppermute | solution.py:278
  26.6 42.1 %collective-permute-start = (f32[256,1024]{1,0:T(8,128)}, f32[256,1024]{1,0:T(8,128)}, u32[]{:S(2)}, u32[]{:S(2)}) collective-permute-start(f32[256,1024]{1,0:T(8,128)} %refs_0_.3), channel_id=1, source_target_pairs={{0,1},{1,0},{2,3},{3,2},{4,5},{5,4},{6,7},{7,6},{8,9},{9,8},{10,11... | collective-permute-start | bytes 3145736 | tf_op jit(solution)/shard_map/ppermute | solution.py:278
  26.8 25.8 %collective-permute-start.5 = (f32[4,256]{1,0:T(4,128)S(1)}, f32[4,256]{1,0:T(4,128)S(1)}, u32[]{:S(2)}, u32[]{:S(2)}) collective-permute-start(f32[4,256]{1,0:T(4,128)S(1)} %fusion.1), channel_id=1, source_target_pairs={{0,4},{4,0},{8,12},{12,8},{16,20},{20,16},{24,28},{28,24},{1,5},{5... | collective-permute-start | bytes 12296 | tf_op jit(solution)/shard_map/ppermute | solution.py:278
  27.1 24.7 %collective-permute-start.1 = (f32[4,256]{1,0:T(4,128)S(1)}, f32[4,256]{1,0:T(4,128)S(1)}, u32[]{:S(2)}, u32[]{:S(2)}) collective-permute-start(f32[4,256]{1,0:T(4,128)S(1)} %fusion.1), channel_id=1, source_target_pairs={{0,1},{1,0},{2,3},{3,2},{4,5},{5,4},{6,7},{7,6},{8,9},{9,8},{10,11... | collective-permute-start | bytes 12296 | tf_op jit(solution)/shard_map/ppermute | solution.py:278
  51.8 20.6 %collective-permute-start.28 = (f32[256,1024]{1,0:T(8,128)}, f32[256,1024]{1,0:T(8,128)}, u32[]{:S(2)}, u32[]{:S(2)}) collective-permute-start(f32[256,1024]{1,0:T(8,128)} %refs_0_.3), channel_id=1, source_target_pairs={{0,4},{4,0},{8,12},{12,8},{16,20},{20,16},{24,28},{28,24},{1,5},{5... | collective-permute-start | bytes 3145736 | tf_op jit(solution)/shard_map/ppermute | solution.py:278
  71.2 22.9 %collective-permute-start.7 = (f32[2,2,64,640]{3,2,1,0:T(8,128)S(1)}, f32[2,2,64,640]{3,2,1,0:T(8,128)S(1)}, u32[]{:S(2)}, u32[]{:S(2)}) collective-permute-start(f32[2,2,64,640]{3,2,1,0:T(8,128)S(1)} %copy-done.21), channel_id=1, source_target_pairs={{0,8},{4,12},{8,0},{12,4},{16,24},{20,28},{24,16},{28,20},{1,9},{5... | collective-permute-start | bytes 1966088 | tf_op jit(solution)/shard_map/ppermute | solution.py:278
  94.1 19.5 %collective-permute-start.8 = (f32[1,2,64,640]{3,2,1,0:T(8,128)S(1)}, f32[1,2,64,640]{3,2,1,0:T(8,128)S(1)}, u32[]{:S(2)}, u32[]{:S(2)}) collective-permute-start(f32[1,2,64,640]{3,2,1,0:T(8,128)S(1)} %slice_add_fusion.10), channel_id=1, source_target_pairs={{0,16},{4,20},{8,24},{12,28},{16,0},{20,4},{24,8},{28,12},{1,17},{... | collective-permute-start | bytes 983048 | tf_op jit(solution)/shard_map/ppermute | solution.py:278
  95.5 22.0 %collective-permute-start.12 = (f32[64,640]{1,0:T(8,128)S(1)}, f32[64,640]{1,0:T(8,128)S(1)}, u32[]{:S(2)}, u32[]{:S(2)}) collective-permute-start(f32[64,640]{1,0:T(8,128)S(1)} %slice_bitcast_fusion), channel_id=1, source_target_pairs={{0,2},{1,3},{2,0},{3,1},{4,6},{5,7},{6,4},{7,5},{8,10},{9,11},{10,... | collective-permute-start | bytes 491528 | tf_op jit(solution)/shard_map/ppermute | solution.py:278
  116.1 34.5 %collective-permute-start.36 = (f32[2,1,64,1664]{3,2,1,0:T(8,128)S(1)}, f32[2,1,64,1664]{3,2,1,0:T(8,128)S(1)}, u32[]{:S(2)}, u32[]{:S(2)}) collective-permute-start(f32[2,1,64,1664]{3,2,1,0:T(8,128)S(1)} %copy-done.20), channel_id=1, source_target_pairs={{0,16},{4,20},{8,24},{12,28},{16,0},{20,4},{24,8},{28,12},{1,17},{... | collective-permute-start | bytes 2555912 | tf_op jit(solution)/shard_map/ppermute | solution.py:278
  117.3 33.5 %collective-permute-start.29 = (f32[2,1,64,1664]{3,2,1,0:T(8,128)}, f32[2,1,64,1664]{3,2,1,0:T(8,128)S(1)}, u32[]{:S(2)}, u32[]{:S(2)}) collective-permute-start(f32[2,1,64,1664]{3,2,1,0:T(8,128)} %get-tuple-element.79), channel_id=1, source_target_pairs={{0,8},{4,12},{8,0},{12,4},{16,24},{20,28},{24,16},{28,20},{1,9},{5... | collective-permute-start | bytes 2555912 | tf_op jit(solution)/shard_map/ppermute | solution.py:278
  117.5 36.1 %collective-permute-start.31 = (f32[2,1,64,1664]{3,2,1,0:T(8,128)S(1)}, f32[2,1,64,1664]{3,2,1,0:T(8,128)S(1)}, u32[]{:S(2)}, u32[]{:S(2)}) collective-permute-start(f32[2,1,64,1664]{3,2,1,0:T(8,128)S(1)} %copy-done.19), channel_id=1, source_target_pairs={{0,8},{4,12},{8,0},{12,4},{16,24},{20,28},{24,16},{28,20},{1,9},{5... | collective-permute-start | bytes 2555912 | tf_op jit(solution)/shard_map/ppermute | solution.py:278
  123.5 104.9 %collective-permute-start.20 = (f32[64,640]{1,0:T(8,128)S(1)}, f32[64,640]{1,0:T(8,128)S(1)}, u32[]{:S(2)}, u32[]{:S(2)}) collective-permute-start(f32[64,640]{1,0:T(8,128)S(1)} %get-tuple-element.92.refs_1_), channel_id=1, source_target_pairs={{0,16},{4,20},{8,24},{12,28},{16,0},{20,4},{24,8},{28,12},{1,17},{... | collective-permute-start | bytes 491528 | tf_op jit(solution)/shard_map/ppermute | solution.py:278
  132.3 96.4 %collective-permute-start.16 = (f32[64,640]{1,0:T(8,128)S(1)}, f32[64,640]{1,0:T(8,128)S(1)}, u32[]{:S(2)}, u32[]{:S(2)}) collective-permute-start(f32[64,640]{1,0:T(8,128)S(1)} %get-tuple-element.92.refs_1_), channel_id=1, source_target_pairs={{0,8},{4,12},{8,0},{12,4},{16,24},{20,28},{24,16},{28,20},{1,9},{5... | collective-permute-start | bytes 491528 | tf_op jit(solution)/shard_map/ppermute | solution.py:278
  150.6 77.7 %collective-permute-start.15 = (f32[64,640]{1,0:T(8,128)S(1)}, f32[64,640]{1,0:T(8,128)S(1)}, u32[]{:S(2)}, u32[]{:S(2)}) collective-permute-start(f32[64,640]{1,0:T(8,128)S(1)} %get-tuple-element.93.refs_0_), channel_id=1, source_target_pairs={{0,8},{4,12},{8,0},{12,4},{16,24},{20,28},{24,16},{28,20},{1,9},{5... | collective-permute-start | bytes 491528 | tf_op jit(solution)/shard_map/ppermute | solution.py:278
  150.8 36.1 %collective-permute-start.35 = (f32[1,1,64,1664]{3,2,1,0:T(8,128)S(1)}, f32[1,1,64,1664]{3,2,1,0:T(8,128)S(1)}, u32[]{:S(2)}, u32[]{:S(2)}) collective-permute-start(f32[1,1,64,1664]{3,2,1,0:T(8,128)S(1)} %slice_add_fusion.2), channel_id=1, source_target_pairs={{0,8},{4,12},{8,0},{12,4},{16,24},{20,28},{24,16},{28,20},{1,9},{5... | collective-permute-start | bytes 1277960 | tf_op jit(solution)/shard_map/ppermute | solution.py:278
  153.6 25.3 %collective-permute-start.37 = (f32[1,1,64,1664]{3,2,1,0:T(8,128)S(1)}, f32[1,1,64,1664]{3,2,1,0:T(8,128)S(1)}, u32[]{:S(2)}, u32[]{:S(2)}) collective-permute-start(f32[1,1,64,1664]{3,2,1,0:T(8,128)S(1)} %slice_add_fusion), channel_id=1, source_target_pairs={{0,8},{4,12},{8,0},{12,4},{16,24},{20,28},{24,16},{28,20},{1,9},{5... | collective-permute-start | bytes 1277960 | tf_op jit(solution)/shard_map/ppermute | solution.py:278
  186.7 20.3 %collective-permute-start.38 = (f32[64,1664]{1,0:T(8,128)S(1)}, f32[64,1664]{1,0:T(8,128)S(1)}, u32[]{:S(2)}, u32[]{:S(2)}) collective-permute-start(f32[64,1664]{1,0:T(8,128)S(1)} %fusion.3), channel_id=1, source_target_pairs={{0,2},{1,3},{2,0},{3,1},{4,6},{5,7},{6,4},{7,5},{8,10},{9,11},{10,... | collective-permute-start | bytes 1277960 | tf_op jit(solution)/shard_map/ppermute | solution.py:278
  187.0 20.2 %collective-permute-start.30 = (f32[1,1,64,1664]{3,2,1,0:T(8,128)S(1)}, f32[1,1,64,1664]{3,2,1,0:T(8,128)S(1)}, u32[]{:S(2)}, u32[]{:S(2)}) collective-permute-start(f32[1,1,64,1664]{3,2,1,0:T(8,128)S(1)} %slice_add_fusion.6), channel_id=1, source_target_pairs={{0,16},{4,20},{8,24},{12,28},{16,0},{20,4},{24,8},{28,12},{1,17},{... | collective-permute-start | bytes 1277960 | tf_op jit(solution)/shard_map/ppermute | solution.py:278
  207.1 19.8 %collective-permute-start.33 = (f32[64,1664]{1,0:T(8,128)S(1)}, f32[64,1664]{1,0:T(8,128)S(1)}, u32[]{:S(2)}, u32[]{:S(2)}) collective-permute-start(f32[64,1664]{1,0:T(8,128)S(1)} %fusion.9), channel_id=1, source_target_pairs={{0,2},{1,3},{2,0},{3,1},{4,6},{5,7},{6,4},{7,5},{8,10},{9,11},{10,... | collective-permute-start | bytes 1277960 | tf_op jit(solution)/shard_map/ppermute | solution.py:278
  207.2 22.3 %collective-permute-start.19 = (f32[64,640]{1,0:T(8,128)S(1)}, f32[64,640]{1,0:T(8,128)S(1)}, u32[]{:S(2)}, u32[]{:S(2)}) collective-permute-start(f32[64,640]{1,0:T(8,128)S(1)} %get-tuple-element.93.refs_0_), channel_id=1, source_target_pairs={{0,16},{4,20},{8,24},{12,28},{16,0},{20,4},{24,8},{28,12},{1,17},{... | collective-permute-start | bytes 491528 | tf_op jit(solution)/shard_map/ppermute | solution.py:278
  236.7 19.1 %collective-permute-start.41 = (f32[64,1664]{1,0:T(8,128)S(1)}, f32[64,1664]{1,0:T(8,128)S(1)}, u32[]{:S(2)}, u32[]{:S(2)}) collective-permute-start(f32[64,1664]{1,0:T(8,128)S(1)} %pad_maximum_fusion.refs_16_), channel_id=1, source_target_pairs={{0,8},{4,12},{8,0},{12,4},{16,24},{20,28},{24,16},{28,20},{1,9},{5... | collective-permute-start | bytes 1277960 | tf_op jit(solution)/shard_map/ppermute | solution.py:278
  238.0 21.6 %collective-permute-start.40 = (f32[64,1664]{1,0:T(8,128)S(1)}, f32[64,1664]{1,0:T(8,128)S(1)}, u32[]{:S(2)}, u32[]{:S(2)}) collective-permute-start(f32[64,1664]{1,0:T(8,128)S(1)} %pad_maximum_fusion.1.refs_17_), channel_id=1, source_target_pairs={{0,4},{4,0},{8,12},{12,8},{16,20},{20,16},{24,28},{28,24},{1,5},{5... | collective-permute-start | bytes 1277960 | tf_op jit(solution)/shard_map/ppermute | solution.py:278
  (79 other events, 1168.5 us)

commit v3 on v2

--- a/solution.py
+++ b/solution.py
@@ -1,5 +1,4 @@
 import functools
-import math
 
 import jax
 import jax.numpy as jnp
@@ -33,12 +32,11 @@
     )
 
 
-def split_rows(parts, high, low, feat):
+def split_rows(parts, samples, high, low, feat):
     extra = high.shape[1] - feat
     for number, part in enumerate(parts):
-        rows = part.shape[0]
-        here = slice(number * rows, (number + 1) * rows)
-        top, rest = split(part[...])
+        here = slice(number * samples, (number + 1) * samples)
+        top, rest = split(part[0:samples, :])
         high[here, 0:feat] = top
         low[here, 0:feat] = rest
         if extra:
@@ -46,15 +44,25 @@
             low[here, feat : feat + extra] = rest[:, 0:extra]
 
 
-def left_rows(parts, turned, column, row, block):
+def left_rows(parts, samples, turned, column, row, block):
     for number, part in enumerate(parts):
-        rows = part.shape[0]
-        turned[:, number * rows : (number + 1) * rows] = part[:, pl.ds(column, TILE)].T
+        here = slice(number * samples, (number + 1) * samples)
+        turned[:, here] = part[0:samples, pl.ds(column, TILE)].T
     return turned[pl.ds(row, block), :]
 
 
-def weighted(rows, weights, lanes):
-    halves = [split(rows * weights[pl.ds(lane, 1), :]) for lane in lanes]
+def keep_place(expert, samples, feat):
+    per_row = feat // samples
+    return lax.div(expert, per_row), pl.multiple_of(lax.rem(expert, per_row) * samples, TILE)
+
+
+def keep_row(parts, samples, expert):
+    row, column = keep_place(expert, samples, parts[0].shape[1])
+    return jnp.concatenate([part[pl.ds(samples + row, 1), pl.ds(column, samples)] for part in parts], axis=1)
+
+
+def weighted(rows, keeps):
+    halves = [split(rows * keep) for keep in keeps]
     tops = [half[0] for half in halves]
     return jnp.concatenate(tops + [half[1] for half in halves], axis=0), jnp.concatenate(tops, axis=0)
 
@@ -88,53 +96,78 @@
 
 def store(outs, seeds, place, number, columns, value):
     output, position = place
+    for out in outs[0::4]:
+        if number < out.shape[1]:
+            break
+        output, number = output + 4, number - out.shape[1]
     if seeds:
         value = value + seeds[output][position, number, :, columns]
     outs[output][position, number, :, columns] = value
 
 
-def act_kernel(turns, block, chips, seeded, place, weights, *refs):
+def prepare_kernel(routes, counts, acts, out):
+    samples, feat = acts.shape
+    experts = counts.shape[1]
+    out[0:samples, :] = acts[...]
+    out[samples:, :] = jnp.zeros((out.shape[0] - samples, feat), F32)
+    hits = []
+    for expert in range(experts):
+        same = [jnp.where(routes[k : k + 1, :] == expert, 1.0, 0.0) for k in range(routes.shape[0])]
+        hits.append(sum(same[1:], same[0]))
+    hit = jnp.concatenate(hits, axis=0)
+    first = lax.broadcasted_iota(jnp.int32, (samples, samples), 0)
+    second = lax.broadcasted_iota(jnp.int32, (samples, samples), 1)
+    rank = dot(hit.astype(BF16), jnp.where(first < second, 1.0, 0.0).astype(BF16))
+    per_row = feat // samples
+    for expert in range(experts):
+        limit = counts[0, expert].astype(F32)
+        keep = jnp.where(rank[expert : expert + 1, :] < limit, hits[expert], 0.0)
+        row, column = samples + expert // per_row, expert % per_row * samples
+        out[row : row + 1, column : column + samples] = keep
+
+
+def act_kernel(turns, block, chips, seeded, samples, place, *refs):
     parts, refs = refs[:2], refs[2:]
-    seeds, refs = (refs[:4], refs[4:]) if seeded else ((), refs)
-    outs, (high, low, turned) = refs[:4], refs[4:]
+    refs, (high, low, turned) = refs[:-3], refs[-3:]
+    seeds, outs = (refs[: len(refs) // 2], refs[len(refs) // 2 :]) if seeded else ((), refs)
     feat = parts[0].shape[1]
     width = outs[0].shape[3]
     mine, expert = place[0], place[1]
-    split_rows(parts, high, low, feat)
-    lanes = [expert ^ (2 * turn) for turn in turns]
+    split_rows(parts, samples, high, low, feat)
+    keeps = [keep_row(parts, samples, expert ^ (2 * turn)) for turn in turns]
     places = slots(chips)
     rows = lax.broadcasted_iota(jnp.int32, (block, width), 0)
     columns = lax.broadcasted_iota(jnp.int32, (block, width), 1)
     corner = jnp.logical_and(rows == block - 1, columns == 0)
     for k in range(chips):
         column, row = band_place(mine ^ (2 * k), block)
-        both, tops = weighted(left_rows(parts, turned, column, row, block), weights, lanes)
+        both, tops = weighted(left_rows(parts, samples, turned, column, row, block), keeps)
         total = three(both, tops, high[:, pl.ds(column, width)], low[:, pl.ds(column, width)])
-        for number, lane in enumerate(lanes):
-            count = jnp.sum(weights[pl.ds(lane, 1), :], axis=1, keepdims=True)
+        for number, keep in enumerate(keeps):
+            count = jnp.sum(keep, axis=1, keepdims=True)
             value = jnp.where(corner, count, total[number * block : (number + 1) * block])
             for half in range(2):
                 here = value[half * (block // 2) : (half + 1) * (block // 2)]
                 store(outs, seeds, places[k, half], number, slice(0, width), here)
 
 
-def grad_kernel(turns, block, chips, seeded, place, weights, *refs):
+def grad_kernel(turns, block, chips, seeded, samples, place, *refs):
     grads, acts, refs = refs[:2], refs[2:4], refs[4:]
-    seeds, refs = (refs[:4], refs[4:]) if seeded else ((), refs)
-    outs, (high, low, act_high, act_low, turned) = refs[:4], refs[4:]
+    refs, (high, low, act_high, act_low, turned) = refs[:-5], refs[-5:]
+    seeds, outs = (refs[: len(refs) // 2], refs[len(refs) // 2 :]) if seeded else ((), refs)
     feat = grads[0].shape[1]
     width = outs[0].shape[3] - feat
     mine, expert = place[0], place[1]
-    split_rows(grads, high, low, feat)
-    split_rows(acts, act_high, act_low, feat)
-    lanes = [expert ^ (2 * turn) for turn in turns]
+    split_rows(grads, samples, high, low, feat)
+    split_rows(acts, samples, act_high, act_low, feat)
+    keeps = [keep_row(acts, samples, expert ^ (2 * turn)) for turn in turns]
     places = slots(chips)
     for k in range(chips):
         column, row = band_place(mine ^ (2 * k), block)
-        both, tops = weighted(left_rows(grads, turned, column, row, block), weights, lanes)
+        both, tops = weighted(left_rows(grads, samples, turned, column, row, block), keeps)
         total = three(both, tops, high[:, pl.ds(column, width)], low[:, pl.ds(column, width)])
         mixed = three(both, tops, act_high[...], act_low[...])
-        for number in range(len(lanes)):
+        for number in range(len(keeps)):
             for half in range(2):
                 first = number * block + half * (block // 2)
                 here = slice(first, first + block // 2)
@@ -146,29 +179,41 @@
     return [pl.BlockSpec(memory_space=pltpu.VMEM)] * count
 
 
-def cost(flops, *arrays):
-    size = sum(4 * math.prod(array.shape) for array in arrays)
-    return pl.CostEstimate(flops=flops, bytes_accessed=size, transcendentals=0)
-
-
-def bands(body, turns, place, weights, parts, seeds, chips, block, width):
-    rows, feat = parts[0].shape
-    extended = pltpu.VMEM((2 * rows, feat + feat // 2), BF16)
-    plain = pltpu.VMEM((2 * rows, feat), BF16)
+def prepare(routes, counts, acts):
+    samples, feat = acts.shape
+    rows = samples + 8 * -(-counts.shape[1] * samples // (8 * feat))
+    return pl.pallas_call(
+        prepare_kernel,
+        out_shape=jax.ShapeDtypeStruct((rows, feat), F32),
+        in_specs=[
+            pl.BlockSpec(memory_space=pltpu.VMEM),
+            pl.BlockSpec(memory_space=pltpu.SMEM),
+            pl.BlockSpec(memory_space=pltpu.VMEM),
+        ],
+        out_specs=pl.BlockSpec(memory_space=pltpu.VMEM),
+        compiler_params=pltpu.CompilerParams(vmem_limit_bytes=VMEM_LIMIT),
+    )(routes.T, counts, acts)
+
+
+def bands(body, groups, place, parts, seeds, samples, chips, block, width):
+    turns = tuple(range(sum(groups)))
+    feat = parts[0].shape[1]
+    extended = pltpu.VMEM((2 * samples, feat + feat // 2), BF16)
+    plain = pltpu.VMEM((2 * samples, feat), BF16)
     scratch = [extended, extended] + ([plain, plain] if len(parts) > 2 else [])
     shapes = [
-        jax.ShapeDtypeStruct((len(group), len(turns), block // 2, width), F32)
+        jax.ShapeDtypeStruct((len(group), count, block // 2, width), F32)
+        for count in groups
         for order in orders(chips)
         for group in held_and_sent(chips, order)
     ]
-    operands = (weights, *parts, *seeds)
+    operands = (*parts, *seeds)
     return pl.pallas_call(
-        functools.partial(body, turns, block, chips, bool(seeds)),
+        functools.partial(body, turns, block, chips, bool(seeds), samples),
         out_shape=shapes,
         in_specs=[pl.BlockSpec(memory_space=pltpu.SMEM)] + whole_in_vmem(len(operands)),
-        out_specs=whole_in_vmem(4),
-        scratch_shapes=scratch + [pltpu.VMEM((TILE, 2 * rows), F32)],
-        cost_estimate=cost(12 * rows * chips * block * width * len(turns), *operands, *shapes),
+        out_specs=whole_in_vmem(len(shapes)),
+        scratch_shapes=scratch + [pltpu.VMEM((TILE, 2 * samples), F32)],
         compiler_params=pltpu.CompilerParams(vmem_limit_bytes=VMEM_LIMIT),
     )(place, *operands)
 
@@ -268,7 +313,6 @@
         out_specs=whole_in_vmem(4),
         scratch_shapes=[pltpu.VMEM((feat, width), F32), pltpu.VMEM(square, F32)]
         + [pltpu.VMEM(square, BF16)] * 6,
-        cost_estimate=cost(36 * block * feat * feat, *act_blocks, *mixed_blocks),
         compiler_params=pltpu.CompilerParams(vmem_limit_bytes=VMEM_LIMIT),
     )(place, *act_blocks, *mixed_blocks, momentum, weights)
 
@@ -278,35 +322,36 @@
     return lax.ppermute(value, axis, [(i, i ^ step) for i in range(size)])
 
 
-def kept_rows(routes, counts, experts):
-    samples = routes.shape[0]
-    ids = jnp.arange(experts, dtype=jnp.int32)
-    hit = jnp.sum((routes.T[None, :, :] == ids[:, None, None]).astype(jnp.int32), axis=1, dtype=jnp.int32)
-    before = jnp.triu(jnp.ones((samples, samples), BF16), 1)
-    rank = dot(hit.astype(BF16), before)
-    return jnp.where(rank < counts[0].astype(F32)[:, None], hit, 0).astype(F32)
-
-
-def to_owner(pieces, chips):
-    results = []
-    for half, order in enumerate(orders(chips)):
-        keep, leave = pieces[2 * half], pieces[2 * half + 1]
-        held, _ = held_and_sent(chips, order)
-        got = swap(leave, "dp", 2 << order[0])
-        sums = {k: keep[i] + got[i] for i, k in enumerate(held)}
-        for bit in order[1:]:
-            low = [k for k in sums if not (k >> bit) & 1]
-            high = [sums[k | (1 << bit)] for k in low]
-            got = swap(jnp.stack(high), "dp", 2 << bit)
-            sums = {k: sums[k] + got[i] for i, k in enumerate(low)}
-        results.append(sums[0])
-    return results
-
-
-def across(near, far):
-    for number in range(far.shape[0]):
-        near = near + swap(far[number], "expert", 2 * (number + 1))
-    return near
+class PlaneSum:
+    def __init__(self, pieces, chips):
+        self.steps = [list(order) for order in orders(chips)]
+        self.offsets = [held_and_sent(chips, order)[0] for order in self.steps]
+        self.held, self.leaving = list(pieces[0::2]), list(pieces[1::2])
+
+    def send(self):
+        self.got = [swap(value, "dp", 2 << order[0]) for value, order in zip(self.leaving, self.steps)]
+
+    def add(self):
+        self.leaving = []
+        for half, order in enumerate(self.steps):
+            offsets = self.offsets[half]
+            sums = {k: self.held[half][i] + self.got[half][i] for i, k in enumerate(offsets)}
+            order.pop(0)
+            if order:
+                offsets = [k for k in offsets if not (k >> order[0]) & 1]
+                self.leaving.append(jnp.stack([sums[k | (1 << order[0])] for k in offsets]))
+            self.offsets[half] = offsets
+            self.held[half] = [sums[k] for k in offsets]
+
+    def finish(self):
+        while self.steps[0]:
+            self.send()
+            self.add()
+        return [held[0] for held in self.held]
+
+
+def across(far):
+    return [swap(far[number], "expert", 2 * (number + 1)) for number in range(far.shape[0])]
 
 
 def to_all(halves, chips):
@@ -322,59 +367,78 @@
     return [pieces[k, half] for k in range(2 * chips) for half in range(2)]
 
 
+def together(*values):
+    return lax.optimization_barrier(values)
+
+
 def on_device(acts, grads_out, routes, counts, old_act_factor, old_grad_factor, momentum, weights):
     devices, experts = lax.axis_size("dp"), lax.axis_size("expert")
     chips = devices // 2
-    feat, block = acts.shape[1], weights.shape[1]
+    samples, feat, block = acts.shape[0], acts.shape[1], weights.shape[1]
     width = feat // 2 + TILE
     mine = lax.axis_index("dp")
     place = jnp.stack([mine, lax.axis_index("expert")]).astype(jnp.int32)
-
-    acts_far = swap(acts, "expert", 1)
-    keep = kept_rows(routes, counts, experts)
-    grads_out, keep = lax.optimization_barrier((grads_out, keep))
-    keep_far = swap(keep, "expert", 1)
-    grads_far = swap(grads_out, "expert", 1)
-    near_keep = jnp.concatenate([keep, swap(keep, "dp", 1)], axis=1)
-    far_keep = jnp.concatenate([keep_far, swap(keep_far, "dp", 1)], axis=1)
-    near_acts = (acts, swap(acts, "dp", 1))
-    near_grads = (grads_out, swap(grads_out, "dp", 1))
 
     def own_band(old):
         start = mine * block // TILE * TILE
         wide = jnp.concatenate([old[0], old[0][:, 0 : width - TILE]], axis=1)
         return 0.5 * lax.dynamic_slice_in_dim(wide, start, width, 1)
 
+    turns = experts // 2
+    size = (samples, chips, block, width)
+    mixed_size = (samples, chips, block, width + feat)
+
+    acts = prepare(routes, counts, acts)
+    acts_far = swap(acts, "expert", 1)
+    near_acts = (acts, swap(acts, "dp", 1))
+    act_seeds = bands(act_kernel, (turns,), place, near_acts, (), *size)
+    grads_out, act_seeds = together(grads_out, act_seeds)
+    grads_far = swap(grads_out, "expert", 1)
+    grad_parts = (grads_out, swap(grads_out, "dp", 1)) + near_acts
+    grad_seeds = bands(grad_kernel, (1, turns - 1), place, grad_parts, (), *mixed_size)
     old_act, old_grad = own_band(old_act_factor), own_band(old_grad_factor)
-    turns = tuple(range(experts // 2))
-    size = (chips, block, width)
-    mixed_size = (chips, block, width + feat)
-    act_seeds = bands(act_kernel, turns, place, near_keep, near_acts, (), *size)
-    grad_parts = near_grads + near_acts
-    far_seeds = bands(grad_kernel, turns[1:], place, near_keep, grad_parts, (), *mixed_size)
-    near_seeds = bands(grad_kernel, turns[:1], place, near_keep, grad_parts, (), *mixed_size)
+    acts_far, grad_seeds, old_act, old_grad = together(acts_far, grad_seeds, old_act, old_grad)
 
     far_acts = (acts_far, swap(acts_far, "dp", 1))
-    act_pieces = bands(act_kernel, turns, place, far_keep, far_acts, act_seeds, *size)
-    grads_far, act_pieces = lax.optimization_barrier((grads_far, act_pieces))
+    act_sum = PlaneSum(bands(act_kernel, (turns,), place, far_acts, act_seeds, *size), chips)
+    act_sum.send()
+    grads_far, act_sum.held = together(grads_far, act_sum.held)
     grad_parts = (grads_far, swap(grads_far, "dp", 1)) + far_acts
-    far_pieces = bands(grad_kernel, turns[1:], place, far_keep, grad_parts, far_seeds, *mixed_size)
-    near_seeds, far_pieces = lax.optimization_barrier((near_seeds, far_pieces))
-    near_pieces = bands(grad_kernel, turns[:1], place, far_keep, grad_parts, near_seeds, *mixed_size)
-
-    act_sums = [across(total[0], total[1:]) for total in to_owner(act_pieces, chips)]
-    far_sums = to_owner(far_pieces, chips)
-    near_sums = to_owner(near_pieces, chips)
-    total = jnp.maximum(act_sums[1][-1:, 0:1], 1.0)
+    act_sum.add()
+    grad_seeds, act_sum.leaving = together(grad_seeds, act_sum.leaving)
+    act_sum.send()
+    pieces = bands(grad_kernel, (1, turns - 1), place, grad_parts, grad_seeds, *mixed_size)
+
+    near_sum, far_sum = PlaneSum(pieces[:4], chips), PlaneSum(pieces[4:], chips)
+    far_sum.send()
+    act_sum.held, far_sum.held = together(act_sum.held, far_sum.held)
+    act_sum.add()
+    act_sums = act_sum.finish()
+    act_across = [across(total[1:]) for total in act_sums]
+    far_sum.add()
+    far_sum.leaving, act_across = together(far_sum.leaving, act_across)
+    far_sums = far_sum.finish()
+    far_sums, near_sum.leaving = together(far_sums, near_sum.leaving)
+    far_across = [across(total) for total in far_sums]
+    near_sum.send()
+    near_sum.add()
+
     step = block // 2
+    act_totals = [sum(there, total[0]) for total, there in zip(act_sums, act_across)]
+    total = jnp.maximum(act_totals[1][-1:, 0:1], 1.0)
     act_halves, mixed_halves = [], []
     for half in range(2):
         here = slice(half * step, (half + 1) * step)
-        act_halves.append(old_act[here] + 0.5 * (act_sums[half] / total))
-        mixed = across(near_sums[half][0], far_sums[half]) / total
+        act_halves.append(old_act[here] + 0.5 * (act_totals[half] / total))
+    near_sum.leaving, act_halves = together(near_sum.leaving, act_halves)
+    near_sums = near_sum.finish()
+    act_blocks = to_all(act_halves, chips)
+    for half in range(2):
+        here = slice(half * step, (half + 1) * step)
+        mixed = sum(far_across[half], near_sums[half][0]) / total
         mixed = jnp.concatenate([old_grad[here] + 0.5 * mixed[:, 0:width], mixed[:, width:]], axis=1)
         mixed_halves.append(mixed)
-    outs = chain(place, to_all(act_halves, chips), to_all(mixed_halves, chips), momentum[0], weights[0])
+    outs = chain(place, act_blocks, to_all(mixed_halves, chips), momentum[0], weights[0])
     return tuple(out[None] for out in outs)
 
 

time: 292 us -> 209 us (0.72)
  waiting for transfers between devices: 180 us -> 92.6 us
  starting transfers between devices: 39.6 us -> 47.4 us
  Pallas kernels: 58.6 us -> 53.4 us
    ppermute x53 -> x50, waiting for transfers between devices: 180 us -> 92.6 us  [swap(): return lax.ppermute(value, axis, [(i, i ^ step) for i in range(size)])]
    ppermute x53 -> x50, starting transfers between devices: 39.6 us -> 47.4 us  [swap(): return lax.ppermute(value, axis, [(i, i ^ step) for i in range(size)])]
    pallas_call x6 -> x5, Pallas kernels: 44.5 us -> 39.2 us  [the longest x4 36.8 us: bands(): pl.pallas_call(functools.partial(body, turns, block, chips, bool(seeds),...]
    unnamed x100 -> x94, local copies, waits for them, and re-layouts: 4.7 us -> 6.61 us
  transfers between devices with their start and end apart: 53 -> 50, of which waited for: 21 -> 22; matrix products, arithmetic and copies ran while one was open for 1% -> 2% of each run, Pallas kernels for 15% -> 18%
where the time goes in v3:
time: 209 us; the launch traced here: 206 us
  waiting for transfers between devices  92.6 us (44%)
  Pallas kernels  53.4 us (26%)
  starting transfers between devices  47.4 us (23%)
  local copies, waits for them, and re-layouts  7.93 us (4%)
  other arithmetic  2.59 us (1%)
    ppermute x50, waiting for transfers between devices, swap(): return lax.ppermute(value, axis, [(i, i ^ step) for i in range(size)])  92.6 us
    ppermute x50, starting transfers between devices, swap(): return lax.ppermute(value, axis, [(i, i ^ step) for i in range(size)])  47.4 us
    pallas_call x4, Pallas kernels, bands(): pl.pallas_call(functools.partial(body, turns, block, chips, bool(seeds),...  36.8 us
    pallas_call x1, Pallas kernels, chain(): pl.pallas_call(functools.partial(chain_kernel, devices), out_shape=[jax.S...  14.2 us
    unnamed x94, local copies, waits for them, and re-layouts  6.61 us
  transfers between devices with their start and end apart: 50, of which 22 were waited for; matrix products, arithmetic and copies ran while one was open for 2% of the time, Pallas kernels for 18%

profile of v3, /device:TPU:25, one launch (start us, length us, event | category | flops | bytes accessed | tf_op | source)
XLA Modules:
  0.0 205.9 jit_solution(8394336673430503662)
XLA Ops:
  0.6 2.4 %shard_map.111.refs_0_.refs_2_ = f32[264,1024]{1,0:T(8,128)} custom-call(s32[2,256]{1,0:T(2,128)} %bitcast.64, s32[1,4]{1,0:T(1,128)} %counts.1, f32[256,1024]{1,0:T(8,128)} %acts.1), custom_call_target="tpu_custom_call" | custom-call | tf_op jit(solution)/shard_map/pallas_call | solution.py:185
  7.3 6.0 %shard_map.112 = (f32[2,2,64,640]{3,2,1,0:T(8,128)}, f32[2,2,64,640]{3,2,1,0:T(8,128)}, f32[2,2,64,640]{3,2,1,0:T(8,128)}, f32[2,2,64,640]{3,2,1,0:T(8,128)}) custom-call(s32[2]{0:T(128)} %pad_add_fusion.place, f32[264,1024]{1,0:T(8,128)} %shard_map.111.refs_0_.refs_2_, f32[264,1024]{1,0:T(8,128)} %copy-done), custom_call_target="tpu_custom_call" | custom-call | tf_op jit(solution)/shard_map/pallas_call | solution.py:211
  17.1 11.0 %shard_map.113 = (f32[2,1,64,1664]{3,2,1,0:T(8,128)}, f32[2,1,64,1664]{3,2,1,0:T(8,128)}, f32[2,1,64,1664]{3,2,1,0:T(8,128)}, f32[2,1,64,1664]{3,2,1,0:T(8,128)}...) custom-call(s32[2]{0:T(128)} %pad_add_fusion.place, ...), custom_call_target="tpu_custom_call" | custom-call | tf_op jit(solution)/shard_map/pallas_call | solution.py:211
  30.4 2.2 %collective-permute-done.4.refs_1_.refs_3_ = f32[264,1024]{1,0:T(8,128)S(1)} collective-permute-done((f32[264,1024]{1,0:T(8,128)S(1)}, f32[264,1024]{1,0:T(8,128)S(1)}, u32[]{:S(2)}, u32[]{:S(2)}) %collective-permute-start.4) | collective-permute-done | bytes 1081376 | tf_op jit(solution)/shard_map/ppermute | solution.py:322
  33.5 6.7 %shard_map.114 = (f32[2,2,64,640]{3,2,1,0:T(8,128)}, f32[2,2,64,640]{3,2,1,0:T(8,128)}, f32[2,2,64,640]{3,2,1,0:T(8,128)}, f32[2,2,64,640]{3,2,1,0:T(8,128)}) custom-call(s32[2]{0:T(128)} %pad_add_fusion.place, f32[264,1024]{1,0:T(8,128)} %copy-done.1, f32[264,1024]{1,0:T(8,128)} %copy-done.2, f32[2,2,64,640]{3,2,1,0:T(8,128)} %get-tuple-element.91.refs_2_, ...), custom_call_target="tpu_custom_call" | custom-call | tf_op jit(solution)/shard_map/pallas_call | solution.py:211
  42.7 12.5 %collective-permute-done.1.refs_0_ = f32[256,1024]{1,0:T(8,128)S(1)} collective-permute-done((f32[256,1024]{1,0:T(8,128)}, f32[256,1024]{1,0:T(8,128)S(1)}, u32[]{:S(2)}, u32[]{:S(2)}) %collective-permute-start.1) | collective-permute-done | bytes 1048608 | tf_op jit(solution)/shard_map/ppermute | solution.py:322
  61.2 13.2 %shard_map.115 = (f32[2,1,64,1664]{3,2,1,0:T(8,128)}, f32[2,1,64,1664]{3,2,1,0:T(8,128)}, f32[2,1,64,1664]{3,2,1,0:T(8,128)}, f32[2,1,64,1664]{3,2,1,0:T(8,128)}...) custom-call(s32[2]{0:T(128)} %pad_add_fusion.place, ...), custom_call_target="tpu_custom_call" | custom-call | tf_op jit(solution)/shard_map/pallas_call | solution.py:211
  75.8 1.8 collective-permute-start.13
  77.7 15.7 %collective-permute-done.8 = f32[2,1,64,1664]{3,2,1,0:T(8,128)S(1)} collective-permute-done((f32[2,1,64,1664]{3,2,1,0:T(8,128)}, f32[2,1,64,1664]{3,2,1,0:T(8,128)S(1)}, u32[]{:S(2)}, u32[]{:S(2)}) %collective-permute-start.8) | collective-permute-done | bytes 852000 | tf_op jit(solution)/shard_map/ppermute | solution.py:322
  94.7 8.3 %collective-permute-done.14 = f32[1,1,64,1664]{3,2,1,0:T(8,128)S(1)} collective-permute-done((f32[1,1,64,1664]{3,2,1,0:T(8,128)S(1)}, f32[1,1,64,1664]{3,2,1,0:T(8,128)S(1)}, u32[]{:S(2)}, u32[]{:S(2)}) %collective-permute-start.14) | collective-permute-done | bytes 426016 | tf_op jit(solution)/shard_map/ppermute | solution.py:322
  107.5 13.5 %collective-permute-done.16 = f32[2,1,64,1664]{3,2,1,0:T(8,128)S(1)} collective-permute-done((f32[2,1,64,1664]{3,2,1,0:T(8,128)S(1)}, f32[2,1,64,1664]{3,2,1,0:T(8,128)S(1)}, u32[]{:S(2)}, u32[]{:S(2)}) %collective-permute-start.16) | collective-permute-done | bytes 852000 | tf_op jit(solution)/shard_map/ppermute | solution.py:322
  124.0 12.2 %collective-permute-done.33 = f32[64,1664]{1,0:T(8,128)S(1)} collective-permute-done((f32[64,1664]{1,0:T(8,128)S(1)}, f32[64,1664]{1,0:T(8,128)S(1)}, u32[]{:S(2)}, u32[]{:S(2)}) %collective-permute-start.33) | collective-permute-done | bytes 426016 | tf_op jit(solution)/shard_map/ppermute | solution.py:322
  136.3 1.8 collective-permute-start.18
  139.4 6.0 %collective-permute-done.35 = f32[64,1664]{1,0:T(8,128)S(1)} collective-permute-done((f32[64,1664]{1,0:T(8,128)S(1)}, f32[64,1664]{1,0:T(8,128)S(1)}, u32[]{:S(2)}, u32[]{:S(2)}) %collective-permute-start.35) | collective-permute-done | bytes 426016 | tf_op jit(solution)/shard_map/ppermute | solution.py:322
  145.4 1.8 collective-permute-start.25
  147.2 2.3 %collective-permute-done.34 = f32[1,1,64,1664]{3,2,1,0:T(8,128)S(1)} collective-permute-done((f32[1,1,64,1664]{3,2,1,0:T(8,128)S(1)}, f32[1,1,64,1664]{3,2,1,0:T(8,128)S(1)}, u32[]{:S(2)}, u32[]{:S(2)}) %collective-permute-start.34) | collective-permute-done | bytes 426016 | tf_op jit(solution)/shard_map/ppermute | solution.py:322
  155.6 2.0 collective-permute-start.27
  158.7 2.8 %collective-permute-start.36 = (f32[64,1664]{1,0:T(8,128)S(1)}, f32[64,1664]{1,0:T(8,128)S(1)}, u32[]{:S(2)}, u32[]{:S(2)}) collective-permute-start(f32[64,1664]{1,0:T(8,128)S(1)} %pad_maximum_fusion.refs_16_), channel_id=1, source_target_pairs={{0,4},{4,0},{8,12},{12,8},{16,20},{20,16},{24,28},{28,24},{1,5},{5... | collective-permute-start | bytes 1277960 | tf_op jit(solution)/shard_map/ppermute | solution.py:322
  168.0 3.7 %collective-permute-start.37 = (f32[64,1664]{1,0:T(8,128)S(1)}, f32[64,1664]{1,0:T(8,128)S(1)}, u32[]{:S(2)}, u32[]{:S(2)}) collective-permute-start(f32[64,1664]{1,0:T(8,128)S(1)} %pad_maximum_fusion.1.refs_17_), channel_id=1, source_target_pairs={{0,4},{4,0},{8,12},{12,8},{16,20},{20,16},{24,28},{28,24},{1,5},{5... | collective-permute-start | bytes 1277960 | tf_op jit(solution)/shard_map/ppermute | solution.py:322
  173.5 3.7 %collective-permute-done.43.refs_25_ = f32[64,1664]{1,0:T(8,128)S(1)} collective-permute-done((f32[64,1664]{1,0:T(8,128)S(1)}, f32[64,1664]{1,0:T(8,128)S(1)}, u32[]{:S(2)}, u32[]{:S(2)}) %collective-permute-start.43) | collective-permute-done | bytes 426016 | tf_op jit(solution)/shard_map/ppermute | solution.py:322
  177.5 3.9 %collective-permute-start.40 = (f32[64,1664]{1,0:T(8,128)S(1)}, f32[64,1664]{1,0:T(8,128)S(1)}, u32[]{:S(2)}, u32[]{:S(2)}) collective-permute-start(f32[64,1664]{1,0:T(8,128)S(1)} %collective-permute-done.38.refs_20_), channel_id=1, source_target_pairs={{0,4},{4,0},{8,12},{12,8},{16,20},{20,16},{24,28},{28,24},{1,5},{5... | collective-permute-start | bytes 1277960 | tf_op jit(solution)/shard_map/ppermute | solution.py:322
  181.9 4.4 %collective-permute-done.46.refs_28_ = f32[64,1664]{1,0:T(8,128)S(1)} collective-permute-done((f32[64,1664]{1,0:T(8,128)S(1)}, f32[64,1664]{1,0:T(8,128)S(1)}, u32[]{:S(2)}, u32[]{:S(2)}) %collective-permute-start.46) | collective-permute-done | bytes 426016 | tf_op jit(solution)/shard_map/ppermute | solution.py:322
  186.3 2.0 collective-permute-start.48
  191.6 14.2 %shard_map.116 = (f32[128,1024]{1,0:T(8,128)}, f32[128,1024]{1,0:T(8,128)}, f32[128,1024]{1,0:T(8,128)}, f32[128,1024]{1,0:T(8,128)}) custom-call(s32[2]{0:T(128)} %pad_add_fusion.place, f32[64,640]{1,0:T(8,128)} %copy-done.16, f32[64,640]{1,0:T(8,128)} %copy-done.15, f32[64,640]{1,0:T(8,128)} %copy-done.33, f32[64,640]{1,0:T(8,128)} %copy-done.36, ...), custom_call_target="tpu_custom_call" | custom-call | tf_op jit(solution)/shard_map/pallas_call | solution.py:309
  (202 shorter events, 49.9 us)
Async XLA Ops:
  3.7 25.7 %collective-permute-start.2 = (f32[264,1024]{1,0:T(8,128)}, f32[264,1024]{1,0:T(8,128)S(1)}, u32[]{:S(2)}, u32[]{:S(2)}) collective-permute-start(f32[264,1024]{1,0:T(8,128)} %shard_map.111.refs_0_.refs_2_), channel_id=1, source_target_pairs={{0,1},{1,0},{2,3},{3,2},{4,5},{5,4},{6,7},{7,6},{8,9},{9,8},{10,11... | collective-permute-start | bytes 3244040 | tf_op jit(solution)/shard_map/ppermute | solution.py:322
  30.2 25.0 %collective-permute-start.1 = (f32[256,1024]{1,0:T(8,128)}, f32[256,1024]{1,0:T(8,128)S(1)}, u32[]{:S(2)}, u32[]{:S(2)}) collective-permute-start(f32[256,1024]{1,0:T(8,128)} %refs_0_), channel_id=1, source_target_pairs={{0,1},{1,0},{2,3},{3,2},{4,5},{5,4},{6,7},{7,6},{8,9},{9,8},{10,11... | collective-permute-start | bytes 3145736 | tf_op jit(solution)/shard_map/ppermute | solution.py:322
  40.2 16.2 %collective-permute-start.6 = (f32[2,2,64,640]{3,2,1,0:T(8,128)}, f32[2,2,64,640]{3,2,1,0:T(8,128)S(1)}, u32[]{:S(2)}, u32[]{:S(2)}) collective-permute-start(f32[2,2,64,640]{3,2,1,0:T(8,128)} %get-tuple-element.107), channel_id=1, source_target_pairs={{0,8},{4,12},{8,0},{12,4},{16,24},{20,28},{24,16},{28,20},{1,9},{5... | collective-permute-start | bytes 1966088 | tf_op jit(solution)/shard_map/ppermute | solution.py:322
  41.5 16.1 %collective-permute-start.7 = (f32[2,2,64,640]{3,2,1,0:T(8,128)}, f32[2,2,64,640]{3,2,1,0:T(8,128)S(1)}, u32[]{:S(2)}, u32[]{:S(2)}) collective-permute-start(f32[2,2,64,640]{3,2,1,0:T(8,128)} %get-tuple-element.109), channel_id=1, source_target_pairs={{0,16},{4,20},{8,24},{12,28},{16,0},{20,4},{24,8},{28,12},{1,17},{... | collective-permute-start | bytes 1966088 | tf_op jit(solution)/shard_map/ppermute | solution.py:322
  57.7 17.1 %collective-permute-start.10 = (f32[1,2,64,640]{3,2,1,0:T(8,128)S(1)}, f32[1,2,64,640]{3,2,1,0:T(8,128)S(1)}, u32[]{:S(2)}, u32[]{:S(2)}) collective-permute-start(f32[1,2,64,640]{3,2,1,0:T(8,128)S(1)} %get-tuple-element.126), channel_id=1, source_target_pairs={{0,16},{4,20},{8,24},{12,28},{16,0},{20,4},{24,8},{28,12},{1,17},{... | collective-permute-start | bytes 983048 | tf_op jit(solution)/shard_map/ppermute | solution.py:322
  59.0 16.8 %collective-permute-start.12 = (f32[1,2,64,640]{3,2,1,0:T(8,128)S(1)}, f32[1,2,64,640]{3,2,1,0:T(8,128)S(1)}, u32[]{:S(2)}, u32[]{:S(2)}) collective-permute-start(f32[1,2,64,640]{3,2,1,0:T(8,128)S(1)} %get-tuple-element.128), channel_id=1, source_target_pairs={{0,8},{4,12},{8,0},{12,4},{16,24},{20,28},{24,16},{28,20},{1,9},{5... | collective-permute-start | bytes 983048 | tf_op jit(solution)/shard_map/ppermute | solution.py:322
  74.4 19.0 %collective-permute-start.8 = (f32[2,1,64,1664]{3,2,1,0:T(8,128)}, f32[2,1,64,1664]{3,2,1,0:T(8,128)S(1)}, u32[]{:S(2)}, u32[]{:S(2)}) collective-permute-start(f32[2,1,64,1664]{3,2,1,0:T(8,128)} %get-tuple-element.122), channel_id=1, source_target_pairs={{0,8},{4,12},{8,0},{12,4},{16,24},{20,28},{24,16},{28,20},{1,9},{5... | collective-permute-start | bytes 2555912 | tf_op jit(solution)/shard_map/ppermute | solution.py:322
  74.8 19.4 %collective-permute-start.11 = (f32[64,640]{1,0:T(8,128)S(1)}, f32[64,640]{1,0:T(8,128)S(1)}, u32[]{:S(2)}, u32[]{:S(2)}) collective-permute-start(f32[64,640]{1,0:T(8,128)S(1)} %slice_bitcast_fusion.3), channel_id=1, source_target_pairs={{0,2},{1,3},{2,0},{3,1},{4,6},{5,7},{6,4},{7,5},{8,10},{9,11},{10,... | collective-permute-start | bytes 491528 | tf_op jit(solution)/shard_map/ppermute | solution.py:322
  75.5 18.7 %collective-permute-start.9 = (f32[2,1,64,1664]{3,2,1,0:T(8,128)S(1)}, f32[2,1,64,1664]{3,2,1,0:T(8,128)S(1)}, u32[]{:S(2)}, u32[]{:S(2)}) collective-permute-start(f32[2,1,64,1664]{3,2,1,0:T(8,128)S(1)} %copy-done.46), channel_id=1, source_target_pairs={{0,16},{4,20},{8,24},{12,28},{16,0},{20,4},{24,8},{28,12},{1,17},{... | collective-permute-start | bytes 2555912 | tf_op jit(solution)/shard_map/ppermute | solution.py:322
  75.8 18.4 %collective-permute-start.13 = (f32[64,640]{1,0:T(8,128)S(1)}, f32[64,640]{1,0:T(8,128)S(1)}, u32[]{:S(2)}, u32[]{:S(2)}) collective-permute-start(f32[64,640]{1,0:T(8,128)S(1)} %slice_bitcast_fusion.2), channel_id=1, source_target_pairs={{0,2},{1,3},{2,0},{3,1},{4,6},{5,7},{6,4},{7,5},{8,10},{9,11},{10,... | collective-permute-start | bytes 491528 | tf_op jit(solution)/shard_map/ppermute | solution.py:322
  104.2 16.8 %collective-permute-start.16 = (f32[2,1,64,1664]{3,2,1,0:T(8,128)S(1)}, f32[2,1,64,1664]{3,2,1,0:T(8,128)S(1)}, u32[]{:S(2)}, u32[]{:S(2)}) collective-permute-start(f32[2,1,64,1664]{3,2,1,0:T(8,128)S(1)} %copy-done.45), channel_id=1, source_target_pairs={{0,8},{4,12},{8,0},{12,4},{16,24},{20,28},{24,16},{28,20},{1,9},{5... | collective-permute-start | bytes 2555912 | tf_op jit(solution)/shard_map/ppermute | solution.py:322
  104.5 16.7 %collective-permute-start.17 = (f32[2,1,64,1664]{3,2,1,0:T(8,128)S(1)}, f32[2,1,64,1664]{3,2,1,0:T(8,128)S(1)}, u32[]{:S(2)}, u32[]{:S(2)}) collective-permute-start(f32[2,1,64,1664]{3,2,1,0:T(8,128)S(1)} %copy-done.44), channel_id=1, source_target_pairs={{0,16},{4,20},{8,24},{12,28},{16,0},{20,4},{24,8},{28,12},{1,17},{... | collective-permute-start | bytes 2555912 | tf_op jit(solution)/shard_map/ppermute | solution.py:322
  106.0 30.3 %collective-permute-start.33 = (f32[64,1664]{1,0:T(8,128)S(1)}, f32[64,1664]{1,0:T(8,128)S(1)}, u32[]{:S(2)}, u32[]{:S(2)}) collective-permute-start(f32[64,1664]{1,0:T(8,128)S(1)} %bitcast.63), channel_id=1, source_target_pairs={{0,2},{1,3},{2,0},{3,1},{4,6},{5,7},{6,4},{7,5},{8,10},{9,11},{10,... | collective-permute-start | bytes 1277960 | tf_op jit(solution)/shard_map/ppermute | solution.py:322
  121.2 16.9 %collective-permute-start.32 = (f32[1,1,64,1664]{3,2,1,0:T(8,128)S(1)}, f32[1,1,64,1664]{3,2,1,0:T(8,128)S(1)}, u32[]{:S(2)}, u32[]{:S(2)}) collective-permute-start(f32[1,1,64,1664]{3,2,1,0:T(8,128)S(1)} %slice_add_fusion.3), channel_id=1, source_target_pairs={{0,16},{4,20},{8,24},{12,28},{16,0},{20,4},{24,8},{28,12},{1,17},{... | collective-permute-start | bytes 1277960 | tf_op jit(solution)/shard_map/ppermute | solution.py:322
  121.9 23.5 %collective-permute-start.35 = (f32[64,1664]{1,0:T(8,128)S(1)}, f32[64,1664]{1,0:T(8,128)S(1)}, u32[]{:S(2)}, u32[]{:S(2)}) collective-permute-start(f32[64,1664]{1,0:T(8,128)S(1)} %bitcast.62), channel_id=1, source_target_pairs={{0,2},{1,3},{2,0},{3,1},{4,6},{5,7},{6,4},{7,5},{8,10},{9,11},{10,... | collective-permute-start | bytes 1277960 | tf_op jit(solution)/shard_map/ppermute | solution.py:322
  122.5 28.3 %collective-permute-start.24 = (f32[64,640]{1,0:T(8,128)S(1)}, f32[64,640]{1,0:T(8,128)S(1)}, u32[]{:S(2)}, u32[]{:S(2)}) collective-permute-start(f32[64,640]{1,0:T(8,128)S(1)} %get-tuple-element.139.refs_0_), channel_id=1, source_target_pairs={{0,16},{4,20},{8,24},{12,28},{16,0},{20,4},{24,8},{28,12},{1,17},{... | collective-permute-start | bytes 491528 | tf_op jit(solution)/shard_map/ppermute | solution.py:322
  123.6 28.5 %collective-permute-start.20 = (f32[64,640]{1,0:T(8,128)S(1)}, f32[64,640]{1,0:T(8,128)S(1)}, u32[]{:S(2)}, u32[]{:S(2)}) collective-permute-start(f32[64,640]{1,0:T(8,128)S(1)} %get-tuple-element.139.refs_0_), channel_id=1, source_target_pairs={{0,8},{4,12},{8,0},{12,4},{16,24},{20,28},{24,16},{28,20},{1,9},{5... | collective-permute-start | bytes 491528 | tf_op jit(solution)/shard_map/ppermute | solution.py:322
  136.3 16.0 %collective-permute-start.18 = (f32[64,640]{1,0:T(8,128)S(1)}, f32[64,640]{1,0:T(8,128)S(1)}, u32[]{:S(2)}, u32[]{:S(2)}) collective-permute-start(f32[64,640]{1,0:T(8,128)S(1)} %get-tuple-element.139.refs_0_), channel_id=1, source_target_pairs={{0,4},{4,0},{8,12},{12,8},{16,20},{20,16},{24,28},{28,24},{1,5},{5... | collective-permute-start | bytes 491528 | tf_op jit(solution)/shard_map/ppermute | solution.py:322
  158.4 13.3 %collective-permute-start.38 = (f32[64,1664]{1,0:T(8,128)S(1)}, f32[64,1664]{1,0:T(8,128)S(1)}, u32[]{:S(2)}, u32[]{:S(2)}) collective-permute-start(f32[64,1664]{1,0:T(8,128)S(1)} %pad_maximum_fusion.refs_16_), channel_id=1, source_target_pairs={{0,8},{4,12},{8,0},{12,4},{16,24},{20,28},{24,16},{28,20},{1,9},{5... | collective-permute-start | bytes 1277960 | tf_op jit(solution)/shard_map/ppermute | solution.py:322
  158.7 13.9 %collective-permute-start.36 = (f32[64,1664]{1,0:T(8,128)S(1)}, f32[64,1664]{1,0:T(8,128)S(1)}, u32[]{:S(2)}, u32[]{:S(2)}) collective-permute-start(f32[64,1664]{1,0:T(8,128)S(1)} %pad_maximum_fusion.refs_16_), channel_id=1, source_target_pairs={{0,4},{4,0},{8,12},{12,8},{16,20},{20,16},{24,28},{28,24},{1,5},{5... | collective-permute-start | bytes 1277960 | tf_op jit(solution)/shard_map/ppermute | solution.py:322
  161.4 15.7 %collective-permute-start.43 = (f32[64,1664]{1,0:T(8,128)S(1)}, f32[64,1664]{1,0:T(8,128)S(1)}, u32[]{:S(2)}, u32[]{:S(2)}) collective-permute-start(f32[64,1664]{1,0:T(8,128)S(1)} %pad_maximum_fusion.1.refs_17_), channel_id=1, source_target_pairs={{0,16},{4,20},{8,24},{12,28},{16,0},{20,4},{24,8},{28,12},{1,17},{... | collective-permute-start | bytes 1277960 | tf_op jit(solution)/shard_map/ppermute | solution.py:322
  165.0 12.5 %collective-permute-start.39 = (f32[64,1664]{1,0:T(8,128)S(1)}, f32[64,1664]{1,0:T(8,128)S(1)}, u32[]{:S(2)}, u32[]{:S(2)}) collective-permute-start(f32[64,1664]{1,0:T(8,128)S(1)} %pad_maximum_fusion.1.refs_17_), channel_id=1, source_target_pairs={{0,8},{4,12},{8,0},{12,4},{16,24},{20,28},{24,16},{28,20},{1,9},{5... | collective-permute-start | bytes 1277960 | tf_op jit(solution)/shard_map/ppermute | solution.py:322
  168.0 13.3 %collective-permute-start.37 = (f32[64,1664]{1,0:T(8,128)S(1)}, f32[64,1664]{1,0:T(8,128)S(1)}, u32[]{:S(2)}, u32[]{:S(2)}) collective-permute-start(f32[64,1664]{1,0:T(8,128)S(1)} %pad_maximum_fusion.1.refs_17_), channel_id=1, source_target_pairs={{0,4},{4,0},{8,12},{12,8},{16,20},{20,16},{24,28},{28,24},{1,5},{5... | collective-permute-start | bytes 1277960 | tf_op jit(solution)/shard_map/ppermute | solution.py:322
  172.6 13.7 %collective-permute-start.46 = (f32[64,1664]{1,0:T(8,128)S(1)}, f32[64,1664]{1,0:T(8,128)S(1)}, u32[]{:S(2)}, u32[]{:S(2)}) collective-permute-start(f32[64,1664]{1,0:T(8,128)S(1)} %collective-permute-done.38.refs_20_), channel_id=1, source_target_pairs={{0,16},{4,20},{8,24},{12,28},{16,0},{20,4},{24,8},{28,12},{1,17},{... | collective-permute-start | bytes 1277960 | tf_op jit(solution)/shard_map/ppermute | solution.py:322
  (73 other events, 990.4 us)

commit v4 on v3

--- a/solution.py
+++ b/solution.py
@@ -10,7 +10,7 @@
 F32 = jnp.float32
 BF16 = jnp.bfloat16
 TILE = 128
-VMEM_LIMIT = 56 * 1024 * 1024
+MIB = 1024 * 1024
 
 
 def split(value):
@@ -191,7 +191,7 @@
             pl.BlockSpec(memory_space=pltpu.VMEM),
         ],
         out_specs=pl.BlockSpec(memory_space=pltpu.VMEM),
-        compiler_params=pltpu.CompilerParams(vmem_limit_bytes=VMEM_LIMIT),
+        compiler_params=pltpu.CompilerParams(vmem_limit_bytes=16 * MIB),
     )(routes.T, counts, acts)
 
 
@@ -208,13 +208,14 @@
         for group in held_and_sent(chips, order)
     ]
     operands = (*parts, *seeds)
+    limit = 36 if len(parts) > 2 else 20
     return pl.pallas_call(
         functools.partial(body, turns, block, chips, bool(seeds), samples),
         out_shape=shapes,
         in_specs=[pl.BlockSpec(memory_space=pltpu.SMEM)] + whole_in_vmem(len(operands)),
         out_specs=whole_in_vmem(len(shapes)),
         scratch_shapes=scratch + [pltpu.VMEM((TILE, 2 * samples), F32)],
-        compiler_params=pltpu.CompilerParams(vmem_limit_bytes=VMEM_LIMIT),
+        compiler_params=pltpu.CompilerParams(vmem_limit_bytes=limit * MIB),
     )(place, *operands)
 
 
@@ -250,71 +251,90 @@
     return first[0:rows] + first[rows : 2 * rows] + dot(top, low[...])
 
 
-def chain_kernel(devices, place, *refs):
-    pieces = 2 * devices
-    act_blocks, mixed_blocks = refs[:pieces], refs[pieces : 2 * pieces]
-    momentum, weights, act_out, grad_out, moment_out, weight_out = refs[2 * pieces : 2 * pieces + 6]
-    bands, full, act_high, act_low, high, low, mid_high, mid_low = refs[2 * pieces + 6 :]
-    block, feat = momentum.shape
-    width = act_blocks[0].shape[1]
-    mine = place[0]
-    own = pl.ds(pl.multiple_of(mine * block, block), block)
+def row_pieces(place, block, count):
     step = block // 2
-    here = [
-        pl.ds(pl.multiple_of((mine ^ k) * block + half * step, step), step)
-        for k in range(devices)
-        for half in range(2)
+    return [
+        pl.ds(pl.multiple_of((place[0] ^ (number // 2)) * block + number % 2 * step, step), step)
+        for number in range(count)
     ]
-    for k in range(pieces):
-        bands[here[k], :] = act_blocks[k][...]
+
+
+def factor_rows(place, block, blocks, bands, full):
+    for here, value in zip(row_pieces(place, block, len(blocks)), blocks):
+        bands[here, :] = value[...]
     unfold(bands, full)
-    act_out[...] = full[own, :]
-    act_damp, act_alpha = damping(full)
-    top, rest = split(full[...])
-    act_high[...] = top
-    act_low[...] = rest
-    for k in range(pieces):
-        bands[here[k], :] = mixed_blocks[k][:, 0:width]
-    unfold(bands, full)
-    rows = full[own, :]
-    grad_out[...] = rows
+    return full[pl.ds(pl.multiple_of(place[0] * block, block), block), :]
+
+
+def act_factor_kernel(place, *refs):
+    blocks, (factor, scales, high, low), (bands, full) = refs[:-6], refs[-6:-2], refs[-2:]
+    factor[...] = factor_rows(place, factor.shape[0], blocks, bands, full)
     damp, alpha = damping(full)
-    top, rest = split(full[...])
-    high[...] = top
-    low[...] = rest
-    for k in range(pieces):
-        top, rest = split(mixed_blocks[k][:, width : width + feat])
-        mid_high[here[k], :] = top
-        mid_low[here[k], :] = rest
+    scales[0:1, :] = jnp.broadcast_to(damp, (1, TILE))
+    scales[1:2, :] = jnp.broadcast_to(alpha, (1, TILE))
+    high[...], low[...] = split(full[...])
+
+
+def grad_factor_kernel(place, *refs):
+    blocks, (factor, inverse), (bands, full, high, low) = refs[:-6], refs[-6:-4], refs[-4:]
+    block, feat = factor.shape
+    rows = factor_rows(place, block, blocks, bands, full)
+    factor[...] = rows
+    damp, alpha = damping(full)
+    high[...], low[...] = split(full[...])
     lanes = lax.broadcasted_iota(jnp.int32, (block, feat), 1)
     sublanes = lax.broadcasted_iota(jnp.int32, (block, feat), 0)
-    unit = jnp.where(lanes == sublanes + mine * block, 1.0, 0.0).astype(F32)
+    unit = jnp.where(lanes == sublanes + place[0] * block, 1.0, 0.0).astype(F32)
     rest_rows = unit - alpha * (rows + damp * unit)
     once = 2.0 * rest_rows - alpha * (times(rest_rows, high, low) + damp * rest_rows)
-    left = alpha * (unit + rest_rows + once - alpha * (times(once, high, low) + damp * once))
-    half_way = times(left, mid_high, mid_low)
+    inverse[...] = alpha * (unit + rest_rows + once - alpha * (times(once, high, low) + damp * once))
+
+
+def update_kernel(place, *refs):
+    blocks = refs[:-9]
+    inverse, scales, act_high, act_low, momentum, weights, moment_out, weight_out, full = refs[-9:]
+    for here, value in zip(row_pieces(place, momentum.shape[0], len(blocks)), blocks):
+        full[here, :] = value[...]
+    damp, alpha = scales[0:1, 0:1], scales[1:2, 0:1]
+    half_way = times(inverse[...], *split(full[...]))
     value = half_way
     for _ in range(3):
-        value = half_way + value - act_alpha * (times(value, act_high, act_low) + act_damp * value)
-    moment = 0.9 * momentum[...] + act_alpha * value
+        value = half_way + value - alpha * (times(value, act_high[...], act_low[...]) + damp * value)
+    moment = 0.9 * momentum[...] + alpha * value
     moment_out[...] = moment
     weight_out[...] = weights[...] - 0.5 * moment
 
 
-def chain(place, act_blocks, mixed_blocks, momentum, weights):
-    devices = len(act_blocks) // 2
+def on_core(body, place, operands, shapes, scratch, limit):
+    return pl.pallas_call(
+        body,
+        out_shape=shapes,
+        in_specs=[pl.BlockSpec(memory_space=pltpu.SMEM)] + whole_in_vmem(len(operands)),
+        out_specs=whole_in_vmem(len(shapes)),
+        scratch_shapes=scratch,
+        compiler_params=pltpu.CompilerParams(vmem_limit_bytes=limit * MIB),
+    )(place, *operands)
+
+
+def act_factor_rows(place, blocks, block, feat):
+    shapes = [((block, feat), F32), ((8, TILE), F32), ((feat, feat), BF16), ((feat, feat), BF16)]
+    shapes = [jax.ShapeDtypeStruct(*shape) for shape in shapes]
+    scratch = [pltpu.VMEM((feat, blocks[0].shape[1]), F32), pltpu.VMEM((feat, feat), F32)]
+    return on_core(act_factor_kernel, place, blocks, shapes, scratch, 32)
+
+
+def grad_factor_rows(place, blocks, block, feat):
+    shapes = [jax.ShapeDtypeStruct((block, feat), F32)] * 2
+    scratch = [pltpu.VMEM((feat, blocks[0].shape[1]), F32), pltpu.VMEM((feat, feat), F32)]
+    scratch += [pltpu.VMEM((feat, feat), BF16)] * 2
+    return on_core(grad_factor_kernel, place, blocks, shapes, scratch, 32)
+
+
+def update_rows(place, blocks, inverse, scales, high, low, momentum, weights):
     block, feat = momentum.shape
-    width = act_blocks[0].shape[1]
-    square = (feat, feat)
-    return pl.pallas_call(
-        functools.partial(chain_kernel, devices),
-        out_shape=[jax.ShapeDtypeStruct((block, feat), F32)] * 4,
-        in_specs=[pl.BlockSpec(memory_space=pltpu.SMEM)] + whole_in_vmem(4 * devices + 2),
-        out_specs=whole_in_vmem(4),
-        scratch_shapes=[pltpu.VMEM((feat, width), F32), pltpu.VMEM(square, F32)]
-        + [pltpu.VMEM(square, BF16)] * 6,
-        compiler_params=pltpu.CompilerParams(vmem_limit_bytes=VMEM_LIMIT),
-    )(place, *act_blocks, *mixed_blocks, momentum, weights)
+    operands = (*blocks, inverse, scales, high, low, momentum, weights)
+    shapes = [jax.ShapeDtypeStruct((block, feat), F32)] * 2
+    return on_core(update_kernel, place, operands, shapes, [pltpu.VMEM((feat, feat), F32)], 32)
 
 
 def swap(value, axis, step):
@@ -354,17 +374,36 @@
     return [swap(far[number], "expert", 2 * (number + 1)) for number in range(far.shape[0])]
 
 
-def to_all(halves, chips):
-    pieces = {}
-    for half, order in enumerate(orders(chips)):
-        held = {0: halves[half]}
-        for bit in order:
-            for k in list(held):
-                held[k | (1 << bit)] = swap(held[k], "dp", 2 << bit)
-        for k in range(chips):
-            pieces[2 * k, half] = held[k]
-            pieces[2 * k + 1, half] = swap(held[k], "dp", 1)
-    return [pieces[k, half] for k in range(2 * chips) for half in range(2)]
+class Gather:
+    def __init__(self, halves, chips):
+        self.chips, self.orders = chips, orders(chips)
+        self.held = [{0: value} for value in halves]
+
+    def step(self, half, bit):
+        held = self.held[half]
+        for k in list(held):
+            held[k | (1 << bit)] = swap(held[k], "dp", 2 << bit)
+
+    def begin(self):
+        for half, order in enumerate(self.orders):
+            for bit in order[:1]:
+                self.step(half, bit)
+        return [held[max(held)] for held in self.held]
+
+    def relay(self):
+        for half, order in enumerate(self.orders):
+            for bit in order[1:]:
+                self.step(half, bit)
+
+    def finish(self, *before):
+        pieces = {}
+        for half in range(2):
+            last = self.chips - 1
+            self.held[half][last], before = together(self.held[half][last], before)
+            for k in range(self.chips):
+                pieces[2 * k, half] = self.held[half][k]
+                pieces[2 * k + 1, half] = swap(self.held[half][k], "dp", 1)
+        return [pieces[k, half] for k in range(2 * self.chips) for half in range(2)]
 
 
 def together(*values):
@@ -392,12 +431,12 @@
     acts_far = swap(acts, "expert", 1)
     near_acts = (acts, swap(acts, "dp", 1))
     act_seeds = bands(act_kernel, (turns,), place, near_acts, (), *size)
-    grads_out, act_seeds = together(grads_out, act_seeds)
     grads_far = swap(grads_out, "expert", 1)
     grad_parts = (grads_out, swap(grads_out, "dp", 1)) + near_acts
     grad_seeds = bands(grad_kernel, (1, turns - 1), place, grad_parts, (), *mixed_size)
     old_act, old_grad = own_band(old_act_factor), own_band(old_grad_factor)
-    acts_far, grad_seeds, old_act, old_grad = together(acts_far, grad_seeds, old_act, old_grad)
+    early = (act_seeds, grad_seeds, old_act, old_grad)
+    acts_far, (act_seeds, grad_seeds, old_act, old_grad) = together(acts_far, early)
 
     far_acts = (acts_far, swap(acts_far, "dp", 1))
     act_sum = PlaneSum(bands(act_kernel, (turns,), place, far_acts, act_seeds, *size), chips)
@@ -418,28 +457,47 @@
     far_sum.add()
     far_sum.leaving, act_across = together(far_sum.leaving, act_across)
     far_sums = far_sum.finish()
-    far_sums, near_sum.leaving = together(far_sums, near_sum.leaving)
-    far_across = [across(total) for total in far_sums]
-    near_sum.send()
-    near_sum.add()
 
     step = block // 2
+    parts = [slice(half * step, (half + 1) * step) for half in range(2)]
     act_totals = [sum(there, total[0]) for total, there in zip(act_sums, act_across)]
     total = jnp.maximum(act_totals[1][-1:, 0:1], 1.0)
-    act_halves, mixed_halves = [], []
-    for half in range(2):
-        here = slice(half * step, (half + 1) * step)
-        act_halves.append(old_act[here] + 0.5 * (act_totals[half] / total))
-    near_sum.leaving, act_halves = together(near_sum.leaving, act_halves)
+    act_halves = [old_act[here] + 0.5 * (value / total) for here, value in zip(parts, act_totals)]
+    far_sums, act_halves = together(far_sums, act_halves)
+    across_grad = across(jnp.stack([value[:, :, 0:width] for value in far_sums], axis=1))
+    far_mixed = [value[:, :, width:] for value in far_sums]
+    act_gather = Gather(act_halves, chips)
+    act_gather.begin()
+    act_gather.relay()
+    early = (act_gather.held, across_grad, far_mixed)
+    near_sum.leaving, (act_gather.held, across_grad, far_mixed) = together(near_sum.leaving, early)
+    across_mixed = [across(value) for value in far_mixed]
+    near_sum.send()
+    act_out, *act_square = act_factor_rows(place, act_gather.finish(), block, feat)
+    near_sum.held, across_mixed[0] = together(near_sum.held, across_mixed[0])
+    near_sum.add()
+    near_sum.send()
+    near_sum.held, across_mixed[1], act_square = together(near_sum.held, across_mixed[1], act_square)
+    near_sum.add()
     near_sums = near_sum.finish()
-    act_blocks = to_all(act_halves, chips)
-    for half in range(2):
-        here = slice(half * step, (half + 1) * step)
-        mixed = sum(far_across[half], near_sums[half][0]) / total
-        mixed = jnp.concatenate([old_grad[here] + 0.5 * mixed[:, 0:width], mixed[:, width:]], axis=1)
-        mixed_halves.append(mixed)
-    outs = chain(place, act_blocks, to_all(mixed_halves, chips), momentum[0], weights[0])
-    return tuple(out[None] for out in outs)
+
+    grad_stats = [
+        sum((there[half] for there in across_grad), value[0, :, 0:width]) / total
+        for half, value in enumerate(near_sums)
+    ]
+    mixed = [sum(there, value[0, :, width:]) / total for value, there in zip(near_sums, across_mixed)]
+    grad_halves = [old_grad[here] + 0.5 * value for here, value in zip(parts, grad_stats)]
+    grad_gather = Gather(grad_halves, chips)
+    arrived = grad_gather.begin()
+    mixed, arrived = together(mixed, arrived)
+    mixed_gather = Gather(mixed, chips)
+    mixed_gather.begin()
+    grad_gather.relay()
+    mixed_gather.relay()
+    grad_out, inverse = grad_factor_rows(place, grad_gather.finish(), block, feat)
+    mixed_blocks = mixed_gather.finish(inverse)
+    outs = update_rows(place, mixed_blocks, inverse, *act_square, momentum[0], weights[0])
+    return tuple(out[None] for out in (act_out, grad_out, *outs))
 
 
 def solution(mesh):

time: 209 us -> 211 us (level)
  Pallas kernels: 53.4 us -> 35.7 us
  waiting for transfers between devices: 92.6 us -> 109 us
  starting transfers between devices: 47.4 us -> 53.5 us
  local copies, waits for them, and re-layouts: 7.93 us -> 5.81 us
    ppermute x50 -> x65, waiting for transfers between devices: 92.6 us -> 109 us  [swap(): return lax.ppermute(value, axis, [(i, i ^ step) for i in range(size)])]
    pallas_call x4, Pallas kernels: 36.8 us -> 22.5 us  [bands(): pl.pallas_call(functools.partial(body, turns, block, chips, bool(seeds),...]
    ppermute x50 -> x65, starting transfers between devices: 47.4 us -> 53.5 us  [swap(): return lax.ppermute(value, axis, [(i, i ^ step) for i in range(size)])]
    unnamed x94 -> x10, local copies, waits for them, and re-layouts: 6.61 us -> 2.57 us
    pallas_call x1 -> x3, Pallas kernels: 14.2 us -> 12.4 us  [on_core(): pl.pallas_call(body, out_shape=shapes, in_specs=[pl.BlockSpec(memory_spac...]
  transfers between devices with their start and end apart: 50 -> 65, of which waited for: 22 -> 27; matrix products, arithmetic and copies ran while one was open for 2% -> 3% of each run, Pallas kernels for 18% -> 14%
where the time goes in v4:
time: 211 us; the launch traced here: 208 us
  waiting for transfers between devices  109 us (52%)
  starting transfers between devices  53.5 us (25%)
  Pallas kernels  35.7 us (17%)
  local copies, waits for them, and re-layouts  5.81 us (3%)
  other arithmetic  2.22 us (1%)
    ppermute x65, waiting for transfers between devices, swap(): return lax.ppermute(value, axis, [(i, i ^ step) for i in range(size)])  109 us
    ppermute x65, starting transfers between devices, swap(): return lax.ppermute(value, axis, [(i, i ^ step) for i in range(size)])  53.5 us
    pallas_call x4, Pallas kernels, bands(): pl.pallas_call(functools.partial(body, turns, block, chips, bool(seeds),...  22.5 us
    pallas_call x3, Pallas kernels, on_core(): pl.pallas_call(body, out_shape=shapes, in_specs=[pl.BlockSpec(memory_spac...  12.4 us
  transfers between devices with their start and end apart: 65, of which 27 were waited for; matrix products, arithmetic and copies ran while one was open for 3% of the time, Pallas kernels for 14%

profile of v4, /device:TPU:25, one launch (start us, length us, event | category | flops | bytes accessed | tf_op | source)
XLA Modules:
  0.0 207.9 jit_solution(12445075290208357184)
XLA Ops:
  9.0 3.7 %shard_map.112 = (f32[2,2,64,640]{3,2,1,0:T(8,128)S(1)}, f32[2,2,64,640]{3,2,1,0:T(8,128)S(1)}, f32[2,2,64,640]{3,2,1,0:T(8,128)S(1)}, f32[2,2,64,640]{3,2,1,0:T(8,128)S(1)}) custom-call(s32[2]{0:T(128)S(1)} %pad_add_fusion.place, f32[264,1024]{1,0:T(8,128)S(1)} %shard_map.111.refs_0_.refs_2_, f32[264,1024]{1,0:T(8,128)S(1)} %collective-permute-done.2.refs_1_.refs_3_), custom_call_target="tpu_custom_call" | custom-call | tf_op jit(solution)/shard_map/pallas_call | solution.py:212
  12.8 7.9 %shard_map.113 = (f32[2,1,64,1664]{3,2,1,0:T(8,128)S(1)}, f32[2,1,64,1664]{3,2,1,0:T(8,128)S(1)}, f32[2,1,64,1664]{3,2,1,0:T(8,128)S(1)}, f32[2,1,64,1664]{3,2,1...) custom-call(s32[2]{0:T(128)S(1)} %pad_add_fusion.place, ...), custom_call_target="tpu_custom_call" | custom-call | tf_op jit(solution)/shard_map/pallas_call | solution.py:212
  20.6 9.4 %collective-permute-done.1.refs_0_.refs_2_ = f32[264,1024]{1,0:T(8,128)S(1)} collective-permute-done((f32[264,1024]{1,0:T(8,128)S(1)}, f32[264,1024]{1,0:T(8,128)S(1)}, u32[]{:S(2)}, u32[]{:S(2)}) %collective-permute-start.1) | collective-permute-done | bytes 1081376 | tf_op jit(solution)/shard_map/ppermute | solution.py:342
  33.2 3.8 %shard_map.114 = (f32[2,2,64,640]{3,2,1,0:T(8,128)S(1)}, f32[2,2,64,640]{3,2,1,0:T(8,128)S(1)}, f32[2,2,64,640]{3,2,1,0:T(8,128)S(1)}, f32[2,2,64,640]{3,2,1,0:T(8,128)S(1)}) custom-call(s32[2]{0:T(128)S(1)} %pad_add_fusion.place, f32[264,1024]{1,0:T(8,128)S(1)} %collective-permute-done.1.refs_0_.refs_2_, ...), custom_call_target="tpu_custom_call" | custom-call | tf_op jit(solution)/shard_map/pallas_call | solution.py:212
  39.5 16.4 %collective-permute-done.refs_0_ = f32[256,1024]{1,0:T(8,128)S(1)} collective-permute-done((f32[256,1024]{1,0:T(8,128)}, f32[256,1024]{1,0:T(8,128)S(1)}, u32[]{:S(2)}, u32[]{:S(2)}) %collective-permute-start) | collective-permute-done | bytes 1048608 | tf_op jit(solution)/shard_map/ppermute | solution.py:342
  59.4 7.2 %shard_map.115 = (f32[2,1,64,1664]{3,2,1,0:T(8,128)S(1)}, f32[2,1,64,1664]{3,2,1,0:T(8,128)S(1)}, f32[2,1,64,1664]{3,2,1,0:T(8,128)S(1)}, f32[2,1,64,1664]{3,2,1...) custom-call(s32[2]{0:T(128)S(1)} %pad_add_fusion.place, ...), custom_call_target="tpu_custom_call" | custom-call | tf_op jit(solution)/shard_map/pallas_call | solution.py:212
  69.0 2.4 %collective-permute-start.13 = (f32[64,640]{1,0:T(8,128)S(1)}, f32[64,640]{1,0:T(8,128)S(1)}, u32[]{:S(2)}, u32[]{:S(2)}) collective-permute-start(f32[64,640]{1,0:T(8,128)S(1)} %slice_bitcast_fusion.4), channel_id=1, source_target_pairs={{0,2},{1,3},{2,0},{3,1},{4,6},{5,7},{6,4},{7,5},{8,10},{9,11},{10,... | collective-permute-start | bytes 491528 | tf_op jit(solution)/shard_map/ppermute | solution.py:342
  71.3 15.3 %collective-permute-done.8 = f32[2,1,64,1664]{3,2,1,0:T(8,128)S(1)} collective-permute-done((f32[2,1,64,1664]{3,2,1,0:T(8,128)S(1)}, f32[2,1,64,1664]{3,2,1,0:T(8,128)S(1)}, u32[]{:S(2)}, u32[]{:S(2)}) %collective-permute-start.8) | collective-permute-done | bytes 852000 | tf_op jit(solution)/shard_map/ppermute | solution.py:342
  90.3 6.5 %collective-permute-done.14 = f32[1,1,64,1664]{3,2,1,0:T(8,128)S(1)} collective-permute-done((f32[1,1,64,1664]{3,2,1,0:T(8,128)S(1)}, f32[1,1,64,1664]{3,2,1,0:T(8,128)S(1)}, u32[]{:S(2)}, u32[]{:S(2)}) %collective-permute-start.14) | collective-permute-done | bytes 426016 | tf_op jit(solution)/shard_map/ppermute | solution.py:342
  110.0 6.3 %collective-permute-done.22 = f32[2,64,640]{2,1,0:T(8,128)S(1)} collective-permute-done((f32[2,64,640]{2,1,0:T(8,128)S(1)}, f32[2,64,640]{2,1,0:T(8,128)S(1)}, u32[]{:S(2)}, u32[]{:S(2)}) %collective-permute-start.22) | collective-permute-done | bytes 327712 | tf_op jit(solution)/shard_map/ppermute | solution.py:342
  125.7 3.2 %shard_map.116 = (f32[128,1024]{1,0:T(8,128)}, f32[8,128]{1,0:T(8,128)S(1)}, bf16[1024,1024]{1,0:T(8,128)(2,1)S(1)}, bf16[1024,1024]{1,0:T(8,128)(2,1)S(1)}) custom-call(s32[2]{0:T(128)S(1)} %pad_add_fusion.place, f32[64,640]{1,0:T(8,128)S(1)} %get-tuple-element.162.refs_0_, f32[64,640]{1,0:T(8,128)S(1)} %get-tuple-element.163.refs_1_, ...), custom_call_target="tpu_custom_call" | custom-call | tf_op jit(solution)/shard_map/pallas_call | solution.py:309
  128.8 13.0 %collective-permute-done.31 = f32[64,1024]{1,0:T(8,128)S(1)} collective-permute-done((f32[64,1024]{1,0:T(8,128)S(1)}, f32[64,1024]{1,0:T(8,128)S(1)}, u32[]{:S(2)}, u32[]{:S(2)}) %collective-permute-start.31) | collective-permute-done | bytes 262176 | tf_op jit(solution)/shard_map/ppermute | solution.py:342
  142.6 4.8 %collective-permute-done.34 = f32[64,1024]{1,0:T(8,128)S(1)} collective-permute-done((f32[64,1024]{1,0:T(8,128)S(1)}, f32[64,1024]{1,0:T(8,128)S(1)}, u32[]{:S(2)}, u32[]{:S(2)}) %collective-permute-start.34) | collective-permute-done | bytes 262176 | tf_op jit(solution)/shard_map/ppermute | solution.py:342
  147.4 5.4 %collective-permute-done.35 = f32[1,1,64,1664]{3,2,1,0:T(8,128)S(1)} collective-permute-done((f32[1,1,64,1664]{3,2,1,0:T(8,128)S(1)}, f32[1,1,64,1664]{3,2,1,0:T(8,128)S(1)}, u32[]{:S(2)}, u32[]{:S(2)}) %collective-permute-start.35) | collective-permute-done | bytes 426016 | tf_op jit(solution)/shard_map/ppermute | solution.py:342
  154.5 2.3 %collective-permute-start.38 = (f32[64,640]{1,0:T(8,128)S(1)}, f32[64,640]{1,0:T(8,128)S(1)}, u32[]{:S(2)}, u32[]{:S(2)}) collective-permute-start(f32[64,640]{1,0:T(8,128)S(1)} %get-tuple-element.206.refs_1_), channel_id=1, source_target_pairs={{0,4},{4,0},{8,12},{12,8},{16,20},{20,16},{24,28},{28,24},{1,5},{5... | collective-permute-start | bytes 491528 | tf_op jit(solution)/shard_map/ppermute | solution.py:342
  160.5 2.8 %collective-permute-done.39.refs_4_ = f32[64,640]{1,0:T(8,128)S(1)} collective-permute-done((f32[64,640]{1,0:T(8,128)S(1)}, f32[64,640]{1,0:T(8,128)S(1)}, u32[]{:S(2)}, u32[]{:S(2)}) %collective-permute-start.39) | collective-permute-done | bytes 163872 | tf_op jit(solution)/shard_map/ppermute | solution.py:342
  164.7 2.4 %collective-permute-start.46 = (f32[64,640]{1,0:T(8,128)S(1)}, f32[64,640]{1,0:T(8,128)S(1)}, u32[]{:S(2)}, u32[]{:S(2)}) collective-permute-start(f32[64,640]{1,0:T(8,128)S(1)} %collective-permute-done.44.refs_9_), channel_id=1, source_target_pairs={{0,4},{4,0},{8,12},{12,8},{16,20},{20,16},{24,28},{28,24},{1,5},{5... | collective-permute-start | bytes 491528 | tf_op jit(solution)/shard_map/ppermute | solution.py:342
  167.4 5.3 %collective-permute-done.48.refs_13_ = f32[64,640]{1,0:T(8,128)S(1)} collective-permute-done((f32[64,640]{1,0:T(8,128)S(1)}, f32[64,640]{1,0:T(8,128)S(1)}, u32[]{:S(2)}, u32[]{:S(2)}) %collective-permute-start.48) | collective-permute-done | bytes 163872 | tf_op jit(solution)/shard_map/ppermute | solution.py:342
  172.8 2.7 %collective-permute-start.45 = (f32[64,640]{1,0:T(8,128)S(1)}, f32[64,640]{1,0:T(8,128)S(1)}, u32[]{:S(2)}, u32[]{:S(2)}) collective-permute-start(f32[64,640]{1,0:T(8,128)S(1)} %collective-permute-done.43.refs_8_), channel_id=1, source_target_pairs={{0,4},{4,0},{8,12},{12,8},{16,20},{20,16},{24,28},{28,24},{1,5},{5... | collective-permute-start | bytes 491528 | tf_op jit(solution)/shard_map/ppermute | solution.py:342
  179.7 3.4 %collective-permute-done.58.refs_9_ = f32[64,1024]{1,0:T(8,128)S(1)} collective-permute-done((f32[64,1024]{1,0:T(8,128)S(1)}, f32[64,1024]{1,0:T(8,128)S(1)}, u32[]{:S(2)}, u32[]{:S(2)}) %collective-permute-start.58) | collective-permute-done | bytes 262176 | tf_op jit(solution)/shard_map/ppermute | solution.py:342
  184.2 4.4 %collective-permute-done.57.refs_8_ = f32[64,1024]{1,0:T(8,128)S(1)} collective-permute-done((f32[64,1024]{1,0:T(8,128)S(1)}, f32[64,1024]{1,0:T(8,128)S(1)}, u32[]{:S(2)}, u32[]{:S(2)}) %collective-permute-start.57) | collective-permute-done | bytes 262176 | tf_op jit(solution)/shard_map/ppermute | solution.py:342
  188.6 2.2 %collective-permute-start.51 = (f32[64,1024]{1,0:T(8,128)S(1)}, f32[64,1024]{1,0:T(8,128)S(1)}, u32[]{:S(2)}, u32[]{:S(2)}) collective-permute-start(f32[64,1024]{1,0:T(8,128)S(1)} %fusion.15.refs_0_), channel_id=1, source_target_pairs={{0,4},{4,0},{8,12},{12,8},{16,20},{20,16},{24,28},{28,24},{1,5},{5... | collective-permute-start | bytes 786440 | tf_op jit(solution)/shard_map/ppermute | solution.py:342
  195.5 3.7 %shard_map.117 = (f32[128,1024]{1,0:T(8,128)}, f32[128,1024]{1,0:T(8,128)S(1)}) custom-call(s32[2]{0:T(128)S(1)} %pad_add_fusion.place, f32[64,640]{1,0:T(8,128)S(1)} %get-tuple-element.207.refs_0_, f32[64,640]{1,0:T(8,128)S(1)} %get-tuple-element.206.refs_1_, f32[64,640]{1,0:T(8,128)S(1)} %collective-permute-done.37.refs_2_, ...), custom_call_target="tpu_custom_call" | custom-call | tf_op jit(solution)/shard_map/pallas_call | solution.py:309
  202.3 5.6 %shard_map.118 = (f32[128,1024]{1,0:T(8,128)}, f32[128,1024]{1,0:T(8,128)}) custom-call(s32[2]{0:T(128)S(1)} %pad_add_fusion.place, f32[64,1024]{1,0:T(8,128)S(1)} %fusion.15.refs_0_, f32[64,1024]{1,0:T(8,128)S(1)} %fusion.13.refs_1_, f32[64,1024]{1,0:T(8,128)S(1)} %collective-permute-done.51.refs_2_, f32[64,1024]{1,0:T(8,128)S(1)} %collective-permute-done.52.refs_3_, ...), custom_call_target="tpu_custom_call" | custom-call | tf_op jit(solution)/shard_map/pallas_call | solution.py:309
  (153 shorter events, 66.4 us)
Async XLA Ops:
  4.6 25.4 %collective-permute-start.1 = (f32[264,1024]{1,0:T(8,128)S(1)}, f32[264,1024]{1,0:T(8,128)S(1)}, u32[]{:S(2)}, u32[]{:S(2)}) collective-permute-start(f32[264,1024]{1,0:T(8,128)S(1)} %shard_map.111.refs_0_.refs_2_), channel_id=1, source_target_pairs={{0,1},{1,0},{2,3},{3,2},{4,5},{5,4},{6,7},{7,6},{8,9},{9,8},{10,11... | collective-permute-start | bytes 3244040 | tf_op jit(solution)/shard_map/ppermute | solution.py:342
  30.9 25.0 %collective-permute-start = (f32[256,1024]{1,0:T(8,128)}, f32[256,1024]{1,0:T(8,128)S(1)}, u32[]{:S(2)}, u32[]{:S(2)}) collective-permute-start(f32[256,1024]{1,0:T(8,128)} %refs_0_.1), channel_id=1, source_target_pairs={{0,1},{1,0},{2,3},{3,2},{4,5},{5,4},{6,7},{7,6},{8,9},{9,8},{10,11... | collective-permute-start | bytes 3145736 | tf_op jit(solution)/shard_map/ppermute | solution.py:342
  37.0 19.7 %collective-permute-start.6 = (f32[2,2,64,640]{3,2,1,0:T(8,128)S(1)}, f32[2,2,64,640]{3,2,1,0:T(8,128)S(1)}, u32[]{:S(2)}, u32[]{:S(2)}) collective-permute-start(f32[2,2,64,640]{3,2,1,0:T(8,128)S(1)} %get-tuple-element.130), channel_id=1, source_target_pairs={{0,8},{4,12},{8,0},{12,4},{16,24},{20,28},{24,16},{28,20},{1,9},{5... | collective-permute-start | bytes 1966088 | tf_op jit(solution)/shard_map/ppermute | solution.py:342
  38.3 18.5 %collective-permute-start.7 = (f32[2,2,64,640]{3,2,1,0:T(8,128)S(1)}, f32[2,2,64,640]{3,2,1,0:T(8,128)S(1)}, u32[]{:S(2)}, u32[]{:S(2)}) collective-permute-start(f32[2,2,64,640]{3,2,1,0:T(8,128)S(1)} %get-tuple-element.132), channel_id=1, source_target_pairs={{0,16},{4,20},{8,24},{12,28},{16,0},{20,4},{24,8},{28,12},{1,17},{... | collective-permute-start | bytes 1966088 | tf_op jit(solution)/shard_map/ppermute | solution.py:342
  56.9 10.6 %collective-permute-start.10 = (f32[1,2,64,640]{3,2,1,0:T(8,128)S(1)}, f32[1,2,64,640]{3,2,1,0:T(8,128)S(1)}, u32[]{:S(2)}, u32[]{:S(2)}) collective-permute-start(f32[1,2,64,640]{3,2,1,0:T(8,128)S(1)} %get-tuple-element.150), channel_id=1, source_target_pairs={{0,16},{4,20},{8,24},{12,28},{16,0},{20,4},{24,8},{28,12},{1,17},{... | collective-permute-start | bytes 983048 | tf_op jit(solution)/shard_map/ppermute | solution.py:342
  58.2 10.8 %collective-permute-start.12 = (f32[1,2,64,640]{3,2,1,0:T(8,128)S(1)}, f32[1,2,64,640]{3,2,1,0:T(8,128)S(1)}, u32[]{:S(2)}, u32[]{:S(2)}) collective-permute-start(f32[1,2,64,640]{3,2,1,0:T(8,128)S(1)} %get-tuple-element.152), channel_id=1, source_target_pairs={{0,8},{4,12},{8,0},{12,4},{16,24},{20,28},{24,16},{28,20},{1,9},{5... | collective-permute-start | bytes 983048 | tf_op jit(solution)/shard_map/ppermute | solution.py:342
  66.6 20.0 %collective-permute-start.8 = (f32[2,1,64,1664]{3,2,1,0:T(8,128)S(1)}, f32[2,1,64,1664]{3,2,1,0:T(8,128)S(1)}, u32[]{:S(2)}, u32[]{:S(2)}) collective-permute-start(f32[2,1,64,1664]{3,2,1,0:T(8,128)S(1)} %get-tuple-element.146), channel_id=1, source_target_pairs={{0,8},{4,12},{8,0},{12,4},{16,24},{20,28},{24,16},{28,20},{1,9},{5... | collective-permute-start | bytes 2555912 | tf_op jit(solution)/shard_map/ppermute | solution.py:342
  67.5 19.7 %collective-permute-start.11 = (f32[64,640]{1,0:T(8,128)S(1)}, f32[64,640]{1,0:T(8,128)S(1)}, u32[]{:S(2)}, u32[]{:S(2)}) collective-permute-start(f32[64,640]{1,0:T(8,128)S(1)} %slice_bitcast_fusion.5), channel_id=1, source_target_pairs={{0,2},{1,3},{2,0},{3,1},{4,6},{5,7},{6,4},{7,5},{8,10},{9,11},{10,... | collective-permute-start | bytes 491528 | tf_op jit(solution)/shard_map/ppermute | solution.py:342
  67.7 19.6 %collective-permute-start.9 = (f32[2,1,64,1664]{3,2,1,0:T(8,128)S(1)}, f32[2,1,64,1664]{3,2,1,0:T(8,128)S(1)}, u32[]{:S(2)}, u32[]{:S(2)}) collective-permute-start(f32[2,1,64,1664]{3,2,1,0:T(8,128)S(1)} %get-tuple-element.148), channel_id=1, source_target_pairs={{0,16},{4,20},{8,24},{12,28},{16,0},{20,4},{24,8},{28,12},{1,17},{... | collective-permute-start | bytes 2555912 | tf_op jit(solution)/shard_map/ppermute | solution.py:342
  69.0 18.3 %collective-permute-start.13 = (f32[64,640]{1,0:T(8,128)S(1)}, f32[64,640]{1,0:T(8,128)S(1)}, u32[]{:S(2)}, u32[]{:S(2)}) collective-permute-start(f32[64,640]{1,0:T(8,128)S(1)} %slice_bitcast_fusion.4), channel_id=1, source_target_pairs={{0,2},{1,3},{2,0},{3,1},{4,6},{5,7},{6,4},{7,5},{8,10},{9,11},{10,... | collective-permute-start | bytes 491528 | tf_op jit(solution)/shard_map/ppermute | solution.py:342
  99.3 17.1 %collective-permute-start.22 = (f32[2,64,640]{2,1,0:T(8,128)S(1)}, f32[2,64,640]{2,1,0:T(8,128)S(1)}, u32[]{:S(2)}, u32[]{:S(2)}) collective-permute-start(f32[2,64,640]{2,1,0:T(8,128)S(1)} %maximum_bitcast_fusion), channel_id=1, source_target_pairs={{0,2},{1,3},{2,0},{3,1},{4,6},{5,7},{6,4},{7,5},{8,10},{9,11},{10,... | collective-permute-start | bytes 983048 | tf_op jit(solution)/shard_map/ppermute | solution.py:342
  116.3 25.5 %collective-permute-start.32 = (f32[2,1,64,1664]{3,2,1,0:T(8,128)S(1)}, f32[2,1,64,1664]{3,2,1,0:T(8,128)S(1)}, u32[]{:S(2)}, u32[]{:S(2)}) collective-permute-start(f32[2,1,64,1664]{3,2,1,0:T(8,128)S(1)} %get-tuple-element.176), channel_id=1, source_target_pairs={{0,8},{4,12},{8,0},{12,4},{16,24},{20,28},{24,16},{28,20},{1,9},{5... | collective-permute-start | bytes 2555912 | tf_op jit(solution)/shard_map/ppermute | solution.py:342
  119.6 22.6 %collective-permute-start.33 = (f32[2,1,64,1664]{3,2,1,0:T(8,128)S(1)}, f32[2,1,64,1664]{3,2,1,0:T(8,128)S(1)}, u32[]{:S(2)}, u32[]{:S(2)}) collective-permute-start(f32[2,1,64,1664]{3,2,1,0:T(8,128)S(1)} %get-tuple-element.178), channel_id=1, source_target_pairs={{0,16},{4,20},{8,24},{12,28},{16,0},{20,4},{24,8},{28,12},{1,17},{... | collective-permute-start | bytes 2555912 | tf_op jit(solution)/shard_map/ppermute | solution.py:342
  121.6 20.3 %collective-permute-start.31 = (f32[64,1024]{1,0:T(8,128)S(1)}, f32[64,1024]{1,0:T(8,128)S(1)}, u32[]{:S(2)}, u32[]{:S(2)}) collective-permute-start(f32[64,1024]{1,0:T(8,128)S(1)} %bitcast.86), channel_id=1, source_target_pairs={{0,2},{1,3},{2,0},{3,1},{4,6},{5,7},{6,4},{7,5},{8,10},{9,11},{10,... | collective-permute-start | bytes 786440 | tf_op jit(solution)/shard_map/ppermute | solution.py:342
  123.9 23.5 %collective-permute-start.34 = (f32[64,1024]{1,0:T(8,128)S(1)}, f32[64,1024]{1,0:T(8,128)S(1)}, u32[]{:S(2)}, u32[]{:S(2)}) collective-permute-start(f32[64,1024]{1,0:T(8,128)S(1)} %bitcast.85), channel_id=1, source_target_pairs={{0,2},{1,3},{2,0},{3,1},{4,6},{5,7},{6,4},{7,5},{8,10},{9,11},{10,... | collective-permute-start | bytes 786440 | tf_op jit(solution)/shard_map/ppermute | solution.py:342
  141.9 10.9 %collective-permute-start.35 = (f32[1,1,64,1664]{3,2,1,0:T(8,128)S(1)}, f32[1,1,64,1664]{3,2,1,0:T(8,128)S(1)}, u32[]{:S(2)}, u32[]{:S(2)}) collective-permute-start(f32[1,1,64,1664]{3,2,1,0:T(8,128)S(1)} %get-tuple-element.200), channel_id=1, source_target_pairs={{0,16},{4,20},{8,24},{12,28},{16,0},{20,4},{24,8},{28,12},{1,17},{... | collective-permute-start | bytes 1277960 | tf_op jit(solution)/shard_map/ppermute | solution.py:342
  163.3 13.8 %collective-permute-start.53 = (f32[64,1024]{1,0:T(8,128)S(1)}, f32[64,1024]{1,0:T(8,128)S(1)}, u32[]{:S(2)}, u32[]{:S(2)}) collective-permute-start(f32[64,1024]{1,0:T(8,128)S(1)} %fusion.15.refs_0_), channel_id=1, source_target_pairs={{0,8},{4,12},{8,0},{12,4},{16,24},{20,28},{24,16},{28,20},{1,9},{5... | collective-permute-start | bytes 786440 | tf_op jit(solution)/shard_map/ppermute | solution.py:342
  164.7 10.8 %collective-permute-start.46 = (f32[64,640]{1,0:T(8,128)S(1)}, f32[64,640]{1,0:T(8,128)S(1)}, u32[]{:S(2)}, u32[]{:S(2)}) collective-permute-start(f32[64,640]{1,0:T(8,128)S(1)} %collective-permute-done.44.refs_9_), channel_id=1, source_target_pairs={{0,4},{4,0},{8,12},{12,8},{16,20},{20,16},{24,28},{28,24},{1,5},{5... | collective-permute-start | bytes 491528 | tf_op jit(solution)/shard_map/ppermute | solution.py:342
  176.8 11.8 %collective-permute-start.57 = (f32[64,1024]{1,0:T(8,128)S(1)}, f32[64,1024]{1,0:T(8,128)S(1)}, u32[]{:S(2)}, u32[]{:S(2)}) collective-permute-start(f32[64,1024]{1,0:T(8,128)S(1)} %fusion.15.refs_0_), channel_id=1, source_target_pairs={{0,16},{4,20},{8,24},{12,28},{16,0},{20,4},{24,8},{28,12},{1,17},{... | collective-permute-start | bytes 786440 | tf_op jit(solution)/shard_map/ppermute | solution.py:342
  177.1 17.2 %collective-permute-start.61 = (f32[64,1024]{1,0:T(8,128)S(1)}, f32[64,1024]{1,0:T(8,128)S(1)}, u32[]{:S(2)}, u32[]{:S(2)}) collective-permute-start(f32[64,1024]{1,0:T(8,128)S(1)} %collective-permute-done.53.refs_4_), channel_id=1, source_target_pairs={{0,16},{4,20},{8,24},{12,28},{16,0},{20,4},{24,8},{28,12},{1,17},{... | collective-permute-start | bytes 786440 | tf_op jit(solution)/shard_map/ppermute | solution.py:342
  178.3 12.5 %collective-permute-start.50 = (f32[64,640]{1,0:T(8,128)S(1)}, f32[64,640]{1,0:T(8,128)S(1)}, u32[]{:S(2)}, u32[]{:S(2)}) collective-permute-start(f32[64,640]{1,0:T(8,128)S(1)} %collective-permute-done.48.refs_13_), channel_id=1, source_target_pairs={{0,4},{4,0},{8,12},{12,8},{16,20},{20,16},{24,28},{28,24},{1,5},{5... | collective-permute-start | bytes 491528 | tf_op jit(solution)/shard_map/ppermute | solution.py:342
  179.6 12.4 %collective-permute-start.49 = (f32[64,640]{1,0:T(8,128)S(1)}, f32[64,640]{1,0:T(8,128)S(1)}, u32[]{:S(2)}, u32[]{:S(2)}) collective-permute-start(f32[64,640]{1,0:T(8,128)S(1)} %collective-permute-done.47.refs_12_), channel_id=1, source_target_pairs={{0,4},{4,0},{8,12},{12,8},{16,20},{20,16},{24,28},{28,24},{1,5},{5... | collective-permute-start | bytes 491528 | tf_op jit(solution)/shard_map/ppermute | solution.py:342
  183.0 16.2 %collective-permute-start.62 = (f32[64,1024]{1,0:T(8,128)S(1)}, f32[64,1024]{1,0:T(8,128)S(1)}, u32[]{:S(2)}, u32[]{:S(2)}) collective-permute-start(f32[64,1024]{1,0:T(8,128)S(1)} %collective-permute-done.58.refs_9_), channel_id=1, source_target_pairs={{0,8},{4,12},{8,0},{12,4},{16,24},{20,28},{24,16},{28,20},{1,9},{5... | collective-permute-start | bytes 786440 | tf_op jit(solution)/shard_map/ppermute | solution.py:342
  188.6 10.7 %collective-permute-start.51 = (f32[64,1024]{1,0:T(8,128)S(1)}, f32[64,1024]{1,0:T(8,128)S(1)}, u32[]{:S(2)}, u32[]{:S(2)}) collective-permute-start(f32[64,1024]{1,0:T(8,128)S(1)} %fusion.15.refs_0_), channel_id=1, source_target_pairs={{0,4},{4,0},{8,12},{12,8},{16,20},{20,16},{24,28},{28,24},{1,5},{5... | collective-permute-start | bytes 786440 | tf_op jit(solution)/shard_map/ppermute | solution.py:342
  (46 other events, 312.4 us)

commit v5 on v4

--- a/solution.py
+++ b/solution.py
@@ -251,17 +251,29 @@
     return first[0:rows] + first[rows : 2 * rows] + dot(top, low[...])
 
 
-def row_pieces(place, block, count):
+def gather_order(order):
+    offsets = [0]
+    for bit in order:
+        offsets += [k | (1 << bit) for k in offsets]
+    return offsets
+
+
+def row_pieces(place, block, blocks):
     step = block // 2
-    return [
-        pl.ds(pl.multiple_of((place[0] ^ (number // 2)) * block + number % 2 * step, step), step)
-        for number in range(count)
-    ]
+    chips = len(blocks) // 2
+    pieces = []
+    for number, value in enumerate(blocks):
+        core, position = number // chips, number % chips
+        for half, order in enumerate(orders(chips)):
+            owner = place[0] ^ (2 * gather_order(order)[position] + core)
+            here = pl.ds(pl.multiple_of(owner * block + half * step, step), step)
+            pieces.append((here, value[half * step : (half + 1) * step, :]))
+    return pieces
 
 
 def factor_rows(place, block, blocks, bands, full):
-    for here, value in zip(row_pieces(place, block, len(blocks)), blocks):
-        bands[here, :] = value[...]
+    for here, value in row_pieces(place, block, blocks):
+        bands[here, :] = value
     unfold(bands, full)
     return full[pl.ds(pl.multiple_of(place[0] * block, block), block), :]
 
@@ -293,8 +305,8 @@
 def update_kernel(place, *refs):
     blocks = refs[:-9]
     inverse, scales, act_high, act_low, momentum, weights, moment_out, weight_out, full = refs[-9:]
-    for here, value in zip(row_pieces(place, momentum.shape[0], len(blocks)), blocks):
-        full[here, :] = value[...]
+    for here, value in row_pieces(place, momentum.shape[0], blocks):
+        full[here, :] = value
     damp, alpha = scales[0:1, 0:1], scales[1:2, 0:1]
     half_way = times(inverse[...], *split(full[...]))
     value = half_way
@@ -377,33 +389,21 @@
 class Gather:
     def __init__(self, halves, chips):
         self.chips, self.orders = chips, orders(chips)
-        self.held = [{0: value} for value in halves]
-
-    def step(self, half, bit):
-        held = self.held[half]
-        for k in list(held):
-            held[k | (1 << bit)] = swap(held[k], "dp", 2 << bit)
+        self.held = [[value] for value in halves]
 
     def begin(self):
-        for half, order in enumerate(self.orders):
-            for bit in order[:1]:
-                self.step(half, bit)
-        return [held[max(held)] for held in self.held]
+        for held, order in zip(self.held, self.orders):
+            held += [swap(held[0], "dp", 2 << bit) for bit in order[:1]]
 
     def relay(self):
-        for half, order in enumerate(self.orders):
+        for held, order in zip(self.held, self.orders):
             for bit in order[1:]:
-                self.step(half, bit)
+                held += [swap(value, "dp", 2 << bit) for value in held]
 
     def finish(self, *before):
-        pieces = {}
-        for half in range(2):
-            last = self.chips - 1
-            self.held[half][last], before = together(self.held[half][last], before)
-            for k in range(self.chips):
-                pieces[2 * k, half] = self.held[half][k]
-                pieces[2 * k + 1, half] = swap(self.held[half][k], "dp", 1)
-        return [pieces[k, half] for k in range(2 * self.chips) for half in range(2)]
+        mine = [jnp.concatenate(pair, axis=0) for pair in zip(*self.held)]
+        mine[-1], before = together(mine[-1], before)
+        return mine + [swap(value, "dp", 1) for value in mine]
 
 
 def together(*values):
@@ -456,45 +456,45 @@
     act_across = [across(total[1:]) for total in act_sums]
     far_sum.add()
     far_sum.leaving, act_across = together(far_sum.leaving, act_across)
-    far_sums = far_sum.finish()
+    far_sum.send()
 
     step = block // 2
     parts = [slice(half * step, (half + 1) * step) for half in range(2)]
     act_totals = [sum(there, total[0]) for total, there in zip(act_sums, act_across)]
     total = jnp.maximum(act_totals[1][-1:, 0:1], 1.0)
     act_halves = [old_act[here] + 0.5 * (value / total) for here, value in zip(parts, act_totals)]
-    far_sums, act_halves = together(far_sums, act_halves)
-    across_grad = across(jnp.stack([value[:, :, 0:width] for value in far_sums], axis=1))
-    far_mixed = [value[:, :, width:] for value in far_sums]
     act_gather = Gather(act_halves, chips)
     act_gather.begin()
-    act_gather.relay()
-    early = (act_gather.held, across_grad, far_mixed)
-    near_sum.leaving, (act_gather.held, across_grad, far_mixed) = together(near_sum.leaving, early)
-    across_mixed = [across(value) for value in far_mixed]
+    far_sum.add()
+    far_sums = far_sum.finish()
+    far_sums, near_sum.leaving = together(far_sums, near_sum.leaving)
+    across_grad = across(jnp.stack([value[:, :, 0:width] for value in far_sums], axis=1))
+    across_mixed = [across(value[:, :, width:]) for value in far_sums]
     near_sum.send()
-    act_out, *act_square = act_factor_rows(place, act_gather.finish(), block, feat)
-    near_sum.held, across_mixed[0] = together(near_sum.held, across_mixed[0])
+    early = (across_grad, across_mixed[0])
+    near_sum.held, (across_grad, across_mixed[0]) = together(near_sum.held, early)
     near_sum.add()
     near_sum.send()
-    near_sum.held, across_mixed[1], act_square = together(near_sum.held, across_mixed[1], act_square)
     near_sum.add()
-    near_sums = near_sum.finish()
-
-    grad_stats = [
-        sum((there[half] for there in across_grad), value[0, :, 0:width]) / total
-        for half, value in enumerate(near_sums)
+    near_sums, act_gather.held = together(near_sum.finish(), act_gather.held)
+    act_gather.relay()
+
+    def of_near(half, far, columns):
+        return sum(far, near_sums[half][0, :, columns]) / total
+
+    grad_halves = [
+        old_grad[here] + 0.5 * of_near(half, [there[half] for there in across_grad], slice(0, width))
+        for half, here in enumerate(parts)
     ]
-    mixed = [sum(there, value[0, :, width:]) / total for value, there in zip(near_sums, across_mixed)]
-    grad_halves = [old_grad[here] + 0.5 * value for here, value in zip(parts, grad_stats)]
     grad_gather = Gather(grad_halves, chips)
-    arrived = grad_gather.begin()
-    mixed, arrived = together(mixed, arrived)
-    mixed_gather = Gather(mixed, chips)
+    grad_gather.begin()
+    mixed_gather = Gather([of_near(half, across_mixed[half], slice(width, None)) for half in range(2)], chips)
     mixed_gather.begin()
     grad_gather.relay()
     mixed_gather.relay()
-    grad_out, inverse = grad_factor_rows(place, grad_gather.finish(), block, feat)
+    act_out, *act_square = act_factor_rows(place, act_gather.finish(), block, feat)
+    grad_blocks, act_square = together(grad_gather.finish(), act_square)
+    grad_out, inverse = grad_factor_rows(place, grad_blocks, block, feat)
     mixed_blocks = mixed_gather.finish(inverse)
     outs = update_rows(place, mixed_blocks, inverse, *act_square, momentum[0], weights[0])
     return tuple(out[None] for out in (act_out, grad_out, *outs))

time: 211 us -> 199 us (0.943)
  waiting for transfers between devices: 109 us -> 102 us
  starting transfers between devices: 53.5 us -> 48.9 us
    ppermute x65 -> x53, waiting for transfers between devices: 109 us -> 102 us  [swap(): return lax.ppermute(value, axis, [(i, i ^ step) for i in range(size)])]
    ppermute x65 -> x53, starting transfers between devices: 53.5 us -> 48.9 us  [swap(): return lax.ppermute(value, axis, [(i, i ^ step) for i in range(size)])]
  transfers between devices with their start and end apart: 65 -> 53, of which waited for: 27 -> 19; matrix products, arithmetic and copies ran while one was open for 3% -> 3% of each run, Pallas kernels for 14% -> 15%
where the time goes in v5:
time: 199 us; the launch traced here: 197 us
  waiting for transfers between devices  102 us (51%)
  starting transfers between devices  48.9 us (25%)
  Pallas kernels  35.3 us (18%)
  local copies, waits for them, and re-layouts  6 us (3%)
  other arithmetic  2.31 us (1%)
    ppermute x53, waiting for transfers between devices, swap(): return lax.ppermute(value, axis, [(i, i ^ step) for i in range(size)])  102 us
    ppermute x53, starting transfers between devices, swap(): return lax.ppermute(value, axis, [(i, i ^ step) for i in range(size)])  48.9 us
    pallas_call x4, Pallas kernels, bands(): pl.pallas_call(functools.partial(body, turns, block, chips, bool(seeds),...  22.5 us
    pallas_call x3, Pallas kernels, on_core(): pl.pallas_call(body, out_shape=shapes, in_specs=[pl.BlockSpec(memory_spac...  12 us
  transfers between devices with their start and end apart: 53, of which 19 were waited for; matrix products, arithmetic and copies ran while one was open for 3% of the time, Pallas kernels for 15%

profile of v5, /device:TPU:25, one launch (start us, length us, event | category | flops | bytes accessed | tf_op | source)
XLA Modules:
  0.0 196.6 jit_solution(11407987887147302180)
XLA Ops:
  9.0 3.7 %shard_map.112 = (f32[2,2,64,640]{3,2,1,0:T(8,128)S(1)}, f32[2,2,64,640]{3,2,1,0:T(8,128)S(1)}, f32[2,2,64,640]{3,2,1,0:T(8,128)S(1)}, f32[2,2,64,640]{3,2,1,0:T(8,128)S(1)}) custom-call(s32[2]{0:T(128)S(1)} %pad_add_fusion.place, f32[264,1024]{1,0:T(8,128)S(1)} %shard_map.111.refs_0_.refs_2_, f32[264,1024]{1,0:T(8,128)S(1)} %collective-permute-done.2.refs_1_.refs_3_), custom_call_target="tpu_custom_call" | custom-call | tf_op jit(solution)/shard_map/pallas_call | solution.py:212
  12.8 7.9 %shard_map.113 = (f32[2,1,64,1664]{3,2,1,0:T(8,128)S(1)}, f32[2,1,64,1664]{3,2,1,0:T(8,128)S(1)}, f32[2,1,64,1664]{3,2,1,0:T(8,128)S(1)}, f32[2,1,64,1664]{3,2,1...) custom-call(s32[2]{0:T(128)S(1)} %pad_add_fusion.place, ...), custom_call_target="tpu_custom_call" | custom-call | tf_op jit(solution)/shard_map/pallas_call | solution.py:212
  20.6 9.4 %collective-permute-done.1.refs_0_.refs_2_ = f32[264,1024]{1,0:T(8,128)S(1)} collective-permute-done((f32[264,1024]{1,0:T(8,128)S(1)}, f32[264,1024]{1,0:T(8,128)S(1)}, u32[]{:S(2)}, u32[]{:S(2)}) %collective-permute-start.1) | collective-permute-done | bytes 1081376 | tf_op jit(solution)/shard_map/ppermute | solution.py:354
  31.1 2.2 %collective-permute-done.4.refs_1_.refs_3_ = f32[264,1024]{1,0:T(8,128)S(1)} collective-permute-done((f32[264,1024]{1,0:T(8,128)S(1)}, f32[264,1024]{1,0:T(8,128)S(1)}, u32[]{:S(2)}, u32[]{:S(2)}) %collective-permute-start.4) | collective-permute-done | bytes 1081376 | tf_op jit(solution)/shard_map/ppermute | solution.py:354
  33.2 3.8 %shard_map.114 = (f32[2,2,64,640]{3,2,1,0:T(8,128)S(1)}, f32[2,2,64,640]{3,2,1,0:T(8,128)S(1)}, f32[2,2,64,640]{3,2,1,0:T(8,128)S(1)}, f32[2,2,64,640]{3,2,1,0:T(8,128)S(1)}) custom-call(s32[2]{0:T(128)S(1)} %pad_add_fusion.place, f32[264,1024]{1,0:T(8,128)S(1)} %collective-permute-done.1.refs_0_.refs_2_, ...), custom_call_target="tpu_custom_call" | custom-call | tf_op jit(solution)/shard_map/pallas_call | solution.py:212
  39.5 16.4 %collective-permute-done.refs_0_ = f32[256,1024]{1,0:T(8,128)S(1)} collective-permute-done((f32[256,1024]{1,0:T(8,128)}, f32[256,1024]{1,0:T(8,128)S(1)}, u32[]{:S(2)}, u32[]{:S(2)}) %collective-permute-start) | collective-permute-done | bytes 1048608 | tf_op jit(solution)/shard_map/ppermute | solution.py:354
  59.4 7.2 %shard_map.115 = (f32[2,1,64,1664]{3,2,1,0:T(8,128)S(1)}, f32[2,1,64,1664]{3,2,1,0:T(8,128)S(1)}, f32[2,1,64,1664]{3,2,1,0:T(8,128)S(1)}, f32[2,1,64,1664]{3,2,1...) custom-call(s32[2]{0:T(128)S(1)} %pad_add_fusion.place, ...), custom_call_target="tpu_custom_call" | custom-call | tf_op jit(solution)/shard_map/pallas_call | solution.py:212
  69.0 2.4 %collective-permute-start.13 = (f32[64,640]{1,0:T(8,128)S(1)}, f32[64,640]{1,0:T(8,128)S(1)}, u32[]{:S(2)}, u32[]{:S(2)}) collective-permute-start(f32[64,640]{1,0:T(8,128)S(1)} %slice_bitcast_fusion.4), channel_id=1, source_target_pairs={{0,2},{1,3},{2,0},{3,1},{4,6},{5,7},{6,4},{7,5},{8,10},{9,11},{10,... | collective-permute-start | bytes 491528 | tf_op jit(solution)/shard_map/ppermute | solution.py:354
  71.3 15.3 %collective-permute-done.8 = f32[2,1,64,1664]{3,2,1,0:T(8,128)S(1)} collective-permute-done((f32[2,1,64,1664]{3,2,1,0:T(8,128)S(1)}, f32[2,1,64,1664]{3,2,1,0:T(8,128)S(1)}, u32[]{:S(2)}, u32[]{:S(2)}) %collective-permute-start.8) | collective-permute-done | bytes 852000 | tf_op jit(solution)/shard_map/ppermute | solution.py:354
  90.2 6.6 %collective-permute-done.14 = f32[1,1,64,1664]{3,2,1,0:T(8,128)S(1)} collective-permute-done((f32[1,1,64,1664]{3,2,1,0:T(8,128)S(1)}, f32[1,1,64,1664]{3,2,1,0:T(8,128)S(1)}, u32[]{:S(2)}, u32[]{:S(2)}) %collective-permute-start.14) | collective-permute-done | bytes 426016 | tf_op jit(solution)/shard_map/ppermute | solution.py:354
  99.2 1.9 collective-permute-start.17
  103.3 17.6 %collective-permute-done.17 = f32[64,1024]{1,0:T(8,128)S(1)} collective-permute-done((f32[64,1024]{1,0:T(8,128)S(1)}, f32[64,1024]{1,0:T(8,128)S(1)}, u32[]{:S(2)}, u32[]{:S(2)}) %collective-permute-start.17) | collective-permute-done | bytes 262176 | tf_op jit(solution)/shard_map/ppermute | solution.py:354
  121.7 6.2 %collective-permute-done.16 = f32[2,64,640]{2,1,0:T(8,128)S(1)} collective-permute-done((f32[2,64,640]{2,1,0:T(8,128)S(1)}, f32[2,64,640]{2,1,0:T(8,128)S(1)}, u32[]{:S(2)}, u32[]{:S(2)}) %collective-permute-start.16) | collective-permute-done | bytes 327712 | tf_op jit(solution)/shard_map/ppermute | solution.py:354
  129.2 9.8 %collective-permute-done.19 = f32[1,1,64,1664]{3,2,1,0:T(8,128)S(1)} collective-permute-done((f32[1,1,64,1664]{3,2,1,0:T(8,128)S(1)}, f32[1,1,64,1664]{3,2,1,0:T(8,128)S(1)}, u32[]{:S(2)}, u32[]{:S(2)}) %collective-permute-start.19) | collective-permute-done | bytes 426016 | tf_op jit(solution)/shard_map/ppermute | solution.py:354
  143.9 3.1 %collective-permute-done.26 = f32[64,640]{1,0:T(8,128)S(1)} collective-permute-done((f32[64,640]{1,0:T(8,128)S(1)}, f32[64,640]{1,0:T(8,128)S(1)}, u32[]{:S(2)}, u32[]{:S(2)}) %collective-permute-start.26) | collective-permute-done | bytes 163872 | tf_op jit(solution)/shard_map/ppermute | solution.py:354
  157.9 4.2 %collective-permute-done.43 = f32[64,1024]{1,0:T(8,128)S(1)} collective-permute-done((f32[64,1024]{1,0:T(8,128)S(1)}, f32[64,1024]{1,0:T(8,128)S(1)}, u32[]{:S(2)}, u32[]{:S(2)}) %collective-permute-start.43) | collective-permute-done | bytes 262176 | tf_op jit(solution)/shard_map/ppermute | solution.py:354
  162.0 6.1 %collective-permute-start.29 = (f32[128,640]{1,0:T(8,128)S(1)}, f32[128,640]{1,0:T(8,128)S(1)}, u32[]{:S(2)}, u32[]{:S(2)}) collective-permute-start(f32[128,640]{1,0:T(8,128)S(1)} %constant_dynamic-update-slice_fusion.2.refs_1_), channel_id=1, source_target_pairs={{0,4},{4,0},{8,12},{12,8},{16,20},{20,16},{24,28},{28,24},{1,5},{5... | collective-permute-start | bytes 983048 | tf_op jit(solution)/shard_map/ppermute | solution.py:354
  168.2 4.2 %collective-permute-start.28 = (f32[128,640]{1,0:T(8,128)S(1)}, f32[128,640]{1,0:T(8,128)S(1)}, u32[]{:S(2)}, u32[]{:S(2)}) collective-permute-start(f32[128,640]{1,0:T(8,128)S(1)} %constant_dynamic-update-slice_fusion.refs_0_), channel_id=1, source_target_pairs={{0,4},{4,0},{8,12},{12,8},{16,20},{20,16},{24,28},{28,24},{1,5},{5... | collective-permute-start | bytes 983048 | tf_op jit(solution)/shard_map/ppermute | solution.py:354
  174.1 1.9 collective-permute-start.38
  176.5 2.9 %collective-permute-done.47 = f32[64,1024]{1,0:T(8,128)S(1)} collective-permute-done((f32[64,1024]{1,0:T(8,128)S(1)}, f32[64,1024]{1,0:T(8,128)S(1)}, u32[]{:S(2)}, u32[]{:S(2)}) %collective-permute-start.47) | collective-permute-done | bytes 262176 | tf_op jit(solution)/shard_map/ppermute | solution.py:354
  179.4 2.2 %collective-permute-start.41 = (f32[128,640]{1,0:T(8,128)S(1)}, f32[128,640]{1,0:T(8,128)S(1)}, u32[]{:S(2)}, u32[]{:S(2)}) collective-permute-start(f32[128,640]{1,0:T(8,128)S(1)} %pad_maximum_fusion.4.refs_3_), channel_id=1, source_target_pairs={{0,4},{4,0},{8,12},{12,8},{16,20},{20,16},{24,28},{28,24},{1,5},{5... | collective-permute-start | bytes 983048 | tf_op jit(solution)/shard_map/ppermute | solution.py:354
  181.6 2.6 %shard_map.116 = (f32[128,1024]{1,0:T(8,128)}, f32[8,128]{1,0:T(8,128)S(1)}, bf16[1024,1024]{1,0:T(8,128)(2,1)S(1)}, bf16[1024,1024]{1,0:T(8,128)(2,1)S(1)}) custom-call(s32[2]{0:T(128)S(1)} %pad_add_fusion.place, f32[128,640]{1,0:T(8,128)S(1)} %constant_dynamic-update-slice_fusion.refs_0_, f32[128,640]{1,0:T(8,128)S(1)} %constant_dynamic-update-slice_fusion.2.refs_1_, ...), custom_call_target="tpu_custom_call" | custom-call | tf_op jit(solution)/shard_map/pallas_call | solution.py:321
  185.1 3.7 %shard_map.117 = (f32[128,1024]{1,0:T(8,128)}, f32[128,1024]{1,0:T(8,128)S(1)}) custom-call(s32[2]{0:T(128)S(1)} %pad_add_fusion.place, f32[128,640]{1,0:T(8,128)S(1)} %pad_maximum_fusion.3.refs_0_, f32[128,640]{1,0:T(8,128)S(1)} %constant_dynamic-update-slice_fusion.6.refs_1_, f32[128,640]{1,0:T(8,128)S(1)} %constant_dynamic-update-slice_fusion.8.refs_2_, ...), custom_call_target="tpu_custom_call" | custom-call | tf_op jit(solution)/shard_map/pallas_call | solution.py:321
  190.8 5.7 %shard_map.118 = (f32[128,1024]{1,0:T(8,128)}, f32[128,1024]{1,0:T(8,128)}) custom-call(s32[2]{0:T(128)S(1)} %pad_add_fusion.place, f32[128,1024]{1,0:T(8,128)S(1)} %pad_maximum_fusion.refs_0_, f32[128,1024]{1,0:T(8,128)S(1)} %constant_dynamic-update-slice_fusion.10.refs_1_, f32[128,1024]{1,0:T(8,128)S(1)} %constant_dynamic-update-slice_fusion.12.refs_2_, ...), custom_call_target="tpu_custom_call" | custom-call | tf_op jit(solution)/shard_map/pallas_call | solution.py:321
  (148 shorter events, 47.9 us)
Async XLA Ops:
  4.6 25.4 %collective-permute-start.1 = (f32[264,1024]{1,0:T(8,128)S(1)}, f32[264,1024]{1,0:T(8,128)S(1)}, u32[]{:S(2)}, u32[]{:S(2)}) collective-permute-start(f32[264,1024]{1,0:T(8,128)S(1)} %shard_map.111.refs_0_.refs_2_), channel_id=1, source_target_pairs={{0,1},{1,0},{2,3},{3,2},{4,5},{5,4},{6,7},{7,6},{8,9},{9,8},{10,11... | collective-permute-start | bytes 3244040 | tf_op jit(solution)/shard_map/ppermute | solution.py:354
  30.9 25.0 %collective-permute-start = (f32[256,1024]{1,0:T(8,128)}, f32[256,1024]{1,0:T(8,128)S(1)}, u32[]{:S(2)}, u32[]{:S(2)}) collective-permute-start(f32[256,1024]{1,0:T(8,128)} %refs_0_.1), channel_id=1, source_target_pairs={{0,1},{1,0},{2,3},{3,2},{4,5},{5,4},{6,7},{7,6},{8,9},{9,8},{10,11... | collective-permute-start | bytes 3145736 | tf_op jit(solution)/shard_map/ppermute | solution.py:354
  37.0 19.7 %collective-permute-start.6 = (f32[2,2,64,640]{3,2,1,0:T(8,128)S(1)}, f32[2,2,64,640]{3,2,1,0:T(8,128)S(1)}, u32[]{:S(2)}, u32[]{:S(2)}) collective-permute-start(f32[2,2,64,640]{3,2,1,0:T(8,128)S(1)} %get-tuple-element.127), channel_id=1, source_target_pairs={{0,8},{4,12},{8,0},{12,4},{16,24},{20,28},{24,16},{28,20},{1,9},{5... | collective-permute-start | bytes 1966088 | tf_op jit(solution)/shard_map/ppermute | solution.py:354
  38.3 18.5 %collective-permute-start.7 = (f32[2,2,64,640]{3,2,1,0:T(8,128)S(1)}, f32[2,2,64,640]{3,2,1,0:T(8,128)S(1)}, u32[]{:S(2)}, u32[]{:S(2)}) collective-permute-start(f32[2,2,64,640]{3,2,1,0:T(8,128)S(1)} %get-tuple-element.129), channel_id=1, source_target_pairs={{0,16},{4,20},{8,24},{12,28},{16,0},{20,4},{24,8},{28,12},{1,17},{... | collective-permute-start | bytes 1966088 | tf_op jit(solution)/shard_map/ppermute | solution.py:354
  66.6 20.0 %collective-permute-start.8 = (f32[2,1,64,1664]{3,2,1,0:T(8,128)S(1)}, f32[2,1,64,1664]{3,2,1,0:T(8,128)S(1)}, u32[]{:S(2)}, u32[]{:S(2)}) collective-permute-start(f32[2,1,64,1664]{3,2,1,0:T(8,128)S(1)} %get-tuple-element.143), channel_id=1, source_target_pairs={{0,8},{4,12},{8,0},{12,4},{16,24},{20,28},{24,16},{28,20},{1,9},{5... | collective-permute-start | bytes 2555912 | tf_op jit(solution)/shard_map/ppermute | solution.py:354
  67.5 19.7 %collective-permute-start.11 = (f32[64,640]{1,0:T(8,128)S(1)}, f32[64,640]{1,0:T(8,128)S(1)}, u32[]{:S(2)}, u32[]{:S(2)}) collective-permute-start(f32[64,640]{1,0:T(8,128)S(1)} %slice_bitcast_fusion.5), channel_id=1, source_target_pairs={{0,2},{1,3},{2,0},{3,1},{4,6},{5,7},{6,4},{7,5},{8,10},{9,11},{10,... | collective-permute-start | bytes 491528 | tf_op jit(solution)/shard_map/ppermute | solution.py:354
  67.7 19.6 %collective-permute-start.9 = (f32[2,1,64,1664]{3,2,1,0:T(8,128)S(1)}, f32[2,1,64,1664]{3,2,1,0:T(8,128)S(1)}, u32[]{:S(2)}, u32[]{:S(2)}) collective-permute-start(f32[2,1,64,1664]{3,2,1,0:T(8,128)S(1)} %get-tuple-element.145), channel_id=1, source_target_pairs={{0,16},{4,20},{8,24},{12,28},{16,0},{20,4},{24,8},{28,12},{1,17},{... | collective-permute-start | bytes 2555912 | tf_op jit(solution)/shard_map/ppermute | solution.py:354
  69.0 18.3 %collective-permute-start.13 = (f32[64,640]{1,0:T(8,128)S(1)}, f32[64,640]{1,0:T(8,128)S(1)}, u32[]{:S(2)}, u32[]{:S(2)}) collective-permute-start(f32[64,640]{1,0:T(8,128)S(1)} %slice_bitcast_fusion.4), channel_id=1, source_target_pairs={{0,2},{1,3},{2,0},{3,1},{4,6},{5,7},{6,4},{7,5},{8,10},{9,11},{10,... | collective-permute-start | bytes 491528 | tf_op jit(solution)/shard_map/ppermute | solution.py:354
  98.4 29.6 %collective-permute-start.18 = (f32[2,1,64,1664]{3,2,1,0:T(8,128)S(1)}, f32[2,1,64,1664]{3,2,1,0:T(8,128)S(1)}, u32[]{:S(2)}, u32[]{:S(2)}) collective-permute-start(f32[2,1,64,1664]{3,2,1,0:T(8,128)S(1)} %get-tuple-element.157), channel_id=1, source_target_pairs={{0,8},{4,12},{8,0},{12,4},{16,24},{20,28},{24,16},{28,20},{1,9},{5... | collective-permute-start | bytes 2555912 | tf_op jit(solution)/shard_map/ppermute | solution.py:354
  99.2 21.8 %collective-permute-start.17 = (f32[64,1024]{1,0:T(8,128)S(1)}, f32[64,1024]{1,0:T(8,128)S(1)}, u32[]{:S(2)}, u32[]{:S(2)}) collective-permute-start(f32[64,1024]{1,0:T(8,128)S(1)} %slice_bitcast_fusion.1), channel_id=1, source_target_pairs={{0,2},{1,3},{2,0},{3,1},{4,6},{5,7},{6,4},{7,5},{8,10},{9,11},{10,... | collective-permute-start | bytes 786440 | tf_op jit(solution)/shard_map/ppermute | solution.py:354
  101.2 26.8 %collective-permute-start.16 = (f32[2,64,640]{2,1,0:T(8,128)S(1)}, f32[2,64,640]{2,1,0:T(8,128)S(1)}, u32[]{:S(2)}, u32[]{:S(2)}) collective-permute-start(f32[2,64,640]{2,1,0:T(8,128)S(1)} %maximum_bitcast_fusion), channel_id=1, source_target_pairs={{0,2},{1,3},{2,0},{3,1},{4,6},{5,7},{6,4},{7,5},{8,10},{9,11},{10,... | collective-permute-start | bytes 983048 | tf_op jit(solution)/shard_map/ppermute | solution.py:354
  101.7 26.4 %collective-permute-start.20 = (f32[2,1,64,1664]{3,2,1,0:T(8,128)S(1)}, f32[2,1,64,1664]{3,2,1,0:T(8,128)S(1)}, u32[]{:S(2)}, u32[]{:S(2)}) collective-permute-start(f32[2,1,64,1664]{3,2,1,0:T(8,128)S(1)} %get-tuple-element.159), channel_id=1, source_target_pairs={{0,16},{4,20},{8,24},{12,28},{16,0},{20,4},{24,8},{28,12},{1,17},{... | collective-permute-start | bytes 2555912 | tf_op jit(solution)/shard_map/ppermute | solution.py:354
  101.8 37.4 %collective-permute-start.23 = (f32[64,640]{1,0:T(8,128)S(1)}, f32[64,640]{1,0:T(8,128)S(1)}, u32[]{:S(2)}, u32[]{:S(2)}) collective-permute-start(f32[64,640]{1,0:T(8,128)S(1)} %get-tuple-element.164), channel_id=1, source_target_pairs={{0,16},{4,20},{8,24},{12,28},{16,0},{20,4},{24,8},{28,12},{1,17},{... | collective-permute-start | bytes 491528 | tf_op jit(solution)/shard_map/ppermute | solution.py:354
  121.0 18.2 %collective-permute-start.22 = (f32[64,640]{1,0:T(8,128)S(1)}, f32[64,640]{1,0:T(8,128)S(1)}, u32[]{:S(2)}, u32[]{:S(2)}) collective-permute-start(f32[64,640]{1,0:T(8,128)S(1)} %get-tuple-element.163), channel_id=1, source_target_pairs={{0,8},{4,12},{8,0},{12,4},{16,24},{20,28},{24,16},{28,20},{1,9},{5... | collective-permute-start | bytes 491528 | tf_op jit(solution)/shard_map/ppermute | solution.py:354
  128.0 15.1 %collective-permute-start.42 = (f32[64,1024]{1,0:T(8,128)S(1)}, f32[64,1024]{1,0:T(8,128)S(1)}, u32[]{:S(2)}, u32[]{:S(2)}) collective-permute-start(f32[64,1024]{1,0:T(8,128)S(1)} %slice_bitcast_fusion), channel_id=1, source_target_pairs={{0,2},{1,3},{2,0},{3,1},{4,6},{5,7},{6,4},{7,5},{8,10},{9,11},{10,... | collective-permute-start | bytes 786440 | tf_op jit(solution)/shard_map/ppermute | solution.py:354
  128.0 11.0 %collective-permute-start.19 = (f32[1,1,64,1664]{3,2,1,0:T(8,128)S(1)}, f32[1,1,64,1664]{3,2,1,0:T(8,128)S(1)}, u32[]{:S(2)}, u32[]{:S(2)}) collective-permute-start(f32[1,1,64,1664]{3,2,1,0:T(8,128)S(1)} %slice_add_fusion.2), channel_id=1, source_target_pairs={{0,16},{4,20},{8,24},{12,28},{16,0},{20,4},{24,8},{28,12},{1,17},{... | collective-permute-start | bytes 1277960 | tf_op jit(solution)/shard_map/ppermute | solution.py:354
  128.2 10.9 %collective-permute-start.21 = (f32[1,1,64,1664]{3,2,1,0:T(8,128)S(1)}, f32[1,1,64,1664]{3,2,1,0:T(8,128)S(1)}, u32[]{:S(2)}, u32[]{:S(2)}) collective-permute-start(f32[1,1,64,1664]{3,2,1,0:T(8,128)S(1)} %slice_add_fusion), channel_id=1, source_target_pairs={{0,8},{4,12},{8,0},{12,4},{16,24},{20,28},{24,16},{28,20},{1,9},{5... | collective-permute-start | bytes 1277960 | tf_op jit(solution)/shard_map/ppermute | solution.py:354
  142.1 11.9 %collective-permute-start.25 = (f32[64,640]{1,0:T(8,128)S(1)}, f32[64,640]{1,0:T(8,128)S(1)}, u32[]{:S(2)}, u32[]{:S(2)}) collective-permute-start(f32[64,640]{1,0:T(8,128)S(1)} %get-tuple-element.164), channel_id=1, source_target_pairs={{0,8},{4,12},{8,0},{12,4},{16,24},{20,28},{24,16},{28,20},{1,9},{5... | collective-permute-start | bytes 491528 | tf_op jit(solution)/shard_map/ppermute | solution.py:354
  154.0 14.2 %collective-permute-start.46 = (f32[64,1024]{1,0:T(8,128)S(1)}, f32[64,1024]{1,0:T(8,128)S(1)}, u32[]{:S(2)}, u32[]{:S(2)}) collective-permute-start(f32[64,1024]{1,0:T(8,128)S(1)} %fusion.14), channel_id=1, source_target_pairs={{0,8},{4,12},{8,0},{12,4},{16,24},{20,28},{24,16},{28,20},{1,9},{5... | collective-permute-start | bytes 786440 | tf_op jit(solution)/shard_map/ppermute | solution.py:354
  154.9 17.5 %collective-permute-start.44 = (f32[64,1024]{1,0:T(8,128)S(1)}, f32[64,1024]{1,0:T(8,128)S(1)}, u32[]{:S(2)}, u32[]{:S(2)}) collective-permute-start(f32[64,1024]{1,0:T(8,128)S(1)} %fusion.14), channel_id=1, source_target_pairs={{0,16},{4,20},{8,24},{12,28},{16,0},{20,4},{24,8},{28,12},{1,17},{... | collective-permute-start | bytes 786440 | tf_op jit(solution)/shard_map/ppermute | solution.py:354
  156.5 15.8 %collective-permute-start.36 = (f32[64,640]{1,0:T(8,128)S(1)}, f32[64,640]{1,0:T(8,128)S(1)}, u32[]{:S(2)}, u32[]{:S(2)}) collective-permute-start(f32[64,640]{1,0:T(8,128)S(1)} %collective-permute-done.32), channel_id=1, source_target_pairs={{0,16},{4,20},{8,24},{12,28},{16,0},{20,4},{24,8},{28,12},{1,17},{... | collective-permute-start | bytes 491528 | tf_op jit(solution)/shard_map/ppermute | solution.py:354
  157.1 15.8 %collective-permute-start.37 = (f32[64,640]{1,0:T(8,128)S(1)}, f32[64,640]{1,0:T(8,128)S(1)}, u32[]{:S(2)}, u32[]{:S(2)}) collective-permute-start(f32[64,640]{1,0:T(8,128)S(1)} %collective-permute-done.33), channel_id=1, source_target_pairs={{0,8},{4,12},{8,0},{12,4},{16,24},{20,28},{24,16},{28,20},{1,9},{5... | collective-permute-start | bytes 491528 | tf_op jit(solution)/shard_map/ppermute | solution.py:354
  162.0 11.2 %collective-permute-start.29 = (f32[128,640]{1,0:T(8,128)S(1)}, f32[128,640]{1,0:T(8,128)S(1)}, u32[]{:S(2)}, u32[]{:S(2)}) collective-permute-start(f32[128,640]{1,0:T(8,128)S(1)} %constant_dynamic-update-slice_fusion.2.refs_1_), channel_id=1, source_target_pairs={{0,4},{4,0},{8,12},{12,8},{16,20},{20,16},{24,28},{28,24},{1,5},{5... | collective-permute-start | bytes 983048 | tf_op jit(solution)/shard_map/ppermute | solution.py:354
  173.2 11.0 %collective-permute-start.48 = (f32[64,1024]{1,0:T(8,128)S(1)}, f32[64,1024]{1,0:T(8,128)S(1)}, u32[]{:S(2)}, u32[]{:S(2)}) collective-permute-start(f32[64,1024]{1,0:T(8,128)S(1)} %collective-permute-done.44), channel_id=1, source_target_pairs={{0,8},{4,12},{8,0},{12,4},{16,24},{20,28},{24,16},{28,20},{1,9},{5... | collective-permute-start | bytes 786440 | tf_op jit(solution)/shard_map/ppermute | solution.py:354
  (34 other events, 210.8 us)

commit v6 on v5

--- a/solution.py
+++ b/solution.py
@@ -389,16 +389,25 @@
 class Gather:
     def __init__(self, halves, chips):
         self.chips, self.orders = chips, orders(chips)
-        self.held = [[value] for value in halves]
+        self.halves, self.whole = halves, {}
 
     def begin(self):
-        for held, order in zip(self.held, self.orders):
-            held += [swap(held[0], "dp", 2 << bit) for bit in order[:1]]
+        block = jnp.concatenate(self.halves, axis=0)
+        self.whole = {order[0]: swap(block, "dp", 2 << order[0]) for order in self.orders}
 
     def relay(self):
-        for held, order in zip(self.held, self.orders):
-            for bit in order[1:]:
-                held += [swap(value, "dp", 2 << bit) for value in held]
+        step = self.halves[0].shape[0]
+        self.held = []
+        for half, order in enumerate(self.orders):
+            held = [self.halves[half]]
+            for bit in order:
+                came = [swap(value, "dp", 2 << bit) for value in held[1:]]
+                if bit in self.whole:
+                    own = self.whole[bit][half * step : (half + 1) * step]
+                else:
+                    own = swap(held[0], "dp", 2 << bit)
+                held += [own] + came
+            self.held.append(held)
 
     def finish(self, *before):
         mine = [jnp.concatenate(pair, axis=0) for pair in zip(*self.held)]
@@ -453,46 +462,48 @@
     act_sum.held, far_sum.held = together(act_sum.held, far_sum.held)
     act_sum.add()
     act_sums = act_sum.finish()
-    act_across = [across(total[1:]) for total in act_sums]
+    act_across = across(jnp.stack([value[1:] for value in act_sums], axis=1))
+    near_sum.leaving, act_across = together(near_sum.leaving, act_across)
+    near_sum.send()
     far_sum.add()
     far_sum.leaving, act_across = together(far_sum.leaving, act_across)
     far_sum.send()
+    near_sum.add()
+    near_sum.send()
+    far_sum.add()
+    far_sums = far_sum.finish()
 
     step = block // 2
     parts = [slice(half * step, (half + 1) * step) for half in range(2)]
-    act_totals = [sum(there, total[0]) for total, there in zip(act_sums, act_across)]
+    act_totals = [
+        sum((there[half] for there in act_across), value[0]) for half, value in enumerate(act_sums)
+    ]
     total = jnp.maximum(act_totals[1][-1:, 0:1], 1.0)
     act_halves = [old_act[here] + 0.5 * (value / total) for here, value in zip(parts, act_totals)]
+    far_sums, act_halves = together(far_sums, act_halves)
+    across_grad = across(jnp.stack([value[:, :, 0:width] for value in far_sums], axis=1))
+    across_mixed = across(jnp.stack([value[:, :, width:] for value in far_sums], axis=1))
     act_gather = Gather(act_halves, chips)
     act_gather.begin()
-    far_sum.add()
-    far_sums = far_sum.finish()
-    far_sums, near_sum.leaving = together(far_sums, near_sum.leaving)
-    across_grad = across(jnp.stack([value[:, :, 0:width] for value in far_sums], axis=1))
-    across_mixed = [across(value[:, :, width:]) for value in far_sums]
-    near_sum.send()
-    early = (across_grad, across_mixed[0])
-    near_sum.held, (across_grad, across_mixed[0]) = together(near_sum.held, early)
+    near_sum.held, across_grad = together(near_sum.held, across_grad)
     near_sum.add()
-    near_sum.send()
-    near_sum.add()
-    near_sums, act_gather.held = together(near_sum.finish(), act_gather.held)
-    act_gather.relay()
+    near_sums = near_sum.finish()
 
     def of_near(half, far, columns):
-        return sum(far, near_sums[half][0, :, columns]) / total
+        return sum((there[half] for there in far), near_sums[half][0, :, columns]) / total
 
     grad_halves = [
-        old_grad[here] + 0.5 * of_near(half, [there[half] for there in across_grad], slice(0, width))
+        old_grad[here] + 0.5 * of_near(half, across_grad, slice(0, width))
         for half, here in enumerate(parts)
     ]
     grad_gather = Gather(grad_halves, chips)
     grad_gather.begin()
-    mixed_gather = Gather([of_near(half, across_mixed[half], slice(width, None)) for half in range(2)], chips)
-    mixed_gather.begin()
+    across_mixed, grad_gather.whole = together(across_mixed, grad_gather.whole)
+    act_gather.relay()
     grad_gather.relay()
+    act_out, *act_square = act_factor_rows(place, act_gather.finish(), block, feat)
+    mixed_gather = Gather([of_near(half, across_mixed, slice(width, None)) for half in range(2)], chips)
     mixed_gather.relay()
-    act_out, *act_square = act_factor_rows(place, act_gather.finish(), block, feat)
     grad_blocks, act_square = together(grad_gather.finish(), act_square)
     grad_out, inverse = grad_factor_rows(place, grad_blocks, block, feat)
     mixed_blocks = mixed_gather.finish(inverse)

time: 199 us -> 197 us (0.990)
  starting transfers between devices: 48.9 us -> 37.8 us
  waiting for transfers between devices: 102 us -> 111 us
    ppermute x53 -> x47, starting transfers between devices: 48.9 us -> 37.8 us  [swap(): return lax.ppermute(value, axis, [(i, i ^ step) for i in range(size)])]
    ppermute x53 -> x47, waiting for transfers between devices: 102 us -> 111 us  [swap(): return lax.ppermute(value, axis, [(i, i ^ step) for i in range(size)])]
  transfers between devices with their start and end apart: 53 -> 47, of which waited for: 19 -> 12; matrix products, arithmetic and copies ran while one was open for 3% -> 3% of each run, Pallas kernels for 15% -> 15%
where the time goes in v6:
time: 197 us; the launch traced here: 195 us
  waiting for transfers between devices  111 us (56%)
  starting transfers between devices  37.8 us (19%)
  Pallas kernels  35.4 us (18%)
  local copies, waits for them, and re-layouts  6 us (3%)
  other arithmetic  2.45 us (1%)
    ppermute x47, waiting for transfers between devices, swap(): return lax.ppermute(value, axis, [(i, i ^ step) for i in range(size)])  111 us
    ppermute x47, starting transfers between devices, swap(): return lax.ppermute(value, axis, [(i, i ^ step) for i in range(size)])  37.8 us
    pallas_call x4, Pallas kernels, bands(): pl.pallas_call(functools.partial(body, turns, block, chips, bool(seeds),...  22.6 us
    pallas_call x3, Pallas kernels, on_core(): pl.pallas_call(body, out_shape=shapes, in_specs=[pl.BlockSpec(memory_spac...  12 us
  transfers between devices with their start and end apart: 47, of which 12 were waited for; matrix products, arithmetic and copies ran while one was open for 3% of the time, Pallas kernels for 15%

profile of v6, /device:TPU:25, one launch (start us, length us, event | category | flops | bytes accessed | tf_op | source)
XLA Modules:
  0.0 194.6 jit_solution(4040805009587315098)
XLA Ops:
  6.1 1.7 slice.229
  9.0 3.7 %shard_map.112 = (f32[2,2,64,640]{3,2,1,0:T(8,128)S(1)}, f32[2,2,64,640]{3,2,1,0:T(8,128)S(1)}, f32[2,2,64,640]{3,2,1,0:T(8,128)S(1)}, f32[2,2,64,640]{3,2,1,0:T(8,128)S(1)}) custom-call(s32[2]{0:T(128)S(1)} %pad_add_fusion.place, f32[264,1024]{1,0:T(8,128)S(1)} %shard_map.111.refs_0_.refs_2_, f32[264,1024]{1,0:T(8,128)S(1)} %collective-permute-done.2.refs_1_.refs_3_), custom_call_target="tpu_custom_call" | custom-call | tf_op jit(solution)/shard_map/pallas_call | solution.py:212
  12.8 7.9 %shard_map.113 = (f32[2,1,64,1664]{3,2,1,0:T(8,128)S(1)}, f32[2,1,64,1664]{3,2,1,0:T(8,128)S(1)}, f32[2,1,64,1664]{3,2,1,0:T(8,128)S(1)}, f32[2,1,64,1664]{3,2,1...) custom-call(s32[2]{0:T(128)S(1)} %pad_add_fusion.place, ...), custom_call_target="tpu_custom_call" | custom-call | tf_op jit(solution)/shard_map/pallas_call | solution.py:212
  20.7 9.4 %collective-permute-done.1.refs_0_.refs_2_ = f32[264,1024]{1,0:T(8,128)S(1)} collective-permute-done((f32[264,1024]{1,0:T(8,128)S(1)}, f32[264,1024]{1,0:T(8,128)S(1)}, u32[]{:S(2)}, u32[]{:S(2)}) %collective-permute-start.1) | collective-permute-done | bytes 1081376 | tf_op jit(solution)/shard_map/ppermute | solution.py:354
  31.1 2.2 %collective-permute-done.4.refs_1_.refs_3_ = f32[264,1024]{1,0:T(8,128)S(1)} collective-permute-done((f32[264,1024]{1,0:T(8,128)S(1)}, f32[264,1024]{1,0:T(8,128)S(1)}, u32[]{:S(2)}, u32[]{:S(2)}) %collective-permute-start.4) | collective-permute-done | bytes 1081376 | tf_op jit(solution)/shard_map/ppermute | solution.py:354
  33.2 3.8 %shard_map.114 = (f32[2,2,64,640]{3,2,1,0:T(8,128)S(1)}, f32[2,2,64,640]{3,2,1,0:T(8,128)S(1)}, f32[2,2,64,640]{3,2,1,0:T(8,128)S(1)}, f32[2,2,64,640]{3,2,1,0:T(8,128)S(1)}) custom-call(s32[2]{0:T(128)S(1)} %pad_add_fusion.place, f32[264,1024]{1,0:T(8,128)S(1)} %collective-permute-done.1.refs_0_.refs_2_, ...), custom_call_target="tpu_custom_call" | custom-call | tf_op jit(solution)/shard_map/pallas_call | solution.py:212
  39.5 16.4 %collective-permute-done.refs_0_ = f32[256,1024]{1,0:T(8,128)S(1)} collective-permute-done((f32[256,1024]{1,0:T(8,128)}, f32[256,1024]{1,0:T(8,128)S(1)}, u32[]{:S(2)}, u32[]{:S(2)}) %collective-permute-start) | collective-permute-done | bytes 1048608 | tf_op jit(solution)/shard_map/ppermute | solution.py:354
  59.4 7.2 %shard_map.115 = (f32[2,1,64,1664]{3,2,1,0:T(8,128)S(1)}, f32[2,1,64,1664]{3,2,1,0:T(8,128)S(1)}, f32[2,1,64,1664]{3,2,1,0:T(8,128)S(1)}, f32[2,1,64,1664]{3,2,1...) custom-call(s32[2]{0:T(128)S(1)} %pad_add_fusion.place, ...), custom_call_target="tpu_custom_call" | custom-call | tf_op jit(solution)/shard_map/pallas_call | solution.py:212
  69.0 17.4 %collective-permute-done.12 = f32[2,64,640]{2,1,0:T(8,128)S(1)} collective-permute-done((f32[2,64,640]{2,1,0:T(8,128)S(1)}, f32[2,64,640]{2,1,0:T(8,128)S(1)}, u32[]{:S(2)}, u32[]{:S(2)}) %collective-permute-start.12) | collective-permute-done | bytes 327712 | tf_op jit(solution)/shard_map/ppermute | solution.py:354
  90.7 15.7 %collective-permute-done.23 = f32[2,1,64,1664]{3,2,1,0:T(8,128)S(1)} collective-permute-done((f32[2,1,64,1664]{3,2,1,0:T(8,128)S(1)}, f32[2,1,64,1664]{3,2,1,0:T(8,128)S(1)}, u32[]{:S(2)}, u32[]{:S(2)}) %collective-permute-start.23) | collective-permute-done | bytes 852000 | tf_op jit(solution)/shard_map/ppermute | solution.py:354
  107.7 7.8 %collective-permute-done.13 = f32[1,1,64,1664]{3,2,1,0:T(8,128)S(1)} collective-permute-done((f32[1,1,64,1664]{3,2,1,0:T(8,128)S(1)}, f32[1,1,64,1664]{3,2,1,0:T(8,128)S(1)}, u32[]{:S(2)}, u32[]{:S(2)}) %collective-permute-start.13) | collective-permute-done | bytes 426016 | tf_op jit(solution)/shard_map/ppermute | solution.py:354
  117.5 27.8 %collective-permute-done.25 = f32[2,64,640]{2,1,0:T(8,128)S(1)} collective-permute-done((f32[2,64,640]{2,1,0:T(8,128)S(1)}, f32[2,64,640]{2,1,0:T(8,128)S(1)}, u32[]{:S(2)}, u32[]{:S(2)}) %collective-permute-start.25) | collective-permute-done | bytes 327712 | tf_op jit(solution)/shard_map/ppermute | solution.py:354
  145.6 1.4 collective-permute-start.29
  147.2 1.5 collective-permute-start.17
  148.8 8.5 %collective-permute-done.18 = f32[64,640]{1,0:T(8,128)S(1)} collective-permute-done((f32[64,640]{1,0:T(8,128)S(1)}, f32[64,640]{1,0:T(8,128)S(1)}, u32[]{:S(2)}, u32[]{:S(2)}) %collective-permute-start.18) | collective-permute-done | bytes 163872 | tf_op jit(solution)/shard_map/ppermute | solution.py:354
  157.2 2.1 %collective-permute-start.19 = (f32[128,640]{1,0:T(8,128)S(1)}, f32[128,640]{1,0:T(8,128)S(1)}, u32[]{:S(2)}, u32[]{:S(2)}) collective-permute-start(f32[128,640]{1,0:T(8,128)S(1)} %constant_dynamic-update-slice_fusion.refs_0_), channel_id=1, source_target_pairs={{0,4},{4,0},{8,12},{12,8},{16,20},{20,16},{24,28},{28,24},{1,5},{5... | collective-permute-start | bytes 983048 | tf_op jit(solution)/shard_map/ppermute | solution.py:354
  168.2 2.6 %shard_map.116 = (f32[128,1024]{1,0:T(8,128)}, f32[8,128]{1,0:T(8,128)S(1)}, bf16[1024,1024]{1,0:T(8,128)(2,1)S(1)}, bf16[1024,1024]{1,0:T(8,128)(2,1)S(1)}) custom-call(s32[2]{0:T(128)S(1)} %pad_add_fusion.place, f32[128,640]{1,0:T(8,128)S(1)} %constant_dynamic-update-slice_fusion.refs_0_, f32[128,640]{1,0:T(8,128)S(1)} %pad_maximum_fusion.2.refs_1_, ...), custom_call_target="tpu_custom_call" | custom-call | tf_op jit(solution)/shard_map/pallas_call | solution.py:321
  170.8 1.5 collective-permute-done.37
  172.3 2.8 %collective-permute-start.34 = (f32[128,640]{1,0:T(8,128)S(1)}, f32[128,640]{1,0:T(8,128)S(1)}, u32[]{:S(2)}, u32[]{:S(2)}) collective-permute-start(f32[128,640]{1,0:T(8,128)S(1)} %pad_maximum_fusion.6.refs_1_), channel_id=1, source_target_pairs={{0,4},{4,0},{8,12},{12,8},{16,20},{20,16},{24,28},{28,24},{1,5},{5... | collective-permute-start | bytes 983048 | tf_op jit(solution)/shard_map/ppermute | solution.py:354
  175.7 2.2 %collective-permute-done.40 = f32[64,1024]{1,0:T(8,128)S(1)} collective-permute-done((f32[64,1024]{1,0:T(8,128)S(1)}, f32[64,1024]{1,0:T(8,128)S(1)}, u32[]{:S(2)}, u32[]{:S(2)}) %collective-permute-start.40) | collective-permute-done | bytes 262176 | tf_op jit(solution)/shard_map/ppermute | solution.py:354
  179.8 2.3 %collective-permute-start.43 = (f32[128,1024]{1,0:T(8,128)S(1)}, f32[128,1024]{1,0:T(8,128)S(1)}, u32[]{:S(2)}, u32[]{:S(2)}) collective-permute-start(f32[128,1024]{1,0:T(8,128)S(1)} %pad_maximum_fusion.refs_0_), channel_id=1, source_target_pairs={{0,4},{4,0},{8,12},{12,8},{16,20},{20,16},{24,28},{28,24},{1,5},{5... | collective-permute-start | bytes 1572872 | tf_op jit(solution)/shard_map/ppermute | solution.py:354
  182.6 3.7 %shard_map.117 = (f32[128,1024]{1,0:T(8,128)}, f32[128,1024]{1,0:T(8,128)S(1)}) custom-call(s32[2]{0:T(128)S(1)} %pad_add_fusion.place, f32[128,640]{1,0:T(8,128)S(1)} %pad_maximum_fusion.5.refs_0_, f32[128,640]{1,0:T(8,128)S(1)} %pad_maximum_fusion.6.refs_1_, f32[128,640]{1,0:T(8,128)S(1)} %pad_maximum_fusion.7.refs_2_, ...), custom_call_target="tpu_custom_call" | custom-call | tf_op jit(solution)/shard_map/pallas_call | solution.py:321
  187.3 1.5 collective-permute-done.46.refs_7_
  188.8 5.7 %shard_map.118 = (f32[128,1024]{1,0:T(8,128)}, f32[128,1024]{1,0:T(8,128)}) custom-call(s32[2]{0:T(128)S(1)} %pad_add_fusion.place, f32[128,1024]{1,0:T(8,128)S(1)} %pad_maximum_fusion.refs_0_, f32[128,1024]{1,0:T(8,128)S(1)} %constant_dynamic-update-slice_fusion.2.refs_1_, f32[128,1024]{1,0:T(8,128)S(1)} %constant_dynamic-update-slice_fusion.4.refs_2_, ...), custom_call_target="tpu_custom_call" | custom-call | tf_op jit(solution)/shard_map/pallas_call | solution.py:321
  (137 shorter events, 36.1 us)
Async XLA Ops:
  4.6 25.4 %collective-permute-start.1 = (f32[264,1024]{1,0:T(8,128)S(1)}, f32[264,1024]{1,0:T(8,128)S(1)}, u32[]{:S(2)}, u32[]{:S(2)}) collective-permute-start(f32[264,1024]{1,0:T(8,128)S(1)} %shard_map.111.refs_0_.refs_2_), channel_id=1, source_target_pairs={{0,1},{1,0},{2,3},{3,2},{4,5},{5,4},{6,7},{7,6},{8,9},{9,8},{10,11... | collective-permute-start | bytes 3244040 | tf_op jit(solution)/shard_map/ppermute | solution.py:354
  30.9 25.0 %collective-permute-start = (f32[256,1024]{1,0:T(8,128)}, f32[256,1024]{1,0:T(8,128)S(1)}, u32[]{:S(2)}, u32[]{:S(2)}) collective-permute-start(f32[256,1024]{1,0:T(8,128)} %refs_0_.1), channel_id=1, source_target_pairs={{0,1},{1,0},{2,3},{3,2},{4,5},{5,4},{6,7},{7,6},{8,9},{9,8},{10,11... | collective-permute-start | bytes 3145736 | tf_op jit(solution)/shard_map/ppermute | solution.py:354
  37.0 19.7 %collective-permute-start.5 = (f32[2,2,64,640]{3,2,1,0:T(8,128)S(1)}, f32[2,2,64,640]{3,2,1,0:T(8,128)S(1)}, u32[]{:S(2)}, u32[]{:S(2)}) collective-permute-start(f32[2,2,64,640]{3,2,1,0:T(8,128)S(1)} %get-tuple-element.116), channel_id=1, source_target_pairs={{0,8},{4,12},{8,0},{12,4},{16,24},{20,28},{24,16},{28,20},{1,9},{5... | collective-permute-start | bytes 1966088 | tf_op jit(solution)/shard_map/ppermute | solution.py:354
  38.3 18.5 %collective-permute-start.6 = (f32[2,2,64,640]{3,2,1,0:T(8,128)S(1)}, f32[2,2,64,640]{3,2,1,0:T(8,128)S(1)}, u32[]{:S(2)}, u32[]{:S(2)}) collective-permute-start(f32[2,2,64,640]{3,2,1,0:T(8,128)S(1)} %get-tuple-element.118), channel_id=1, source_target_pairs={{0,16},{4,20},{8,24},{12,28},{16,0},{20,4},{24,8},{28,12},{1,17},{... | collective-permute-start | bytes 1966088 | tf_op jit(solution)/shard_map/ppermute | solution.py:354
  56.9 11.9 %collective-permute-start.10 = (f32[1,2,64,640]{3,2,1,0:T(8,128)S(1)}, f32[1,2,64,640]{3,2,1,0:T(8,128)S(1)}, u32[]{:S(2)}, u32[]{:S(2)}) collective-permute-start(f32[1,2,64,640]{3,2,1,0:T(8,128)S(1)} %get-tuple-element.145), channel_id=1, source_target_pairs={{0,16},{4,20},{8,24},{12,28},{16,0},{20,4},{24,8},{28,12},{1,17},{... | collective-permute-start | bytes 983048 | tf_op jit(solution)/shard_map/ppermute | solution.py:354
  66.6 20.7 %collective-permute-start.8 = (f32[2,1,64,1664]{3,2,1,0:T(8,128)S(1)}, f32[2,1,64,1664]{3,2,1,0:T(8,128)S(1)}, u32[]{:S(2)}, u32[]{:S(2)}) collective-permute-start(f32[2,1,64,1664]{3,2,1,0:T(8,128)S(1)} %get-tuple-element.139), channel_id=1, source_target_pairs={{0,8},{4,12},{8,0},{12,4},{16,24},{20,28},{24,16},{28,20},{1,9},{5... | collective-permute-start | bytes 2555912 | tf_op jit(solution)/shard_map/ppermute | solution.py:354
  67.5 19.9 %collective-permute-start.9 = (f32[2,1,64,1664]{3,2,1,0:T(8,128)S(1)}, f32[2,1,64,1664]{3,2,1,0:T(8,128)S(1)}, u32[]{:S(2)}, u32[]{:S(2)}) collective-permute-start(f32[2,1,64,1664]{3,2,1,0:T(8,128)S(1)} %get-tuple-element.141), channel_id=1, source_target_pairs={{0,16},{4,20},{8,24},{12,28},{16,0},{20,4},{24,8},{28,12},{1,17},{... | collective-permute-start | bytes 2555912 | tf_op jit(solution)/shard_map/ppermute | solution.py:354
  68.9 17.5 %collective-permute-start.12 = (f32[2,64,640]{2,1,0:T(8,128)S(1)}, f32[2,64,640]{2,1,0:T(8,128)S(1)}, u32[]{:S(2)}, u32[]{:S(2)}) collective-permute-start(f32[2,64,640]{2,1,0:T(8,128)S(1)} %maximum_bitcast_fusion.1), channel_id=1, source_target_pairs={{0,2},{1,3},{2,0},{3,1},{4,6},{5,7},{6,4},{7,5},{8,10},{9,11},{10,... | collective-permute-start | bytes 983048 | tf_op jit(solution)/shard_map/ppermute | solution.py:354
  86.4 20.0 %collective-permute-start.23 = (f32[2,1,64,1664]{3,2,1,0:T(8,128)S(1)}, f32[2,1,64,1664]{3,2,1,0:T(8,128)S(1)}, u32[]{:S(2)}, u32[]{:S(2)}) collective-permute-start(f32[2,1,64,1664]{3,2,1,0:T(8,128)S(1)} %get-tuple-element.158), channel_id=1, source_target_pairs={{0,8},{4,12},{8,0},{12,4},{16,24},{20,28},{24,16},{28,20},{1,9},{5... | collective-permute-start | bytes 2555912 | tf_op jit(solution)/shard_map/ppermute | solution.py:354
  86.7 20.2 %collective-permute-start.24 = (f32[2,1,64,1664]{3,2,1,0:T(8,128)S(1)}, f32[2,1,64,1664]{3,2,1,0:T(8,128)S(1)}, u32[]{:S(2)}, u32[]{:S(2)}) collective-permute-start(f32[2,1,64,1664]{3,2,1,0:T(8,128)S(1)} %get-tuple-element.160), channel_id=1, source_target_pairs={{0,16},{4,20},{8,24},{12,28},{16,0},{20,4},{24,8},{28,12},{1,17},{... | collective-permute-start | bytes 2555912 | tf_op jit(solution)/shard_map/ppermute | solution.py:354
  88.0 27.5 %collective-permute-start.13 = (f32[1,1,64,1664]{3,2,1,0:T(8,128)S(1)}, f32[1,1,64,1664]{3,2,1,0:T(8,128)S(1)}, u32[]{:S(2)}, u32[]{:S(2)}) collective-permute-start(f32[1,1,64,1664]{3,2,1,0:T(8,128)S(1)} %slice_add_fusion.6), channel_id=1, source_target_pairs={{0,16},{4,20},{8,24},{12,28},{16,0},{20,4},{24,8},{28,12},{1,17},{... | collective-permute-start | bytes 1277960 | tf_op jit(solution)/shard_map/ppermute | solution.py:354
  89.2 26.4 %collective-permute-start.14 = (f32[1,1,64,1664]{3,2,1,0:T(8,128)S(1)}, f32[1,1,64,1664]{3,2,1,0:T(8,128)S(1)}, u32[]{:S(2)}, u32[]{:S(2)}) collective-permute-start(f32[1,1,64,1664]{3,2,1,0:T(8,128)S(1)} %slice_add_fusion.5), channel_id=1, source_target_pairs={{0,8},{4,12},{8,0},{12,4},{16,24},{20,28},{24,16},{28,20},{1,9},{5... | collective-permute-start | bytes 1277960 | tf_op jit(solution)/shard_map/ppermute | solution.py:354
  106.5 38.8 %collective-permute-start.26 = (f32[1,1,64,1664]{3,2,1,0:T(8,128)S(1)}, f32[1,1,64,1664]{3,2,1,0:T(8,128)S(1)}, u32[]{:S(2)}, u32[]{:S(2)}) collective-permute-start(f32[1,1,64,1664]{3,2,1,0:T(8,128)S(1)} %get-tuple-element.188), channel_id=1, source_target_pairs={{0,16},{4,20},{8,24},{12,28},{16,0},{20,4},{24,8},{28,12},{1,17},{... | collective-permute-start | bytes 1277960 | tf_op jit(solution)/shard_map/ppermute | solution.py:354
  106.9 38.4 %collective-permute-start.27 = (f32[1,1,64,1664]{3,2,1,0:T(8,128)S(1)}, f32[1,1,64,1664]{3,2,1,0:T(8,128)S(1)}, u32[]{:S(2)}, u32[]{:S(2)}) collective-permute-start(f32[1,1,64,1664]{3,2,1,0:T(8,128)S(1)} %get-tuple-element.190), channel_id=1, source_target_pairs={{0,8},{4,12},{8,0},{12,4},{16,24},{20,28},{24,16},{28,20},{1,9},{5... | collective-permute-start | bytes 1277960 | tf_op jit(solution)/shard_map/ppermute | solution.py:354
  115.7 31.3 %collective-permute-start.16 = (f32[128,640]{1,0:T(8,128)S(1)}, f32[128,640]{1,0:T(8,128)S(1)}, u32[]{:S(2)}, u32[]{:S(2)}) collective-permute-start(f32[128,640]{1,0:T(8,128)S(1)} %constant_dynamic-update-slice_fusion.refs_0_), channel_id=1, source_target_pairs={{0,16},{4,20},{8,24},{12,28},{16,0},{20,4},{24,8},{28,12},{1,17},{... | collective-permute-start | bytes 983048 | tf_op jit(solution)/shard_map/ppermute | solution.py:354
  116.4 30.8 %collective-permute-start.15 = (f32[128,640]{1,0:T(8,128)S(1)}, f32[128,640]{1,0:T(8,128)S(1)}, u32[]{:S(2)}, u32[]{:S(2)}) collective-permute-start(f32[128,640]{1,0:T(8,128)S(1)} %constant_dynamic-update-slice_fusion.refs_0_), channel_id=1, source_target_pairs={{0,8},{4,12},{8,0},{12,4},{16,24},{20,28},{24,16},{28,20},{1,9},{5... | collective-permute-start | bytes 983048 | tf_op jit(solution)/shard_map/ppermute | solution.py:354
  117.3 28.0 %collective-permute-start.25 = (f32[2,64,640]{2,1,0:T(8,128)S(1)}, f32[2,64,640]{2,1,0:T(8,128)S(1)}, u32[]{:S(2)}, u32[]{:S(2)}) collective-permute-start(f32[2,64,640]{2,1,0:T(8,128)S(1)} %maximum_bitcast_fusion.2), channel_id=1, source_target_pairs={{0,2},{1,3},{2,0},{3,1},{4,6},{5,7},{6,4},{7,5},{8,10},{9,11},{10,... | collective-permute-start | bytes 983048 | tf_op jit(solution)/shard_map/ppermute | solution.py:354
  145.3 14.0 %collective-permute-start.28 = (f32[2,64,1024]{2,1,0:T(8,128)S(1)}, f32[2,64,1024]{2,1,0:T(8,128)S(1)}, u32[]{:S(2)}, u32[]{:S(2)}) collective-permute-start(f32[2,64,1024]{2,1,0:T(8,128)S(1)} %maximum_bitcast_fusion), channel_id=1, source_target_pairs={{0,2},{1,3},{2,0},{3,1},{4,6},{5,7},{6,4},{7,5},{8,10},{9,11},{10,... | collective-permute-start | bytes 1572872 | tf_op jit(solution)/shard_map/ppermute | solution.py:354
  145.5 15.0 %collective-permute-start.30 = (f32[128,640]{1,0:T(8,128)S(1)}, f32[128,640]{1,0:T(8,128)S(1)}, u32[]{:S(2)}, u32[]{:S(2)}) collective-permute-start(f32[128,640]{1,0:T(8,128)S(1)} %pad_maximum_fusion.5.refs_0_), channel_id=1, source_target_pairs={{0,16},{4,20},{8,24},{12,28},{16,0},{20,4},{24,8},{28,12},{1,17},{... | collective-permute-start | bytes 983048 | tf_op jit(solution)/shard_map/ppermute | solution.py:354
  145.6 15.0 %collective-permute-start.29 = (f32[128,640]{1,0:T(8,128)S(1)}, f32[128,640]{1,0:T(8,128)S(1)}, u32[]{:S(2)}, u32[]{:S(2)}) collective-permute-start(f32[128,640]{1,0:T(8,128)S(1)} %pad_maximum_fusion.5.refs_0_), channel_id=1, source_target_pairs={{0,8},{4,12},{8,0},{12,4},{16,24},{20,28},{24,16},{28,20},{1,9},{5... | collective-permute-start | bytes 983048 | tf_op jit(solution)/shard_map/ppermute | solution.py:354
  147.2 12.0 %collective-permute-start.17 = (f32[64,640]{1,0:T(8,128)S(1)}, f32[64,640]{1,0:T(8,128)S(1)}, u32[]{:S(2)}, u32[]{:S(2)}) collective-permute-start(f32[64,640]{1,0:T(8,128)S(1)} %get-tuple-element.207), channel_id=1, source_target_pairs={{0,16},{4,20},{8,24},{12,28},{16,0},{20,4},{24,8},{28,12},{1,17},{... | collective-permute-start | bytes 491528 | tf_op jit(solution)/shard_map/ppermute | solution.py:354
  163.3 11.8 %collective-permute-start.33 = (f32[128,640]{1,0:T(8,128)S(1)}, f32[128,640]{1,0:T(8,128)S(1)}, u32[]{:S(2)}, u32[]{:S(2)}) collective-permute-start(f32[128,640]{1,0:T(8,128)S(1)} %pad_maximum_fusion.5.refs_0_), channel_id=1, source_target_pairs={{0,4},{4,0},{8,12},{12,8},{16,20},{20,16},{24,28},{28,24},{1,5},{5... | collective-permute-start | bytes 983048 | tf_op jit(solution)/shard_map/ppermute | solution.py:354
  166.0 11.9 %collective-permute-start.40 = (f32[64,1024]{1,0:T(8,128)S(1)}, f32[64,1024]{1,0:T(8,128)S(1)}, u32[]{:S(2)}, u32[]{:S(2)}) collective-permute-start(f32[64,1024]{1,0:T(8,128)S(1)} %get-tuple-element.199), channel_id=1, source_target_pairs={{0,8},{4,12},{8,0},{12,4},{16,24},{20,28},{24,16},{28,20},{1,9},{5... | collective-permute-start | bytes 786440 | tf_op jit(solution)/shard_map/ppermute | solution.py:354
  167.2 11.3 %collective-permute-start.38 = (f32[64,1024]{1,0:T(8,128)S(1)}, f32[64,1024]{1,0:T(8,128)S(1)}, u32[]{:S(2)}, u32[]{:S(2)}) collective-permute-start(f32[64,1024]{1,0:T(8,128)S(1)} %get-tuple-element.199), channel_id=1, source_target_pairs={{0,16},{4,20},{8,24},{12,28},{16,0},{20,4},{24,8},{28,12},{1,17},{... | collective-permute-start | bytes 786440 | tf_op jit(solution)/shard_map/ppermute | solution.py:354
  (28 other events, 153.1 us)

commit v7 on v6

--- a/solution.py
+++ b/solution.py
@@ -94,12 +94,8 @@
     return places
 
 
-def store(outs, seeds, place, number, columns, value):
-    output, position = place
-    for out in outs[0::4]:
-        if number < out.shape[1]:
-            break
-        output, number = output + 4, number - out.shape[1]
+def store(outs, seeds, group, place, number, columns, value):
+    output, position = 4 * group + place[0], place[1]
     if seeds:
         value = value + seeds[output][position, number, :, columns]
     outs[output][position, number, :, columns] = value
@@ -148,7 +144,7 @@
             value = jnp.where(corner, count, total[number * block : (number + 1) * block])
             for half in range(2):
                 here = value[half * (block // 2) : (half + 1) * (block // 2)]
-                store(outs, seeds, places[k, half], number, slice(0, width), here)
+                store(outs, seeds, 0, places[k, half], number, slice(0, width), here)
 
 
 def grad_kernel(turns, block, chips, seeded, samples, place, *refs):
@@ -156,7 +152,7 @@
     refs, (high, low, act_high, act_low, turned) = refs[:-5], refs[-5:]
     seeds, outs = (refs[: len(refs) // 2], refs[len(refs) // 2 :]) if seeded else ((), refs)
     feat = grads[0].shape[1]
-    width = outs[0].shape[3] - feat
+    width = outs[0].shape[3]
     mine, expert = place[0], place[1]
     split_rows(grads, samples, high, low, feat)
     split_rows(acts, samples, act_high, act_low, feat)
@@ -171,8 +167,13 @@
             for half in range(2):
                 first = number * block + half * (block // 2)
                 here = slice(first, first + block // 2)
-                store(outs, seeds, places[k, half], number, slice(0, width), total[here])
-                store(outs, seeds, places[k, half], number, slice(width, width + feat), mixed[here])
+                place = places[k, half]
+                if number:
+                    store(outs, seeds, 2, place, number - 1, slice(0, width), total[here])
+                    store(outs, seeds, 2, place, number - 1, slice(width, width + feat), mixed[here])
+                else:
+                    store(outs, seeds, 0, place, 0, slice(0, width), total[here])
+                    store(outs, seeds, 1, place, 0, slice(0, feat), mixed[here])
 
 
 def whole_in_vmem(count):
@@ -195,22 +196,21 @@
     )(routes.T, counts, acts)
 
 
-def bands(body, groups, place, parts, seeds, samples, chips, block, width):
-    turns = tuple(range(sum(groups)))
+def bands(body, turns, groups, place, parts, seeds, samples, chips, block):
     feat = parts[0].shape[1]
     extended = pltpu.VMEM((2 * samples, feat + feat // 2), BF16)
     plain = pltpu.VMEM((2 * samples, feat), BF16)
     scratch = [extended, extended] + ([plain, plain] if len(parts) > 2 else [])
     shapes = [
         jax.ShapeDtypeStruct((len(group), count, block // 2, width), F32)
-        for count in groups
+        for count, width in groups
         for order in orders(chips)
         for group in held_and_sent(chips, order)
     ]
     operands = (*parts, *seeds)
     limit = 36 if len(parts) > 2 else 20
     return pl.pallas_call(
-        functools.partial(body, turns, block, chips, bool(seeds), samples),
+        functools.partial(body, range(turns), block, chips, bool(seeds), samples),
         out_shape=shapes,
         in_specs=[pl.BlockSpec(memory_space=pltpu.SMEM)] + whole_in_vmem(len(operands)),
         out_specs=whole_in_vmem(len(shapes)),
@@ -411,7 +411,10 @@
 
     def finish(self, *before):
         mine = [jnp.concatenate(pair, axis=0) for pair in zip(*self.held)]
-        mine[-1], before = together(mine[-1], before)
+        if before:
+            mine[-1], before = together(mine[-1], before)
+        else:
+            mine = list(together(*mine))
         return mine + [swap(value, "dp", 1) for value in mine]
 
 
@@ -433,43 +436,46 @@
         return 0.5 * lax.dynamic_slice_in_dim(wide, start, width, 1)
 
     turns = experts // 2
-    size = (samples, chips, block, width)
-    mixed_size = (samples, chips, block, width + feat)
+    size = (samples, chips, block)
+    act_groups = ((turns, width),)
+    grad_groups = ((1, width), (1, feat), (turns - 1, width + feat))
 
     acts = prepare(routes, counts, acts)
     acts_far = swap(acts, "expert", 1)
     near_acts = (acts, swap(acts, "dp", 1))
-    act_seeds = bands(act_kernel, (turns,), place, near_acts, (), *size)
+    act_seeds = bands(act_kernel, turns, act_groups, place, near_acts, (), *size)
     grads_far = swap(grads_out, "expert", 1)
     grad_parts = (grads_out, swap(grads_out, "dp", 1)) + near_acts
-    grad_seeds = bands(grad_kernel, (1, turns - 1), place, grad_parts, (), *mixed_size)
+    grad_seeds = bands(grad_kernel, turns, grad_groups, place, grad_parts, (), *size)
     old_act, old_grad = own_band(old_act_factor), own_band(old_grad_factor)
     early = (act_seeds, grad_seeds, old_act, old_grad)
     acts_far, (act_seeds, grad_seeds, old_act, old_grad) = together(acts_far, early)
 
     far_acts = (acts_far, swap(acts_far, "dp", 1))
-    act_sum = PlaneSum(bands(act_kernel, (turns,), place, far_acts, act_seeds, *size), chips)
+    act_sum = PlaneSum(bands(act_kernel, turns, act_groups, place, far_acts, act_seeds, *size), chips)
     act_sum.send()
     grads_far, act_sum.held = together(grads_far, act_sum.held)
     grad_parts = (grads_far, swap(grads_far, "dp", 1)) + far_acts
     act_sum.add()
     grad_seeds, act_sum.leaving = together(grad_seeds, act_sum.leaving)
     act_sum.send()
-    pieces = bands(grad_kernel, (1, turns - 1), place, grad_parts, grad_seeds, *mixed_size)
-
-    near_sum, far_sum = PlaneSum(pieces[:4], chips), PlaneSum(pieces[4:], chips)
+    pieces = bands(grad_kernel, turns, grad_groups, place, grad_parts, grad_seeds, *size)
+
+    grad_sum, mixed_sum, far_sum = [PlaneSum(pieces[first : first + 4], chips) for first in (0, 4, 8)]
     far_sum.send()
     act_sum.held, far_sum.held = together(act_sum.held, far_sum.held)
     act_sum.add()
     act_sums = act_sum.finish()
     act_across = across(jnp.stack([value[1:] for value in act_sums], axis=1))
-    near_sum.leaving, act_across = together(near_sum.leaving, act_across)
-    near_sum.send()
+    grad_sum.leaving, far_sum.got = together(grad_sum.leaving, far_sum.got)
+    grad_sum.send()
     far_sum.add()
     far_sum.leaving, act_across = together(far_sum.leaving, act_across)
     far_sum.send()
-    near_sum.add()
-    near_sum.send()
+    grad_sum.add()
+    mixed_sum.leaving, grad_sum.leaving = together(mixed_sum.leaving, grad_sum.leaving)
+    mixed_sum.send()
+    grad_sum.send()
     far_sum.add()
     far_sums = far_sum.finish()
 
@@ -480,29 +486,34 @@
     ]
     total = jnp.maximum(act_totals[1][-1:, 0:1], 1.0)
     act_halves = [old_act[here] + 0.5 * (value / total) for here, value in zip(parts, act_totals)]
-    far_sums, act_halves = together(far_sums, act_halves)
     across_grad = across(jnp.stack([value[:, :, 0:width] for value in far_sums], axis=1))
-    across_mixed = across(jnp.stack([value[:, :, width:] for value in far_sums], axis=1))
+    far_mixed = jnp.stack([value[:, :, width:] for value in far_sums], axis=1)
+    grad_sum.add()
+    grad_sums = grad_sum.finish()
+    mixed_sum.held, across_grad = together(mixed_sum.held, across_grad)
+    mixed_sum.add()
+    mixed_sum.leaving, far_mixed = together(mixed_sum.leaving, far_mixed)
+    mixed_sum.send()
+    across_mixed = across(far_mixed)
+
+    def both(near, far):
+        return [sum((there[half] for there in far), value[0]) / total for half, value in enumerate(near)]
+
+    grad_halves = [old_grad[here] + 0.5 * value for here, value in zip(parts, both(grad_sums, across_grad))]
+    grad_gather = Gather(grad_halves, chips)
+    grad_gather.begin()
+    early = (grad_gather.whole, mixed_sum.got)
+    act_halves, (grad_gather.whole, mixed_sum.got) = together(act_halves, early)
+    mixed_sum.add()
+    mixed_sums = mixed_sum.finish()
     act_gather = Gather(act_halves, chips)
     act_gather.begin()
-    near_sum.held, across_grad = together(near_sum.held, across_grad)
-    near_sum.add()
-    near_sums = near_sum.finish()
-
-    def of_near(half, far, columns):
-        return sum((there[half] for there in far), near_sums[half][0, :, columns]) / total
-
-    grad_halves = [
-        old_grad[here] + 0.5 * of_near(half, across_grad, slice(0, width))
-        for half, here in enumerate(parts)
-    ]
-    grad_gather = Gather(grad_halves, chips)
-    grad_gather.begin()
-    across_mixed, grad_gather.whole = together(across_mixed, grad_gather.whole)
+    across_mixed, act_gather.whole = together(across_mixed, act_gather.whole)
     act_gather.relay()
     grad_gather.relay()
     act_out, *act_square = act_factor_rows(place, act_gather.finish(), block, feat)
-    mixed_gather = Gather([of_near(half, across_mixed, slice(width, None)) for half in range(2)], chips)
+    mixed_gather = Gather(both(mixed_sums, across_mixed), chips)
+    mixed_gather.begin()
     mixed_gather.relay()
     grad_blocks, act_square = together(grad_gather.finish(), act_square)
     grad_out, inverse = grad_factor_rows(place, grad_blocks, block, feat)

time: 197 us -> 188 us (0.954)
  waiting for transfers between devices: 111 us -> 99.6 us
  starting transfers between devices: 37.8 us -> 40.7 us
    ppermute x47 -> x49, waiting for transfers between devices: 111 us -> 99.6 us  [swap(): return lax.ppermute(value, axis, [(i, i ^ step) for i in range(size)])]
    ppermute x47 -> x49, starting transfers between devices: 37.8 us -> 40.7 us  [swap(): return lax.ppermute(value, axis, [(i, i ^ step) for i in range(size)])]
  transfers between devices with their start and end apart: 47 -> 49, of which waited for: 12 -> 20; matrix products, arithmetic and copies ran while one was open for 3% -> 3% of each run, Pallas kernels for 15% -> 16%
where the time goes in v7:
time: 188 us; the launch traced here: 186 us
  waiting for transfers between devices  99.6 us (53%)
  starting transfers between devices  40.7 us (22%)
  Pallas kernels  35.3 us (19%)
  local copies, waits for them, and re-layouts  6 us (3%)
  other arithmetic  2.54 us (1%)
    ppermute x49, waiting for transfers between devices, swap(): return lax.ppermute(value, axis, [(i, i ^ step) for i in range(size)])  99.6 us
    ppermute x49, starting transfers between devices, swap(): return lax.ppermute(value, axis, [(i, i ^ step) for i in range(size)])  40.7 us
    pallas_call x4, Pallas kernels, bands(): pl.pallas_call(functools.partial(body, range(turns), block, chips, bool(s...  22.5 us
    pallas_call x3, Pallas kernels, on_core(): pl.pallas_call(body, out_shape=shapes, in_specs=[pl.BlockSpec(memory_spac...  12 us
  transfers between devices with their start and end apart: 49, of which 20 were waited for; matrix products, arithmetic and copies ran while one was open for 3% of the time, Pallas kernels for 16%

profile of v7, /device:TPU:25, one launch (start us, length us, event | category | flops | bytes accessed | tf_op | source)
XLA Modules:
  0.0 185.8 jit_solution(10993433961095781054)
XLA Ops:
  6.1 1.7 slice.261
  9.0 3.7 %shard_map.112 = (f32[2,2,64,640]{3,2,1,0:T(8,128)S(1)}, f32[2,2,64,640]{3,2,1,0:T(8,128)S(1)}, f32[2,2,64,640]{3,2,1,0:T(8,128)S(1)}, f32[2,2,64,640]{3,2,1,0:T(8,128)S(1)}) custom-call(s32[2]{0:T(128)S(1)} %pad_add_fusion.place, f32[264,1024]{1,0:T(8,128)S(1)} %shard_map.111.refs_0_.refs_2_, f32[264,1024]{1,0:T(8,128)S(1)} %collective-permute-done.1.refs_1_.refs_3_), custom_call_target="tpu_custom_call" | custom-call | tf_op jit(solution)/shard_map/pallas_call | solution.py:212
  12.8 7.9 %shard_map.113 = (f32[2,1,64,640]{3,2,1,0:T(8,128)S(1)}, f32[2,1,64,640]{3,2,1,0:T(8,128)S(1)}, f32[2,1,64,640]{3,2,1,0:T(8,128)S(1)}, f32[2,1,64,640]{3,2,1,0:T...) custom-call(s32[2]{0:T(128)S(1)} %pad_add_fusion.place, ...), custom_call_target="tpu_custom_call" | custom-call | tf_op jit(solution)/shard_map/pallas_call | solution.py:212
  20.6 9.4 %collective-permute-done.refs_0_.refs_2_ = f32[264,1024]{1,0:T(8,128)S(1)} collective-permute-done((f32[264,1024]{1,0:T(8,128)S(1)}, f32[264,1024]{1,0:T(8,128)S(1)}, u32[]{:S(2)}, u32[]{:S(2)}) %collective-permute-start) | collective-permute-done | bytes 1081376 | tf_op jit(solution)/shard_map/ppermute | solution.py:354
  31.1 2.2 %collective-permute-done.4.refs_1_.refs_3_ = f32[264,1024]{1,0:T(8,128)S(1)} collective-permute-done((f32[264,1024]{1,0:T(8,128)S(1)}, f32[264,1024]{1,0:T(8,128)S(1)}, u32[]{:S(2)}, u32[]{:S(2)}) %collective-permute-start.4) | collective-permute-done | bytes 1081376 | tf_op jit(solution)/shard_map/ppermute | solution.py:354
  33.2 3.8 %shard_map.114 = (f32[2,2,64,640]{3,2,1,0:T(8,128)S(1)}, f32[2,2,64,640]{3,2,1,0:T(8,128)S(1)}, f32[2,2,64,640]{3,2,1,0:T(8,128)S(1)}, f32[2,2,64,640]{3,2,1,0:T(8,128)S(1)}) custom-call(s32[2]{0:T(128)S(1)} %pad_add_fusion.place, f32[264,1024]{1,0:T(8,128)S(1)} %collective-permute-done.refs_0_.refs_2_, ...), custom_call_target="tpu_custom_call" | custom-call | tf_op jit(solution)/shard_map/pallas_call | solution.py:212
  39.5 16.4 %collective-permute-done.3.refs_0_ = f32[256,1024]{1,0:T(8,128)S(1)} collective-permute-done((f32[256,1024]{1,0:T(8,128)}, f32[256,1024]{1,0:T(8,128)S(1)}, u32[]{:S(2)}, u32[]{:S(2)}) %collective-permute-start.3) | collective-permute-done | bytes 1048608 | tf_op jit(solution)/shard_map/ppermute | solution.py:354
  59.4 7.2 %shard_map.115 = (f32[2,1,64,640]{3,2,1,0:T(8,128)S(1)}, f32[2,1,64,640]{3,2,1,0:T(8,128)S(1)}, f32[2,1,64,640]{3,2,1,0:T(8,128)S(1)}, f32[2,1,64,640]{3,2,1,0:T...) custom-call(s32[2]{0:T(128)S(1)} %pad_add_fusion.place, ...), custom_call_target="tpu_custom_call" | custom-call | tf_op jit(solution)/shard_map/pallas_call | solution.py:212
  69.0 17.6 %collective-permute-done.9 = f32[2,1,64,1664]{3,2,1,0:T(8,128)S(1)} collective-permute-done((f32[2,1,64,1664]{3,2,1,0:T(8,128)S(1)}, f32[2,1,64,1664]{3,2,1,0:T(8,128)S(1)}, u32[]{:S(2)}, u32[]{:S(2)}) %collective-permute-start.9) | collective-permute-done | bytes 852000 | tf_op jit(solution)/shard_map/ppermute | solution.py:354
  91.5 3.4 %collective-permute-done.13 = f32[2,1,64,640]{3,2,1,0:T(8,128)S(1)} collective-permute-done((f32[2,1,64,640]{3,2,1,0:T(8,128)S(1)}, f32[2,1,64,640]{3,2,1,0:T(8,128)S(1)}, u32[]{:S(2)}, u32[]{:S(2)}) %collective-permute-start.13) | collective-permute-done | bytes 327712 | tf_op jit(solution)/shard_map/ppermute | solution.py:354
  95.0 1.4 collective-permute-start.15
  97.9 6.2 %collective-permute-done.16 = f32[1,1,64,1664]{3,2,1,0:T(8,128)S(1)} collective-permute-done((f32[1,1,64,1664]{3,2,1,0:T(8,128)S(1)}, f32[1,1,64,1664]{3,2,1,0:T(8,128)S(1)}, u32[]{:S(2)}, u32[]{:S(2)}) %collective-permute-start.16) | collective-permute-done | bytes 426016 | tf_op jit(solution)/shard_map/ppermute | solution.py:354
  104.1 1.4 collective-permute-start.23
  105.9 15.1 %collective-permute-done.18 = f32[2,64,640]{2,1,0:T(8,128)S(1)} collective-permute-done((f32[2,64,640]{2,1,0:T(8,128)S(1)}, f32[2,64,640]{2,1,0:T(8,128)S(1)}, u32[]{:S(2)}, u32[]{:S(2)}) %collective-permute-start.18) | collective-permute-done | bytes 327712 | tf_op jit(solution)/shard_map/ppermute | solution.py:354
  124.4 3.3 %collective-permute-done.21 = f32[128,640]{1,0:T(8,128)S(1)} collective-permute-done((f32[128,640]{1,0:T(8,128)S(1)}, f32[128,640]{1,0:T(8,128)S(1)}, u32[]{:S(2)}, u32[]{:S(2)}) %collective-permute-start.21) | collective-permute-done | bytes 327712 | tf_op jit(solution)/shard_map/ppermute | solution.py:354
  127.8 5.6 %collective-permute-done.24 = f32[1,1,64,1024]{3,2,1,0:T(8,128)S(1)} collective-permute-done((f32[1,1,64,1024]{3,2,1,0:T(8,128)S(1)}, f32[1,1,64,1024]{3,2,1,0:T(8,128)S(1)}, u32[]{:S(2)}, u32[]{:S(2)}) %collective-permute-start.24) | collective-permute-done | bytes 262176 | tf_op jit(solution)/shard_map/ppermute | solution.py:354
  136.7 6.4 %collective-permute-done.35 = f32[64,640]{1,0:T(8,128)S(1)} collective-permute-done((f32[64,640]{1,0:T(8,128)S(1)}, f32[64,640]{1,0:T(8,128)S(1)}, u32[]{:S(2)}, u32[]{:S(2)}) %collective-permute-start.35) | collective-permute-done | bytes 163872 | tf_op jit(solution)/shard_map/ppermute | solution.py:354
  143.1 5.3 %collective-permute-start.37 = (f32[128,640]{1,0:T(8,128)S(1)}, f32[128,640]{1,0:T(8,128)S(1)}, u32[]{:S(2)}, u32[]{:S(2)}) collective-permute-start(f32[128,640]{1,0:T(8,128)S(1)} %pad_maximum_fusion.5.refs_0_), channel_id=1, source_target_pairs={{0,4},{4,0},{8,12},{12,8},{16,20},{20,16},{24,28},{28,24},{1,5},{5... | collective-permute-start | bytes 983048 | tf_op jit(solution)/shard_map/ppermute | solution.py:354
  151.9 2.1 %collective-permute-done.29 = f32[64,640]{1,0:T(8,128)S(1)} collective-permute-done((f32[64,640]{1,0:T(8,128)S(1)}, f32[64,640]{1,0:T(8,128)S(1)}, u32[]{:S(2)}, u32[]{:S(2)}) %collective-permute-start.29) | collective-permute-done | bytes 163872 | tf_op jit(solution)/shard_map/ppermute | solution.py:354
  154.8 1.9 %collective-permute-start.31 = (f32[128,640]{1,0:T(8,128)S(1)}, f32[128,640]{1,0:T(8,128)S(1)}, u32[]{:S(2)}, u32[]{:S(2)}) collective-permute-start(f32[128,640]{1,0:T(8,128)S(1)} %constant_dynamic-update-slice_fusion.refs_0_), channel_id=1, source_target_pairs={{0,4},{4,0},{8,12},{12,8},{16,20},{20,16},{24,28},{28,24},{1,5},{5... | collective-permute-start | bytes 983048 | tf_op jit(solution)/shard_map/ppermute | solution.py:354
  158.8 6.4 %collective-permute-done.42 = f32[128,1024]{1,0:T(8,128)S(1)} collective-permute-done((f32[128,1024]{1,0:T(8,128)S(1)}, f32[128,1024]{1,0:T(8,128)S(1)}, u32[]{:S(2)}, u32[]{:S(2)}) %collective-permute-start.42) | collective-permute-done | bytes 524320 | tf_op jit(solution)/shard_map/ppermute | solution.py:354
  169.2 2.6 %shard_map.116 = (f32[128,1024]{1,0:T(8,128)}, f32[8,128]{1,0:T(8,128)S(1)}, bf16[1024,1024]{1,0:T(8,128)(2,1)S(1)}, bf16[1024,1024]{1,0:T(8,128)(2,1)S(1)}) custom-call(s32[2]{0:T(128)S(1)} %pad_add_fusion.place, f32[128,640]{1,0:T(8,128)S(1)} %constant_dynamic-update-slice_fusion.refs_0_, f32[128,640]{1,0:T(8,128)S(1)} %pad_maximum_fusion.6.refs_1_, ...), custom_call_target="tpu_custom_call" | custom-call | tf_op jit(solution)/shard_map/pallas_call | solution.py:321
  172.8 3.7 %shard_map.117 = (f32[128,1024]{1,0:T(8,128)}, f32[128,1024]{1,0:T(8,128)S(1)}) custom-call(s32[2]{0:T(128)S(1)} %pad_add_fusion.place, f32[128,640]{1,0:T(8,128)S(1)} %pad_maximum_fusion.5.refs_0_, f32[128,640]{1,0:T(8,128)S(1)} %pad_maximum_fusion.9.refs_1_, f32[128,640]{1,0:T(8,128)S(1)} %pad_maximum_fusion.10.refs_2_, ...), custom_call_target="tpu_custom_call" | custom-call | tf_op jit(solution)/shard_map/pallas_call | solution.py:321
  180.1 5.7 %shard_map.118 = (f32[128,1024]{1,0:T(8,128)}, f32[128,1024]{1,0:T(8,128)}) custom-call(s32[2]{0:T(128)S(1)} %pad_add_fusion.place, f32[128,1024]{1,0:T(8,128)S(1)} %pad_maximum_fusion.1.refs_0_, f32[128,1024]{1,0:T(8,128)S(1)} %pad_maximum_fusion.2.refs_1_, f32[128,1024]{1,0:T(8,128)S(1)} %pad_maximum_fusion.3.refs_2_, ...), custom_call_target="tpu_custom_call" | custom-call | tf_op jit(solution)/shard_map/pallas_call | solution.py:321
  (141 shorter events, 43.7 us)
Async XLA Ops:
  4.6 25.4 %collective-permute-start = (f32[264,1024]{1,0:T(8,128)S(1)}, f32[264,1024]{1,0:T(8,128)S(1)}, u32[]{:S(2)}, u32[]{:S(2)}) collective-permute-start(f32[264,1024]{1,0:T(8,128)S(1)} %shard_map.111.refs_0_.refs_2_), channel_id=1, source_target_pairs={{0,1},{1,0},{2,3},{3,2},{4,5},{5,4},{6,7},{7,6},{8,9},{9,8},{10,11... | collective-permute-start | bytes 3244040 | tf_op jit(solution)/shard_map/ppermute | solution.py:354
  30.9 25.0 %collective-permute-start.3 = (f32[256,1024]{1,0:T(8,128)}, f32[256,1024]{1,0:T(8,128)S(1)}, u32[]{:S(2)}, u32[]{:S(2)}) collective-permute-start(f32[256,1024]{1,0:T(8,128)} %refs_0_.1), channel_id=1, source_target_pairs={{0,1},{1,0},{2,3},{3,2},{4,5},{5,4},{6,7},{7,6},{8,9},{9,8},{10,11... | collective-permute-start | bytes 3145736 | tf_op jit(solution)/shard_map/ppermute | solution.py:354
  37.0 19.7 %collective-permute-start.5 = (f32[2,2,64,640]{3,2,1,0:T(8,128)S(1)}, f32[2,2,64,640]{3,2,1,0:T(8,128)S(1)}, u32[]{:S(2)}, u32[]{:S(2)}) collective-permute-start(f32[2,2,64,640]{3,2,1,0:T(8,128)S(1)} %get-tuple-element.155), channel_id=1, source_target_pairs={{0,8},{4,12},{8,0},{12,4},{16,24},{20,28},{24,16},{28,20},{1,9},{5... | collective-permute-start | bytes 1966088 | tf_op jit(solution)/shard_map/ppermute | solution.py:354
  38.3 18.5 %collective-permute-start.6 = (f32[2,2,64,640]{3,2,1,0:T(8,128)S(1)}, f32[2,2,64,640]{3,2,1,0:T(8,128)S(1)}, u32[]{:S(2)}, u32[]{:S(2)}) collective-permute-start(f32[2,2,64,640]{3,2,1,0:T(8,128)S(1)} %get-tuple-element.157), channel_id=1, source_target_pairs={{0,16},{4,20},{8,24},{12,28},{16,0},{20,4},{24,8},{28,12},{1,17},{... | collective-permute-start | bytes 1966088 | tf_op jit(solution)/shard_map/ppermute | solution.py:354
  56.9 11.8 %collective-permute-start.11 = (f32[1,2,64,640]{3,2,1,0:T(8,128)S(1)}, f32[1,2,64,640]{3,2,1,0:T(8,128)S(1)}, u32[]{:S(2)}, u32[]{:S(2)}) collective-permute-start(f32[1,2,64,640]{3,2,1,0:T(8,128)S(1)} %get-tuple-element.196), channel_id=1, source_target_pairs={{0,8},{4,12},{8,0},{12,4},{16,24},{20,28},{24,16},{28,20},{1,9},{5... | collective-permute-start | bytes 983048 | tf_op jit(solution)/shard_map/ppermute | solution.py:354
  66.6 20.0 %collective-permute-start.9 = (f32[2,1,64,1664]{3,2,1,0:T(8,128)S(1)}, f32[2,1,64,1664]{3,2,1,0:T(8,128)S(1)}, u32[]{:S(2)}, u32[]{:S(2)}) collective-permute-start(f32[2,1,64,1664]{3,2,1,0:T(8,128)S(1)} %get-tuple-element.190), channel_id=1, source_target_pairs={{0,8},{4,12},{8,0},{12,4},{16,24},{20,28},{24,16},{28,20},{1,9},{5... | collective-permute-start | bytes 2555912 | tf_op jit(solution)/shard_map/ppermute | solution.py:354
  67.5 19.8 %collective-permute-start.10 = (f32[2,1,64,1664]{3,2,1,0:T(8,128)S(1)}, f32[2,1,64,1664]{3,2,1,0:T(8,128)S(1)}, u32[]{:S(2)}, u32[]{:S(2)}) collective-permute-start(f32[2,1,64,1664]{3,2,1,0:T(8,128)S(1)} %get-tuple-element.191), channel_id=1, source_target_pairs={{0,16},{4,20},{8,24},{12,28},{16,0},{20,4},{24,8},{28,12},{1,17},{... | collective-permute-start | bytes 2555912 | tf_op jit(solution)/shard_map/ppermute | solution.py:354
  68.9 20.1 %collective-permute-start.12 = (f32[2,64,640]{2,1,0:T(8,128)S(1)}, f32[2,64,640]{2,1,0:T(8,128)S(1)}, u32[]{:S(2)}, u32[]{:S(2)}) collective-permute-start(f32[2,64,640]{2,1,0:T(8,128)S(1)} %maximum_bitcast_fusion), channel_id=1, source_target_pairs={{0,2},{1,3},{2,0},{3,1},{4,6},{5,7},{6,4},{7,5},{8,10},{9,11},{10,... | collective-permute-start | bytes 983048 | tf_op jit(solution)/shard_map/ppermute | solution.py:354
  89.5 14.6 %collective-permute-start.16 = (f32[1,1,64,1664]{3,2,1,0:T(8,128)S(1)}, f32[1,1,64,1664]{3,2,1,0:T(8,128)S(1)}, u32[]{:S(2)}, u32[]{:S(2)}) collective-permute-start(f32[1,1,64,1664]{3,2,1,0:T(8,128)S(1)} %slice_add_fusion.1), channel_id=1, source_target_pairs={{0,16},{4,20},{8,24},{12,28},{16,0},{20,4},{24,8},{28,12},{1,17},{... | collective-permute-start | bytes 1277960 | tf_op jit(solution)/shard_map/ppermute | solution.py:354
  89.9 15.7 %collective-permute-start.17 = (f32[1,1,64,1664]{3,2,1,0:T(8,128)S(1)}, f32[1,1,64,1664]{3,2,1,0:T(8,128)S(1)}, u32[]{:S(2)}, u32[]{:S(2)}) collective-permute-start(f32[1,1,64,1664]{3,2,1,0:T(8,128)S(1)} %slice_add_fusion), channel_id=1, source_target_pairs={{0,8},{4,12},{8,0},{12,4},{16,24},{20,28},{24,16},{28,20},{1,9},{5... | collective-permute-start | bytes 1277960 | tf_op jit(solution)/shard_map/ppermute | solution.py:354
  95.0 26.0 %collective-permute-start.15 = (f32[1,1,64,640]{3,2,1,0:T(8,128)S(1)}, f32[1,1,64,640]{3,2,1,0:T(8,128)S(1)}, u32[]{:S(2)}, u32[]{:S(2)}) collective-permute-start(f32[1,1,64,640]{3,2,1,0:T(8,128)S(1)} %slice_add_fusion.12), channel_id=1, source_target_pairs={{0,16},{4,20},{8,24},{12,28},{16,0},{20,4},{24,8},{28,12},{1,17},{... | collective-permute-start | bytes 491528 | tf_op jit(solution)/shard_map/ppermute | solution.py:354
  96.4 24.6 %collective-permute-start.19 = (f32[1,1,64,640]{3,2,1,0:T(8,128)S(1)}, f32[1,1,64,640]{3,2,1,0:T(8,128)S(1)}, u32[]{:S(2)}, u32[]{:S(2)}) collective-permute-start(f32[1,1,64,640]{3,2,1,0:T(8,128)S(1)} %slice_add_fusion.11), channel_id=1, source_target_pairs={{0,8},{4,12},{8,0},{12,4},{16,24},{20,28},{24,16},{28,20},{1,9},{5... | collective-permute-start | bytes 491528 | tf_op jit(solution)/shard_map/ppermute | solution.py:354
  97.5 24.9 %collective-permute-start.22 = (f32[2,1,64,1024]{3,2,1,0:T(8,128)S(1)}, f32[2,1,64,1024]{3,2,1,0:T(8,128)S(1)}, u32[]{:S(2)}, u32[]{:S(2)}) collective-permute-start(f32[2,1,64,1024]{3,2,1,0:T(8,128)S(1)} %get-tuple-element.213), channel_id=1, source_target_pairs={{0,8},{4,12},{8,0},{12,4},{16,24},{20,28},{24,16},{28,20},{1,9},{5... | collective-permute-start | bytes 1572872 | tf_op jit(solution)/shard_map/ppermute | solution.py:354
  104.1 18.4 %collective-permute-start.23 = (f32[2,1,64,1024]{3,2,1,0:T(8,128)S(1)}, f32[2,1,64,1024]{3,2,1,0:T(8,128)S(1)}, u32[]{:S(2)}, u32[]{:S(2)}) collective-permute-start(f32[2,1,64,1024]{3,2,1,0:T(8,128)S(1)} %get-tuple-element.215), channel_id=1, source_target_pairs={{0,16},{4,20},{8,24},{12,28},{16,0},{20,4},{24,8},{28,12},{1,17},{... | collective-permute-start | bytes 1572872 | tf_op jit(solution)/shard_map/ppermute | solution.py:354
  105.7 15.3 %collective-permute-start.18 = (f32[2,64,640]{2,1,0:T(8,128)S(1)}, f32[2,64,640]{2,1,0:T(8,128)S(1)}, u32[]{:S(2)}, u32[]{:S(2)}) collective-permute-start(f32[2,64,640]{2,1,0:T(8,128)S(1)} %maximum_bitcast_fusion.1), channel_id=1, source_target_pairs={{0,2},{1,3},{2,0},{3,1},{4,6},{5,7},{6,4},{7,5},{8,10},{9,11},{10,... | collective-permute-start | bytes 983048 | tf_op jit(solution)/shard_map/ppermute | solution.py:354
  124.4 24.0 %collective-permute-start.26 = (f32[2,64,1024]{2,1,0:T(8,128)S(1)}, f32[2,64,1024]{2,1,0:T(8,128)S(1)}, u32[]{:S(2)}, u32[]{:S(2)}) collective-permute-start(f32[2,64,1024]{2,1,0:T(8,128)S(1)} %bitcast.94), channel_id=1, source_target_pairs={{0,2},{1,3},{2,0},{3,1},{4,6},{5,7},{6,4},{7,5},{8,10},{9,11},{10,... | collective-permute-start | bytes 1572872 | tf_op jit(solution)/shard_map/ppermute | solution.py:354
  133.4 15.0 %collective-permute-start.28 = (f32[128,640]{1,0:T(8,128)S(1)}, f32[128,640]{1,0:T(8,128)S(1)}, u32[]{:S(2)}, u32[]{:S(2)}) collective-permute-start(f32[128,640]{1,0:T(8,128)S(1)} %constant_dynamic-update-slice_fusion.refs_0_), channel_id=1, source_target_pairs={{0,16},{4,20},{8,24},{12,28},{16,0},{20,4},{24,8},{28,12},{1,17},{... | collective-permute-start | bytes 983048 | tf_op jit(solution)/shard_map/ppermute | solution.py:354
  134.7 13.7 %collective-permute-start.27 = (f32[128,640]{1,0:T(8,128)S(1)}, f32[128,640]{1,0:T(8,128)S(1)}, u32[]{:S(2)}, u32[]{:S(2)}) collective-permute-start(f32[128,640]{1,0:T(8,128)S(1)} %constant_dynamic-update-slice_fusion.refs_0_), channel_id=1, source_target_pairs={{0,8},{4,12},{8,0},{12,4},{16,24},{20,28},{24,16},{28,20},{1,9},{5... | collective-permute-start | bytes 983048 | tf_op jit(solution)/shard_map/ppermute | solution.py:354
  143.1 13.7 %collective-permute-start.37 = (f32[128,640]{1,0:T(8,128)S(1)}, f32[128,640]{1,0:T(8,128)S(1)}, u32[]{:S(2)}, u32[]{:S(2)}) collective-permute-start(f32[128,640]{1,0:T(8,128)S(1)} %pad_maximum_fusion.5.refs_0_), channel_id=1, source_target_pairs={{0,4},{4,0},{8,12},{12,8},{16,20},{20,16},{24,28},{28,24},{1,5},{5... | collective-permute-start | bytes 983048 | tf_op jit(solution)/shard_map/ppermute | solution.py:354
  150.5 14.7 %collective-permute-start.42 = (f32[128,1024]{1,0:T(8,128)S(1)}, f32[128,1024]{1,0:T(8,128)S(1)}, u32[]{:S(2)}, u32[]{:S(2)}) collective-permute-start(f32[128,1024]{1,0:T(8,128)S(1)} %pad_maximum_fusion.1.refs_0_), channel_id=1, source_target_pairs={{0,16},{4,20},{8,24},{12,28},{16,0},{20,4},{24,8},{28,12},{1,17},{... | collective-permute-start | bytes 1572872 | tf_op jit(solution)/shard_map/ppermute | solution.py:354
  151.2 15.2 %collective-permute-start.41 = (f32[128,1024]{1,0:T(8,128)S(1)}, f32[128,1024]{1,0:T(8,128)S(1)}, u32[]{:S(2)}, u32[]{:S(2)}) collective-permute-start(f32[128,1024]{1,0:T(8,128)S(1)} %pad_maximum_fusion.1.refs_0_), channel_id=1, source_target_pairs={{0,8},{4,12},{8,0},{12,4},{16,24},{20,28},{24,16},{28,20},{1,9},{5... | collective-permute-start | bytes 1572872 | tf_op jit(solution)/shard_map/ppermute | solution.py:354
  156.8 15.0 %collective-permute-start.38 = (f32[128,640]{1,0:T(8,128)S(1)}, f32[128,640]{1,0:T(8,128)S(1)}, u32[]{:S(2)}, u32[]{:S(2)}) collective-permute-start(f32[128,640]{1,0:T(8,128)S(1)} %pad_maximum_fusion.9.refs_1_), channel_id=1, source_target_pairs={{0,4},{4,0},{8,12},{12,8},{16,20},{20,16},{24,28},{28,24},{1,5},{5... | collective-permute-start | bytes 983048 | tf_op jit(solution)/shard_map/ppermute | solution.py:354
  158.0 14.8 %collective-permute-start.39 = (f32[128,640]{1,0:T(8,128)S(1)}, f32[128,640]{1,0:T(8,128)S(1)}, u32[]{:S(2)}, u32[]{:S(2)}) collective-permute-start(f32[128,640]{1,0:T(8,128)S(1)} %pad_maximum_fusion.10.refs_2_), channel_id=1, source_target_pairs={{0,4},{4,0},{8,12},{12,8},{16,20},{20,16},{24,28},{28,24},{1,5},{5... | collective-permute-start | bytes 983048 | tf_op jit(solution)/shard_map/ppermute | solution.py:354
  158.4 14.4 %collective-permute-start.40 = (f32[128,640]{1,0:T(8,128)S(1)}, f32[128,640]{1,0:T(8,128)S(1)}, u32[]{:S(2)}, u32[]{:S(2)}) collective-permute-start(f32[128,640]{1,0:T(8,128)S(1)} %pad_maximum_fusion.11.refs_3_), channel_id=1, source_target_pairs={{0,4},{4,0},{8,12},{12,8},{16,20},{20,16},{24,28},{28,24},{1,5},{5... | collective-permute-start | bytes 983048 | tf_op jit(solution)/shard_map/ppermute | solution.py:354
  (30 other events, 155.2 us)

commit v8 on v7

--- a/solution.py
+++ b/solution.py
@@ -101,11 +101,19 @@
     outs[output][position, number, :, columns] = value
 
 
-def prepare_kernel(routes, counts, acts, out):
+def prepare_kernel(routes_ref, counts_ref, acts, out, routes, counts, sems):
     samples, feat = acts.shape
     experts = counts.shape[1]
-    out[0:samples, :] = acts[...]
+    copies = [
+        pltpu.make_async_copy(routes_ref, routes, sems.at[0]),
+        pltpu.make_async_copy(counts_ref, counts, sems.at[1]),
+        pltpu.make_async_copy(acts, out.at[pl.ds(0, samples), :], sems.at[2]),
+    ]
+    for copy in copies:
+        copy.start()
     out[samples:, :] = jnp.zeros((out.shape[0] - samples, feat), F32)
+    for copy in copies[:2]:
+        copy.wait()
     hits = []
     for expert in range(experts):
         same = [jnp.where(routes[k : k + 1, :] == expert, 1.0, 0.0) for k in range(routes.shape[0])]
@@ -120,6 +128,7 @@
         keep = jnp.where(rank[expert : expert + 1, :] < limit, hits[expert], 0.0)
         row, column = samples + expert // per_row, expert % per_row * samples
         out[row : row + 1, column : column + samples] = keep
+    copies[2].wait()
 
 
 def act_kernel(turns, block, chips, seeded, samples, place, *refs):
@@ -186,12 +195,13 @@
     return pl.pallas_call(
         prepare_kernel,
         out_shape=jax.ShapeDtypeStruct((rows, feat), F32),
-        in_specs=[
-            pl.BlockSpec(memory_space=pltpu.VMEM),
-            pl.BlockSpec(memory_space=pltpu.SMEM),
-            pl.BlockSpec(memory_space=pltpu.VMEM),
+        in_specs=[pl.BlockSpec(memory_space=pltpu.HBM)] * 3,
+        out_specs=pl.BlockSpec(memory_space=pltpu.VMEM),
+        scratch_shapes=[
+            pltpu.VMEM(routes.shape[::-1], jnp.int32),
+            pltpu.SMEM(counts.shape, jnp.int32),
+            pltpu.SemaphoreType.DMA((3,)),
         ],
-        out_specs=pl.BlockSpec(memory_space=pltpu.VMEM),
         compiler_params=pltpu.CompilerParams(vmem_limit_bytes=16 * MIB),
     )(routes.T, counts, acts)
 
@@ -258,9 +268,11 @@
     return offsets
 
 
-def row_pieces(place, block, blocks):
+def row_pieces(place, block, chips, arrays):
     step = block // 2
-    chips = len(blocks) // 2
+    blocks = [
+        value[first : first + block, :] for value in arrays for first in range(0, value.shape[0], block)
+    ]
     pieces = []
     for number, value in enumerate(blocks):
         core, position = number // chips, number % chips
@@ -272,7 +284,7 @@
 
 
 def factor_rows(place, block, blocks, bands, full):
-    for here, value in row_pieces(place, block, blocks):
+    for here, value in row_pieces(place, block, bands.shape[0] // (2 * block), blocks):
         bands[here, :] = value
     unfold(bands, full)
     return full[pl.ds(pl.multiple_of(place[0] * block, block), block), :]
@@ -305,7 +317,8 @@
 def update_kernel(place, *refs):
     blocks = refs[:-9]
     inverse, scales, act_high, act_low, momentum, weights, moment_out, weight_out, full = refs[-9:]
-    for here, value in row_pieces(place, momentum.shape[0], blocks):
+    block = momentum.shape[0]
+    for here, value in row_pieces(place, block, full.shape[0] // (2 * block), blocks):
         full[here, :] = value
     damp, alpha = scales[0:1, 0:1], scales[1:2, 0:1]
     half_way = times(inverse[...], *split(full[...]))
@@ -409,13 +422,10 @@
                 held += [own] + came
             self.held.append(held)
 
-    def finish(self, *before):
-        mine = [jnp.concatenate(pair, axis=0) for pair in zip(*self.held)]
-        if before:
-            mine[-1], before = together(mine[-1], before)
-        else:
-            mine = list(together(*mine))
-        return mine + [swap(value, "dp", 1) for value in mine]
+    def exchange(self, first=0, last=None):
+        pairs = list(zip(*self.held))[first:last]
+        mine = jnp.concatenate([value for pair in pairs for value in pair], axis=0)
+        return mine, swap(mine, "dp", 1)
 
 
 def together(*values):
@@ -508,16 +518,19 @@
     mixed_sums = mixed_sum.finish()
     act_gather = Gather(act_halves, chips)
     act_gather.begin()
-    across_mixed, act_gather.whole = together(across_mixed, act_gather.whole)
+    grad_gather.relay()
     act_gather.relay()
-    grad_gather.relay()
-    act_out, *act_square = act_factor_rows(place, act_gather.finish(), block, feat)
+    across_mixed, _ = together(across_mixed, act_gather.whole)
+    act_out, *act_square = act_factor_rows(place, act_gather.exchange(), block, feat)
     mixed_gather = Gather(both(mixed_sums, across_mixed), chips)
     mixed_gather.begin()
+    grad_blocks, act_square = together(grad_gather.exchange(), act_square)
+    grad_out, inverse = grad_factor_rows(place, grad_blocks, block, feat)
+    mixed_gather.whole, inverse = together(mixed_gather.whole, inverse)
     mixed_gather.relay()
-    grad_blocks, act_square = together(grad_gather.finish(), act_square)
-    grad_out, inverse = grad_factor_rows(place, grad_blocks, block, feat)
-    mixed_blocks = mixed_gather.finish(inverse)
+    mine, theirs = mixed_gather.exchange(0, -1)
+    my_last, their_last = mixed_gather.exchange(-1)
+    mixed_blocks = (mine, my_last, theirs, their_last)
     outs = update_rows(place, mixed_blocks, inverse, *act_square, momentum[0], weights[0])
     return tuple(out[None] for out in (act_out, grad_out, *outs))
 

time: 188 us -> 190 us (1.011)
  waiting for transfers between devices: 99.6 us -> 106 us
  starting transfers between devices: 40.7 us -> 37.4 us
    ppermute x49 -> x41, waiting for transfers between devices: 99.6 us -> 106 us  [swap(): return lax.ppermute(value, axis, [(i, i ^ step) for i in range(size)])]
    ppermute x49 -> x41, starting transfers between devices: 40.7 us -> 37.4 us  [swap(): return lax.ppermute(value, axis, [(i, i ^ step) for i in range(size)])]
  transfers between devices with their start and end apart: 49 -> 41, of which waited for: 20 -> 18; matrix products, arithmetic and copies ran while one was open for 3% -> 3% of each run, Pallas kernels for 16% -> 15%
where the time goes in v8:
time: 190 us; the launch traced here: 189 us
  waiting for transfers between devices  106 us (56%)
  starting transfers between devices  37.4 us (20%)
  Pallas kernels  35.1 us (18%)
  local copies, waits for them, and re-layouts  6.21 us (3%)
  other arithmetic  2.27 us (1%)
    ppermute x41, waiting for transfers between devices, swap(): return lax.ppermute(value, axis, [(i, i ^ step) for i in range(size)])  106 us
    ppermute x41, starting transfers between devices, swap(): return lax.ppermute(value, axis, [(i, i ^ step) for i in range(size)])  37.4 us
    pallas_call x4, Pallas kernels, bands(): pl.pallas_call(functools.partial(body, range(turns), block, chips, bool(s...  22.6 us
    pallas_call x3, Pallas kernels, on_core(): pl.pallas_call(body, out_shape=shapes, in_specs=[pl.BlockSpec(memory_spac...  11.8 us
  transfers between devices with their start and end apart: 41, of which 18 were waited for; matrix products, arithmetic and copies ran while one was open for 3% of the time, Pallas kernels for 15%

profile of v8, /device:TPU:25, one launch (start us, length us, event | category | flops | bytes accessed | tf_op | source)
XLA Modules:
  0.0 188.6 jit_solution(7139859373345971674)
XLA Ops:
  6.2 1.7 slice.261
  9.1 3.7 %shard_map.112 = (f32[2,2,64,640]{3,2,1,0:T(8,128)S(1)}, f32[2,2,64,640]{3,2,1,0:T(8,128)S(1)}, f32[2,2,64,640]{3,2,1,0:T(8,128)S(1)}, f32[2,2,64,640]{3,2,1,0:T(8,128)S(1)}) custom-call(s32[2]{0:T(128)S(1)} %pad_add_fusion.place, f32[264,1024]{1,0:T(8,128)S(1)} %shard_map.111.refs_0_.refs_2_, f32[264,1024]{1,0:T(8,128)S(1)} %collective-permute-done.1.refs_1_.refs_3_), custom_call_target="tpu_custom_call" | custom-call | tf_op jit(solution)/shard_map/pallas_call | solution.py:222
  12.8 7.9 %shard_map.113 = (f32[2,1,64,640]{3,2,1,0:T(8,128)S(1)}, f32[2,1,64,640]{3,2,1,0:T(8,128)S(1)}, f32[2,1,64,640]{3,2,1,0:T(8,128)S(1)}, f32[2,1,64,640]{3,2,1,0:T...) custom-call(s32[2]{0:T(128)S(1)} %pad_add_fusion.place, ...), custom_call_target="tpu_custom_call" | custom-call | tf_op jit(solution)/shard_map/pallas_call | solution.py:222
  20.8 9.4 %collective-permute-done.refs_0_.refs_2_ = f32[264,1024]{1,0:T(8,128)S(1)} collective-permute-done((f32[264,1024]{1,0:T(8,128)S(1)}, f32[264,1024]{1,0:T(8,128)S(1)}, u32[]{:S(2)}, u32[]{:S(2)}) %collective-permute-start) | collective-permute-done | bytes 1081376 | tf_op jit(solution)/shard_map/ppermute | solution.py:367
  31.1 2.2 %collective-permute-done.4.refs_1_.refs_3_ = f32[264,1024]{1,0:T(8,128)S(1)} collective-permute-done((f32[264,1024]{1,0:T(8,128)S(1)}, f32[264,1024]{1,0:T(8,128)S(1)}, u32[]{:S(2)}, u32[]{:S(2)}) %collective-permute-start.4) | collective-permute-done | bytes 1081376 | tf_op jit(solution)/shard_map/ppermute | solution.py:367
  33.3 3.8 %shard_map.114 = (f32[2,2,64,640]{3,2,1,0:T(8,128)S(1)}, f32[2,2,64,640]{3,2,1,0:T(8,128)S(1)}, f32[2,2,64,640]{3,2,1,0:T(8,128)S(1)}, f32[2,2,64,640]{3,2,1,0:T(8,128)S(1)}) custom-call(s32[2]{0:T(128)S(1)} %pad_add_fusion.place, f32[264,1024]{1,0:T(8,128)S(1)} %collective-permute-done.refs_0_.refs_2_, ...), custom_call_target="tpu_custom_call" | custom-call | tf_op jit(solution)/shard_map/pallas_call | solution.py:222
  39.6 16.4 %collective-permute-done.3.refs_0_ = f32[256,1024]{1,0:T(8,128)S(1)} collective-permute-done((f32[256,1024]{1,0:T(8,128)}, f32[256,1024]{1,0:T(8,128)S(1)}, u32[]{:S(2)}, u32[]{:S(2)}) %collective-permute-start.3) | collective-permute-done | bytes 1048608 | tf_op jit(solution)/shard_map/ppermute | solution.py:367
  59.4 7.2 %shard_map.115 = (f32[2,1,64,640]{3,2,1,0:T(8,128)S(1)}, f32[2,1,64,640]{3,2,1,0:T(8,128)S(1)}, f32[2,1,64,640]{3,2,1,0:T(8,128)S(1)}, f32[2,1,64,640]{3,2,1,0:T...) custom-call(s32[2]{0:T(128)S(1)} %pad_add_fusion.place, ...), custom_call_target="tpu_custom_call" | custom-call | tf_op jit(solution)/shard_map/pallas_call | solution.py:222
  69.1 17.6 %collective-permute-done.9 = f32[2,1,64,1664]{3,2,1,0:T(8,128)S(1)} collective-permute-done((f32[2,1,64,1664]{3,2,1,0:T(8,128)S(1)}, f32[2,1,64,1664]{3,2,1,0:T(8,128)S(1)}, u32[]{:S(2)}, u32[]{:S(2)}) %collective-permute-start.9) | collective-permute-done | bytes 852000 | tf_op jit(solution)/shard_map/ppermute | solution.py:367
  91.6 3.5 %collective-permute-done.13 = f32[2,1,64,640]{3,2,1,0:T(8,128)S(1)} collective-permute-done((f32[2,1,64,640]{3,2,1,0:T(8,128)S(1)}, f32[2,1,64,640]{3,2,1,0:T(8,128)S(1)}, u32[]{:S(2)}, u32[]{:S(2)}) %collective-permute-start.13) | collective-permute-done | bytes 327712 | tf_op jit(solution)/shard_map/ppermute | solution.py:367
  98.0 6.2 %collective-permute-done.16 = f32[1,1,64,1664]{3,2,1,0:T(8,128)S(1)} collective-permute-done((f32[1,1,64,1664]{3,2,1,0:T(8,128)S(1)}, f32[1,1,64,1664]{3,2,1,0:T(8,128)S(1)}, u32[]{:S(2)}, u32[]{:S(2)}) %collective-permute-start.16) | collective-permute-done | bytes 426016 | tf_op jit(solution)/shard_map/ppermute | solution.py:367
  106.0 15.1 %collective-permute-done.18 = f32[2,64,640]{2,1,0:T(8,128)S(1)} collective-permute-done((f32[2,64,640]{2,1,0:T(8,128)S(1)}, f32[2,64,640]{2,1,0:T(8,128)S(1)}, u32[]{:S(2)}, u32[]{:S(2)}) %collective-permute-start.18) | collective-permute-done | bytes 327712 | tf_op jit(solution)/shard_map/ppermute | solution.py:367
  124.6 3.3 %collective-permute-done.21 = f32[128,640]{1,0:T(8,128)S(1)} collective-permute-done((f32[128,640]{1,0:T(8,128)S(1)}, f32[128,640]{1,0:T(8,128)S(1)}, u32[]{:S(2)}, u32[]{:S(2)}) %collective-permute-start.21) | collective-permute-done | bytes 327712 | tf_op jit(solution)/shard_map/ppermute | solution.py:367
  127.9 5.6 %collective-permute-done.24 = f32[1,1,64,1024]{3,2,1,0:T(8,128)S(1)} collective-permute-done((f32[1,1,64,1024]{3,2,1,0:T(8,128)S(1)}, f32[1,1,64,1024]{3,2,1,0:T(8,128)S(1)}, u32[]{:S(2)}, u32[]{:S(2)}) %collective-permute-start.24) | collective-permute-done | bytes 262176 | tf_op jit(solution)/shard_map/ppermute | solution.py:367
  136.8 6.4 %collective-permute-done.31 = f32[64,640]{1,0:T(8,128)S(1)} collective-permute-done((f32[64,640]{1,0:T(8,128)S(1)}, f32[64,640]{1,0:T(8,128)S(1)}, u32[]{:S(2)}, u32[]{:S(2)}) %collective-permute-start.31) | collective-permute-done | bytes 163872 | tf_op jit(solution)/shard_map/ppermute | solution.py:367
  144.3 4.7 %collective-permute-done.28 = f32[64,640]{1,0:T(8,128)S(1)} collective-permute-done((f32[64,640]{1,0:T(8,128)S(1)}, f32[64,640]{1,0:T(8,128)S(1)}, u32[]{:S(2)}, u32[]{:S(2)}) %collective-permute-start.28) | collective-permute-done | bytes 163872 | tf_op jit(solution)/shard_map/ppermute | solution.py:367
  149.8 6.3 %collective-permute-start.30 = (f32[512,640]{1,0:T(8,128)S(1)}, f32[512,640]{1,0:T(8,128)S(1)}, u32[]{:S(2)}, u32[]{:S(2)}) collective-permute-start(f32[512,640]{1,0:T(8,128)S(1)} %constant_dynamic-update-slice_fusion.2.refs_0_), channel_id=1, source_target_pairs={{0,4},{4,0},{8,12},{12,8},{16,20},{20,16},{24,28},{28,24},{1,5},{5... | collective-permute-start | bytes 3932168 | tf_op jit(solution)/shard_map/ppermute | solution.py:367
  158.8 2.6 %shard_map.116 = (f32[128,1024]{1,0:T(8,128)}, f32[8,128]{1,0:T(8,128)S(1)}, bf16[1024,1024]{1,0:T(8,128)(2,1)S(1)}, bf16[1024,1024]{1,0:T(8,128)(2,1)S(1)}) custom-call(s32[2]{0:T(128)S(1)} %pad_add_fusion.place, f32[512,640]{1,0:T(8,128)S(1)} %constant_dynamic-update-slice_fusion.2.refs_0_, f32[512,640]{1,0:T(8,128)S(1)} %collective-permute-done.30.refs_1_), custom_call_target="tpu_custom_call" | custom-call | tf_op jit(solution)/shard_map/pallas_call | solution.py:334
  161.4 3.5 %shard_map.117 = (f32[128,1024]{1,0:T(8,128)}, f32[128,1024]{1,0:T(8,128)S(1)}) custom-call(s32[2]{0:T(128)S(1)} %pad_add_fusion.place, f32[512,640]{1,0:T(8,128)S(1)} %constant_dynamic-update-slice_fusion.8.refs_0_, f32[512,640]{1,0:T(8,128)S(1)} %collective-permute-done.33.refs_1_), custom_call_target="tpu_custom_call" | custom-call | tf_op jit(solution)/shard_map/pallas_call | solution.py:334
  164.8 4.7 %collective-permute-done.36 = f32[128,1024]{1,0:T(8,128)S(1)} collective-permute-done((f32[128,1024]{1,0:T(8,128)S(1)}, f32[128,1024]{1,0:T(8,128)S(1)}, u32[]{:S(2)}, u32[]{:S(2)}) %collective-permute-start.36) | collective-permute-done | bytes 524320 | tf_op jit(solution)/shard_map/ppermute | solution.py:367
  169.7 1.5 collective-permute-start.39
  173.4 5.7 %collective-permute-done.37 = f32[64,1024]{1,0:T(8,128)S(1)} collective-permute-done((f32[64,1024]{1,0:T(8,128)S(1)}, f32[64,1024]{1,0:T(8,128)S(1)}, u32[]{:S(2)}, u32[]{:S(2)}) %collective-permute-start.37) | collective-permute-done | bytes 262176 | tf_op jit(solution)/shard_map/ppermute | solution.py:367
  181.4 1.5 collective-permute-done.40.refs_3_
  182.9 5.7 %shard_map.118 = (f32[128,1024]{1,0:T(8,128)}, f32[128,1024]{1,0:T(8,128)}) custom-call(s32[2]{0:T(128)S(1)} %pad_add_fusion.place, f32[384,1024]{1,0:T(8,128)S(1)} %slice_dynamic-update-slice_fusion.refs_0_, f32[128,1024]{1,0:T(8,128)S(1)} %constant_dynamic-update-slice_fusion.18.refs_1_, f32[384,1024]{1,0:T(8,128)S(1)} %collective-permute-done.39.refs_2_, ...), custom_call_target="tpu_custom_call" | custom-call | tf_op jit(solution)/shard_map/pallas_call | solution.py:334
  (130 shorter events, 40.9 us)
Async XLA Ops:
  4.7 25.4 %collective-permute-start = (f32[264,1024]{1,0:T(8,128)S(1)}, f32[264,1024]{1,0:T(8,128)S(1)}, u32[]{:S(2)}, u32[]{:S(2)}) collective-permute-start(f32[264,1024]{1,0:T(8,128)S(1)} %shard_map.111.refs_0_.refs_2_), channel_id=1, source_target_pairs={{0,1},{1,0},{2,3},{3,2},{4,5},{5,4},{6,7},{7,6},{8,9},{9,8},{10,11... | collective-permute-start | bytes 3244040 | tf_op jit(solution)/shard_map/ppermute | solution.py:367
  31.0 25.0 %collective-permute-start.3 = (f32[256,1024]{1,0:T(8,128)}, f32[256,1024]{1,0:T(8,128)S(1)}, u32[]{:S(2)}, u32[]{:S(2)}) collective-permute-start(f32[256,1024]{1,0:T(8,128)} %refs_0_.1), channel_id=1, source_target_pairs={{0,1},{1,0},{2,3},{3,2},{4,5},{5,4},{6,7},{7,6},{8,9},{9,8},{10,11... | collective-permute-start | bytes 3145736 | tf_op jit(solution)/shard_map/ppermute | solution.py:367
  37.1 19.7 %collective-permute-start.5 = (f32[2,2,64,640]{3,2,1,0:T(8,128)S(1)}, f32[2,2,64,640]{3,2,1,0:T(8,128)S(1)}, u32[]{:S(2)}, u32[]{:S(2)}) collective-permute-start(f32[2,2,64,640]{3,2,1,0:T(8,128)S(1)} %get-tuple-element.141), channel_id=1, source_target_pairs={{0,8},{4,12},{8,0},{12,4},{16,24},{20,28},{24,16},{28,20},{1,9},{5... | collective-permute-start | bytes 1966088 | tf_op jit(solution)/shard_map/ppermute | solution.py:367
  38.3 18.5 %collective-permute-start.6 = (f32[2,2,64,640]{3,2,1,0:T(8,128)S(1)}, f32[2,2,64,640]{3,2,1,0:T(8,128)S(1)}, u32[]{:S(2)}, u32[]{:S(2)}) collective-permute-start(f32[2,2,64,640]{3,2,1,0:T(8,128)S(1)} %get-tuple-element.143), channel_id=1, source_target_pairs={{0,16},{4,20},{8,24},{12,28},{16,0},{20,4},{24,8},{28,12},{1,17},{... | collective-permute-start | bytes 1966088 | tf_op jit(solution)/shard_map/ppermute | solution.py:367
  56.9 11.9 %collective-permute-start.11 = (f32[1,2,64,640]{3,2,1,0:T(8,128)S(1)}, f32[1,2,64,640]{3,2,1,0:T(8,128)S(1)}, u32[]{:S(2)}, u32[]{:S(2)}) collective-permute-start(f32[1,2,64,640]{3,2,1,0:T(8,128)S(1)} %get-tuple-element.182), channel_id=1, source_target_pairs={{0,8},{4,12},{8,0},{12,4},{16,24},{20,28},{24,16},{28,20},{1,9},{5... | collective-permute-start | bytes 983048 | tf_op jit(solution)/shard_map/ppermute | solution.py:367
  58.2 10.7 %collective-permute-start.8 = (f32[1,2,64,640]{3,2,1,0:T(8,128)S(1)}, f32[1,2,64,640]{3,2,1,0:T(8,128)S(1)}, u32[]{:S(2)}, u32[]{:S(2)}) collective-permute-start(f32[1,2,64,640]{3,2,1,0:T(8,128)S(1)} %get-tuple-element.172), channel_id=1, source_target_pairs={{0,16},{4,20},{8,24},{12,28},{16,0},{20,4},{24,8},{28,12},{1,17},{... | collective-permute-start | bytes 983048 | tf_op jit(solution)/shard_map/ppermute | solution.py:367
  66.6 20.0 %collective-permute-start.9 = (f32[2,1,64,1664]{3,2,1,0:T(8,128)S(1)}, f32[2,1,64,1664]{3,2,1,0:T(8,128)S(1)}, u32[]{:S(2)}, u32[]{:S(2)}) collective-permute-start(f32[2,1,64,1664]{3,2,1,0:T(8,128)S(1)} %get-tuple-element.176), channel_id=1, source_target_pairs={{0,8},{4,12},{8,0},{12,4},{16,24},{20,28},{24,16},{28,20},{1,9},{5... | collective-permute-start | bytes 2555912 | tf_op jit(solution)/shard_map/ppermute | solution.py:367
  67.5 19.9 %collective-permute-start.10 = (f32[2,1,64,1664]{3,2,1,0:T(8,128)S(1)}, f32[2,1,64,1664]{3,2,1,0:T(8,128)S(1)}, u32[]{:S(2)}, u32[]{:S(2)}) collective-permute-start(f32[2,1,64,1664]{3,2,1,0:T(8,128)S(1)} %get-tuple-element.177), channel_id=1, source_target_pairs={{0,16},{4,20},{8,24},{12,28},{16,0},{20,4},{24,8},{28,12},{1,17},{... | collective-permute-start | bytes 2555912 | tf_op jit(solution)/shard_map/ppermute | solution.py:367
  68.9 20.1 %collective-permute-start.12 = (f32[2,64,640]{2,1,0:T(8,128)S(1)}, f32[2,64,640]{2,1,0:T(8,128)S(1)}, u32[]{:S(2)}, u32[]{:S(2)}) collective-permute-start(f32[2,64,640]{2,1,0:T(8,128)S(1)} %maximum_bitcast_fusion), channel_id=1, source_target_pairs={{0,2},{1,3},{2,0},{3,1},{4,6},{5,7},{6,4},{7,5},{8,10},{9,11},{10,... | collective-permute-start | bytes 983048 | tf_op jit(solution)/shard_map/ppermute | solution.py:367
  89.6 14.5 %collective-permute-start.16 = (f32[1,1,64,1664]{3,2,1,0:T(8,128)S(1)}, f32[1,1,64,1664]{3,2,1,0:T(8,128)S(1)}, u32[]{:S(2)}, u32[]{:S(2)}) collective-permute-start(f32[1,1,64,1664]{3,2,1,0:T(8,128)S(1)} %slice_add_fusion.1), channel_id=1, source_target_pairs={{0,16},{4,20},{8,24},{12,28},{16,0},{20,4},{24,8},{28,12},{1,17},{... | collective-permute-start | bytes 1277960 | tf_op jit(solution)/shard_map/ppermute | solution.py:367
  89.9 15.8 %collective-permute-start.17 = (f32[1,1,64,1664]{3,2,1,0:T(8,128)S(1)}, f32[1,1,64,1664]{3,2,1,0:T(8,128)S(1)}, u32[]{:S(2)}, u32[]{:S(2)}) collective-permute-start(f32[1,1,64,1664]{3,2,1,0:T(8,128)S(1)} %slice_add_fusion), channel_id=1, source_target_pairs={{0,8},{4,12},{8,0},{12,4},{16,24},{20,28},{24,16},{28,20},{1,9},{5... | collective-permute-start | bytes 1277960 | tf_op jit(solution)/shard_map/ppermute | solution.py:367
  95.1 26.0 %collective-permute-start.15 = (f32[1,1,64,640]{3,2,1,0:T(8,128)S(1)}, f32[1,1,64,640]{3,2,1,0:T(8,128)S(1)}, u32[]{:S(2)}, u32[]{:S(2)}) collective-permute-start(f32[1,1,64,640]{3,2,1,0:T(8,128)S(1)} %slice_add_fusion.12), channel_id=1, source_target_pairs={{0,16},{4,20},{8,24},{12,28},{16,0},{20,4},{24,8},{28,12},{1,17},{... | collective-permute-start | bytes 491528 | tf_op jit(solution)/shard_map/ppermute | solution.py:367
  96.5 24.7 %collective-permute-start.19 = (f32[1,1,64,640]{3,2,1,0:T(8,128)S(1)}, f32[1,1,64,640]{3,2,1,0:T(8,128)S(1)}, u32[]{:S(2)}, u32[]{:S(2)}) collective-permute-start(f32[1,1,64,640]{3,2,1,0:T(8,128)S(1)} %slice_add_fusion.11), channel_id=1, source_target_pairs={{0,8},{4,12},{8,0},{12,4},{16,24},{20,28},{24,16},{28,20},{1,9},{5... | collective-permute-start | bytes 491528 | tf_op jit(solution)/shard_map/ppermute | solution.py:367
  97.6 24.9 %collective-permute-start.22 = (f32[2,1,64,1024]{3,2,1,0:T(8,128)S(1)}, f32[2,1,64,1024]{3,2,1,0:T(8,128)S(1)}, u32[]{:S(2)}, u32[]{:S(2)}) collective-permute-start(f32[2,1,64,1024]{3,2,1,0:T(8,128)S(1)} %get-tuple-element.199), channel_id=1, source_target_pairs={{0,8},{4,12},{8,0},{12,4},{16,24},{20,28},{24,16},{28,20},{1,9},{5... | collective-permute-start | bytes 1572872 | tf_op jit(solution)/shard_map/ppermute | solution.py:367
  104.2 18.4 %collective-permute-start.23 = (f32[2,1,64,1024]{3,2,1,0:T(8,128)S(1)}, f32[2,1,64,1024]{3,2,1,0:T(8,128)S(1)}, u32[]{:S(2)}, u32[]{:S(2)}) collective-permute-start(f32[2,1,64,1024]{3,2,1,0:T(8,128)S(1)} %get-tuple-element.201), channel_id=1, source_target_pairs={{0,16},{4,20},{8,24},{12,28},{16,0},{20,4},{24,8},{28,12},{1,17},{... | collective-permute-start | bytes 1572872 | tf_op jit(solution)/shard_map/ppermute | solution.py:367
  105.8 15.3 %collective-permute-start.18 = (f32[2,64,640]{2,1,0:T(8,128)S(1)}, f32[2,64,640]{2,1,0:T(8,128)S(1)}, u32[]{:S(2)}, u32[]{:S(2)}) collective-permute-start(f32[2,64,640]{2,1,0:T(8,128)S(1)} %maximum_bitcast_fusion.1), channel_id=1, source_target_pairs={{0,2},{1,3},{2,0},{3,1},{4,6},{5,7},{6,4},{7,5},{8,10},{9,11},{10,... | collective-permute-start | bytes 983048 | tf_op jit(solution)/shard_map/ppermute | solution.py:367
  122.6 10.9 %collective-permute-start.24 = (f32[1,1,64,1024]{3,2,1,0:T(8,128)S(1)}, f32[1,1,64,1024]{3,2,1,0:T(8,128)S(1)}, u32[]{:S(2)}, u32[]{:S(2)}) collective-permute-start(f32[1,1,64,1024]{3,2,1,0:T(8,128)S(1)} %slice_add_fusion.9), channel_id=1, source_target_pairs={{0,16},{4,20},{8,24},{12,28},{16,0},{20,4},{24,8},{28,12},{1,17},{... | collective-permute-start | bytes 786440 | tf_op jit(solution)/shard_map/ppermute | solution.py:367
  123.9 9.6 %collective-permute-start.25 = (f32[1,1,64,1024]{3,2,1,0:T(8,128)S(1)}, f32[1,1,64,1024]{3,2,1,0:T(8,128)S(1)}, u32[]{:S(2)}, u32[]{:S(2)}) collective-permute-start(f32[1,1,64,1024]{3,2,1,0:T(8,128)S(1)} %slice_add_fusion.8), channel_id=1, source_target_pairs={{0,8},{4,12},{8,0},{12,4},{16,24},{20,28},{24,16},{28,20},{1,9},{5... | collective-permute-start | bytes 786440 | tf_op jit(solution)/shard_map/ppermute | solution.py:367
  124.5 31.7 %collective-permute-start.34 = (f32[2,64,1024]{2,1,0:T(8,128)S(1)}, f32[2,64,1024]{2,1,0:T(8,128)S(1)}, u32[]{:S(2)}, u32[]{:S(2)}) collective-permute-start(f32[2,64,1024]{2,1,0:T(8,128)S(1)} %bitcast.102), channel_id=1, source_target_pairs={{0,2},{1,3},{2,0},{3,1},{4,6},{5,7},{6,4},{7,5},{8,10},{9,11},{10,... | collective-permute-start | bytes 1572872 | tf_op jit(solution)/shard_map/ppermute | solution.py:367
  133.6 9.9 %collective-permute-start.27 = (f32[128,640]{1,0:T(8,128)S(1)}, f32[128,640]{1,0:T(8,128)S(1)}, u32[]{:S(2)}, u32[]{:S(2)}) collective-permute-start(f32[128,640]{1,0:T(8,128)S(1)} %get-tuple-element.254), channel_id=1, source_target_pairs={{0,16},{4,20},{8,24},{12,28},{16,0},{20,4},{24,8},{28,12},{1,17},{... | collective-permute-start | bytes 983048 | tf_op jit(solution)/shard_map/ppermute | solution.py:367
  136.0 20.1 %collective-permute-start.32 = (f32[64,640]{1,0:T(8,128)S(1)}, f32[64,640]{1,0:T(8,128)S(1)}, u32[]{:S(2)}, u32[]{:S(2)}) collective-permute-start(f32[64,640]{1,0:T(8,128)S(1)} %get-tuple-element.244), channel_id=1, source_target_pairs={{0,8},{4,12},{8,0},{12,4},{16,24},{20,28},{24,16},{28,20},{1,9},{5... | collective-permute-start | bytes 491528 | tf_op jit(solution)/shard_map/ppermute | solution.py:367
  156.4 13.1 %collective-permute-start.36 = (f32[128,1024]{1,0:T(8,128)S(1)}, f32[128,1024]{1,0:T(8,128)S(1)}, u32[]{:S(2)}, u32[]{:S(2)}) collective-permute-start(f32[128,1024]{1,0:T(8,128)S(1)} %pad_maximum_fusion.1), channel_id=1, source_target_pairs={{0,16},{4,20},{8,24},{12,28},{16,0},{20,4},{24,8},{28,12},{1,17},{... | collective-permute-start | bytes 1572872 | tf_op jit(solution)/shard_map/ppermute | solution.py:367
  156.5 13.0 %collective-permute-start.35 = (f32[128,1024]{1,0:T(8,128)S(1)}, f32[128,1024]{1,0:T(8,128)S(1)}, u32[]{:S(2)}, u32[]{:S(2)}) collective-permute-start(f32[128,1024]{1,0:T(8,128)S(1)} %pad_maximum_fusion.1), channel_id=1, source_target_pairs={{0,8},{4,12},{8,0},{12,4},{16,24},{20,28},{24,16},{28,20},{1,9},{5... | collective-permute-start | bytes 1572872 | tf_op jit(solution)/shard_map/ppermute | solution.py:367
  169.7 13.2 %collective-permute-start.39 = (f32[384,1024]{1,0:T(8,128)S(1)}, f32[384,1024]{1,0:T(8,128)S(1)}, u32[]{:S(2)}, u32[]{:S(2)}) collective-permute-start(f32[384,1024]{1,0:T(8,128)S(1)} %slice_dynamic-update-slice_fusion.refs_0_), channel_id=1, source_target_pairs={{0,4},{4,0},{8,12},{12,8},{16,20},{20,16},{24,28},{28,24},{1,5},{5... | collective-permute-start | bytes 4718600 | tf_op jit(solution)/shard_map/ppermute | solution.py:367
  (22 other events, 137.5 us)

commit v9 on v8

--- a/solution.py
+++ b/solution.py
@@ -422,6 +422,11 @@
                 held += [own] + came
             self.held.append(held)
 
+    def hold_last(self, value):
+        last, value = together([held[-1] for held in self.held], value)
+        self.held = [held[:-1] + [block] for held, block in zip(self.held, last)]
+        return value
+
     def exchange(self, first=0, last=None):
         pairs = list(zip(*self.held))[first:last]
         mine = jnp.concatenate([value for pair in pairs for value in pair], axis=0)
@@ -521,14 +526,15 @@
     grad_gather.relay()
     act_gather.relay()
     across_mixed, _ = together(across_mixed, act_gather.whole)
-    act_out, *act_square = act_factor_rows(place, act_gather.exchange(), block, feat)
     mixed_gather = Gather(both(mixed_sums, across_mixed), chips)
     mixed_gather.begin()
+    mixed_gather.whole = act_gather.hold_last(mixed_gather.whole)
+    mixed_gather.relay()
+    mine, theirs = mixed_gather.exchange(0, -1)
+    act_out, *act_square = act_factor_rows(place, act_gather.exchange(), block, feat)
     grad_blocks, act_square = together(grad_gather.exchange(), act_square)
     grad_out, inverse = grad_factor_rows(place, grad_blocks, block, feat)
-    mixed_gather.whole, inverse = together(mixed_gather.whole, inverse)
-    mixed_gather.relay()
-    mine, theirs = mixed_gather.exchange(0, -1)
+    inverse = mixed_gather.hold_last(inverse)
     my_last, their_last = mixed_gather.exchange(-1)
     mixed_blocks = (mine, my_last, theirs, their_last)
     outs = update_rows(place, mixed_blocks, inverse, *act_square, momentum[0], weights[0])

time: 190 us -> 188 us (0.989); the launches traced: 189 us -> 185 us
  waiting for transfers between devices: 106 us -> 103 us
    ppermute x41, waiting for transfers between devices: 106 us -> 103 us  [swap(): return lax.ppermute(value, axis, [(i, i ^ step) for i in range(size)])]
  transfers between devices with their start and end apart: 41 -> 41, of which waited for: 18 -> 15; matrix products, arithmetic and copies ran while one was open for 3% -> 3% of each run, Pallas kernels for 15% -> 16%
where the time goes in v9:
time: 188 us; the launch traced here: 185 us
  waiting for transfers between devices  103 us (55%)
  starting transfers between devices  36.3 us (19%)
  Pallas kernels  35.3 us (19%)
  local copies, waits for them, and re-layouts  6.21 us (3%)
  other arithmetic  2.22 us (1%)
    ppermute x41, waiting for transfers between devices, swap(): return lax.ppermute(value, axis, [(i, i ^ step) for i in range(size)])  103 us
    ppermute x41, starting transfers between devices, swap(): return lax.ppermute(value, axis, [(i, i ^ step) for i in range(size)])  36.3 us
    pallas_call x4, Pallas kernels, bands(): pl.pallas_call(functools.partial(body, range(turns), block, chips, bool(s...  22.6 us
    pallas_call x3, Pallas kernels, on_core(): pl.pallas_call(body, out_shape=shapes, in_specs=[pl.BlockSpec(memory_spac...  11.9 us
  transfers between devices with their start and end apart: 41, of which 15 were waited for; matrix products, arithmetic and copies ran while one was open for 3% of the time, Pallas kernels for 16%

profile of v9, /device:TPU:25, one launch (start us, length us, event | category | flops | bytes accessed | tf_op | source)
XLA Modules:
  0.0 184.7 jit_solution(14662065456701679186)
XLA Ops:
  6.2 1.7 slice.261
  9.1 3.7 %shard_map.112 = (f32[2,2,64,640]{3,2,1,0:T(8,128)S(1)}, f32[2,2,64,640]{3,2,1,0:T(8,128)S(1)}, f32[2,2,64,640]{3,2,1,0:T(8,128)S(1)}, f32[2,2,64,640]{3,2,1,0:T(8,128)S(1)}) custom-call(s32[2]{0:T(128)S(1)} %pad_add_fusion.place, f32[264,1024]{1,0:T(8,128)S(1)} %shard_map.111.refs_0_.refs_2_, f32[264,1024]{1,0:T(8,128)S(1)} %collective-permute-done.1.refs_1_.refs_3_), custom_call_target="tpu_custom_call" | custom-call | tf_op jit(solution)/shard_map/pallas_call | solution.py:222
  12.8 7.9 %shard_map.113 = (f32[2,1,64,640]{3,2,1,0:T(8,128)S(1)}, f32[2,1,64,640]{3,2,1,0:T(8,128)S(1)}, f32[2,1,64,640]{3,2,1,0:T(8,128)S(1)}, f32[2,1,64,640]{3,2,1,0:T...) custom-call(s32[2]{0:T(128)S(1)} %pad_add_fusion.place, ...), custom_call_target="tpu_custom_call" | custom-call | tf_op jit(solution)/shard_map/pallas_call | solution.py:222
  20.8 9.4 %collective-permute-done.refs_0_.refs_2_ = f32[264,1024]{1,0:T(8,128)S(1)} collective-permute-done((f32[264,1024]{1,0:T(8,128)S(1)}, f32[264,1024]{1,0:T(8,128)S(1)}, u32[]{:S(2)}, u32[]{:S(2)}) %collective-permute-start) | collective-permute-done | bytes 1081376 | tf_op jit(solution)/shard_map/ppermute | solution.py:367
  31.1 2.2 %collective-permute-done.4.refs_1_.refs_3_ = f32[264,1024]{1,0:T(8,128)S(1)} collective-permute-done((f32[264,1024]{1,0:T(8,128)S(1)}, f32[264,1024]{1,0:T(8,128)S(1)}, u32[]{:S(2)}, u32[]{:S(2)}) %collective-permute-start.4) | collective-permute-done | bytes 1081376 | tf_op jit(solution)/shard_map/ppermute | solution.py:367
  33.3 3.8 %shard_map.114 = (f32[2,2,64,640]{3,2,1,0:T(8,128)S(1)}, f32[2,2,64,640]{3,2,1,0:T(8,128)S(1)}, f32[2,2,64,640]{3,2,1,0:T(8,128)S(1)}, f32[2,2,64,640]{3,2,1,0:T(8,128)S(1)}) custom-call(s32[2]{0:T(128)S(1)} %pad_add_fusion.place, f32[264,1024]{1,0:T(8,128)S(1)} %collective-permute-done.refs_0_.refs_2_, ...), custom_call_target="tpu_custom_call" | custom-call | tf_op jit(solution)/shard_map/pallas_call | solution.py:222
  39.6 16.4 %collective-permute-done.3.refs_0_ = f32[256,1024]{1,0:T(8,128)S(1)} collective-permute-done((f32[256,1024]{1,0:T(8,128)}, f32[256,1024]{1,0:T(8,128)S(1)}, u32[]{:S(2)}, u32[]{:S(2)}) %collective-permute-start.3) | collective-permute-done | bytes 1048608 | tf_op jit(solution)/shard_map/ppermute | solution.py:367
  59.4 7.2 %shard_map.115 = (f32[2,1,64,640]{3,2,1,0:T(8,128)S(1)}, f32[2,1,64,640]{3,2,1,0:T(8,128)S(1)}, f32[2,1,64,640]{3,2,1,0:T(8,128)S(1)}, f32[2,1,64,640]{3,2,1,0:T...) custom-call(s32[2]{0:T(128)S(1)} %pad_add_fusion.place, ...), custom_call_target="tpu_custom_call" | custom-call | tf_op jit(solution)/shard_map/pallas_call | solution.py:222
  69.1 17.6 %collective-permute-done.9 = f32[2,1,64,1664]{3,2,1,0:T(8,128)S(1)} collective-permute-done((f32[2,1,64,1664]{3,2,1,0:T(8,128)S(1)}, f32[2,1,64,1664]{3,2,1,0:T(8,128)S(1)}, u32[]{:S(2)}, u32[]{:S(2)}) %collective-permute-start.9) | collective-permute-done | bytes 852000 | tf_op jit(solution)/shard_map/ppermute | solution.py:367
  91.6 3.5 %collective-permute-done.13 = f32[2,1,64,640]{3,2,1,0:T(8,128)S(1)} collective-permute-done((f32[2,1,64,640]{3,2,1,0:T(8,128)S(1)}, f32[2,1,64,640]{3,2,1,0:T(8,128)S(1)}, u32[]{:S(2)}, u32[]{:S(2)}) %collective-permute-start.13) | collective-permute-done | bytes 327712 | tf_op jit(solution)/shard_map/ppermute | solution.py:367
  95.1 1.4 collective-permute-start.15
  98.0 6.2 %collective-permute-done.16 = f32[1,1,64,1664]{3,2,1,0:T(8,128)S(1)} collective-permute-done((f32[1,1,64,1664]{3,2,1,0:T(8,128)S(1)}, f32[1,1,64,1664]{3,2,1,0:T(8,128)S(1)}, u32[]{:S(2)}, u32[]{:S(2)}) %collective-permute-start.16) | collective-permute-done | bytes 426016 | tf_op jit(solution)/shard_map/ppermute | solution.py:367
  104.2 1.4 collective-permute-start.23
  106.0 15.1 %collective-permute-done.18 = f32[2,64,640]{2,1,0:T(8,128)S(1)} collective-permute-done((f32[2,64,640]{2,1,0:T(8,128)S(1)}, f32[2,64,640]{2,1,0:T(8,128)S(1)}, u32[]{:S(2)}, u32[]{:S(2)}) %collective-permute-start.18) | collective-permute-done | bytes 327712 | tf_op jit(solution)/shard_map/ppermute | solution.py:367
  122.6 1.3 collective-permute-start.24
  124.6 3.3 %collective-permute-done.21 = f32[128,640]{1,0:T(8,128)S(1)} collective-permute-done((f32[128,640]{1,0:T(8,128)S(1)}, f32[128,640]{1,0:T(8,128)S(1)}, u32[]{:S(2)}, u32[]{:S(2)}) %collective-permute-start.21) | collective-permute-done | bytes 327712 | tf_op jit(solution)/shard_map/ppermute | solution.py:367
  127.9 5.6 %collective-permute-done.24 = f32[1,1,64,1024]{3,2,1,0:T(8,128)S(1)} collective-permute-done((f32[1,1,64,1024]{3,2,1,0:T(8,128)S(1)}, f32[1,1,64,1024]{3,2,1,0:T(8,128)S(1)}, u32[]{:S(2)}, u32[]{:S(2)}) %collective-permute-start.24) | collective-permute-done | bytes 262176 | tf_op jit(solution)/shard_map/ppermute | solution.py:367
  136.8 6.4 %collective-permute-done.34 = f32[64,640]{1,0:T(8,128)S(1)} collective-permute-done((f32[64,640]{1,0:T(8,128)S(1)}, f32[64,640]{1,0:T(8,128)S(1)}, u32[]{:S(2)}, u32[]{:S(2)}) %collective-permute-start.34) | collective-permute-done | bytes 163872 | tf_op jit(solution)/shard_map/ppermute | solution.py:367
  143.2 5.3 %collective-permute-start.36 = (f32[512,640]{1,0:T(8,128)S(1)}, f32[512,640]{1,0:T(8,128)S(1)}, u32[]{:S(2)}, u32[]{:S(2)}) collective-permute-start(f32[512,640]{1,0:T(8,128)S(1)} %constant_dynamic-update-slice_fusion.8.refs_0_), channel_id=1, source_target_pairs={{0,4},{4,0},{8,12},{12,8},{16,20},{20,16},{24,28},{28,24},{1,5},{5... | collective-permute-start | bytes 3932168 | tf_op jit(solution)/shard_map/ppermute | solution.py:367
  152.0 13.5 %collective-permute-done.28 = f32[64,640]{1,0:T(8,128)S(1)} collective-permute-done((f32[64,640]{1,0:T(8,128)S(1)}, f32[64,640]{1,0:T(8,128)S(1)}, u32[]{:S(2)}, u32[]{:S(2)}) %collective-permute-start.28) | collective-permute-done | bytes 163872 | tf_op jit(solution)/shard_map/ppermute | solution.py:367
  170.1 2.6 %shard_map.116 = (f32[128,1024]{1,0:T(8,128)}, f32[8,128]{1,0:T(8,128)S(1)}, bf16[1024,1024]{1,0:T(8,128)(2,1)S(1)}, bf16[1024,1024]{1,0:T(8,128)(2,1)S(1)}) custom-call(s32[2]{0:T(128)S(1)} %pad_add_fusion.place, f32[512,640]{1,0:T(8,128)S(1)} %constant_dynamic-update-slice_fusion.2.refs_0_, f32[512,640]{1,0:T(8,128)S(1)} %collective-permute-done.33.refs_1_), custom_call_target="tpu_custom_call" | custom-call | tf_op jit(solution)/shard_map/pallas_call | solution.py:334
  172.7 3.6 %shard_map.117 = (f32[128,1024]{1,0:T(8,128)}, f32[128,1024]{1,0:T(8,128)S(1)}) custom-call(s32[2]{0:T(128)S(1)} %pad_add_fusion.place, f32[512,640]{1,0:T(8,128)S(1)} %constant_dynamic-update-slice_fusion.8.refs_0_, f32[512,640]{1,0:T(8,128)S(1)} %collective-permute-done.36.refs_1_), custom_call_target="tpu_custom_call" | custom-call | tf_op jit(solution)/shard_map/pallas_call | solution.py:334
  177.4 1.5 collective-permute-done.40.refs_3_
  178.9 5.7 %shard_map.118 = (f32[128,1024]{1,0:T(8,128)}, f32[128,1024]{1,0:T(8,128)}) custom-call(s32[2]{0:T(128)S(1)} %pad_add_fusion.place, f32[384,1024]{1,0:T(8,128)S(1)} %slice_dynamic-update-slice_fusion.refs_0_, f32[128,1024]{1,0:T(8,128)S(1)} %constant_dynamic-update-slice_fusion.18.refs_1_, f32[384,1024]{1,0:T(8,128)S(1)} %collective-permute-done.39.refs_2_, ...), custom_call_target="tpu_custom_call" | custom-call | tf_op jit(solution)/shard_map/pallas_call | solution.py:334
  (130 shorter events, 36.6 us)
Async XLA Ops:
  4.7 25.4 %collective-permute-start = (f32[264,1024]{1,0:T(8,128)S(1)}, f32[264,1024]{1,0:T(8,128)S(1)}, u32[]{:S(2)}, u32[]{:S(2)}) collective-permute-start(f32[264,1024]{1,0:T(8,128)S(1)} %shard_map.111.refs_0_.refs_2_), channel_id=1, source_target_pairs={{0,1},{1,0},{2,3},{3,2},{4,5},{5,4},{6,7},{7,6},{8,9},{9,8},{10,11... | collective-permute-start | bytes 3244040 | tf_op jit(solution)/shard_map/ppermute | solution.py:367
  31.0 25.0 %collective-permute-start.3 = (f32[256,1024]{1,0:T(8,128)}, f32[256,1024]{1,0:T(8,128)S(1)}, u32[]{:S(2)}, u32[]{:S(2)}) collective-permute-start(f32[256,1024]{1,0:T(8,128)} %refs_0_.1), channel_id=1, source_target_pairs={{0,1},{1,0},{2,3},{3,2},{4,5},{5,4},{6,7},{7,6},{8,9},{9,8},{10,11... | collective-permute-start | bytes 3145736 | tf_op jit(solution)/shard_map/ppermute | solution.py:367
  37.1 19.7 %collective-permute-start.5 = (f32[2,2,64,640]{3,2,1,0:T(8,128)S(1)}, f32[2,2,64,640]{3,2,1,0:T(8,128)S(1)}, u32[]{:S(2)}, u32[]{:S(2)}) collective-permute-start(f32[2,2,64,640]{3,2,1,0:T(8,128)S(1)} %get-tuple-element.145), channel_id=1, source_target_pairs={{0,8},{4,12},{8,0},{12,4},{16,24},{20,28},{24,16},{28,20},{1,9},{5... | collective-permute-start | bytes 1966088 | tf_op jit(solution)/shard_map/ppermute | solution.py:367
  38.3 18.5 %collective-permute-start.6 = (f32[2,2,64,640]{3,2,1,0:T(8,128)S(1)}, f32[2,2,64,640]{3,2,1,0:T(8,128)S(1)}, u32[]{:S(2)}, u32[]{:S(2)}) collective-permute-start(f32[2,2,64,640]{3,2,1,0:T(8,128)S(1)} %get-tuple-element.147), channel_id=1, source_target_pairs={{0,16},{4,20},{8,24},{12,28},{16,0},{20,4},{24,8},{28,12},{1,17},{... | collective-permute-start | bytes 1966088 | tf_op jit(solution)/shard_map/ppermute | solution.py:367
  56.9 11.9 %collective-permute-start.11 = (f32[1,2,64,640]{3,2,1,0:T(8,128)S(1)}, f32[1,2,64,640]{3,2,1,0:T(8,128)S(1)}, u32[]{:S(2)}, u32[]{:S(2)}) collective-permute-start(f32[1,2,64,640]{3,2,1,0:T(8,128)S(1)} %get-tuple-element.186), channel_id=1, source_target_pairs={{0,8},{4,12},{8,0},{12,4},{16,24},{20,28},{24,16},{28,20},{1,9},{5... | collective-permute-start | bytes 983048 | tf_op jit(solution)/shard_map/ppermute | solution.py:367
  66.6 20.0 %collective-permute-start.9 = (f32[2,1,64,1664]{3,2,1,0:T(8,128)S(1)}, f32[2,1,64,1664]{3,2,1,0:T(8,128)S(1)}, u32[]{:S(2)}, u32[]{:S(2)}) collective-permute-start(f32[2,1,64,1664]{3,2,1,0:T(8,128)S(1)} %get-tuple-element.180), channel_id=1, source_target_pairs={{0,8},{4,12},{8,0},{12,4},{16,24},{20,28},{24,16},{28,20},{1,9},{5... | collective-permute-start | bytes 2555912 | tf_op jit(solution)/shard_map/ppermute | solution.py:367
  67.5 19.9 %collective-permute-start.10 = (f32[2,1,64,1664]{3,2,1,0:T(8,128)S(1)}, f32[2,1,64,1664]{3,2,1,0:T(8,128)S(1)}, u32[]{:S(2)}, u32[]{:S(2)}) collective-permute-start(f32[2,1,64,1664]{3,2,1,0:T(8,128)S(1)} %get-tuple-element.181), channel_id=1, source_target_pairs={{0,16},{4,20},{8,24},{12,28},{16,0},{20,4},{24,8},{28,12},{1,17},{... | collective-permute-start | bytes 2555912 | tf_op jit(solution)/shard_map/ppermute | solution.py:367
  68.9 20.1 %collective-permute-start.12 = (f32[2,64,640]{2,1,0:T(8,128)S(1)}, f32[2,64,640]{2,1,0:T(8,128)S(1)}, u32[]{:S(2)}, u32[]{:S(2)}) collective-permute-start(f32[2,64,640]{2,1,0:T(8,128)S(1)} %maximum_bitcast_fusion), channel_id=1, source_target_pairs={{0,2},{1,3},{2,0},{3,1},{4,6},{5,7},{6,4},{7,5},{8,10},{9,11},{10,... | collective-permute-start | bytes 983048 | tf_op jit(solution)/shard_map/ppermute | solution.py:367
  89.6 14.5 %collective-permute-start.16 = (f32[1,1,64,1664]{3,2,1,0:T(8,128)S(1)}, f32[1,1,64,1664]{3,2,1,0:T(8,128)S(1)}, u32[]{:S(2)}, u32[]{:S(2)}) collective-permute-start(f32[1,1,64,1664]{3,2,1,0:T(8,128)S(1)} %slice_add_fusion.1), channel_id=1, source_target_pairs={{0,16},{4,20},{8,24},{12,28},{16,0},{20,4},{24,8},{28,12},{1,17},{... | collective-permute-start | bytes 1277960 | tf_op jit(solution)/shard_map/ppermute | solution.py:367
  89.9 15.8 %collective-permute-start.17 = (f32[1,1,64,1664]{3,2,1,0:T(8,128)S(1)}, f32[1,1,64,1664]{3,2,1,0:T(8,128)S(1)}, u32[]{:S(2)}, u32[]{:S(2)}) collective-permute-start(f32[1,1,64,1664]{3,2,1,0:T(8,128)S(1)} %slice_add_fusion), channel_id=1, source_target_pairs={{0,8},{4,12},{8,0},{12,4},{16,24},{20,28},{24,16},{28,20},{1,9},{5... | collective-permute-start | bytes 1277960 | tf_op jit(solution)/shard_map/ppermute | solution.py:367
  95.1 26.0 %collective-permute-start.15 = (f32[1,1,64,640]{3,2,1,0:T(8,128)S(1)}, f32[1,1,64,640]{3,2,1,0:T(8,128)S(1)}, u32[]{:S(2)}, u32[]{:S(2)}) collective-permute-start(f32[1,1,64,640]{3,2,1,0:T(8,128)S(1)} %slice_add_fusion.12), channel_id=1, source_target_pairs={{0,16},{4,20},{8,24},{12,28},{16,0},{20,4},{24,8},{28,12},{1,17},{... | collective-permute-start | bytes 491528 | tf_op jit(solution)/shard_map/ppermute | solution.py:367
  96.5 24.7 %collective-permute-start.19 = (f32[1,1,64,640]{3,2,1,0:T(8,128)S(1)}, f32[1,1,64,640]{3,2,1,0:T(8,128)S(1)}, u32[]{:S(2)}, u32[]{:S(2)}) collective-permute-start(f32[1,1,64,640]{3,2,1,0:T(8,128)S(1)} %slice_add_fusion.11), channel_id=1, source_target_pairs={{0,8},{4,12},{8,0},{12,4},{16,24},{20,28},{24,16},{28,20},{1,9},{5... | collective-permute-start | bytes 491528 | tf_op jit(solution)/shard_map/ppermute | solution.py:367
  97.6 24.9 %collective-permute-start.22 = (f32[2,1,64,1024]{3,2,1,0:T(8,128)S(1)}, f32[2,1,64,1024]{3,2,1,0:T(8,128)S(1)}, u32[]{:S(2)}, u32[]{:S(2)}) collective-permute-start(f32[2,1,64,1024]{3,2,1,0:T(8,128)S(1)} %get-tuple-element.203), channel_id=1, source_target_pairs={{0,8},{4,12},{8,0},{12,4},{16,24},{20,28},{24,16},{28,20},{1,9},{5... | collective-permute-start | bytes 1572872 | tf_op jit(solution)/shard_map/ppermute | solution.py:367
  104.2 18.4 %collective-permute-start.23 = (f32[2,1,64,1024]{3,2,1,0:T(8,128)S(1)}, f32[2,1,64,1024]{3,2,1,0:T(8,128)S(1)}, u32[]{:S(2)}, u32[]{:S(2)}) collective-permute-start(f32[2,1,64,1024]{3,2,1,0:T(8,128)S(1)} %get-tuple-element.205), channel_id=1, source_target_pairs={{0,16},{4,20},{8,24},{12,28},{16,0},{20,4},{24,8},{28,12},{1,17},{... | collective-permute-start | bytes 1572872 | tf_op jit(solution)/shard_map/ppermute | solution.py:367
  105.8 15.3 %collective-permute-start.18 = (f32[2,64,640]{2,1,0:T(8,128)S(1)}, f32[2,64,640]{2,1,0:T(8,128)S(1)}, u32[]{:S(2)}, u32[]{:S(2)}) collective-permute-start(f32[2,64,640]{2,1,0:T(8,128)S(1)} %maximum_bitcast_fusion.1), channel_id=1, source_target_pairs={{0,2},{1,3},{2,0},{3,1},{4,6},{5,7},{6,4},{7,5},{8,10},{9,11},{10,... | collective-permute-start | bytes 983048 | tf_op jit(solution)/shard_map/ppermute | solution.py:367
  122.6 10.9 %collective-permute-start.24 = (f32[1,1,64,1024]{3,2,1,0:T(8,128)S(1)}, f32[1,1,64,1024]{3,2,1,0:T(8,128)S(1)}, u32[]{:S(2)}, u32[]{:S(2)}) collective-permute-start(f32[1,1,64,1024]{3,2,1,0:T(8,128)S(1)} %slice_add_fusion.9), channel_id=1, source_target_pairs={{0,16},{4,20},{8,24},{12,28},{16,0},{20,4},{24,8},{28,12},{1,17},{... | collective-permute-start | bytes 786440 | tf_op jit(solution)/shard_map/ppermute | solution.py:367
  124.5 24.0 %collective-permute-start.30 = (f32[2,64,1024]{2,1,0:T(8,128)S(1)}, f32[2,64,1024]{2,1,0:T(8,128)S(1)}, u32[]{:S(2)}, u32[]{:S(2)}) collective-permute-start(f32[2,64,1024]{2,1,0:T(8,128)S(1)} %bitcast.102), channel_id=1, source_target_pairs={{0,2},{1,3},{2,0},{3,1},{4,6},{5,7},{6,4},{7,5},{8,10},{9,11},{10,... | collective-permute-start | bytes 1572872 | tf_op jit(solution)/shard_map/ppermute | solution.py:367
  133.6 15.0 %collective-permute-start.27 = (f32[128,640]{1,0:T(8,128)S(1)}, f32[128,640]{1,0:T(8,128)S(1)}, u32[]{:S(2)}, u32[]{:S(2)}) collective-permute-start(f32[128,640]{1,0:T(8,128)S(1)} %get-tuple-element.262), channel_id=1, source_target_pairs={{0,16},{4,20},{8,24},{12,28},{16,0},{20,4},{24,8},{28,12},{1,17},{... | collective-permute-start | bytes 983048 | tf_op jit(solution)/shard_map/ppermute | solution.py:367
  134.8 13.7 %collective-permute-start.26 = (f32[128,640]{1,0:T(8,128)S(1)}, f32[128,640]{1,0:T(8,128)S(1)}, u32[]{:S(2)}, u32[]{:S(2)}) collective-permute-start(f32[128,640]{1,0:T(8,128)S(1)} %get-tuple-element.262), channel_id=1, source_target_pairs={{0,8},{4,12},{8,0},{12,4},{16,24},{20,28},{24,16},{28,20},{1,9},{5... | collective-permute-start | bytes 983048 | tf_op jit(solution)/shard_map/ppermute | solution.py:367
  143.2 29.5 %collective-permute-start.36 = (f32[512,640]{1,0:T(8,128)S(1)}, f32[512,640]{1,0:T(8,128)S(1)}, u32[]{:S(2)}, u32[]{:S(2)}) collective-permute-start(f32[512,640]{1,0:T(8,128)S(1)} %constant_dynamic-update-slice_fusion.8.refs_0_), channel_id=1, source_target_pairs={{0,4},{4,0},{8,12},{12,8},{16,20},{20,16},{24,28},{28,24},{1,5},{5... | collective-permute-start | bytes 3932168 | tf_op jit(solution)/shard_map/ppermute | solution.py:367
  148.8 17.4 %collective-permute-start.32 = (f32[128,1024]{1,0:T(8,128)S(1)}, f32[128,1024]{1,0:T(8,128)S(1)}, u32[]{:S(2)}, u32[]{:S(2)}) collective-permute-start(f32[128,1024]{1,0:T(8,128)S(1)} %pad_maximum_fusion.1), channel_id=1, source_target_pairs={{0,16},{4,20},{8,24},{12,28},{16,0},{20,4},{24,8},{28,12},{1,17},{... | collective-permute-start | bytes 1572872 | tf_op jit(solution)/shard_map/ppermute | solution.py:367
  149.5 16.7 %collective-permute-start.31 = (f32[128,1024]{1,0:T(8,128)S(1)}, f32[128,1024]{1,0:T(8,128)S(1)}, u32[]{:S(2)}, u32[]{:S(2)}) collective-permute-start(f32[128,1024]{1,0:T(8,128)S(1)} %pad_maximum_fusion.1), channel_id=1, source_target_pairs={{0,8},{4,12},{8,0},{12,4},{16,24},{20,28},{24,16},{28,20},{1,9},{5... | collective-permute-start | bytes 1572872 | tf_op jit(solution)/shard_map/ppermute | solution.py:367
  150.4 15.1 %collective-permute-start.28 = (f32[64,640]{1,0:T(8,128)S(1)}, f32[64,640]{1,0:T(8,128)S(1)}, u32[]{:S(2)}, u32[]{:S(2)}) collective-permute-start(f32[64,640]{1,0:T(8,128)S(1)} %get-tuple-element.258), channel_id=1, source_target_pairs={{0,16},{4,20},{8,24},{12,28},{16,0},{20,4},{24,8},{28,12},{1,17},{... | collective-permute-start | bytes 491528 | tf_op jit(solution)/shard_map/ppermute | solution.py:367
  151.2 15.0 %collective-permute-start.29 = (f32[64,640]{1,0:T(8,128)S(1)}, f32[64,640]{1,0:T(8,128)S(1)}, u32[]{:S(2)}, u32[]{:S(2)}) collective-permute-start(f32[64,640]{1,0:T(8,128)S(1)} %get-tuple-element.256), channel_id=1, source_target_pairs={{0,8},{4,12},{8,0},{12,4},{16,24},{20,28},{24,16},{28,20},{1,9},{5... | collective-permute-start | bytes 491528 | tf_op jit(solution)/shard_map/ppermute | solution.py:367
  (22 other events, 130.5 us)

commit v10 on v9

--- a/solution.py
+++ b/solution.py
@@ -32,11 +32,17 @@
     )
 
 
-def split_rows(parts, samples, high, low, feat):
+def rows_of(part, window):
+    first, count = window
+    return slice(0, count) if part.shape[0] == count else slice(first, first + count)
+
+
+def split_rows(parts, window, high, low, feat):
     extra = high.shape[1] - feat
+    count = window[1]
     for number, part in enumerate(parts):
-        here = slice(number * samples, (number + 1) * samples)
-        top, rest = split(part[0:samples, :])
+        here = slice(number * count, (number + 1) * count)
+        top, rest = split(part[rows_of(part, window), :])
         high[here, 0:feat] = top
         low[here, 0:feat] = rest
         if extra:
@@ -44,21 +50,21 @@
             low[here, feat : feat + extra] = rest[:, 0:extra]
 
 
-def left_rows(parts, samples, turned, column, row, block):
+def left_rows(parts, window, turned, column, row, block):
+    count = window[1]
     for number, part in enumerate(parts):
-        here = slice(number * samples, (number + 1) * samples)
-        turned[:, here] = part[0:samples, pl.ds(column, TILE)].T
+        here = slice(number * count, (number + 1) * count)
+        turned[:, here] = part[rows_of(part, window), pl.ds(column, TILE)].T
     return turned[pl.ds(row, block), :]
 
 
-def keep_place(expert, samples, feat):
-    per_row = feat // samples
-    return lax.div(expert, per_row), pl.multiple_of(lax.rem(expert, per_row) * samples, TILE)
-
-
-def keep_row(parts, samples, expert):
-    row, column = keep_place(expert, samples, parts[0].shape[1])
-    return jnp.concatenate([part[pl.ds(samples + row, 1), pl.ds(column, samples)] for part in parts], axis=1)
+def keep_row(parts, samples, window, expert):
+    first, count = window
+    per_row = parts[0].shape[1] // samples
+    row = samples + lax.div(expert, per_row)
+    column = pl.multiple_of(lax.rem(expert, per_row) * samples, TILE)
+    keeps = [part[pl.ds(row, 1), pl.ds(column, samples)] for part in parts]
+    return jnp.concatenate([keep[:, first : first + count] for keep in keeps], axis=1)
 
 
 def weighted(rows, keeps):
@@ -131,22 +137,22 @@
     copies[2].wait()
 
 
-def act_kernel(turns, block, chips, seeded, samples, place, *refs):
+def act_kernel(turns, block, chips, seeded, samples, window, place, *refs):
     parts, refs = refs[:2], refs[2:]
     refs, (high, low, turned) = refs[:-3], refs[-3:]
     seeds, outs = (refs[: len(refs) // 2], refs[len(refs) // 2 :]) if seeded else ((), refs)
     feat = parts[0].shape[1]
     width = outs[0].shape[3]
     mine, expert = place[0], place[1]
-    split_rows(parts, samples, high, low, feat)
-    keeps = [keep_row(parts, samples, expert ^ (2 * turn)) for turn in turns]
+    split_rows(parts, window, high, low, feat)
+    keeps = [keep_row(parts, samples, window, expert ^ (2 * turn)) for turn in turns]
     places = slots(chips)
     rows = lax.broadcasted_iota(jnp.int32, (block, width), 0)
     columns = lax.broadcasted_iota(jnp.int32, (block, width), 1)
     corner = jnp.logical_and(rows == block - 1, columns == 0)
     for k in range(chips):
         column, row = band_place(mine ^ (2 * k), block)
-        both, tops = weighted(left_rows(parts, samples, turned, column, row, block), keeps)
+        both, tops = weighted(left_rows(parts, window, turned, column, row, block), keeps)
         total = three(both, tops, high[:, pl.ds(column, width)], low[:, pl.ds(column, width)])
         for number, keep in enumerate(keeps):
             count = jnp.sum(keep, axis=1, keepdims=True)
@@ -156,20 +162,20 @@
                 store(outs, seeds, 0, places[k, half], number, slice(0, width), here)
 
 
-def grad_kernel(turns, block, chips, seeded, samples, place, *refs):
+def grad_kernel(turns, block, chips, seeded, samples, window, place, *refs):
     grads, acts, refs = refs[:2], refs[2:4], refs[4:]
     refs, (high, low, act_high, act_low, turned) = refs[:-5], refs[-5:]
     seeds, outs = (refs[: len(refs) // 2], refs[len(refs) // 2 :]) if seeded else ((), refs)
     feat = grads[0].shape[1]
     width = outs[0].shape[3]
     mine, expert = place[0], place[1]
-    split_rows(grads, samples, high, low, feat)
-    split_rows(acts, samples, act_high, act_low, feat)
-    keeps = [keep_row(acts, samples, expert ^ (2 * turn)) for turn in turns]
+    split_rows(grads, window, high, low, feat)
+    split_rows(acts, window, act_high, act_low, feat)
+    keeps = [keep_row(acts, samples, window, expert ^ (2 * turn)) for turn in turns]
     places = slots(chips)
     for k in range(chips):
         column, row = band_place(mine ^ (2 * k), block)
-        both, tops = weighted(left_rows(grads, samples, turned, column, row, block), keeps)
+        both, tops = weighted(left_rows(grads, window, turned, column, row, block), keeps)
         total = three(both, tops, high[:, pl.ds(column, width)], low[:, pl.ds(column, width)])
         mixed = three(both, tops, act_high[...], act_low[...])
         for number in range(len(keeps)):
@@ -202,14 +208,15 @@
             pltpu.SMEM(counts.shape, jnp.int32),
             pltpu.SemaphoreType.DMA((3,)),
         ],
-        compiler_params=pltpu.CompilerParams(vmem_limit_bytes=16 * MIB),
+        compiler_params=pltpu.CompilerParams(vmem_limit_bytes=60 * MIB),
     )(routes.T, counts, acts)
 
 
-def bands(body, turns, groups, place, parts, seeds, samples, chips, block):
+def bands(body, turns, groups, place, parts, seeds, samples, chips, block, window=None):
     feat = parts[0].shape[1]
-    extended = pltpu.VMEM((2 * samples, feat + feat // 2), BF16)
-    plain = pltpu.VMEM((2 * samples, feat), BF16)
+    window = window or (0, samples)
+    extended = pltpu.VMEM((2 * window[1], feat + feat // 2), BF16)
+    plain = pltpu.VMEM((2 * window[1], feat), BF16)
     scratch = [extended, extended] + ([plain, plain] if len(parts) > 2 else [])
     shapes = [
         jax.ShapeDtypeStruct((len(group), count, block // 2, width), F32)
@@ -220,11 +227,11 @@
     operands = (*parts, *seeds)
     limit = 36 if len(parts) > 2 else 20
     return pl.pallas_call(
-        functools.partial(body, range(turns), block, chips, bool(seeds), samples),
+        functools.partial(body, range(turns), block, chips, bool(seeds), samples, window),
         out_shape=shapes,
         in_specs=[pl.BlockSpec(memory_space=pltpu.SMEM)] + whole_in_vmem(len(operands)),
         out_specs=whole_in_vmem(len(shapes)),
-        scratch_shapes=scratch + [pltpu.VMEM((TILE, 2 * samples), F32)],
+        scratch_shapes=scratch + [pltpu.VMEM((TILE, 2 * window[1]), F32)],
         compiler_params=pltpu.CompilerParams(vmem_limit_bytes=limit * MIB),
     )(place, *operands)
 
@@ -459,7 +466,8 @@
     acts_far = swap(acts, "expert", 1)
     near_acts = (acts, swap(acts, "dp", 1))
     act_seeds = bands(act_kernel, turns, act_groups, place, near_acts, (), *size)
-    grads_far = swap(grads_out, "expert", 1)
+    windows = [(0, samples // 2), (samples // 2, samples - samples // 2)]
+    grads_far = [swap(grads_out[first : first + count], "expert", 1) for first, count in windows]
     grad_parts = (grads_out, swap(grads_out, "dp", 1)) + near_acts
     grad_seeds = bands(grad_kernel, turns, grad_groups, place, grad_parts, (), *size)
     old_act, old_grad = own_band(old_act_factor), own_band(old_grad_factor)
@@ -469,12 +477,15 @@
     far_acts = (acts_far, swap(acts_far, "dp", 1))
     act_sum = PlaneSum(bands(act_kernel, turns, act_groups, place, far_acts, act_seeds, *size), chips)
     act_sum.send()
-    grads_far, act_sum.held = together(grads_far, act_sum.held)
-    grad_parts = (grads_far, swap(grads_far, "dp", 1)) + far_acts
+    grads_far[0], act_sum.held = together(grads_far[0], act_sum.held)
+    grad_parts = (grads_far[0], swap(grads_far[0], "dp", 1)) + far_acts
+    grad_seeds = bands(grad_kernel, turns, grad_groups, place, grad_parts, grad_seeds, *size, windows[0])
+    act_sum.got, grads_far[1], grad_seeds = together(act_sum.got, grads_far[1], grad_seeds)
+    grad_parts = (grads_far[1], swap(grads_far[1], "dp", 1)) + far_acts
     act_sum.add()
     grad_seeds, act_sum.leaving = together(grad_seeds, act_sum.leaving)
     act_sum.send()
-    pieces = bands(grad_kernel, turns, grad_groups, place, grad_parts, grad_seeds, *size)
+    pieces = bands(grad_kernel, turns, grad_groups, place, grad_parts, grad_seeds, *size, windows[1])
 
     grad_sum, mixed_sum, far_sum = [PlaneSum(pieces[first : first + 4], chips) for first in (0, 4, 8)]
     far_sum.send()

time: 188 us -> 190 us (1.011)
  waiting for transfers between devices: 103 us -> 107 us
  Pallas kernels: 35.3 us -> 37.6 us
  local copies, waits for them, and re-layouts: 6.21 us -> 4.1 us
    ppermute x41 -> x43, waiting for transfers between devices: 103 us -> 107 us  [swap(): return lax.ppermute(value, axis, [(i, i ^ step) for i in range(size)])]
    unnamed x19 -> x17, local copies, waits for them, and re-layouts: 2.7 us -> 0.16 us
    pallas_call x4 -> x5, Pallas kernels: 22.6 us -> 23.2 us  [bands(): pl.pallas_call(functools.partial(body, range(turns), block, chips, bool(s...]
    ppermute x41 -> x43, starting transfers between devices: 36.3 us -> 35.9 us  [swap(): return lax.ppermute(value, axis, [(i, i ^ step) for i in range(size)])]
  transfers between devices with their start and end apart: 41 -> 43, of which waited for: 15 -> 20; matrix products, arithmetic and copies ran while one was open for 3% -> 3% of each run, Pallas kernels for 16% -> 16%
where the time goes in v10:
time: 190 us; the launch traced here: 188 us
  waiting for transfers between devices  107 us (56%)
  Pallas kernels  37.6 us (20%)
  starting transfers between devices  35.9 us (19%)
  local copies, waits for them, and re-layouts  4.1 us (2%)
  other arithmetic  2.38 us (1%)
    ppermute x43, waiting for transfers between devices, swap(): return lax.ppermute(value, axis, [(i, i ^ step) for i in range(size)])  107 us
    ppermute x43, starting transfers between devices, swap(): return lax.ppermute(value, axis, [(i, i ^ step) for i in range(size)])  35.9 us
    pallas_call x5, Pallas kernels, bands(): pl.pallas_call(functools.partial(body, range(turns), block, chips, bool(s...  23.2 us
    pallas_call x3, Pallas kernels, on_core(): pl.pallas_call(body, out_shape=shapes, in_specs=[pl.BlockSpec(memory_spac...  12 us
  transfers between devices with their start and end apart: 43, of which 20 were waited for; matrix products, arithmetic and copies ran while one was open for 3% of the time, Pallas kernels for 16%

profile of v10, /device:TPU:25, one launch (start us, length us, event | category | flops | bytes accessed | tf_op | source)
XLA Modules:
  0.0 188.3 jit_solution(4743078775609580844)
XLA Ops:
  0.6 2.4 %shard_map.111.refs_0_.refs_2_ = f32[264,1024]{1,0:T(8,128)} custom-call(s32[2,256]{1,0:T(2,128)} %bitcast.102, s32[1,4]{1,0:T(1,128)} %counts_ref.1, f32[256,1024]{1,0:T(8,128)} %acts.1), custom_call_target="tpu_custom_call" | custom-call | tf_op jit(solution)/shard_map/pallas_call | solution.py:201
  4.3 1.8 slice.269
  7.3 3.7 %shard_map.112 = (f32[2,2,64,640]{3,2,1,0:T(8,128)S(1)}, f32[2,2,64,640]{3,2,1,0:T(8,128)S(1)}, f32[2,2,64,640]{3,2,1,0:T(8,128)S(1)}, f32[2,2,64,640]{3,2,1,0:T(8,128)S(1)}) custom-call(s32[2]{0:T(128)S(1)} %pad_add_fusion.place, f32[264,1024]{1,0:T(8,128)S(1)} %copy-done, f32[264,1024]{1,0:T(8,128)S(1)} %collective-permute-done.1.refs_1_.refs_3_), custom_call_target="tpu_custom_call" | custom-call | tf_op jit(solution)/shard_map/pallas_call | solution.py:229
  11.0 7.9 %shard_map.113 = (f32[2,1,64,640]{3,2,1,0:T(8,128)S(1)}, f32[2,1,64,640]{3,2,1,0:T(8,128)S(1)}, f32[2,1,64,640]{3,2,1,0:T(8,128)S(1)}, f32[2,1,64,640]{3,2,1,0:T...) custom-call(s32[2]{0:T(128)S(1)} %pad_add_fusion.place, ...), custom_call_target="tpu_custom_call" | custom-call | tf_op jit(solution)/shard_map/pallas_call | solution.py:229
  18.9 10.5 %collective-permute-done.refs_0_.refs_2_ = f32[264,1024]{1,0:T(8,128)S(1)} collective-permute-done((f32[264,1024]{1,0:T(8,128)}, f32[264,1024]{1,0:T(8,128)S(1)}, u32[]{:S(2)}, u32[]{:S(2)}) %collective-permute-start) | collective-permute-done | bytes 1081376 | tf_op jit(solution)/shard_map/ppermute | solution.py:374
  32.6 3.7 %shard_map.114 = (f32[2,2,64,640]{3,2,1,0:T(8,128)S(1)}, f32[2,2,64,640]{3,2,1,0:T(8,128)S(1)}, f32[2,2,64,640]{3,2,1,0:T(8,128)S(1)}, f32[2,2,64,640]{3,2,1,0:T(8,128)S(1)}) custom-call(s32[2]{0:T(128)S(1)} %pad_add_fusion.place, f32[264,1024]{1,0:T(8,128)S(1)} %collective-permute-done.refs_0_.refs_2_, ...), custom_call_target="tpu_custom_call" | custom-call | tf_op jit(solution)/shard_map/pallas_call | solution.py:229
  38.8 6.4 %collective-permute-done.3.refs_0_ = f32[128,1024]{1,0:T(8,128)S(1)} collective-permute-done((f32[128,1024]{1,0:T(8,128)S(1)}, f32[128,1024]{1,0:T(8,128)S(1)}, u32[]{:S(2)}, u32[]{:S(2)}) %collective-permute-start.3) | collective-permute-done | bytes 524320 | tf_op jit(solution)/shard_map/ppermute | solution.py:374
  47.5 4.1 %shard_map.115 = (f32[2,1,64,640]{3,2,1,0:T(8,128)S(1)}, f32[2,1,64,640]{3,2,1,0:T(8,128)S(1)}, f32[2,1,64,640]{3,2,1,0:T(8,128)S(1)}, f32[2,1,64,640]{3,2,1,0:T...) custom-call(s32[2]{0:T(128)S(1)} %pad_add_fusion.place, ...), custom_call_target="tpu_custom_call" | custom-call | tf_op jit(solution)/shard_map/pallas_call | solution.py:229
  51.6 7.9 %collective-permute-done.7.refs_0_ = f32[128,1024]{1,0:T(8,128)S(1)} collective-permute-done((f32[128,1024]{1,0:T(8,128)S(1)}, f32[128,1024]{1,0:T(8,128)S(1)}, u32[]{:S(2)}, u32[]{:S(2)}) %collective-permute-start.7) | collective-permute-done | bytes 524320 | tf_op jit(solution)/shard_map/ppermute | solution.py:374
  63.0 3.9 %shard_map.116 = (f32[2,1,64,640]{3,2,1,0:T(8,128)S(1)}, f32[2,1,64,640]{3,2,1,0:T(8,128)S(1)}, f32[2,1,64,640]{3,2,1,0:T(8,128)S(1)}, f32[2,1,64,640]{3,2,1,0:T...) custom-call(s32[2]{0:T(128)S(1)} %pad_add_fusion.place, ...), custom_call_target="tpu_custom_call" | custom-call | tf_op jit(solution)/shard_map/pallas_call | solution.py:229
  68.2 1.6 collective-permute-done.13
  71.0 17.1 %collective-permute-done.11 = f32[2,1,64,1664]{3,2,1,0:T(8,128)S(1)} collective-permute-done((f32[2,1,64,1664]{3,2,1,0:T(8,128)S(1)}, f32[2,1,64,1664]{3,2,1,0:T(8,128)S(1)}, u32[]{:S(2)}, u32[]{:S(2)}) %collective-permute-start.11) | collective-permute-done | bytes 852000 | tf_op jit(solution)/shard_map/ppermute | solution.py:374
  93.3 3.8 %collective-permute-done.15 = f32[2,1,64,640]{3,2,1,0:T(8,128)S(1)} collective-permute-done((f32[2,1,64,640]{3,2,1,0:T(8,128)S(1)}, f32[2,1,64,640]{3,2,1,0:T(8,128)S(1)}, u32[]{:S(2)}, u32[]{:S(2)}) %collective-permute-start.15) | collective-permute-done | bytes 327712 | tf_op jit(solution)/shard_map/ppermute | solution.py:374
  100.0 6.3 %collective-permute-done.18 = f32[1,1,64,1664]{3,2,1,0:T(8,128)S(1)} collective-permute-done((f32[1,1,64,1664]{3,2,1,0:T(8,128)S(1)}, f32[1,1,64,1664]{3,2,1,0:T(8,128)S(1)}, u32[]{:S(2)}, u32[]{:S(2)}) %collective-permute-start.18) | collective-permute-done | bytes 426016 | tf_op jit(solution)/shard_map/ppermute | solution.py:374
  108.1 15.9 %collective-permute-done.20 = f32[2,64,640]{2,1,0:T(8,128)S(1)} collective-permute-done((f32[2,64,640]{2,1,0:T(8,128)S(1)}, f32[2,64,640]{2,1,0:T(8,128)S(1)}, u32[]{:S(2)}, u32[]{:S(2)}) %collective-permute-start.20) | collective-permute-done | bytes 327712 | tf_op jit(solution)/shard_map/ppermute | solution.py:374
  127.5 4.1 %collective-permute-done.23 = f32[128,640]{1,0:T(8,128)S(1)} collective-permute-done((f32[128,640]{1,0:T(8,128)S(1)}, f32[128,640]{1,0:T(8,128)S(1)}, u32[]{:S(2)}, u32[]{:S(2)}) %collective-permute-start.23) | collective-permute-done | bytes 327712 | tf_op jit(solution)/shard_map/ppermute | solution.py:374
  131.6 5.6 %collective-permute-done.26 = f32[1,1,64,1024]{3,2,1,0:T(8,128)S(1)} collective-permute-done((f32[1,1,64,1024]{3,2,1,0:T(8,128)S(1)}, f32[1,1,64,1024]{3,2,1,0:T(8,128)S(1)}, u32[]{:S(2)}, u32[]{:S(2)}) %collective-permute-start.26) | collective-permute-done | bytes 262176 | tf_op jit(solution)/shard_map/ppermute | solution.py:374
  140.5 6.5 %collective-permute-done.36 = f32[64,640]{1,0:T(8,128)S(1)} collective-permute-done((f32[64,640]{1,0:T(8,128)S(1)}, f32[64,640]{1,0:T(8,128)S(1)}, u32[]{:S(2)}, u32[]{:S(2)}) %collective-permute-start.36) | collective-permute-done | bytes 163872 | tf_op jit(solution)/shard_map/ppermute | solution.py:374
  147.9 4.3 %collective-permute-start.38 = (f32[512,640]{1,0:T(8,128)S(1)}, f32[512,640]{1,0:T(8,128)S(1)}, u32[]{:S(2)}, u32[]{:S(2)}) collective-permute-start(f32[512,640]{1,0:T(8,128)S(1)} %constant_dynamic-update-slice_fusion.8.refs_0_), channel_id=1, source_target_pairs={{0,4},{4,0},{8,12},{12,8},{16,20},{20,16},{24,28},{28,24},{1,5},{5... | collective-permute-start | bytes 3932168 | tf_op jit(solution)/shard_map/ppermute | solution.py:374
  155.7 13.9 %collective-permute-done.30 = f32[64,640]{1,0:T(8,128)S(1)} collective-permute-done((f32[64,640]{1,0:T(8,128)S(1)}, f32[64,640]{1,0:T(8,128)S(1)}, u32[]{:S(2)}, u32[]{:S(2)}) %collective-permute-start.30) | collective-permute-done | bytes 163872 | tf_op jit(solution)/shard_map/ppermute | solution.py:374
  173.4 2.6 %shard_map.117 = (f32[128,1024]{1,0:T(8,128)}, f32[8,128]{1,0:T(8,128)S(1)}, bf16[1024,1024]{1,0:T(8,128)(2,1)S(1)}, bf16[1024,1024]{1,0:T(8,128)(2,1)S(1)}) custom-call(s32[2]{0:T(128)S(1)} %pad_add_fusion.place, f32[512,640]{1,0:T(8,128)S(1)} %constant_dynamic-update-slice_fusion.2.refs_0_, f32[512,640]{1,0:T(8,128)S(1)} %collective-permute-done.35.refs_1_), custom_call_target="tpu_custom_call" | custom-call | tf_op jit(solution)/shard_map/pallas_call | solution.py:341
  176.1 3.7 %shard_map.118 = (f32[128,1024]{1,0:T(8,128)}, f32[128,1024]{1,0:T(8,128)S(1)}) custom-call(s32[2]{0:T(128)S(1)} %pad_add_fusion.place, f32[512,640]{1,0:T(8,128)S(1)} %constant_dynamic-update-slice_fusion.8.refs_0_, f32[512,640]{1,0:T(8,128)S(1)} %collective-permute-done.38.refs_1_), custom_call_target="tpu_custom_call" | custom-call | tf_op jit(solution)/shard_map/pallas_call | solution.py:341
  181.1 1.5 collective-permute-done.42.refs_3_
  182.6 5.7 %shard_map.119 = (f32[128,1024]{1,0:T(8,128)}, f32[128,1024]{1,0:T(8,128)}) custom-call(s32[2]{0:T(128)S(1)} %pad_add_fusion.place, f32[384,1024]{1,0:T(8,128)S(1)} %slice_dynamic-update-slice_fusion.refs_0_, f32[128,1024]{1,0:T(8,128)S(1)} %constant_dynamic-update-slice_fusion.18.refs_1_, f32[384,1024]{1,0:T(8,128)S(1)} %collective-permute-done.41.refs_2_, ...), custom_call_target="tpu_custom_call" | custom-call | tf_op jit(solution)/shard_map/pallas_call | solution.py:341
  (134 shorter events, 41.6 us)
Async XLA Ops:
  3.7 25.7 %collective-permute-start = (f32[264,1024]{1,0:T(8,128)}, f32[264,1024]{1,0:T(8,128)S(1)}, u32[]{:S(2)}, u32[]{:S(2)}) collective-permute-start(f32[264,1024]{1,0:T(8,128)} %shard_map.111.refs_0_.refs_2_), channel_id=1, source_target_pairs={{0,1},{1,0},{2,3},{3,2},{4,5},{5,4},{6,7},{7,6},{8,9},{9,8},{10,11... | collective-permute-start | bytes 3244040 | tf_op jit(solution)/shard_map/ppermute | solution.py:374
  31.6 13.6 %collective-permute-start.3 = (f32[128,1024]{1,0:T(8,128)S(1)}, f32[128,1024]{1,0:T(8,128)S(1)}, u32[]{:S(2)}, u32[]{:S(2)}) collective-permute-start(f32[128,1024]{1,0:T(8,128)S(1)} %get-tuple-element.302), channel_id=1, source_target_pairs={{0,1},{1,0},{2,3},{3,2},{4,5},{5,4},{6,7},{7,6},{8,9},{9,8},{10,11... | collective-permute-start | bytes 1572872 | tf_op jit(solution)/shard_map/ppermute | solution.py:374
  36.3 23.2 %collective-permute-start.5 = (f32[2,2,64,640]{3,2,1,0:T(8,128)S(1)}, f32[2,2,64,640]{3,2,1,0:T(8,128)S(1)}, u32[]{:S(2)}, u32[]{:S(2)}) collective-permute-start(f32[2,2,64,640]{3,2,1,0:T(8,128)S(1)} %get-tuple-element.172), channel_id=1, source_target_pairs={{0,8},{4,12},{8,0},{12,4},{16,24},{20,28},{24,16},{28,20},{1,9},{5... | collective-permute-start | bytes 1966088 | tf_op jit(solution)/shard_map/ppermute | solution.py:374
  37.6 21.9 %collective-permute-start.6 = (f32[2,2,64,640]{3,2,1,0:T(8,128)S(1)}, f32[2,2,64,640]{3,2,1,0:T(8,128)S(1)}, u32[]{:S(2)}, u32[]{:S(2)}) collective-permute-start(f32[2,2,64,640]{3,2,1,0:T(8,128)S(1)} %get-tuple-element.173), channel_id=1, source_target_pairs={{0,16},{4,20},{8,24},{12,28},{16,0},{20,4},{24,8},{28,12},{1,17},{... | collective-permute-start | bytes 1966088 | tf_op jit(solution)/shard_map/ppermute | solution.py:374
  46.0 13.6 %collective-permute-start.7 = (f32[128,1024]{1,0:T(8,128)S(1)}, f32[128,1024]{1,0:T(8,128)S(1)}, u32[]{:S(2)}, u32[]{:S(2)}) collective-permute-start(f32[128,1024]{1,0:T(8,128)S(1)} %get-tuple-element.303), channel_id=1, source_target_pairs={{0,1},{1,0},{2,3},{3,2},{4,5},{5,4},{6,7},{7,6},{8,9},{9,8},{10,11... | collective-permute-start | bytes 1572872 | tf_op jit(solution)/shard_map/ppermute | solution.py:374
  66.9 21.2 %collective-permute-start.11 = (f32[2,1,64,1664]{3,2,1,0:T(8,128)S(1)}, f32[2,1,64,1664]{3,2,1,0:T(8,128)S(1)}, u32[]{:S(2)}, u32[]{:S(2)}) collective-permute-start(f32[2,1,64,1664]{3,2,1,0:T(8,128)S(1)} %get-tuple-element.234), channel_id=1, source_target_pairs={{0,8},{4,12},{8,0},{12,4},{16,24},{20,28},{24,16},{28,20},{1,9},{5... | collective-permute-start | bytes 2555912 | tf_op jit(solution)/shard_map/ppermute | solution.py:374
  67.2 21.8 %collective-permute-start.12 = (f32[2,1,64,1664]{3,2,1,0:T(8,128)S(1)}, f32[2,1,64,1664]{3,2,1,0:T(8,128)S(1)}, u32[]{:S(2)}, u32[]{:S(2)}) collective-permute-start(f32[2,1,64,1664]{3,2,1,0:T(8,128)S(1)} %get-tuple-element.235), channel_id=1, source_target_pairs={{0,16},{4,20},{8,24},{12,28},{16,0},{20,4},{24,8},{28,12},{1,17},{... | collective-permute-start | bytes 2555912 | tf_op jit(solution)/shard_map/ppermute | solution.py:374
  70.9 19.8 %collective-permute-start.14 = (f32[2,64,640]{2,1,0:T(8,128)S(1)}, f32[2,64,640]{2,1,0:T(8,128)S(1)}, u32[]{:S(2)}, u32[]{:S(2)}) collective-permute-start(f32[2,64,640]{2,1,0:T(8,128)S(1)} %maximum_bitcast_fusion), channel_id=1, source_target_pairs={{0,2},{1,3},{2,0},{3,1},{4,6},{5,7},{6,4},{7,5},{8,10},{9,11},{10,... | collective-permute-start | bytes 983048 | tf_op jit(solution)/shard_map/ppermute | solution.py:374
  91.3 15.1 %collective-permute-start.18 = (f32[1,1,64,1664]{3,2,1,0:T(8,128)S(1)}, f32[1,1,64,1664]{3,2,1,0:T(8,128)S(1)}, u32[]{:S(2)}, u32[]{:S(2)}) collective-permute-start(f32[1,1,64,1664]{3,2,1,0:T(8,128)S(1)} %slice_add_fusion.1), channel_id=1, source_target_pairs={{0,16},{4,20},{8,24},{12,28},{16,0},{20,4},{24,8},{28,12},{1,17},{... | collective-permute-start | bytes 1277960 | tf_op jit(solution)/shard_map/ppermute | solution.py:374
  91.5 16.2 %collective-permute-start.19 = (f32[1,1,64,1664]{3,2,1,0:T(8,128)S(1)}, f32[1,1,64,1664]{3,2,1,0:T(8,128)S(1)}, u32[]{:S(2)}, u32[]{:S(2)}) collective-permute-start(f32[1,1,64,1664]{3,2,1,0:T(8,128)S(1)} %slice_add_fusion), channel_id=1, source_target_pairs={{0,8},{4,12},{8,0},{12,4},{16,24},{20,28},{24,16},{28,20},{1,9},{5... | collective-permute-start | bytes 1277960 | tf_op jit(solution)/shard_map/ppermute | solution.py:374
  97.3 26.7 %collective-permute-start.17 = (f32[1,1,64,640]{3,2,1,0:T(8,128)S(1)}, f32[1,1,64,640]{3,2,1,0:T(8,128)S(1)}, u32[]{:S(2)}, u32[]{:S(2)}) collective-permute-start(f32[1,1,64,640]{3,2,1,0:T(8,128)S(1)} %slice_add_fusion.10), channel_id=1, source_target_pairs={{0,16},{4,20},{8,24},{12,28},{16,0},{20,4},{24,8},{28,12},{1,17},{... | collective-permute-start | bytes 491528 | tf_op jit(solution)/shard_map/ppermute | solution.py:374
  98.6 25.5 %collective-permute-start.21 = (f32[1,1,64,640]{3,2,1,0:T(8,128)S(1)}, f32[1,1,64,640]{3,2,1,0:T(8,128)S(1)}, u32[]{:S(2)}, u32[]{:S(2)}) collective-permute-start(f32[1,1,64,640]{3,2,1,0:T(8,128)S(1)} %slice_add_fusion.9), channel_id=1, source_target_pairs={{0,8},{4,12},{8,0},{12,4},{16,24},{20,28},{24,16},{28,20},{1,9},{5... | collective-permute-start | bytes 491528 | tf_op jit(solution)/shard_map/ppermute | solution.py:374
  99.6 25.8 %collective-permute-start.24 = (f32[2,1,64,1024]{3,2,1,0:T(8,128)S(1)}, f32[2,1,64,1024]{3,2,1,0:T(8,128)S(1)}, u32[]{:S(2)}, u32[]{:S(2)}) collective-permute-start(f32[2,1,64,1024]{3,2,1,0:T(8,128)S(1)} %get-tuple-element.257), channel_id=1, source_target_pairs={{0,8},{4,12},{8,0},{12,4},{16,24},{20,28},{24,16},{28,20},{1,9},{5... | collective-permute-start | bytes 1572872 | tf_op jit(solution)/shard_map/ppermute | solution.py:374
  106.4 19.1 %collective-permute-start.25 = (f32[2,1,64,1024]{3,2,1,0:T(8,128)S(1)}, f32[2,1,64,1024]{3,2,1,0:T(8,128)S(1)}, u32[]{:S(2)}, u32[]{:S(2)}) collective-permute-start(f32[2,1,64,1024]{3,2,1,0:T(8,128)S(1)} %get-tuple-element.259), channel_id=1, source_target_pairs={{0,16},{4,20},{8,24},{12,28},{16,0},{20,4},{24,8},{28,12},{1,17},{... | collective-permute-start | bytes 1572872 | tf_op jit(solution)/shard_map/ppermute | solution.py:374
  107.9 16.1 %collective-permute-start.20 = (f32[2,64,640]{2,1,0:T(8,128)S(1)}, f32[2,64,640]{2,1,0:T(8,128)S(1)}, u32[]{:S(2)}, u32[]{:S(2)}) collective-permute-start(f32[2,64,640]{2,1,0:T(8,128)S(1)} %maximum_bitcast_fusion.1), channel_id=1, source_target_pairs={{0,2},{1,3},{2,0},{3,1},{4,6},{5,7},{6,4},{7,5},{8,10},{9,11},{10,... | collective-permute-start | bytes 983048 | tf_op jit(solution)/shard_map/ppermute | solution.py:374
  125.5 11.7 %collective-permute-start.26 = (f32[1,1,64,1024]{3,2,1,0:T(8,128)S(1)}, f32[1,1,64,1024]{3,2,1,0:T(8,128)S(1)}, u32[]{:S(2)}, u32[]{:S(2)}) collective-permute-start(f32[1,1,64,1024]{3,2,1,0:T(8,128)S(1)} %slice_add_fusion.7), channel_id=1, source_target_pairs={{0,16},{4,20},{8,24},{12,28},{16,0},{20,4},{24,8},{28,12},{1,17},{... | collective-permute-start | bytes 786440 | tf_op jit(solution)/shard_map/ppermute | solution.py:374
  127.4 24.8 %collective-permute-start.32 = (f32[2,64,1024]{2,1,0:T(8,128)S(1)}, f32[2,64,1024]{2,1,0:T(8,128)S(1)}, u32[]{:S(2)}, u32[]{:S(2)}) collective-permute-start(f32[2,64,1024]{2,1,0:T(8,128)S(1)} %bitcast.101), channel_id=1, source_target_pairs={{0,2},{1,3},{2,0},{3,1},{4,6},{5,7},{6,4},{7,5},{8,10},{9,11},{10,... | collective-permute-start | bytes 1572872 | tf_op jit(solution)/shard_map/ppermute | solution.py:374
  137.2 15.0 %collective-permute-start.29 = (f32[128,640]{1,0:T(8,128)S(1)}, f32[128,640]{1,0:T(8,128)S(1)}, u32[]{:S(2)}, u32[]{:S(2)}) collective-permute-start(f32[128,640]{1,0:T(8,128)S(1)} %get-tuple-element.318), channel_id=1, source_target_pairs={{0,16},{4,20},{8,24},{12,28},{16,0},{20,4},{24,8},{28,12},{1,17},{... | collective-permute-start | bytes 983048 | tf_op jit(solution)/shard_map/ppermute | solution.py:374
  138.5 13.7 %collective-permute-start.28 = (f32[128,640]{1,0:T(8,128)S(1)}, f32[128,640]{1,0:T(8,128)S(1)}, u32[]{:S(2)}, u32[]{:S(2)}) collective-permute-start(f32[128,640]{1,0:T(8,128)S(1)} %get-tuple-element.318), channel_id=1, source_target_pairs={{0,8},{4,12},{8,0},{12,4},{16,24},{20,28},{24,16},{28,20},{1,9},{5... | collective-permute-start | bytes 983048 | tf_op jit(solution)/shard_map/ppermute | solution.py:374
  147.9 28.1 %collective-permute-start.38 = (f32[512,640]{1,0:T(8,128)S(1)}, f32[512,640]{1,0:T(8,128)S(1)}, u32[]{:S(2)}, u32[]{:S(2)}) collective-permute-start(f32[512,640]{1,0:T(8,128)S(1)} %constant_dynamic-update-slice_fusion.8.refs_0_), channel_id=1, source_target_pairs={{0,4},{4,0},{8,12},{12,8},{16,20},{20,16},{24,28},{28,24},{1,5},{5... | collective-permute-start | bytes 3932168 | tf_op jit(solution)/shard_map/ppermute | solution.py:374
  152.4 17.1 %collective-permute-start.34 = (f32[128,1024]{1,0:T(8,128)S(1)}, f32[128,1024]{1,0:T(8,128)S(1)}, u32[]{:S(2)}, u32[]{:S(2)}) collective-permute-start(f32[128,1024]{1,0:T(8,128)S(1)} %pad_maximum_fusion.1), channel_id=1, source_target_pairs={{0,16},{4,20},{8,24},{12,28},{16,0},{20,4},{24,8},{28,12},{1,17},{... | collective-permute-start | bytes 1572872 | tf_op jit(solution)/shard_map/ppermute | solution.py:374
  152.8 16.8 %collective-permute-start.33 = (f32[128,1024]{1,0:T(8,128)S(1)}, f32[128,1024]{1,0:T(8,128)S(1)}, u32[]{:S(2)}, u32[]{:S(2)}) collective-permute-start(f32[128,1024]{1,0:T(8,128)S(1)} %pad_maximum_fusion.1), channel_id=1, source_target_pairs={{0,8},{4,12},{8,0},{12,4},{16,24},{20,28},{24,16},{28,20},{1,9},{5... | collective-permute-start | bytes 1572872 | tf_op jit(solution)/shard_map/ppermute | solution.py:374
  153.6 15.9 %collective-permute-start.30 = (f32[64,640]{1,0:T(8,128)S(1)}, f32[64,640]{1,0:T(8,128)S(1)}, u32[]{:S(2)}, u32[]{:S(2)}) collective-permute-start(f32[64,640]{1,0:T(8,128)S(1)} %get-tuple-element.314), channel_id=1, source_target_pairs={{0,16},{4,20},{8,24},{12,28},{16,0},{20,4},{24,8},{28,12},{1,17},{... | collective-permute-start | bytes 491528 | tf_op jit(solution)/shard_map/ppermute | solution.py:374
  154.9 14.6 %collective-permute-start.31 = (f32[64,640]{1,0:T(8,128)S(1)}, f32[64,640]{1,0:T(8,128)S(1)}, u32[]{:S(2)}, u32[]{:S(2)}) collective-permute-start(f32[64,640]{1,0:T(8,128)S(1)} %get-tuple-element.312), channel_id=1, source_target_pairs={{0,8},{4,12},{8,0},{12,4},{16,24},{20,28},{24,16},{28,20},{1,9},{5... | collective-permute-start | bytes 491528 | tf_op jit(solution)/shard_map/ppermute | solution.py:374
  (23 other events, 148.4 us)

commit v11 on v9

--- a/solution.py
+++ b/solution.py
@@ -10,6 +10,7 @@
 F32 = jnp.float32
 BF16 = jnp.bfloat16
 TILE = 128
+EXTRA = 8
 MIB = 1024 * 1024
 
 
@@ -94,11 +95,36 @@
     return places
 
 
-def store(outs, seeds, group, place, number, columns, value):
+def pack(band, row, count):
+    block, width = band.shape[0], band.shape[1] - TILE
+    rows = lax.broadcasted_iota(jnp.int32, (block, TILE), 0) + row
+    columns = lax.broadcasted_iota(jnp.int32, (block, TILE), 1)
+    last = band[:, width:]
+    first = jnp.where(rows > columns, last, band[:, 0:TILE])
+    diagonal = jnp.sum(jnp.where(rows == columns, last, 0.0), axis=0, keepdims=True)
+    places = lax.broadcasted_iota(jnp.int32, (EXTRA, TILE), 0)
+    extra = jnp.where(places == 0, diagonal, jnp.where(places == 1, count, 0.0))
+    extra = jnp.concatenate([extra, jnp.zeros((EXTRA, width - TILE), F32)], axis=1)
+    packed = jnp.concatenate([first, band[:, TILE:width]], axis=1)
+    return packed[0 : block // 2], jnp.concatenate([packed[block // 2 :], extra], axis=0)
+
+
+def piece_shape(kind, half, block, feat):
+    step, width = block // 2, feat // 2
+    factor = step + EXTRA * half
+    if kind == "factor":
+        return factor, width
+    if kind == "mixed":
+        return step, feat
+    return factor + step * (feat // width), width
+
+
+def store(outs, seeds, group, place, number, first, value):
     output, position = 4 * group + place[0], place[1]
+    here = slice(first, first + value.shape[0])
     if seeds:
-        value = value + seeds[output][position, number, :, columns]
-    outs[output][position, number, :, columns] = value
+        value = value + seeds[output][position, number, here, :]
+    outs[output][position, number, here, :] = value
 
 
 def prepare_kernel(routes_ref, counts_ref, acts, out, routes, counts, sems):
@@ -136,24 +162,20 @@
     refs, (high, low, turned) = refs[:-3], refs[-3:]
     seeds, outs = (refs[: len(refs) // 2], refs[len(refs) // 2 :]) if seeded else ((), refs)
     feat = parts[0].shape[1]
-    width = outs[0].shape[3]
+    width = feat // 2 + TILE
     mine, expert = place[0], place[1]
     split_rows(parts, samples, high, low, feat)
     keeps = [keep_row(parts, samples, expert ^ (2 * turn)) for turn in turns]
     places = slots(chips)
-    rows = lax.broadcasted_iota(jnp.int32, (block, width), 0)
-    columns = lax.broadcasted_iota(jnp.int32, (block, width), 1)
-    corner = jnp.logical_and(rows == block - 1, columns == 0)
     for k in range(chips):
         column, row = band_place(mine ^ (2 * k), block)
         both, tops = weighted(left_rows(parts, samples, turned, column, row, block), keeps)
         total = three(both, tops, high[:, pl.ds(column, width)], low[:, pl.ds(column, width)])
         for number, keep in enumerate(keeps):
             count = jnp.sum(keep, axis=1, keepdims=True)
-            value = jnp.where(corner, count, total[number * block : (number + 1) * block])
+            packed = pack(total[number * block : (number + 1) * block], row, count)
             for half in range(2):
-                here = value[half * (block // 2) : (half + 1) * (block // 2)]
-                store(outs, seeds, 0, places[k, half], number, slice(0, width), here)
+                store(outs, seeds, 0, places[k, half], number, 0, packed[half])
 
 
 def grad_kernel(turns, block, chips, seeded, samples, place, *refs):
@@ -161,7 +183,7 @@
     refs, (high, low, act_high, act_low, turned) = refs[:-5], refs[-5:]
     seeds, outs = (refs[: len(refs) // 2], refs[len(refs) // 2 :]) if seeded else ((), refs)
     feat = grads[0].shape[1]
-    width = outs[0].shape[3]
+    step, width = block // 2, feat // 2
     mine, expert = place[0], place[1]
     split_rows(grads, samples, high, low, feat)
     split_rows(acts, samples, act_high, act_low, feat)
@@ -170,19 +192,24 @@
     for k in range(chips):
         column, row = band_place(mine ^ (2 * k), block)
         both, tops = weighted(left_rows(grads, samples, turned, column, row, block), keeps)
-        total = three(both, tops, high[:, pl.ds(column, width)], low[:, pl.ds(column, width)])
+        here = pl.ds(column, width + TILE)
+        total = three(both, tops, high[:, here], low[:, here])
         mixed = three(both, tops, act_high[...], act_low[...])
         for number in range(len(keeps)):
+            packed = pack(total[number * block : (number + 1) * block], row, 0.0)
             for half in range(2):
-                first = number * block + half * (block // 2)
-                here = slice(first, first + block // 2)
-                place = places[k, half]
+                spot = places[k, half]
+                first = number * block + half * step
+                value = mixed[first : first + step]
                 if number:
-                    store(outs, seeds, 2, place, number - 1, slice(0, width), total[here])
-                    store(outs, seeds, 2, place, number - 1, slice(width, width + feat), mixed[here])
+                    store(outs, seeds, 2, spot, number - 1, 0, packed[half])
+                    for part in range(feat // width):
+                        below = packed[half].shape[0] + part * step
+                        columns = slice(part * width, (part + 1) * width)
+                        store(outs, seeds, 2, spot, number - 1, below, value[:, columns])
                 else:
-                    store(outs, seeds, 0, place, 0, slice(0, width), total[here])
-                    store(outs, seeds, 1, place, 0, slice(0, feat), mixed[here])
+                    store(outs, seeds, 0, spot, 0, 0, packed[half])
+                    store(outs, seeds, 1, spot, 0, 0, value)
 
 
 def whole_in_vmem(count):
@@ -202,7 +229,7 @@
             pltpu.SMEM(counts.shape, jnp.int32),
             pltpu.SemaphoreType.DMA((3,)),
         ],
-        compiler_params=pltpu.CompilerParams(vmem_limit_bytes=16 * MIB),
+        compiler_params=pltpu.CompilerParams(vmem_limit_bytes=60 * MIB),
     )(routes.T, counts, acts)
 
 
@@ -212,9 +239,9 @@
     plain = pltpu.VMEM((2 * samples, feat), BF16)
     scratch = [extended, extended] + ([plain, plain] if len(parts) > 2 else [])
     shapes = [
-        jax.ShapeDtypeStruct((len(group), count, block // 2, width), F32)
-        for count, width in groups
-        for order in orders(chips)
+        jax.ShapeDtypeStruct((len(group), count, *piece_shape(kind, half, block, feat)), F32)
+        for count, kind in groups
+        for half, order in enumerate(orders(chips))
         for group in held_and_sent(chips, order)
     ]
     operands = (*parts, *seeds)
@@ -229,18 +256,30 @@
     )(place, *operands)
 
 
-def unfold(bands, full):
+def unfold(bands, extras, full):
     tiles = full.shape[0] // TILE
-    first_column = lax.broadcasted_iota(jnp.int32, (TILE, TILE), 1) == 0
+    per_tile = extras.shape[0] // EXTRA // tiles
+    rows = lax.broadcasted_iota(jnp.int32, (TILE, TILE), 0)
+    columns = lax.broadcasted_iota(jnp.int32, (TILE, TILE), 1)
+
+    def put(i, j, value):
+        full[i * TILE : (i + 1) * TILE, j * TILE : (j + 1) * TILE] = value
+
+    firsts = [bands[i * TILE : (i + 1) * TILE, 0:TILE] for i in range(tiles)]
+    turned = [value.T for value in firsts]
     for i in range(tiles):
-        for step in range(tiles // 2 + 1):
-            j = (i + step) % tiles
+        put(i, i, jnp.where(rows <= columns, firsts[i], turned[i]))
+        for step in range(1, tiles // 2):
             here = bands[i * TILE : (i + 1) * TILE, step * TILE : (step + 1) * TILE]
-            if step == 0:
-                here = jnp.where(first_column, here.T, here)
-            full[i * TILE : (i + 1) * TILE, j * TILE : (j + 1) * TILE] = here
-            if 0 < step < tiles // 2:
-                full[j * TILE : (j + 1) * TILE, i * TILE : (i + 1) * TILE] = here.T
+            put(i, (i + step) % tiles, here)
+            put((i + step) % tiles, i, here.T)
+    for i in range(tiles // 2):
+        j = i + tiles // 2
+        places = [EXTRA * (i * per_tile + owner) for owner in range(per_tile)]
+        diagonal = sum(extras[place : place + 1, :] for place in places)
+        here = jnp.where(rows > columns, firsts[i], jnp.where(rows < columns, turned[j], diagonal))
+        put(i, j, here)
+        put(j, i, here.T)
 
 
 def damping(full):
@@ -268,31 +307,36 @@
     return offsets
 
 
-def row_pieces(place, block, chips, arrays):
+def row_pieces(place, block, chips, arrays, extra):
     step = block // 2
-    blocks = [
-        value[first : first + block, :] for value in arrays for first in range(0, value.shape[0], block)
-    ]
-    pieces = []
-    for number, value in enumerate(blocks):
+    firsts = [(value, first) for value in arrays for first in range(0, value.shape[0], block + extra)]
+    pieces, extras = [], []
+    for number, (value, first) in enumerate(firsts):
         core, position = number // chips, number % chips
         for half, order in enumerate(orders(chips)):
             owner = place[0] ^ (2 * gather_order(order)[position] + core)
             here = pl.ds(pl.multiple_of(owner * block + half * step, step), step)
-            pieces.append((here, value[half * step : (half + 1) * step, :]))
-    return pieces
-
-
-def factor_rows(place, block, blocks, bands, full):
-    for here, value in row_pieces(place, block, bands.shape[0] // (2 * block), blocks):
-        bands[here, :] = value
-    unfold(bands, full)
+            pieces.append((here, value.at[first + half * step : first + (half + 1) * step]))
+        if extra:
+            here = pl.ds(pl.multiple_of(owner * EXTRA, EXTRA), EXTRA)
+            extras.append((here, value.at[first + block : first + block + extra]))
+    return pieces, extras
+
+
+def factor_rows(place, block, blocks, bands, extras, full):
+    chips = full.shape[0] // (2 * block)
+    pieces, others = row_pieces(place, block, chips, blocks, EXTRA)
+    for here, value in pieces:
+        bands[here, :] = value[...]
+    for here, value in others:
+        extras[here, :] = value[:, 0:TILE]
+    unfold(bands, extras, full)
     return full[pl.ds(pl.multiple_of(place[0] * block, block), block), :]
 
 
 def act_factor_kernel(place, *refs):
-    blocks, (factor, scales, high, low), (bands, full) = refs[:-6], refs[-6:-2], refs[-2:]
-    factor[...] = factor_rows(place, factor.shape[0], blocks, bands, full)
+    blocks, (factor, scales, high, low), (bands, extras, full) = refs[:-7], refs[-7:-3], refs[-3:]
+    factor[...] = factor_rows(place, factor.shape[0], blocks, bands, extras, full)
     damp, alpha = damping(full)
     scales[0:1, :] = jnp.broadcast_to(damp, (1, TILE))
     scales[1:2, :] = jnp.broadcast_to(alpha, (1, TILE))
@@ -300,9 +344,9 @@
 
 
 def grad_factor_kernel(place, *refs):
-    blocks, (factor, inverse), (bands, full, high, low) = refs[:-6], refs[-6:-4], refs[-4:]
+    blocks, (factor, inverse), (bands, extras, full, high, low) = refs[:-7], refs[-7:-5], refs[-5:]
     block, feat = factor.shape
-    rows = factor_rows(place, block, blocks, bands, full)
+    rows = factor_rows(place, block, blocks, bands, extras, full)
     factor[...] = rows
     damp, alpha = damping(full)
     high[...], low[...] = split(full[...])
@@ -318,8 +362,8 @@
     blocks = refs[:-9]
     inverse, scales, act_high, act_low, momentum, weights, moment_out, weight_out, full = refs[-9:]
     block = momentum.shape[0]
-    for here, value in row_pieces(place, block, full.shape[0] // (2 * block), blocks):
-        full[here, :] = value
+    for here, value in row_pieces(place, block, full.shape[0] // (2 * block), blocks, 0)[0]:
+        full[here, :] = value[...]
     damp, alpha = scales[0:1, 0:1], scales[1:2, 0:1]
     half_way = times(inverse[...], *split(full[...]))
     value = half_way
@@ -341,16 +385,21 @@
     )(place, *operands)
 
 
+def factor_scratch(block, feat):
+    shapes = [(feat, feat // 2), (EXTRA * feat // block, TILE), (feat, feat)]
+    return [pltpu.VMEM(shape, F32) for shape in shapes]
+
+
 def act_factor_rows(place, blocks, block, feat):
     shapes = [((block, feat), F32), ((8, TILE), F32), ((feat, feat), BF16), ((feat, feat), BF16)]
     shapes = [jax.ShapeDtypeStruct(*shape) for shape in shapes]
-    scratch = [pltpu.VMEM((feat, blocks[0].shape[1]), F32), pltpu.VMEM((feat, feat), F32)]
+    scratch = factor_scratch(block, feat)
     return on_core(act_factor_kernel, place, blocks, shapes, scratch, 32)
 
 
 def grad_factor_rows(place, blocks, block, feat):
     shapes = [jax.ShapeDtypeStruct((block, feat), F32)] * 2
-    scratch = [pltpu.VMEM((feat, blocks[0].shape[1]), F32), pltpu.VMEM((feat, feat), F32)]
+    scratch = factor_scratch(block, feat)
     scratch += [pltpu.VMEM((feat, feat), BF16)] * 2
     return on_core(grad_factor_kernel, place, blocks, shapes, scratch, 32)
 
@@ -409,14 +458,14 @@
         self.whole = {order[0]: swap(block, "dp", 2 << order[0]) for order in self.orders}
 
     def relay(self):
-        step = self.halves[0].shape[0]
+        first = self.halves[0].shape[0]
         self.held = []
         for half, order in enumerate(self.orders):
             held = [self.halves[half]]
             for bit in order:
                 came = [swap(value, "dp", 2 << bit) for value in held[1:]]
                 if bit in self.whole:
-                    own = self.whole[bit][half * step : (half + 1) * step]
+                    own = self.whole[bit][first:] if half else self.whole[bit][:first]
                 else:
                     own = swap(held[0], "dp", 2 << bit)
                 held += [own] + came
@@ -441,19 +490,20 @@
     devices, experts = lax.axis_size("dp"), lax.axis_size("expert")
     chips = devices // 2
     samples, feat, block = acts.shape[0], acts.shape[1], weights.shape[1]
-    width = feat // 2 + TILE
+    step, width = block // 2, feat // 2
     mine = lax.axis_index("dp")
     place = jnp.stack([mine, lax.axis_index("expert")]).astype(jnp.int32)
 
     def own_band(old):
         start = mine * block // TILE * TILE
-        wide = jnp.concatenate([old[0], old[0][:, 0 : width - TILE]], axis=1)
-        return 0.5 * lax.dynamic_slice_in_dim(wide, start, width, 1)
+        wide = jnp.concatenate([old[0], old[0][:, 0:width]], axis=1)
+        band = lax.dynamic_slice_in_dim(wide, start, width + TILE, 1)
+        return [0.5 * half for half in pack(band, mine * block - start, 0.0)]
 
     turns = experts // 2
     size = (samples, chips, block)
-    act_groups = ((turns, width),)
-    grad_groups = ((1, width), (1, feat), (turns - 1, width + feat))
+    act_groups = ((turns, "factor"),)
+    grad_groups = ((1, "factor"), (1, "mixed"), (turns - 1, "both"))
 
     acts = prepare(routes, counts, acts)
     acts_far = swap(acts, "expert", 1)
@@ -469,19 +519,18 @@
     far_acts = (acts_far, swap(acts_far, "dp", 1))
     act_sum = PlaneSum(bands(act_kernel, turns, act_groups, place, far_acts, act_seeds, *size), chips)
     act_sum.send()
-    grads_far, act_sum.held = together(grads_far, act_sum.held)
+    act_sum.add()
+    act_sum.send()
+    grads_far, _ = together(grads_far, act_sum.leaving)
     grad_parts = (grads_far, swap(grads_far, "dp", 1)) + far_acts
-    act_sum.add()
-    grad_seeds, act_sum.leaving = together(grad_seeds, act_sum.leaving)
-    act_sum.send()
     pieces = bands(grad_kernel, turns, grad_groups, place, grad_parts, grad_seeds, *size)
 
     grad_sum, mixed_sum, far_sum = [PlaneSum(pieces[first : first + 4], chips) for first in (0, 4, 8)]
     far_sum.send()
-    act_sum.held, far_sum.held = together(act_sum.held, far_sum.held)
+    act_sum.got, far_sum.held = together(act_sum.got, far_sum.held)
     act_sum.add()
     act_sums = act_sum.finish()
-    act_across = across(jnp.stack([value[1:] for value in act_sums], axis=1))
+    act_across = across(jnp.concatenate([value[1:] for value in act_sums], axis=1))
     grad_sum.leaving, far_sum.got = together(grad_sum.leaving, far_sum.got)
     grad_sum.send()
     far_sum.add()
@@ -494,15 +543,21 @@
     far_sum.add()
     far_sums = far_sum.finish()
 
-    step = block // 2
-    parts = [slice(half * step, (half + 1) * step) for half in range(2)]
+    factors = [slice(0, step), slice(step, block + EXTRA)]
     act_totals = [
-        sum((there[half] for there in act_across), value[0]) for half, value in enumerate(act_sums)
+        sum((there[factors[half]] for there in act_across), value[0]) for half, value in enumerate(act_sums)
     ]
-    total = jnp.maximum(act_totals[1][-1:, 0:1], 1.0)
-    act_halves = [old_act[here] + 0.5 * (value / total) for here, value in zip(parts, act_totals)]
-    across_grad = across(jnp.stack([value[:, :, 0:width] for value in far_sums], axis=1))
-    far_mixed = jnp.stack([value[:, :, width:] for value in far_sums], axis=1)
+    total = jnp.maximum(act_totals[1][step + 1 : step + 2, 0:1], 1.0)
+    act_halves = [old + 0.5 * (value / total) for old, value in zip(old_act, act_totals)]
+    sizes = [step, step + EXTRA]
+    across_grad = across(jnp.concatenate([value[:, 0:size] for value, size in zip(far_sums, sizes)], axis=1))
+    far_mixed = jnp.concatenate(
+        [
+            jnp.concatenate([value[:, size : size + step], value[:, size + step :]], axis=2)
+            for value, size in zip(far_sums, sizes)
+        ],
+        axis=1,
+    )
     grad_sum.add()
     grad_sums = grad_sum.finish()
     mixed_sum.held, across_grad = together(mixed_sum.held, across_grad)
@@ -511,10 +566,11 @@
     mixed_sum.send()
     across_mixed = across(far_mixed)
 
-    def both(near, far):
-        return [sum((there[half] for there in far), value[0]) / total for half, value in enumerate(near)]
-
-    grad_halves = [old_grad[here] + 0.5 * value for here, value in zip(parts, both(grad_sums, across_grad))]
+    def both(near, far, rows):
+        return [sum((there[here] for there in far), value[0]) / total for value, here in zip(near, rows)]
+
+    grad_stats = both(grad_sums, across_grad, factors)
+    grad_halves = [old + 0.5 * value for old, value in zip(old_grad, grad_stats)]
     grad_gather = Gather(grad_halves, chips)
     grad_gather.begin()
     early = (grad_gather.whole, mixed_sum.got)
@@ -526,7 +582,7 @@
     grad_gather.relay()
     act_gather.relay()
     across_mixed, _ = together(across_mixed, act_gather.whole)
-    mixed_gather = Gather(both(mixed_sums, across_mixed), chips)
+    mixed_gather = Gather(both(mixed_sums, across_mixed, [slice(0, step), slice(step, block)]), chips)
     mixed_gather.begin()
     mixed_gather.whole = act_gather.hold_last(mixed_gather.whole)
     mixed_gather.relay()

time: 188 us -> 178 us (0.947); the launches traced: 185 us -> 178 us
  waiting for transfers between devices: 103 us -> 89 us
  starting transfers between devices: 36.3 us -> 40.7 us
  other arithmetic: 2.22 us -> 4.21 us
    ppermute x41, waiting for transfers between devices: 103 us -> 89 us  [swap(): return lax.ppermute(value, axis, [(i, i ^ step) for i in range(size)])]
    ppermute x41, starting transfers between devices: 36.3 us -> 40.7 us  [swap(): return lax.ppermute(value, axis, [(i, i ^ step) for i in range(size)])]
    unnamed x19 -> x17, local copies, waits for them, and re-layouts: 2.7 us -> 0.14 us
    concatenate x0 -> x2, other arithmetic: none -> 1.91 us  [the longest x1 1.87 us: own_band(): wide = jnp.concatenate([old[0], old[0][:, 0:width]], axis=1)]
    slice x9 -> x16, local copies, waits for them, and re-layouts: 3.33 us -> 5.04 us  [the longest x2 3.34 us: own_band(): wide = jnp.concatenate([old[0], old[0][:, 0:width]], axis=1)]
  transfers between devices with their start and end apart: 41 -> 41, of which waited for: 15 -> 20; matrix products, arithmetic and copies ran while one was open for 3% -> 5% of each run, Pallas kernels for 16% -> 16%
where the time goes in v11:
time: 178 us
  waiting for transfers between devices  89 us (50%)
  starting transfers between devices  40.7 us (23%)
  Pallas kernels  36.7 us (21%)
  local copies, waits for them, and re-layouts  5.27 us (3%)
  other arithmetic  4.21 us (2%)
  between operations  1.83 us (1%)
    ppermute x41, waiting for transfers between devices, swap(): return lax.ppermute(value, axis, [(i, i ^ step) for i in range(size)])  89 us
    ppermute x41, starting transfers between devices, swap(): return lax.ppermute(value, axis, [(i, i ^ step) for i in range(size)])  40.7 us
    pallas_call x4, Pallas kernels, bands(): pl.pallas_call(functools.partial(body, range(turns), block, chips, bool(s...  22.4 us
    pallas_call x3, Pallas kernels, on_core(): pl.pallas_call(body, out_shape=shapes, in_specs=[pl.BlockSpec(memory_spac...  11.9 us
  transfers between devices with their start and end apart: 41, of which 20 were waited for; matrix products, arithmetic and copies ran while one was open for 5% of the time, Pallas kernels for 16%

profile of v11, /device:TPU:25, one launch (start us, length us, event | category | flops | bytes accessed | tf_op | source)
XLA Modules:
  0.0 177.7 jit_solution(11380693926071325797)
XLA Ops:
  0.6 2.4 %shard_map.111.refs_0_.refs_2_ = f32[264,1024]{1,0:T(8,128)} custom-call(s32[2,256]{1,0:T(2,128)} %bitcast.82, s32[1,4]{1,0:T(1,128)} %counts_ref.1, f32[256,1024]{1,0:T(8,128)} %acts.1), custom_call_target="tpu_custom_call" | custom-call | tf_op jit(solution)/shard_map/pallas_call | solution.py:222
  7.7 1.9 %fusion = (f32[128,640]{1,0:T(8,128)S(1)}, f32[128,640]{1,0:T(8,128)}) fusion(s32[]{:T(128)S(6)} %select_n.36, f32[128,1024]{1,0:T(8,128)} %bitcast.78, f32[128,512]{1,0:T(8,128)} %slice.308, f32[128,512]{1,0:T(8,128)} %slice.302, f32[128,1024]{1,0:T(8,128)} %bitcast.80), kind=kLoop, calls=%fused_computation.10 | loop fusion | flops 163840 | bytes 2228228 | tf_op jit(solution)/shard_map/concatenate | solution.py:499
  11.8 3.7 %shard_map.112 = (f32[2,2,64,512]{3,2,1,0:T(8,128)S(1)}, f32[2,2,64,512]{3,2,1,0:T(8,128)S(1)}, f32[2,2,72,512]{3,2,1,0:T(8,128)S(1)}, f32[2,2,72,512]{3,2,1,0:T(8,128)S(1)}) custom-call(s32[2]{0:T(128)S(1)} %pad_add_fusion.place, f32[264,1024]{1,0:T(8,128)S(1)} %copy-done, f32[264,1024]{1,0:T(8,128)S(1)} %collective-permute-done.1.refs_1_.refs_3_), custom_call_target="tpu_custom_call" | custom-call | tf_op jit(solution)/shard_map/pallas_call | solution.py:249
  15.6 7.6 %shard_map.113 = (f32[2,1,64,512]{3,2,1,0:T(8,128)S(1)}, f32[2,1,64,512]{3,2,1,0:T(8,128)S(1)}, f32[2,1,72,512]{3,2,1,0:T(8,128)S(1)}, f32[2,1,72,512]{3,2,1,0:T...) custom-call(s32[2]{0:T(128)S(1)} %pad_add_fusion.place, ...), custom_call_target="tpu_custom_call" | custom-call | tf_op jit(solution)/shard_map/pallas_call | solution.py:249
  23.2 6.2 %collective-permute-done.refs_0_.refs_2_ = f32[264,1024]{1,0:T(8,128)S(1)} collective-permute-done((f32[264,1024]{1,0:T(8,128)}, f32[264,1024]{1,0:T(8,128)S(1)}, u32[]{:S(2)}, u32[]{:S(2)}) %collective-permute-start) | collective-permute-done | bytes 1081376 | tf_op jit(solution)/shard_map/ppermute | solution.py:416
  30.4 2.2 %collective-permute-done.3.refs_1_.refs_3_ = f32[264,1024]{1,0:T(8,128)S(1)} collective-permute-done((f32[264,1024]{1,0:T(8,128)S(1)}, f32[264,1024]{1,0:T(8,128)S(1)}, u32[]{:S(2)}, u32[]{:S(2)}) %collective-permute-start.3) | collective-permute-done | bytes 1081376 | tf_op jit(solution)/shard_map/ppermute | solution.py:416
  32.6 3.8 %shard_map.114 = (f32[2,2,64,512]{3,2,1,0:T(8,128)S(1)}, f32[2,2,64,512]{3,2,1,0:T(8,128)S(1)}, f32[2,2,72,512]{3,2,1,0:T(8,128)S(1)}, f32[2,2,72,512]{3,2,1,0:T(8,128)S(1)}) custom-call(s32[2]{0:T(128)S(1)} %pad_add_fusion.place, f32[264,1024]{1,0:T(8,128)S(1)} %collective-permute-done.refs_0_.refs_2_, ...), custom_call_target="tpu_custom_call" | custom-call | tf_op jit(solution)/shard_map/pallas_call | solution.py:249
  38.9 10.7 %collective-permute-done.4 = f32[2,2,64,512]{3,2,1,0:T(8,128)S(1)} collective-permute-done((f32[2,2,64,512]{3,2,1,0:T(8,128)S(1)}, f32[2,2,64,512]{3,2,1,0:T(8,128)S(1)}, u32[]{:S(2)}, u32[]{:S(2)}) %collective-permute-start.4) | collective-permute-done | bytes 524320 | tf_op jit(solution)/shard_map/ppermute | solution.py:416
  49.6 2.2 %collective-permute-done.6 = f32[2,2,72,512]{3,2,1,0:T(8,128)S(1)} collective-permute-done((f32[2,2,72,512]{3,2,1,0:T(8,128)S(1)}, f32[2,2,72,512]{3,2,1,0:T(8,128)S(1)}, u32[]{:S(2)}, u32[]{:S(2)}) %collective-permute-start.6) | collective-permute-done | bytes 589856 | tf_op jit(solution)/shard_map/ppermute | solution.py:416
  51.9 3.1 %collective-permute-done.8.refs_0_ = f32[256,1024]{1,0:T(8,128)S(1)} collective-permute-done((f32[256,1024]{1,0:T(8,128)S(1)}, f32[256,1024]{1,0:T(8,128)S(1)}, u32[]{:S(2)}, u32[]{:S(2)}) %collective-permute-start.8) | collective-permute-done | bytes 1048608 | tf_op jit(solution)/shard_map/ppermute | solution.py:416
  58.3 7.2 %shard_map.115 = (f32[2,1,64,512]{3,2,1,0:T(8,128)S(1)}, f32[2,1,64,512]{3,2,1,0:T(8,128)S(1)}, f32[2,1,72,512]{3,2,1,0:T(8,128)S(1)}, f32[2,1,72,512]{3,2,1,0:T...) custom-call(s32[2]{0:T(128)S(1)} %pad_add_fusion.place, ...), custom_call_target="tpu_custom_call" | custom-call | tf_op jit(solution)/shard_map/pallas_call | solution.py:249
  68.3 15.9 %collective-permute-done.10 = f32[2,1,192,512]{3,2,1,0:T(8,128)S(1)} collective-permute-done((f32[2,1,192,512]{3,2,1,0:T(8,128)S(1)}, f32[2,1,192,512]{3,2,1,0:T(8,128)S(1)}, u32[]{:S(2)}, u32[]{:S(2)}) %collective-permute-start.10) | collective-permute-done | bytes 786464 | tf_op jit(solution)/shard_map/ppermute | solution.py:416
  90.1 2.0 %collective-permute-done.13 = f32[2,1,64,512]{3,2,1,0:T(8,128)S(1)} collective-permute-done((f32[2,1,64,512]{3,2,1,0:T(8,128)S(1)}, f32[2,1,64,512]{3,2,1,0:T(8,128)S(1)}, u32[]{:S(2)}, u32[]{:S(2)}) %collective-permute-start.13) | collective-permute-done | bytes 262176 | tf_op jit(solution)/shard_map/ppermute | solution.py:416
  95.6 5.4 %collective-permute-done.16 = f32[1,1,192,512]{3,2,1,0:T(8,128)S(1)} collective-permute-done((f32[1,1,192,512]{3,2,1,0:T(8,128)S(1)}, f32[1,1,192,512]{3,2,1,0:T(8,128)S(1)}, u32[]{:S(2)}, u32[]{:S(2)}) %collective-permute-start.16) | collective-permute-done | bytes 393248 | tf_op jit(solution)/shard_map/ppermute | solution.py:416
  102.9 12.4 %collective-permute-done.18 = f32[136,512]{1,0:T(8,128)S(1)} collective-permute-done((f32[136,512]{1,0:T(8,128)S(1)}, f32[136,512]{1,0:T(8,128)S(1)}, u32[]{:S(2)}, u32[]{:S(2)}) %collective-permute-start.18) | collective-permute-done | bytes 278560 | tf_op jit(solution)/shard_map/ppermute | solution.py:416
  118.8 2.2 %collective-permute-done.21 = f32[136,512]{1,0:T(8,128)S(1)} collective-permute-done((f32[136,512]{1,0:T(8,128)S(1)}, f32[136,512]{1,0:T(8,128)S(1)}, u32[]{:S(2)}, u32[]{:S(2)}) %collective-permute-start.21) | collective-permute-done | bytes 278560 | tf_op jit(solution)/shard_map/ppermute | solution.py:416
  121.0 4.9 %collective-permute-done.24 = f32[1,1,64,1024]{3,2,1,0:T(8,128)S(1)} collective-permute-done((f32[1,1,64,1024]{3,2,1,0:T(8,128)S(1)}, f32[1,1,64,1024]{3,2,1,0:T(8,128)S(1)}, u32[]{:S(2)}, u32[]{:S(2)}) %collective-permute-start.24) | collective-permute-done | bytes 262176 | tf_op jit(solution)/shard_map/ppermute | solution.py:416
  129.2 5.0 %collective-permute-done.34 = f32[64,512]{1,0:T(8,128)S(1)} collective-permute-done((f32[64,512]{1,0:T(8,128)S(1)}, f32[64,512]{1,0:T(8,128)S(1)}, u32[]{:S(2)}, u32[]{:S(2)}) %collective-permute-start.34) | collective-permute-done | bytes 131104 | tf_op jit(solution)/shard_map/ppermute | solution.py:416
  134.6 6.7 %collective-permute-start.36 = (f32[544,512]{1,0:T(8,128)S(1)}, f32[544,512]{1,0:T(8,128)S(1)}, u32[]{:S(2)}, u32[]{:S(2)}) collective-permute-start(f32[544,512]{1,0:T(8,128)S(1)} %constant_dynamic-update-slice_fusion.8.refs_0_), channel_id=1, source_target_pairs={{0,4},{4,0},{8,12},{12,8},{16,20},{20,16},{24,28},{28,24},{1,5},{5... | collective-permute-start | bytes 3342344 | tf_op jit(solution)/shard_map/ppermute | solution.py:416
  145.5 11.6 %collective-permute-done.28 = f32[64,512]{1,0:T(8,128)S(1)} collective-permute-done((f32[64,512]{1,0:T(8,128)S(1)}, f32[64,512]{1,0:T(8,128)S(1)}, u32[]{:S(2)}, u32[]{:S(2)}) %collective-permute-start.28) | collective-permute-done | bytes 131104 | tf_op jit(solution)/shard_map/ppermute | solution.py:416
  157.5 2.7 %collective-permute-start.33 = (f32[544,512]{1,0:T(8,128)S(1)}, f32[544,512]{1,0:T(8,128)S(1)}, u32[]{:S(2)}, u32[]{:S(2)}) collective-permute-start(f32[544,512]{1,0:T(8,128)S(1)} %constant_dynamic-update-slice_fusion.2.refs_0_), channel_id=1, source_target_pairs={{0,4},{4,0},{8,12},{12,8},{16,20},{20,16},{24,28},{28,24},{1,5},{5... | collective-permute-start | bytes 3342344 | tf_op jit(solution)/shard_map/ppermute | solution.py:416
  162.8 2.7 %shard_map.116 = (f32[128,1024]{1,0:T(8,128)}, f32[8,128]{1,0:T(8,128)S(1)}, bf16[1024,1024]{1,0:T(8,128)(2,1)S(1)}, bf16[1024,1024]{1,0:T(8,128)(2,1)S(1)}) custom-call(s32[2]{0:T(128)S(1)} %pad_add_fusion.place, f32[544,512]{1,0:T(8,128)S(1)} %constant_dynamic-update-slice_fusion.2.refs_0_, f32[544,512]{1,0:T(8,128)S(1)} %collective-permute-done.33.refs_1_), custom_call_target="tpu_custom_call" | custom-call | tf_op jit(solution)/shard_map/pallas_call | solution.py:378
  165.5 3.6 %shard_map.117 = (f32[128,1024]{1,0:T(8,128)}, f32[128,1024]{1,0:T(8,128)S(1)}) custom-call(s32[2]{0:T(128)S(1)} %pad_add_fusion.place, f32[544,512]{1,0:T(8,128)S(1)} %constant_dynamic-update-slice_fusion.8.refs_0_, f32[544,512]{1,0:T(8,128)S(1)} %collective-permute-done.36.refs_1_), custom_call_target="tpu_custom_call" | custom-call | tf_op jit(solution)/shard_map/pallas_call | solution.py:378
  172.1 5.6 %shard_map.118 = (f32[128,1024]{1,0:T(8,128)}, f32[128,1024]{1,0:T(8,128)}) custom-call(s32[2]{0:T(128)S(1)} %pad_add_fusion.place, f32[384,1024]{1,0:T(8,128)S(1)} %slice_dynamic-update-slice_fusion.refs_0_, f32[128,1024]{1,0:T(8,128)S(1)} %constant_dynamic-update-slice_fusion.18.refs_1_, f32[384,1024]{1,0:T(8,128)S(1)} %collective-permute-done.39.refs_2_, ...), custom_call_target="tpu_custom_call" | custom-call | tf_op jit(solution)/shard_map/pallas_call | solution.py:378
  (138 shorter events, 44.0 us)
Async XLA Ops:
  3.8 25.7 %collective-permute-start = (f32[264,1024]{1,0:T(8,128)}, f32[264,1024]{1,0:T(8,128)S(1)}, u32[]{:S(2)}, u32[]{:S(2)}) collective-permute-start(f32[264,1024]{1,0:T(8,128)} %shard_map.111.refs_0_.refs_2_), channel_id=1, source_target_pairs={{0,1},{1,0},{2,3},{3,2},{4,5},{5,4},{6,7},{7,6},{8,9},{9,8},{10,11... | collective-permute-start | bytes 3244040 | tf_op jit(solution)/shard_map/ppermute | solution.py:416
  4.0 11.6 %collective-permute-start.2 = (f32[256,1024]{1,0:T(8,128)S(1)}, f32[256,1024]{1,0:T(8,128)}, u32[]{:S(2)}, u32[]{:S(2)}) collective-permute-start(f32[256,1024]{1,0:T(8,128)S(1)} %copy-done.1), channel_id=1, source_target_pairs={{0,4},{4,0},{8,12},{12,8},{16,20},{20,16},{24,28},{28,24},{1,5},{5... | collective-permute-start | bytes 3145736 | tf_op jit(solution)/shard_map/ppermute | solution.py:416
  30.3 24.8 %collective-permute-start.8 = (f32[256,1024]{1,0:T(8,128)S(1)}, f32[256,1024]{1,0:T(8,128)S(1)}, u32[]{:S(2)}, u32[]{:S(2)}) collective-permute-start(f32[256,1024]{1,0:T(8,128)S(1)} %copy-done.1), channel_id=1, source_target_pairs={{0,1},{1,0},{2,3},{3,2},{4,5},{5,4},{6,7},{7,6},{8,9},{9,8},{10,11... | collective-permute-start | bytes 3145736 | tf_op jit(solution)/shard_map/ppermute | solution.py:416
  36.4 13.2 %collective-permute-start.4 = (f32[2,2,64,512]{3,2,1,0:T(8,128)S(1)}, f32[2,2,64,512]{3,2,1,0:T(8,128)S(1)}, u32[]{:S(2)}, u32[]{:S(2)}) collective-permute-start(f32[2,2,64,512]{3,2,1,0:T(8,128)S(1)} %get-tuple-element.129), channel_id=1, source_target_pairs={{0,8},{4,12},{8,0},{12,4},{16,24},{20,28},{24,16},{28,20},{1,9},{5... | collective-permute-start | bytes 1572872 | tf_op jit(solution)/shard_map/ppermute | solution.py:416
  37.7 14.2 %collective-permute-start.6 = (f32[2,2,72,512]{3,2,1,0:T(8,128)S(1)}, f32[2,2,72,512]{3,2,1,0:T(8,128)S(1)}, u32[]{:S(2)}, u32[]{:S(2)}) collective-permute-start(f32[2,2,72,512]{3,2,1,0:T(8,128)S(1)} %get-tuple-element.131), channel_id=1, source_target_pairs={{0,16},{4,20},{8,24},{12,28},{16,0},{20,4},{24,8},{28,12},{1,17},{... | collective-permute-start | bytes 1769480 | tf_op jit(solution)/shard_map/ppermute | solution.py:416
  65.6 18.6 %collective-permute-start.10 = (f32[2,1,192,512]{3,2,1,0:T(8,128)S(1)}, f32[2,1,192,512]{3,2,1,0:T(8,128)S(1)}, u32[]{:S(2)}, u32[]{:S(2)}) collective-permute-start(f32[2,1,192,512]{3,2,1,0:T(8,128)S(1)} %get-tuple-element.151), channel_id=1, source_target_pairs={{0,8},{4,12},{8,0},{12,4},{16,24},{20,28},{24,16},{28,20},{1,9},{5... | collective-permute-start | bytes 2359304 | tf_op jit(solution)/shard_map/ppermute | solution.py:416
  66.7 19.2 %collective-permute-start.11 = (f32[2,1,200,512]{3,2,1,0:T(8,128)S(1)}, f32[2,1,200,512]{3,2,1,0:T(8,128)S(1)}, u32[]{:S(2)}, u32[]{:S(2)}) collective-permute-start(f32[2,1,200,512]{3,2,1,0:T(8,128)S(1)} %get-tuple-element.152), channel_id=1, source_target_pairs={{0,16},{4,20},{8,24},{12,28},{16,0},{20,4},{24,8},{28,12},{1,17},{... | collective-permute-start | bytes 2457608 | tf_op jit(solution)/shard_map/ppermute | solution.py:416
  68.1 19.3 %collective-permute-start.12 = (f32[136,512]{1,0:T(8,128)S(1)}, f32[136,512]{1,0:T(8,128)S(1)}, u32[]{:S(2)}, u32[]{:S(2)}) collective-permute-start(f32[136,512]{1,0:T(8,128)S(1)} %maximum_bitcast_fusion), channel_id=1, source_target_pairs={{0,2},{1,3},{2,0},{3,1},{4,6},{5,7},{6,4},{7,5},{8,10},{9,11},{10,... | collective-permute-start | bytes 835592 | tf_op jit(solution)/shard_map/ppermute | solution.py:416
  88.0 13.0 %collective-permute-start.16 = (f32[1,1,192,512]{3,2,1,0:T(8,128)S(1)}, f32[1,1,192,512]{3,2,1,0:T(8,128)S(1)}, u32[]{:S(2)}, u32[]{:S(2)}) collective-permute-start(f32[1,1,192,512]{3,2,1,0:T(8,128)S(1)} %slice_add_fusion.1), channel_id=1, source_target_pairs={{0,16},{4,20},{8,24},{12,28},{16,0},{20,4},{24,8},{28,12},{1,17},{... | collective-permute-start | bytes 1179656 | tf_op jit(solution)/shard_map/ppermute | solution.py:416
  88.2 14.4 %collective-permute-start.17 = (f32[1,1,200,512]{3,2,1,0:T(8,128)S(1)}, f32[1,1,200,512]{3,2,1,0:T(8,128)S(1)}, u32[]{:S(2)}, u32[]{:S(2)}) collective-permute-start(f32[1,1,200,512]{3,2,1,0:T(8,128)S(1)} %slice_add_fusion), channel_id=1, source_target_pairs={{0,8},{4,12},{8,0},{12,4},{16,24},{20,28},{24,16},{28,20},{1,9},{5... | collective-permute-start | bytes 1228808 | tf_op jit(solution)/shard_map/ppermute | solution.py:416
  92.5 22.8 %collective-permute-start.15 = (f32[1,1,64,512]{3,2,1,0:T(8,128)S(1)}, f32[1,1,64,512]{3,2,1,0:T(8,128)S(1)}, u32[]{:S(2)}, u32[]{:S(2)}) collective-permute-start(f32[1,1,64,512]{3,2,1,0:T(8,128)S(1)} %slice_add_fusion.12), channel_id=1, source_target_pairs={{0,16},{4,20},{8,24},{12,28},{16,0},{20,4},{24,8},{28,12},{1,17},{... | collective-permute-start | bytes 393224 | tf_op jit(solution)/shard_map/ppermute | solution.py:416
  94.1 21.3 %collective-permute-start.19 = (f32[1,1,72,512]{3,2,1,0:T(8,128)S(1)}, f32[1,1,72,512]{3,2,1,0:T(8,128)S(1)}, u32[]{:S(2)}, u32[]{:S(2)}) collective-permute-start(f32[1,1,72,512]{3,2,1,0:T(8,128)S(1)} %slice_add_fusion.11), channel_id=1, source_target_pairs={{0,8},{4,12},{8,0},{12,4},{16,24},{20,28},{24,16},{28,20},{1,9},{5... | collective-permute-start | bytes 442376 | tf_op jit(solution)/shard_map/ppermute | solution.py:416
  95.4 21.7 %collective-permute-start.22 = (f32[2,1,64,1024]{3,2,1,0:T(8,128)S(1)}, f32[2,1,64,1024]{3,2,1,0:T(8,128)S(1)}, u32[]{:S(2)}, u32[]{:S(2)}) collective-permute-start(f32[2,1,64,1024]{3,2,1,0:T(8,128)S(1)} %get-tuple-element.175), channel_id=1, source_target_pairs={{0,8},{4,12},{8,0},{12,4},{16,24},{20,28},{24,16},{28,20},{1,9},{5... | collective-permute-start | bytes 1572872 | tf_op jit(solution)/shard_map/ppermute | solution.py:416
  100.9 16.1 %collective-permute-start.23 = (f32[2,1,64,1024]{3,2,1,0:T(8,128)S(1)}, f32[2,1,64,1024]{3,2,1,0:T(8,128)S(1)}, u32[]{:S(2)}, u32[]{:S(2)}) collective-permute-start(f32[2,1,64,1024]{3,2,1,0:T(8,128)S(1)} %get-tuple-element.177), channel_id=1, source_target_pairs={{0,16},{4,20},{8,24},{12,28},{16,0},{20,4},{24,8},{28,12},{1,17},{... | collective-permute-start | bytes 1572872 | tf_op jit(solution)/shard_map/ppermute | solution.py:416
  102.7 12.6 %collective-permute-start.18 = (f32[136,512]{1,0:T(8,128)S(1)}, f32[136,512]{1,0:T(8,128)S(1)}, u32[]{:S(2)}, u32[]{:S(2)}) collective-permute-start(f32[136,512]{1,0:T(8,128)S(1)} %maximum_bitcast_fusion.1), channel_id=1, source_target_pairs={{0,2},{1,3},{2,0},{3,1},{4,6},{5,7},{6,4},{7,5},{8,10},{9,11},{10,... | collective-permute-start | bytes 835592 | tf_op jit(solution)/shard_map/ppermute | solution.py:416
  118.7 23.4 %collective-permute-start.30 = (f32[128,1024]{1,0:T(8,128)S(1)}, f32[128,1024]{1,0:T(8,128)S(1)}, u32[]{:S(2)}, u32[]{:S(2)}) collective-permute-start(f32[128,1024]{1,0:T(8,128)S(1)} %bitcast.81), channel_id=1, source_target_pairs={{0,2},{1,3},{2,0},{3,1},{4,6},{5,7},{6,4},{7,5},{8,10},{9,11},{10,... | collective-permute-start | bytes 1572872 | tf_op jit(solution)/shard_map/ppermute | solution.py:416
  126.0 16.1 %collective-permute-start.27 = (f32[136,512]{1,0:T(8,128)S(1)}, f32[136,512]{1,0:T(8,128)S(1)}, u32[]{:S(2)}, u32[]{:S(2)}) collective-permute-start(f32[136,512]{1,0:T(8,128)S(1)} %get-tuple-element.237), channel_id=1, source_target_pairs={{0,16},{4,20},{8,24},{12,28},{16,0},{20,4},{24,8},{28,12},{1,17},{... | collective-permute-start | bytes 835592 | tf_op jit(solution)/shard_map/ppermute | solution.py:416
  127.3 14.8 %collective-permute-start.26 = (f32[136,512]{1,0:T(8,128)S(1)}, f32[136,512]{1,0:T(8,128)S(1)}, u32[]{:S(2)}, u32[]{:S(2)}) collective-permute-start(f32[136,512]{1,0:T(8,128)S(1)} %get-tuple-element.237), channel_id=1, source_target_pairs={{0,8},{4,12},{8,0},{12,4},{16,24},{20,28},{24,16},{28,20},{1,9},{5... | collective-permute-start | bytes 835592 | tf_op jit(solution)/shard_map/ppermute | solution.py:416
  134.6 30.9 %collective-permute-start.36 = (f32[544,512]{1,0:T(8,128)S(1)}, f32[544,512]{1,0:T(8,128)S(1)}, u32[]{:S(2)}, u32[]{:S(2)}) collective-permute-start(f32[544,512]{1,0:T(8,128)S(1)} %constant_dynamic-update-slice_fusion.8.refs_0_), channel_id=1, source_target_pairs={{0,4},{4,0},{8,12},{12,8},{16,20},{20,16},{24,28},{28,24},{1,5},{5... | collective-permute-start | bytes 3342344 | tf_op jit(solution)/shard_map/ppermute | solution.py:416
  142.3 15.1 %collective-permute-start.32 = (f32[128,1024]{1,0:T(8,128)S(1)}, f32[128,1024]{1,0:T(8,128)S(1)}, u32[]{:S(2)}, u32[]{:S(2)}) collective-permute-start(f32[128,1024]{1,0:T(8,128)S(1)} %pad_maximum_fusion), channel_id=1, source_target_pairs={{0,16},{4,20},{8,24},{12,28},{16,0},{20,4},{24,8},{28,12},{1,17},{... | collective-permute-start | bytes 1572872 | tf_op jit(solution)/shard_map/ppermute | solution.py:416
  142.6 14.9 %collective-permute-start.31 = (f32[128,1024]{1,0:T(8,128)S(1)}, f32[128,1024]{1,0:T(8,128)S(1)}, u32[]{:S(2)}, u32[]{:S(2)}) collective-permute-start(f32[128,1024]{1,0:T(8,128)S(1)} %pad_maximum_fusion), channel_id=1, source_target_pairs={{0,8},{4,12},{8,0},{12,4},{16,24},{20,28},{24,16},{28,20},{1,9},{5... | collective-permute-start | bytes 1572872 | tf_op jit(solution)/shard_map/ppermute | solution.py:416
  143.6 13.5 %collective-permute-start.28 = (f32[64,512]{1,0:T(8,128)S(1)}, f32[64,512]{1,0:T(8,128)S(1)}, u32[]{:S(2)}, u32[]{:S(2)}) collective-permute-start(f32[64,512]{1,0:T(8,128)S(1)} %get-tuple-element.235), channel_id=1, source_target_pairs={{0,16},{4,20},{8,24},{12,28},{16,0},{20,4},{24,8},{28,12},{1,17},{... | collective-permute-start | bytes 393224 | tf_op jit(solution)/shard_map/ppermute | solution.py:416
  145.0 12.5 %collective-permute-start.29 = (f32[72,512]{1,0:T(8,128)S(1)}, f32[72,512]{1,0:T(8,128)S(1)}, u32[]{:S(2)}, u32[]{:S(2)}) collective-permute-start(f32[72,512]{1,0:T(8,128)S(1)} %get-tuple-element.233), channel_id=1, source_target_pairs={{0,8},{4,12},{8,0},{12,4},{16,24},{20,28},{24,16},{28,20},{1,9},{5... | collective-permute-start | bytes 442376 | tf_op jit(solution)/shard_map/ppermute | solution.py:416
  160.3 10.2 %collective-permute-start.39 = (f32[384,1024]{1,0:T(8,128)S(1)}, f32[384,1024]{1,0:T(8,128)S(1)}, u32[]{:S(2)}, u32[]{:S(2)}) collective-permute-start(f32[384,1024]{1,0:T(8,128)S(1)} %slice_dynamic-update-slice_fusion.refs_0_), channel_id=1, source_target_pairs={{0,4},{4,0},{8,12},{12,8},{16,20},{20,16},{24,28},{28,24},{1,5},{5... | collective-permute-start | bytes 4718600 | tf_op jit(solution)/shard_map/ppermute | solution.py:416
  (21 other events, 126.7 us)

commit v12 on v11

--- a/solution.py
+++ b/solution.py
@@ -127,18 +127,18 @@
     outs[output][position, number, here, :] = value
 
 
-def prepare_kernel(routes_ref, counts_ref, acts, out, routes, counts, sems):
+def prepare_kernel(routes_ref, counts_ref, acts, out, routes, counts, keeps, sems):
     samples, feat = acts.shape
     experts = counts.shape[1]
     copies = [
-        pltpu.make_async_copy(routes_ref, routes, sems.at[0]),
-        pltpu.make_async_copy(counts_ref, counts, sems.at[1]),
-        pltpu.make_async_copy(acts, out.at[pl.ds(0, samples), :], sems.at[2]),
+        pltpu.make_async_copy(acts, out.at[pl.ds(0, samples), :], sems.at[0]),
+        pltpu.make_async_copy(routes_ref, routes, sems.at[1]),
+        pltpu.make_async_copy(counts_ref, counts, sems.at[2]),
     ]
     for copy in copies:
         copy.start()
-    out[samples:, :] = jnp.zeros((out.shape[0] - samples, feat), F32)
-    for copy in copies[:2]:
+    keeps[...] = jnp.zeros(keeps.shape, F32)
+    for copy in copies[1:]:
         copy.wait()
     hits = []
     for expert in range(experts):
@@ -152,9 +152,12 @@
     for expert in range(experts):
         limit = counts[0, expert].astype(F32)
         keep = jnp.where(rank[expert : expert + 1, :] < limit, hits[expert], 0.0)
-        row, column = samples + expert // per_row, expert % per_row * samples
-        out[row : row + 1, column : column + samples] = keep
-    copies[2].wait()
+        row, column = expert // per_row, expert % per_row * samples
+        keeps[row : row + 1, column : column + samples] = keep
+    last = pltpu.make_async_copy(keeps, out.at[pl.ds(samples, keeps.shape[0]), :], sems.at[3])
+    last.start()
+    last.wait()
+    copies[0].wait()
 
 
 def act_kernel(turns, block, chips, seeded, samples, place, *refs):
@@ -223,11 +226,12 @@
         prepare_kernel,
         out_shape=jax.ShapeDtypeStruct((rows, feat), F32),
         in_specs=[pl.BlockSpec(memory_space=pltpu.HBM)] * 3,
-        out_specs=pl.BlockSpec(memory_space=pltpu.VMEM),
+        out_specs=pl.BlockSpec(memory_space=pltpu.HBM),
         scratch_shapes=[
             pltpu.VMEM(routes.shape[::-1], jnp.int32),
             pltpu.SMEM(counts.shape, jnp.int32),
-            pltpu.SemaphoreType.DMA((3,)),
+            pltpu.VMEM((rows - samples, feat), F32),
+            pltpu.SemaphoreType.DMA((4,)),
         ],
         compiler_params=pltpu.CompilerParams(vmem_limit_bytes=60 * MIB),
     )(routes.T, counts, acts)
@@ -584,13 +588,13 @@
     across_mixed, _ = together(across_mixed, act_gather.whole)
     mixed_gather = Gather(both(mixed_sums, across_mixed, [slice(0, step), slice(step, block)]), chips)
     mixed_gather.begin()
+    grad_out, inverse = grad_factor_rows(place, grad_gather.exchange(), block, feat)
+    inverse = act_gather.hold_last(inverse)
     mixed_gather.whole = act_gather.hold_last(mixed_gather.whole)
     mixed_gather.relay()
     mine, theirs = mixed_gather.exchange(0, -1)
     act_out, *act_square = act_factor_rows(place, act_gather.exchange(), block, feat)
-    grad_blocks, act_square = together(grad_gather.exchange(), act_square)
-    grad_out, inverse = grad_factor_rows(place, grad_blocks, block, feat)
-    inverse = mixed_gather.hold_last(inverse)
+    act_square = mixed_gather.hold_last(act_square)
     my_last, their_last = mixed_gather.exchange(-1)
     mixed_blocks = (mine, my_last, theirs, their_last)
     outs = update_rows(place, mixed_blocks, inverse, *act_square, momentum[0], weights[0])

time: 178 us -> 209 us (1.17)
  Pallas kernels: 36.7 us -> 67 us
    pallas_call x1, Pallas kernels: 2.39 us -> 32.9 us  [prepare(): pl.pallas_call(prepare_kernel, out_shape=jax.ShapeDtypeStruct((rows, feat...]
  transfers between devices with their start and end apart: 41 -> 41, of which waited for: 20 -> 22; matrix products, arithmetic and copies ran while one was open for 5% -> 5% of each run, Pallas kernels for 16% -> 14%
where the time goes in v12:
time: 209 us; the launch traced here: 208 us
  waiting for transfers between devices  89 us (43%)
  Pallas kernels  67 us (32%)
  starting transfers between devices  40.9 us (20%)
  local copies, waits for them, and re-layouts  5.28 us (3%)
  other arithmetic  4.21 us (2%)
    ppermute x41, waiting for transfers between devices, swap(): return lax.ppermute(value, axis, [(i, i ^ step) for i in range(size)])  89 us
    ppermute x41, starting transfers between devices, swap(): return lax.ppermute(value, axis, [(i, i ^ step) for i in range(size)])  40.9 us
    pallas_call x1, Pallas kernels, prepare(): pl.pallas_call(prepare_kernel, out_shape=jax.ShapeDtypeStruct((rows, feat...  32.9 us
    pallas_call x4, Pallas kernels, bands(): pl.pallas_call(functools.partial(body, range(turns), block, chips, bool(s...  22.3 us
    pallas_call x3, Pallas kernels, on_core(): pl.pallas_call(body, out_shape=shapes, in_specs=[pl.BlockSpec(memory_spac...  11.8 us
  transfers between devices with their start and end apart: 41, of which 22 were waited for; matrix products, arithmetic and copies ran while one was open for 5% of the time, Pallas kernels for 14%

profile of v12, /device:TPU:25, one launch (start us, length us, event | category | flops | bytes accessed | tf_op | source)
XLA Modules:
  0.0 208.2 jit_solution(15957650872769173967)
XLA Ops:
  0.6 32.9 %shard_map.111.refs_0_.refs_2_ = f32[264,1024]{1,0:T(8,128)} custom-call(s32[2,256]{1,0:T(2,128)} %bitcast.82, s32[1,4]{1,0:T(1,128)} %counts_ref.1, f32[256,1024]{1,0:T(8,128)} %acts.1), custom_call_target="tpu_custom_call" | custom-call | tf_op jit(solution)/shard_map/pallas_call | solution.py:225
  42.3 3.7 %shard_map.112 = (f32[2,2,64,512]{3,2,1,0:T(8,128)S(1)}, f32[2,2,64,512]{3,2,1,0:T(8,128)S(1)}, f32[2,2,72,512]{3,2,1,0:T(8,128)S(1)}, f32[2,2,72,512]{3,2,1,0:T(8,128)S(1)}) custom-call(s32[2]{0:T(128)S(1)} %pad_add_fusion.place, f32[264,1024]{1,0:T(8,128)S(1)} %copy-done, f32[264,1024]{1,0:T(8,128)S(1)} %collective-permute-done.1.refs_1_.refs_3_), custom_call_target="tpu_custom_call" | custom-call | tf_op jit(solution)/shard_map/pallas_call | solution.py:253
  46.1 7.6 %shard_map.113 = (f32[2,1,64,512]{3,2,1,0:T(8,128)S(1)}, f32[2,1,64,512]{3,2,1,0:T(8,128)S(1)}, f32[2,1,72,512]{3,2,1,0:T(8,128)S(1)}, f32[2,1,72,512]{3,2,1,0:T...) custom-call(s32[2]{0:T(128)S(1)} %pad_add_fusion.place, ...), custom_call_target="tpu_custom_call" | custom-call | tf_op jit(solution)/shard_map/pallas_call | solution.py:253
  53.7 6.3 %collective-permute-done.refs_0_.refs_2_ = f32[264,1024]{1,0:T(8,128)S(1)} collective-permute-done((f32[264,1024]{1,0:T(8,128)}, f32[264,1024]{1,0:T(8,128)S(1)}, u32[]{:S(2)}, u32[]{:S(2)}) %collective-permute-start) | collective-permute-done | bytes 1081376 | tf_op jit(solution)/shard_map/ppermute | solution.py:420
  61.0 2.2 %collective-permute-done.3.refs_1_.refs_3_ = f32[264,1024]{1,0:T(8,128)S(1)} collective-permute-done((f32[264,1024]{1,0:T(8,128)S(1)}, f32[264,1024]{1,0:T(8,128)S(1)}, u32[]{:S(2)}, u32[]{:S(2)}) %collective-permute-start.3) | collective-permute-done | bytes 1081376 | tf_op jit(solution)/shard_map/ppermute | solution.py:420
  63.1 3.8 %shard_map.114 = (f32[2,2,64,512]{3,2,1,0:T(8,128)S(1)}, f32[2,2,64,512]{3,2,1,0:T(8,128)S(1)}, f32[2,2,72,512]{3,2,1,0:T(8,128)S(1)}, f32[2,2,72,512]{3,2,1,0:T(8,128)S(1)}) custom-call(s32[2]{0:T(128)S(1)} %pad_add_fusion.place, f32[264,1024]{1,0:T(8,128)S(1)} %collective-permute-done.refs_0_.refs_2_, ...), custom_call_target="tpu_custom_call" | custom-call | tf_op jit(solution)/shard_map/pallas_call | solution.py:253
  69.4 10.7 %collective-permute-done.4 = f32[2,2,64,512]{3,2,1,0:T(8,128)S(1)} collective-permute-done((f32[2,2,64,512]{3,2,1,0:T(8,128)S(1)}, f32[2,2,64,512]{3,2,1,0:T(8,128)S(1)}, u32[]{:S(2)}, u32[]{:S(2)}) %collective-permute-start.4) | collective-permute-done | bytes 524320 | tf_op jit(solution)/shard_map/ppermute | solution.py:420
  80.1 2.2 %collective-permute-done.6 = f32[2,2,72,512]{3,2,1,0:T(8,128)S(1)} collective-permute-done((f32[2,2,72,512]{3,2,1,0:T(8,128)S(1)}, f32[2,2,72,512]{3,2,1,0:T(8,128)S(1)}, u32[]{:S(2)}, u32[]{:S(2)}) %collective-permute-start.6) | collective-permute-done | bytes 589856 | tf_op jit(solution)/shard_map/ppermute | solution.py:420
  82.4 3.1 %collective-permute-done.8.refs_0_ = f32[256,1024]{1,0:T(8,128)S(1)} collective-permute-done((f32[256,1024]{1,0:T(8,128)S(1)}, f32[256,1024]{1,0:T(8,128)S(1)}, u32[]{:S(2)}, u32[]{:S(2)}) %collective-permute-start.8) | collective-permute-done | bytes 1048608 | tf_op jit(solution)/shard_map/ppermute | solution.py:420
  88.8 7.2 %shard_map.115 = (f32[2,1,64,512]{3,2,1,0:T(8,128)S(1)}, f32[2,1,64,512]{3,2,1,0:T(8,128)S(1)}, f32[2,1,72,512]{3,2,1,0:T(8,128)S(1)}, f32[2,1,72,512]{3,2,1,0:T...) custom-call(s32[2]{0:T(128)S(1)} %pad_add_fusion.place, ...), custom_call_target="tpu_custom_call" | custom-call | tf_op jit(solution)/shard_map/pallas_call | solution.py:253
  98.8 15.9 %collective-permute-done.10 = f32[2,1,192,512]{3,2,1,0:T(8,128)S(1)} collective-permute-done((f32[2,1,192,512]{3,2,1,0:T(8,128)S(1)}, f32[2,1,192,512]{3,2,1,0:T(8,128)S(1)}, u32[]{:S(2)}, u32[]{:S(2)}) %collective-permute-start.10) | collective-permute-done | bytes 786464 | tf_op jit(solution)/shard_map/ppermute | solution.py:420
  120.6 2.0 collective-permute-done.13
  126.1 5.4 %collective-permute-done.16 = f32[1,1,192,512]{3,2,1,0:T(8,128)S(1)} collective-permute-done((f32[1,1,192,512]{3,2,1,0:T(8,128)S(1)}, f32[1,1,192,512]{3,2,1,0:T(8,128)S(1)}, u32[]{:S(2)}, u32[]{:S(2)}) %collective-permute-start.16) | collective-permute-done | bytes 393248 | tf_op jit(solution)/shard_map/ppermute | solution.py:420
  133.5 12.4 %collective-permute-done.18 = f32[136,512]{1,0:T(8,128)S(1)} collective-permute-done((f32[136,512]{1,0:T(8,128)S(1)}, f32[136,512]{1,0:T(8,128)S(1)}, u32[]{:S(2)}, u32[]{:S(2)}) %collective-permute-start.18) | collective-permute-done | bytes 278560 | tf_op jit(solution)/shard_map/ppermute | solution.py:420
  149.3 2.2 %collective-permute-done.21 = f32[136,512]{1,0:T(8,128)S(1)} collective-permute-done((f32[136,512]{1,0:T(8,128)S(1)}, f32[136,512]{1,0:T(8,128)S(1)}, u32[]{:S(2)}, u32[]{:S(2)}) %collective-permute-start.21) | collective-permute-done | bytes 278560 | tf_op jit(solution)/shard_map/ppermute | solution.py:420
  151.5 4.9 %collective-permute-done.24 = f32[1,1,64,1024]{3,2,1,0:T(8,128)S(1)} collective-permute-done((f32[1,1,64,1024]{3,2,1,0:T(8,128)S(1)}, f32[1,1,64,1024]{3,2,1,0:T(8,128)S(1)}, u32[]{:S(2)}, u32[]{:S(2)}) %collective-permute-start.24) | collective-permute-done | bytes 262176 | tf_op jit(solution)/shard_map/ppermute | solution.py:420
  159.8 5.0 %collective-permute-done.30 = f32[64,512]{1,0:T(8,128)S(1)} collective-permute-done((f32[64,512]{1,0:T(8,128)S(1)}, f32[64,512]{1,0:T(8,128)S(1)}, u32[]{:S(2)}, u32[]{:S(2)}) %collective-permute-start.30) | collective-permute-done | bytes 131104 | tf_op jit(solution)/shard_map/ppermute | solution.py:420
  165.1 6.7 %collective-permute-start.32 = (f32[544,512]{1,0:T(8,128)S(1)}, f32[544,512]{1,0:T(8,128)S(1)}, u32[]{:S(2)}, u32[]{:S(2)}) collective-permute-start(f32[544,512]{1,0:T(8,128)S(1)} %constant_dynamic-update-slice_fusion.2.refs_0_), channel_id=1, source_target_pairs={{0,4},{4,0},{8,12},{12,8},{16,20},{20,16},{24,28},{28,24},{1,5},{5... | collective-permute-start | bytes 3342344 | tf_op jit(solution)/shard_map/ppermute | solution.py:420
  176.0 3.4 %shard_map.116 = (f32[128,1024]{1,0:T(8,128)}, f32[128,1024]{1,0:T(8,128)S(1)}) custom-call(s32[2]{0:T(128)S(1)} %pad_add_fusion.place, f32[544,512]{1,0:T(8,128)S(1)} %constant_dynamic-update-slice_fusion.2.refs_0_, f32[544,512]{1,0:T(8,128)S(1)} %collective-permute-done.32.refs_1_), custom_call_target="tpu_custom_call" | custom-call | tf_op jit(solution)/shard_map/pallas_call | solution.py:382
  179.5 8.1 %collective-permute-done.28 = f32[64,512]{1,0:T(8,128)S(1)} collective-permute-done((f32[64,512]{1,0:T(8,128)S(1)}, f32[64,512]{1,0:T(8,128)S(1)}, u32[]{:S(2)}, u32[]{:S(2)}) %collective-permute-start.28) | collective-permute-done | bytes 131104 | tf_op jit(solution)/shard_map/ppermute | solution.py:420
  188.1 2.7 %collective-permute-start.36 = (f32[544,512]{1,0:T(8,128)S(1)}, f32[544,512]{1,0:T(8,128)S(1)}, u32[]{:S(2)}, u32[]{:S(2)}) collective-permute-start(f32[544,512]{1,0:T(8,128)S(1)} %constant_dynamic-update-slice_fusion.8.refs_0_), channel_id=1, source_target_pairs={{0,4},{4,0},{8,12},{12,8},{16,20},{20,16},{24,28},{28,24},{1,5},{5... | collective-permute-start | bytes 3342344 | tf_op jit(solution)/shard_map/ppermute | solution.py:420
  193.3 2.7 %shard_map.117 = (f32[128,1024]{1,0:T(8,128)}, f32[8,128]{1,0:T(8,128)S(1)}, bf16[1024,1024]{1,0:T(8,128)(2,1)S(1)}, bf16[1024,1024]{1,0:T(8,128)(2,1)S(1)}) custom-call(s32[2]{0:T(128)S(1)} %pad_add_fusion.place, f32[544,512]{1,0:T(8,128)S(1)} %constant_dynamic-update-slice_fusion.8.refs_0_, f32[544,512]{1,0:T(8,128)S(1)} %collective-permute-done.36.refs_1_), custom_call_target="tpu_custom_call" | custom-call | tf_op jit(solution)/shard_map/pallas_call | solution.py:382
  196.0 2.5 %collective-permute-done.37 = f32[64,1024]{1,0:T(8,128)S(1)} collective-permute-done((f32[64,1024]{1,0:T(8,128)S(1)}, f32[64,1024]{1,0:T(8,128)S(1)}, u32[]{:S(2)}, u32[]{:S(2)}) %collective-permute-start.37) | collective-permute-done | bytes 262176 | tf_op jit(solution)/shard_map/ppermute | solution.py:420
  202.6 5.6 %shard_map.118 = (f32[128,1024]{1,0:T(8,128)}, f32[128,1024]{1,0:T(8,128)}) custom-call(s32[2]{0:T(128)S(1)} %pad_add_fusion.place, f32[384,1024]{1,0:T(8,128)S(1)} %slice_dynamic-update-slice_fusion.refs_0_, f32[128,1024]{1,0:T(8,128)S(1)} %constant_dynamic-update-slice_fusion.18.refs_1_, f32[384,1024]{1,0:T(8,128)S(1)} %collective-permute-done.39.refs_2_, ...), custom_call_target="tpu_custom_call" | custom-call | tf_op jit(solution)/shard_map/pallas_call | solution.py:382
  (138 shorter events, 47.1 us)
Async XLA Ops:
  34.3 25.7 %collective-permute-start = (f32[264,1024]{1,0:T(8,128)}, f32[264,1024]{1,0:T(8,128)S(1)}, u32[]{:S(2)}, u32[]{:S(2)}) collective-permute-start(f32[264,1024]{1,0:T(8,128)} %shard_map.111.refs_0_.refs_2_), channel_id=1, source_target_pairs={{0,1},{1,0},{2,3},{3,2},{4,5},{5,4},{6,7},{7,6},{8,9},{9,8},{10,11... | collective-permute-start | bytes 3244040 | tf_op jit(solution)/shard_map/ppermute | solution.py:420
  34.5 11.6 %collective-permute-start.2 = (f32[256,1024]{1,0:T(8,128)S(1)}, f32[256,1024]{1,0:T(8,128)}, u32[]{:S(2)}, u32[]{:S(2)}) collective-permute-start(f32[256,1024]{1,0:T(8,128)S(1)} %copy-done.1), channel_id=1, source_target_pairs={{0,4},{4,0},{8,12},{12,8},{16,20},{20,16},{24,28},{28,24},{1,5},{5... | collective-permute-start | bytes 3145736 | tf_op jit(solution)/shard_map/ppermute | solution.py:420
  60.8 24.8 %collective-permute-start.8 = (f32[256,1024]{1,0:T(8,128)S(1)}, f32[256,1024]{1,0:T(8,128)S(1)}, u32[]{:S(2)}, u32[]{:S(2)}) collective-permute-start(f32[256,1024]{1,0:T(8,128)S(1)} %copy-done.1), channel_id=1, source_target_pairs={{0,1},{1,0},{2,3},{3,2},{4,5},{5,4},{6,7},{7,6},{8,9},{9,8},{10,11... | collective-permute-start | bytes 3145736 | tf_op jit(solution)/shard_map/ppermute | solution.py:420
  66.9 13.2 %collective-permute-start.4 = (f32[2,2,64,512]{3,2,1,0:T(8,128)S(1)}, f32[2,2,64,512]{3,2,1,0:T(8,128)S(1)}, u32[]{:S(2)}, u32[]{:S(2)}) collective-permute-start(f32[2,2,64,512]{3,2,1,0:T(8,128)S(1)} %get-tuple-element.129), channel_id=1, source_target_pairs={{0,8},{4,12},{8,0},{12,4},{16,24},{20,28},{24,16},{28,20},{1,9},{5... | collective-permute-start | bytes 1572872 | tf_op jit(solution)/shard_map/ppermute | solution.py:420
  68.2 14.2 %collective-permute-start.6 = (f32[2,2,72,512]{3,2,1,0:T(8,128)S(1)}, f32[2,2,72,512]{3,2,1,0:T(8,128)S(1)}, u32[]{:S(2)}, u32[]{:S(2)}) collective-permute-start(f32[2,2,72,512]{3,2,1,0:T(8,128)S(1)} %get-tuple-element.131), channel_id=1, source_target_pairs={{0,16},{4,20},{8,24},{12,28},{16,0},{20,4},{24,8},{28,12},{1,17},{... | collective-permute-start | bytes 1769480 | tf_op jit(solution)/shard_map/ppermute | solution.py:420
  96.1 18.6 %collective-permute-start.10 = (f32[2,1,192,512]{3,2,1,0:T(8,128)S(1)}, f32[2,1,192,512]{3,2,1,0:T(8,128)S(1)}, u32[]{:S(2)}, u32[]{:S(2)}) collective-permute-start(f32[2,1,192,512]{3,2,1,0:T(8,128)S(1)} %get-tuple-element.151), channel_id=1, source_target_pairs={{0,8},{4,12},{8,0},{12,4},{16,24},{20,28},{24,16},{28,20},{1,9},{5... | collective-permute-start | bytes 2359304 | tf_op jit(solution)/shard_map/ppermute | solution.py:420
  97.2 19.2 %collective-permute-start.11 = (f32[2,1,200,512]{3,2,1,0:T(8,128)S(1)}, f32[2,1,200,512]{3,2,1,0:T(8,128)S(1)}, u32[]{:S(2)}, u32[]{:S(2)}) collective-permute-start(f32[2,1,200,512]{3,2,1,0:T(8,128)S(1)} %get-tuple-element.152), channel_id=1, source_target_pairs={{0,16},{4,20},{8,24},{12,28},{16,0},{20,4},{24,8},{28,12},{1,17},{... | collective-permute-start | bytes 2457608 | tf_op jit(solution)/shard_map/ppermute | solution.py:420
  98.6 19.3 %collective-permute-start.12 = (f32[136,512]{1,0:T(8,128)S(1)}, f32[136,512]{1,0:T(8,128)S(1)}, u32[]{:S(2)}, u32[]{:S(2)}) collective-permute-start(f32[136,512]{1,0:T(8,128)S(1)} %maximum_bitcast_fusion), channel_id=1, source_target_pairs={{0,2},{1,3},{2,0},{3,1},{4,6},{5,7},{6,4},{7,5},{8,10},{9,11},{10,... | collective-permute-start | bytes 835592 | tf_op jit(solution)/shard_map/ppermute | solution.py:420
  118.5 13.0 %collective-permute-start.16 = (f32[1,1,192,512]{3,2,1,0:T(8,128)S(1)}, f32[1,1,192,512]{3,2,1,0:T(8,128)S(1)}, u32[]{:S(2)}, u32[]{:S(2)}) collective-permute-start(f32[1,1,192,512]{3,2,1,0:T(8,128)S(1)} %slice_add_fusion.1), channel_id=1, source_target_pairs={{0,16},{4,20},{8,24},{12,28},{16,0},{20,4},{24,8},{28,12},{1,17},{... | collective-permute-start | bytes 1179656 | tf_op jit(solution)/shard_map/ppermute | solution.py:420
  118.7 14.4 %collective-permute-start.17 = (f32[1,1,200,512]{3,2,1,0:T(8,128)S(1)}, f32[1,1,200,512]{3,2,1,0:T(8,128)S(1)}, u32[]{:S(2)}, u32[]{:S(2)}) collective-permute-start(f32[1,1,200,512]{3,2,1,0:T(8,128)S(1)} %slice_add_fusion), channel_id=1, source_target_pairs={{0,8},{4,12},{8,0},{12,4},{16,24},{20,28},{24,16},{28,20},{1,9},{5... | collective-permute-start | bytes 1228808 | tf_op jit(solution)/shard_map/ppermute | solution.py:420
  123.1 22.8 %collective-permute-start.15 = (f32[1,1,64,512]{3,2,1,0:T(8,128)S(1)}, f32[1,1,64,512]{3,2,1,0:T(8,128)S(1)}, u32[]{:S(2)}, u32[]{:S(2)}) collective-permute-start(f32[1,1,64,512]{3,2,1,0:T(8,128)S(1)} %slice_add_fusion.12), channel_id=1, source_target_pairs={{0,16},{4,20},{8,24},{12,28},{16,0},{20,4},{24,8},{28,12},{1,17},{... | collective-permute-start | bytes 393224 | tf_op jit(solution)/shard_map/ppermute | solution.py:420
  124.6 21.3 %collective-permute-start.19 = (f32[1,1,72,512]{3,2,1,0:T(8,128)S(1)}, f32[1,1,72,512]{3,2,1,0:T(8,128)S(1)}, u32[]{:S(2)}, u32[]{:S(2)}) collective-permute-start(f32[1,1,72,512]{3,2,1,0:T(8,128)S(1)} %slice_add_fusion.11), channel_id=1, source_target_pairs={{0,8},{4,12},{8,0},{12,4},{16,24},{20,28},{24,16},{28,20},{1,9},{5... | collective-permute-start | bytes 442376 | tf_op jit(solution)/shard_map/ppermute | solution.py:420
  125.9 21.7 %collective-permute-start.22 = (f32[2,1,64,1024]{3,2,1,0:T(8,128)S(1)}, f32[2,1,64,1024]{3,2,1,0:T(8,128)S(1)}, u32[]{:S(2)}, u32[]{:S(2)}) collective-permute-start(f32[2,1,64,1024]{3,2,1,0:T(8,128)S(1)} %get-tuple-element.175), channel_id=1, source_target_pairs={{0,8},{4,12},{8,0},{12,4},{16,24},{20,28},{24,16},{28,20},{1,9},{5... | collective-permute-start | bytes 1572872 | tf_op jit(solution)/shard_map/ppermute | solution.py:420
  131.5 16.2 %collective-permute-start.23 = (f32[2,1,64,1024]{3,2,1,0:T(8,128)S(1)}, f32[2,1,64,1024]{3,2,1,0:T(8,128)S(1)}, u32[]{:S(2)}, u32[]{:S(2)}) collective-permute-start(f32[2,1,64,1024]{3,2,1,0:T(8,128)S(1)} %get-tuple-element.177), channel_id=1, source_target_pairs={{0,16},{4,20},{8,24},{12,28},{16,0},{20,4},{24,8},{28,12},{1,17},{... | collective-permute-start | bytes 1572872 | tf_op jit(solution)/shard_map/ppermute | solution.py:420
  133.2 12.6 %collective-permute-start.18 = (f32[136,512]{1,0:T(8,128)S(1)}, f32[136,512]{1,0:T(8,128)S(1)}, u32[]{:S(2)}, u32[]{:S(2)}) collective-permute-start(f32[136,512]{1,0:T(8,128)S(1)} %maximum_bitcast_fusion.1), channel_id=1, source_target_pairs={{0,2},{1,3},{2,0},{3,1},{4,6},{5,7},{6,4},{7,5},{8,10},{9,11},{10,... | collective-permute-start | bytes 835592 | tf_op jit(solution)/shard_map/ppermute | solution.py:420
  149.2 23.4 %collective-permute-start.33 = (f32[128,1024]{1,0:T(8,128)S(1)}, f32[128,1024]{1,0:T(8,128)S(1)}, u32[]{:S(2)}, u32[]{:S(2)}) collective-permute-start(f32[128,1024]{1,0:T(8,128)S(1)} %bitcast.81), channel_id=1, source_target_pairs={{0,2},{1,3},{2,0},{3,1},{4,6},{5,7},{6,4},{7,5},{8,10},{9,11},{10,... | collective-permute-start | bytes 1572872 | tf_op jit(solution)/shard_map/ppermute | solution.py:420
  156.5 16.1 %collective-permute-start.27 = (f32[136,512]{1,0:T(8,128)S(1)}, f32[136,512]{1,0:T(8,128)S(1)}, u32[]{:S(2)}, u32[]{:S(2)}) collective-permute-start(f32[136,512]{1,0:T(8,128)S(1)} %get-tuple-element.237), channel_id=1, source_target_pairs={{0,16},{4,20},{8,24},{12,28},{16,0},{20,4},{24,8},{28,12},{1,17},{... | collective-permute-start | bytes 835592 | tf_op jit(solution)/shard_map/ppermute | solution.py:420
  157.8 14.8 %collective-permute-start.26 = (f32[136,512]{1,0:T(8,128)S(1)}, f32[136,512]{1,0:T(8,128)S(1)}, u32[]{:S(2)}, u32[]{:S(2)}) collective-permute-start(f32[136,512]{1,0:T(8,128)S(1)} %get-tuple-element.237), channel_id=1, source_target_pairs={{0,8},{4,12},{8,0},{12,4},{16,24},{20,28},{24,16},{28,20},{1,9},{5... | collective-permute-start | bytes 835592 | tf_op jit(solution)/shard_map/ppermute | solution.py:420
  165.1 11.0 %collective-permute-start.32 = (f32[544,512]{1,0:T(8,128)S(1)}, f32[544,512]{1,0:T(8,128)S(1)}, u32[]{:S(2)}, u32[]{:S(2)}) collective-permute-start(f32[544,512]{1,0:T(8,128)S(1)} %constant_dynamic-update-slice_fusion.2.refs_0_), channel_id=1, source_target_pairs={{0,4},{4,0},{8,12},{12,8},{16,20},{20,16},{24,28},{28,24},{1,5},{5... | collective-permute-start | bytes 3342344 | tf_op jit(solution)/shard_map/ppermute | solution.py:420
  172.8 15.2 %collective-permute-start.35 = (f32[128,1024]{1,0:T(8,128)S(1)}, f32[128,1024]{1,0:T(8,128)S(1)}, u32[]{:S(2)}, u32[]{:S(2)}) collective-permute-start(f32[128,1024]{1,0:T(8,128)S(1)} %pad_maximum_fusion), channel_id=1, source_target_pairs={{0,16},{4,20},{8,24},{12,28},{16,0},{20,4},{24,8},{28,12},{1,17},{... | collective-permute-start | bytes 1572872 | tf_op jit(solution)/shard_map/ppermute | solution.py:420
  173.1 14.9 %collective-permute-start.34 = (f32[128,1024]{1,0:T(8,128)S(1)}, f32[128,1024]{1,0:T(8,128)S(1)}, u32[]{:S(2)}, u32[]{:S(2)}) collective-permute-start(f32[128,1024]{1,0:T(8,128)S(1)} %pad_maximum_fusion), channel_id=1, source_target_pairs={{0,8},{4,12},{8,0},{12,4},{16,24},{20,28},{24,16},{28,20},{1,9},{5... | collective-permute-start | bytes 1572872 | tf_op jit(solution)/shard_map/ppermute | solution.py:420
  174.2 13.5 %collective-permute-start.28 = (f32[64,512]{1,0:T(8,128)S(1)}, f32[64,512]{1,0:T(8,128)S(1)}, u32[]{:S(2)}, u32[]{:S(2)}) collective-permute-start(f32[64,512]{1,0:T(8,128)S(1)} %get-tuple-element.235), channel_id=1, source_target_pairs={{0,16},{4,20},{8,24},{12,28},{16,0},{20,4},{24,8},{28,12},{1,17},{... | collective-permute-start | bytes 393224 | tf_op jit(solution)/shard_map/ppermute | solution.py:420
  175.5 12.5 %collective-permute-start.29 = (f32[72,512]{1,0:T(8,128)S(1)}, f32[72,512]{1,0:T(8,128)S(1)}, u32[]{:S(2)}, u32[]{:S(2)}) collective-permute-start(f32[72,512]{1,0:T(8,128)S(1)} %get-tuple-element.233), channel_id=1, source_target_pairs={{0,8},{4,12},{8,0},{12,4},{16,24},{20,28},{24,16},{28,20},{1,9},{5... | collective-permute-start | bytes 442376 | tf_op jit(solution)/shard_map/ppermute | solution.py:420
  190.9 10.2 %collective-permute-start.39 = (f32[384,1024]{1,0:T(8,128)S(1)}, f32[384,1024]{1,0:T(8,128)S(1)}, u32[]{:S(2)}, u32[]{:S(2)}) collective-permute-start(f32[384,1024]{1,0:T(8,128)S(1)} %slice_dynamic-update-slice_fusion.refs_0_), channel_id=1, source_target_pairs={{0,4},{4,0},{8,12},{12,8},{16,20},{20,16},{24,28},{28,24},{1,5},{5... | collective-permute-start | bytes 4718600 | tf_op jit(solution)/shard_map/ppermute | solution.py:420
  (21 other events, 163.5 us)

commit v13 on v11

--- a/solution.py
+++ b/solution.py
@@ -127,18 +127,29 @@
     outs[output][position, number, here, :] = value
 
 
-def prepare_kernel(routes_ref, counts_ref, acts, out, routes, counts, sems):
+def prepare_kernel(routes_ref, counts_ref, acts, out, routes, counts, staged, sems):
     samples, feat = acts.shape
     experts = counts.shape[1]
-    copies = [
+    pieces = [pl.ds(first, samples // 4) for first in range(0, samples, samples // 4)]
+    small = [
         pltpu.make_async_copy(routes_ref, routes, sems.at[0]),
         pltpu.make_async_copy(counts_ref, counts, sems.at[1]),
-        pltpu.make_async_copy(acts, out.at[pl.ds(0, samples), :], sems.at[2]),
     ]
-    for copy in copies:
+    reads = [
+        pltpu.make_async_copy(acts.at[here, :], staged.at[here, :], sems.at[2 + number])
+        for number, here in enumerate(pieces)
+    ]
+    writes = [
+        pltpu.make_async_copy(staged.at[here, :], out.at[here, :], sems.at[6 + number])
+        for number, here in enumerate(pieces)
+    ]
+    for copy in small + reads:
         copy.start()
-    out[samples:, :] = jnp.zeros((out.shape[0] - samples, feat), F32)
-    for copy in copies[:2]:
+    staged[samples:, :] = jnp.zeros((out.shape[0] - samples, feat), F32)
+    for read, write in zip(reads, writes):
+        read.wait()
+        write.start()
+    for copy in small:
         copy.wait()
     hits = []
     for expert in range(experts):
@@ -153,8 +164,12 @@
         limit = counts[0, expert].astype(F32)
         keep = jnp.where(rank[expert : expert + 1, :] < limit, hits[expert], 0.0)
         row, column = samples + expert // per_row, expert % per_row * samples
-        out[row : row + 1, column : column + samples] = keep
-    copies[2].wait()
+        staged[row : row + 1, column : column + samples] = keep
+    last = pl.ds(samples, out.shape[0] - samples)
+    writes.append(pltpu.make_async_copy(staged.at[last, :], out.at[last, :], sems.at[10]))
+    writes[-1].start()
+    for write in writes:
+        write.wait()
 
 
 def act_kernel(turns, block, chips, seeded, samples, place, *refs):
@@ -223,11 +238,12 @@
         prepare_kernel,
         out_shape=jax.ShapeDtypeStruct((rows, feat), F32),
         in_specs=[pl.BlockSpec(memory_space=pltpu.HBM)] * 3,
-        out_specs=pl.BlockSpec(memory_space=pltpu.VMEM),
+        out_specs=pl.BlockSpec(memory_space=pltpu.HBM),
         scratch_shapes=[
             pltpu.VMEM(routes.shape[::-1], jnp.int32),
             pltpu.SMEM(counts.shape, jnp.int32),
-            pltpu.SemaphoreType.DMA((3,)),
+            pltpu.VMEM((rows, feat), F32),
+            pltpu.SemaphoreType.DMA((11,)),
         ],
         compiler_params=pltpu.CompilerParams(vmem_limit_bytes=60 * MIB),
     )(routes.T, counts, acts)
@@ -359,13 +375,13 @@
 
 
 def update_kernel(place, *refs):
-    blocks = refs[:-9]
-    inverse, scales, act_high, act_low, momentum, weights, moment_out, weight_out, full = refs[-9:]
+    blocks = refs[:-10]
+    inverse, scales, act_high, act_low, momentum, weights, moment_out, weight_out, high, low = refs[-10:]
     block = momentum.shape[0]
-    for here, value in row_pieces(place, block, full.shape[0] // (2 * block), blocks, 0)[0]:
-        full[here, :] = value[...]
+    for here, value in row_pieces(place, block, high.shape[0] // (2 * block), blocks, 0)[0]:
+        high[here, :], low[here, :] = split(value[...])
     damp, alpha = scales[0:1, 0:1], scales[1:2, 0:1]
-    half_way = times(inverse[...], *split(full[...]))
+    half_way = times(inverse[...], high, low)
     value = half_way
     for _ in range(3):
         value = half_way + value - alpha * (times(value, act_high[...], act_low[...]) + damp * value)
@@ -408,7 +424,7 @@
     block, feat = momentum.shape
     operands = (*blocks, inverse, scales, high, low, momentum, weights)
     shapes = [jax.ShapeDtypeStruct((block, feat), F32)] * 2
-    return on_core(update_kernel, place, operands, shapes, [pltpu.VMEM((feat, feat), F32)], 32)
+    return on_core(update_kernel, place, operands, shapes, [pltpu.VMEM((feat, feat), BF16)] * 2, 32)
 
 
 def swap(value, axis, step):
@@ -584,13 +600,13 @@
     across_mixed, _ = together(across_mixed, act_gather.whole)
     mixed_gather = Gather(both(mixed_sums, across_mixed, [slice(0, step), slice(step, block)]), chips)
     mixed_gather.begin()
+    grad_out, inverse = grad_factor_rows(place, grad_gather.exchange(), block, feat)
+    inverse = act_gather.hold_last(inverse)
     mixed_gather.whole = act_gather.hold_last(mixed_gather.whole)
     mixed_gather.relay()
     mine, theirs = mixed_gather.exchange(0, -1)
     act_out, *act_square = act_factor_rows(place, act_gather.exchange(), block, feat)
-    grad_blocks, act_square = together(grad_gather.exchange(), act_square)
-    grad_out, inverse = grad_factor_rows(place, grad_blocks, block, feat)
-    inverse = mixed_gather.hold_last(inverse)
+    act_square = mixed_gather.hold_last(act_square)
     my_last, their_last = mixed_gather.exchange(-1)
     mixed_blocks = (mine, my_last, theirs, their_last)
     outs = update_rows(place, mixed_blocks, inverse, *act_square, momentum[0], weights[0])

time: 178 us -> 178 us (level)
  transfers between devices with their start and end apart: 41 -> 41, of which waited for: 20 -> 22; matrix products, arithmetic and copies ran while one was open for 5% -> 5% of each run, Pallas kernels for 16% -> 16%
where the time goes in v13:
time: 178 us
  waiting for transfers between devices  88.9 us (50%)
  starting transfers between devices  41 us (23%)
  Pallas kernels  36.8 us (21%)
  local copies, waits for them, and re-layouts  5.28 us (3%)
  other arithmetic  4.21 us (2%)
  between operations  1.82 us (1%)
    ppermute x41, waiting for transfers between devices, swap(): return lax.ppermute(value, axis, [(i, i ^ step) for i in range(size)])  88.9 us
    ppermute x41, starting transfers between devices, swap(): return lax.ppermute(value, axis, [(i, i ^ step) for i in range(size)])  41 us
    pallas_call x4, Pallas kernels, bands(): pl.pallas_call(functools.partial(body, range(turns), block, chips, bool(s...  22.4 us
    pallas_call x3, Pallas kernels, on_core(): pl.pallas_call(body, out_shape=shapes, in_specs=[pl.BlockSpec(memory_spac...  12.2 us
  transfers between devices with their start and end apart: 41, of which 22 were waited for; matrix products, arithmetic and copies ran while one was open for 5% of the time, Pallas kernels for 16%

profile of v13, /device:TPU:25, one launch (start us, length us, event | category | flops | bytes accessed | tf_op | source)
XLA Modules:
  0.0 178.0 jit_solution(6450291428901866941)
XLA Ops:
  0.6 2.2 %shard_map.111.refs_0_.refs_2_ = f32[264,1024]{1,0:T(8,128)} custom-call(s32[2,256]{1,0:T(2,128)} %bitcast.82, s32[1,4]{1,0:T(1,128)} %counts_ref.1, f32[256,1024]{1,0:T(8,128)} %acts.1), custom_call_target="tpu_custom_call" | custom-call | tf_op jit(solution)/shard_map/pallas_call | solution.py:237
  11.6 3.7 %shard_map.112 = (f32[2,2,64,512]{3,2,1,0:T(8,128)S(1)}, f32[2,2,64,512]{3,2,1,0:T(8,128)S(1)}, f32[2,2,72,512]{3,2,1,0:T(8,128)S(1)}, f32[2,2,72,512]{3,2,1,0:T(8,128)S(1)}) custom-call(s32[2]{0:T(128)S(1)} %pad_add_fusion.place, f32[264,1024]{1,0:T(8,128)S(1)} %copy-done, f32[264,1024]{1,0:T(8,128)S(1)} %collective-permute-done.1.refs_1_.refs_3_), custom_call_target="tpu_custom_call" | custom-call | tf_op jit(solution)/shard_map/pallas_call | solution.py:265
  15.3 7.6 %shard_map.113 = (f32[2,1,64,512]{3,2,1,0:T(8,128)S(1)}, f32[2,1,64,512]{3,2,1,0:T(8,128)S(1)}, f32[2,1,72,512]{3,2,1,0:T(8,128)S(1)}, f32[2,1,72,512]{3,2,1,0:T...) custom-call(s32[2]{0:T(128)S(1)} %pad_add_fusion.place, ...), custom_call_target="tpu_custom_call" | custom-call | tf_op jit(solution)/shard_map/pallas_call | solution.py:265
  23.0 6.2 %collective-permute-done.refs_0_.refs_2_ = f32[264,1024]{1,0:T(8,128)S(1)} collective-permute-done((f32[264,1024]{1,0:T(8,128)}, f32[264,1024]{1,0:T(8,128)S(1)}, u32[]{:S(2)}, u32[]{:S(2)}) %collective-permute-start) | collective-permute-done | bytes 1081376 | tf_op jit(solution)/shard_map/ppermute | solution.py:432
  30.2 2.2 %collective-permute-done.3.refs_1_.refs_3_ = f32[264,1024]{1,0:T(8,128)S(1)} collective-permute-done((f32[264,1024]{1,0:T(8,128)S(1)}, f32[264,1024]{1,0:T(8,128)S(1)}, u32[]{:S(2)}, u32[]{:S(2)}) %collective-permute-start.3) | collective-permute-done | bytes 1081376 | tf_op jit(solution)/shard_map/ppermute | solution.py:432
  32.4 3.8 %shard_map.114 = (f32[2,2,64,512]{3,2,1,0:T(8,128)S(1)}, f32[2,2,64,512]{3,2,1,0:T(8,128)S(1)}, f32[2,2,72,512]{3,2,1,0:T(8,128)S(1)}, f32[2,2,72,512]{3,2,1,0:T(8,128)S(1)}) custom-call(s32[2]{0:T(128)S(1)} %pad_add_fusion.place, f32[264,1024]{1,0:T(8,128)S(1)} %collective-permute-done.refs_0_.refs_2_, ...), custom_call_target="tpu_custom_call" | custom-call | tf_op jit(solution)/shard_map/pallas_call | solution.py:265
  38.7 10.7 %collective-permute-done.4 = f32[2,2,64,512]{3,2,1,0:T(8,128)S(1)} collective-permute-done((f32[2,2,64,512]{3,2,1,0:T(8,128)S(1)}, f32[2,2,64,512]{3,2,1,0:T(8,128)S(1)}, u32[]{:S(2)}, u32[]{:S(2)}) %collective-permute-start.4) | collective-permute-done | bytes 524320 | tf_op jit(solution)/shard_map/ppermute | solution.py:432
  49.4 2.2 %collective-permute-done.6 = f32[2,2,72,512]{3,2,1,0:T(8,128)S(1)} collective-permute-done((f32[2,2,72,512]{3,2,1,0:T(8,128)S(1)}, f32[2,2,72,512]{3,2,1,0:T(8,128)S(1)}, u32[]{:S(2)}, u32[]{:S(2)}) %collective-permute-start.6) | collective-permute-done | bytes 589856 | tf_op jit(solution)/shard_map/ppermute | solution.py:432
  51.7 3.1 %collective-permute-done.8.refs_0_ = f32[256,1024]{1,0:T(8,128)S(1)} collective-permute-done((f32[256,1024]{1,0:T(8,128)S(1)}, f32[256,1024]{1,0:T(8,128)S(1)}, u32[]{:S(2)}, u32[]{:S(2)}) %collective-permute-start.8) | collective-permute-done | bytes 1048608 | tf_op jit(solution)/shard_map/ppermute | solution.py:432
  58.1 7.2 %shard_map.115 = (f32[2,1,64,512]{3,2,1,0:T(8,128)S(1)}, f32[2,1,64,512]{3,2,1,0:T(8,128)S(1)}, f32[2,1,72,512]{3,2,1,0:T(8,128)S(1)}, f32[2,1,72,512]{3,2,1,0:T...) custom-call(s32[2]{0:T(128)S(1)} %pad_add_fusion.place, ...), custom_call_target="tpu_custom_call" | custom-call | tf_op jit(solution)/shard_map/pallas_call | solution.py:265
  68.1 15.9 %collective-permute-done.10 = f32[2,1,192,512]{3,2,1,0:T(8,128)S(1)} collective-permute-done((f32[2,1,192,512]{3,2,1,0:T(8,128)S(1)}, f32[2,1,192,512]{3,2,1,0:T(8,128)S(1)}, u32[]{:S(2)}, u32[]{:S(2)}) %collective-permute-start.10) | collective-permute-done | bytes 786464 | tf_op jit(solution)/shard_map/ppermute | solution.py:432
  89.9 2.0 %collective-permute-done.13 = f32[2,1,64,512]{3,2,1,0:T(8,128)S(1)} collective-permute-done((f32[2,1,64,512]{3,2,1,0:T(8,128)S(1)}, f32[2,1,64,512]{3,2,1,0:T(8,128)S(1)}, u32[]{:S(2)}, u32[]{:S(2)}) %collective-permute-start.13) | collective-permute-done | bytes 262176 | tf_op jit(solution)/shard_map/ppermute | solution.py:432
  95.4 5.4 %collective-permute-done.16 = f32[1,1,192,512]{3,2,1,0:T(8,128)S(1)} collective-permute-done((f32[1,1,192,512]{3,2,1,0:T(8,128)S(1)}, f32[1,1,192,512]{3,2,1,0:T(8,128)S(1)}, u32[]{:S(2)}, u32[]{:S(2)}) %collective-permute-start.16) | collective-permute-done | bytes 393248 | tf_op jit(solution)/shard_map/ppermute | solution.py:432
  102.7 12.4 %collective-permute-done.18 = f32[136,512]{1,0:T(8,128)S(1)} collective-permute-done((f32[136,512]{1,0:T(8,128)S(1)}, f32[136,512]{1,0:T(8,128)S(1)}, u32[]{:S(2)}, u32[]{:S(2)}) %collective-permute-start.18) | collective-permute-done | bytes 278560 | tf_op jit(solution)/shard_map/ppermute | solution.py:432
  118.6 2.2 %collective-permute-done.21 = f32[136,512]{1,0:T(8,128)S(1)} collective-permute-done((f32[136,512]{1,0:T(8,128)S(1)}, f32[136,512]{1,0:T(8,128)S(1)}, u32[]{:S(2)}, u32[]{:S(2)}) %collective-permute-start.21) | collective-permute-done | bytes 278560 | tf_op jit(solution)/shard_map/ppermute | solution.py:432
  120.8 4.9 %collective-permute-done.24 = f32[1,1,64,1024]{3,2,1,0:T(8,128)S(1)} collective-permute-done((f32[1,1,64,1024]{3,2,1,0:T(8,128)S(1)}, f32[1,1,64,1024]{3,2,1,0:T(8,128)S(1)}, u32[]{:S(2)}, u32[]{:S(2)}) %collective-permute-start.24) | collective-permute-done | bytes 262176 | tf_op jit(solution)/shard_map/ppermute | solution.py:432
  129.0 5.0 %collective-permute-done.30 = f32[64,512]{1,0:T(8,128)S(1)} collective-permute-done((f32[64,512]{1,0:T(8,128)S(1)}, f32[64,512]{1,0:T(8,128)S(1)}, u32[]{:S(2)}, u32[]{:S(2)}) %collective-permute-start.30) | collective-permute-done | bytes 131104 | tf_op jit(solution)/shard_map/ppermute | solution.py:432
  134.4 6.7 %collective-permute-start.32 = (f32[544,512]{1,0:T(8,128)S(1)}, f32[544,512]{1,0:T(8,128)S(1)}, u32[]{:S(2)}, u32[]{:S(2)}) collective-permute-start(f32[544,512]{1,0:T(8,128)S(1)} %constant_dynamic-update-slice_fusion.2.refs_0_), channel_id=1, source_target_pairs={{0,4},{4,0},{8,12},{12,8},{16,20},{20,16},{24,28},{28,24},{1,5},{5... | collective-permute-start | bytes 3342344 | tf_op jit(solution)/shard_map/ppermute | solution.py:432
  145.3 3.4 %shard_map.116 = (f32[128,1024]{1,0:T(8,128)}, f32[128,1024]{1,0:T(8,128)S(1)}) custom-call(s32[2]{0:T(128)S(1)} %pad_add_fusion.place, f32[544,512]{1,0:T(8,128)S(1)} %constant_dynamic-update-slice_fusion.2.refs_0_, f32[544,512]{1,0:T(8,128)S(1)} %collective-permute-done.32.refs_1_), custom_call_target="tpu_custom_call" | custom-call | tf_op jit(solution)/shard_map/pallas_call | solution.py:394
  148.8 8.1 %collective-permute-done.28 = f32[64,512]{1,0:T(8,128)S(1)} collective-permute-done((f32[64,512]{1,0:T(8,128)S(1)}, f32[64,512]{1,0:T(8,128)S(1)}, u32[]{:S(2)}, u32[]{:S(2)}) %collective-permute-start.28) | collective-permute-done | bytes 131104 | tf_op jit(solution)/shard_map/ppermute | solution.py:432
  157.3 2.7 %collective-permute-start.36 = (f32[544,512]{1,0:T(8,128)S(1)}, f32[544,512]{1,0:T(8,128)S(1)}, u32[]{:S(2)}, u32[]{:S(2)}) collective-permute-start(f32[544,512]{1,0:T(8,128)S(1)} %constant_dynamic-update-slice_fusion.8.refs_0_), channel_id=1, source_target_pairs={{0,4},{4,0},{8,12},{12,8},{16,20},{20,16},{24,28},{28,24},{1,5},{5... | collective-permute-start | bytes 3342344 | tf_op jit(solution)/shard_map/ppermute | solution.py:432
  162.6 2.7 %shard_map.117 = (f32[128,1024]{1,0:T(8,128)}, f32[8,128]{1,0:T(8,128)S(1)}, bf16[1024,1024]{1,0:T(8,128)(2,1)S(1)}, bf16[1024,1024]{1,0:T(8,128)(2,1)S(1)}) custom-call(s32[2]{0:T(128)S(1)} %pad_add_fusion.place, f32[544,512]{1,0:T(8,128)S(1)} %constant_dynamic-update-slice_fusion.8.refs_0_, f32[544,512]{1,0:T(8,128)S(1)} %collective-permute-done.36.refs_1_), custom_call_target="tpu_custom_call" | custom-call | tf_op jit(solution)/shard_map/pallas_call | solution.py:394
  165.3 2.5 %collective-permute-done.37 = f32[64,1024]{1,0:T(8,128)S(1)} collective-permute-done((f32[64,1024]{1,0:T(8,128)S(1)}, f32[64,1024]{1,0:T(8,128)S(1)}, u32[]{:S(2)}, u32[]{:S(2)}) %collective-permute-start.37) | collective-permute-done | bytes 262176 | tf_op jit(solution)/shard_map/ppermute | solution.py:432
  171.9 6.1 %shard_map.118 = (f32[128,1024]{1,0:T(8,128)}, f32[128,1024]{1,0:T(8,128)}) custom-call(s32[2]{0:T(128)S(1)} %pad_add_fusion.place, f32[384,1024]{1,0:T(8,128)S(1)} %slice_dynamic-update-slice_fusion.refs_0_, f32[128,1024]{1,0:T(8,128)S(1)} %constant_dynamic-update-slice_fusion.18.refs_1_, f32[384,1024]{1,0:T(8,128)S(1)} %collective-permute-done.39.refs_2_, ...), custom_call_target="tpu_custom_call" | custom-call | tf_op jit(solution)/shard_map/pallas_call | solution.py:394
  (138 shorter events, 47.1 us)
Async XLA Ops:
  3.6 25.7 %collective-permute-start = (f32[264,1024]{1,0:T(8,128)}, f32[264,1024]{1,0:T(8,128)S(1)}, u32[]{:S(2)}, u32[]{:S(2)}) collective-permute-start(f32[264,1024]{1,0:T(8,128)} %shard_map.111.refs_0_.refs_2_), channel_id=1, source_target_pairs={{0,1},{1,0},{2,3},{3,2},{4,5},{5,4},{6,7},{7,6},{8,9},{9,8},{10,11... | collective-permute-start | bytes 3244040 | tf_op jit(solution)/shard_map/ppermute | solution.py:432
  3.8 11.6 %collective-permute-start.2 = (f32[256,1024]{1,0:T(8,128)S(1)}, f32[256,1024]{1,0:T(8,128)}, u32[]{:S(2)}, u32[]{:S(2)}) collective-permute-start(f32[256,1024]{1,0:T(8,128)S(1)} %copy-done.1), channel_id=1, source_target_pairs={{0,4},{4,0},{8,12},{12,8},{16,20},{20,16},{24,28},{28,24},{1,5},{5... | collective-permute-start | bytes 3145736 | tf_op jit(solution)/shard_map/ppermute | solution.py:432
  30.1 24.8 %collective-permute-start.8 = (f32[256,1024]{1,0:T(8,128)S(1)}, f32[256,1024]{1,0:T(8,128)S(1)}, u32[]{:S(2)}, u32[]{:S(2)}) collective-permute-start(f32[256,1024]{1,0:T(8,128)S(1)} %copy-done.1), channel_id=1, source_target_pairs={{0,1},{1,0},{2,3},{3,2},{4,5},{5,4},{6,7},{7,6},{8,9},{9,8},{10,11... | collective-permute-start | bytes 3145736 | tf_op jit(solution)/shard_map/ppermute | solution.py:432
  36.2 13.2 %collective-permute-start.4 = (f32[2,2,64,512]{3,2,1,0:T(8,128)S(1)}, f32[2,2,64,512]{3,2,1,0:T(8,128)S(1)}, u32[]{:S(2)}, u32[]{:S(2)}) collective-permute-start(f32[2,2,64,512]{3,2,1,0:T(8,128)S(1)} %get-tuple-element.129), channel_id=1, source_target_pairs={{0,8},{4,12},{8,0},{12,4},{16,24},{20,28},{24,16},{28,20},{1,9},{5... | collective-permute-start | bytes 1572872 | tf_op jit(solution)/shard_map/ppermute | solution.py:432
  37.5 14.2 %collective-permute-start.6 = (f32[2,2,72,512]{3,2,1,0:T(8,128)S(1)}, f32[2,2,72,512]{3,2,1,0:T(8,128)S(1)}, u32[]{:S(2)}, u32[]{:S(2)}) collective-permute-start(f32[2,2,72,512]{3,2,1,0:T(8,128)S(1)} %get-tuple-element.131), channel_id=1, source_target_pairs={{0,16},{4,20},{8,24},{12,28},{16,0},{20,4},{24,8},{28,12},{1,17},{... | collective-permute-start | bytes 1769480 | tf_op jit(solution)/shard_map/ppermute | solution.py:432
  65.4 18.6 %collective-permute-start.10 = (f32[2,1,192,512]{3,2,1,0:T(8,128)S(1)}, f32[2,1,192,512]{3,2,1,0:T(8,128)S(1)}, u32[]{:S(2)}, u32[]{:S(2)}) collective-permute-start(f32[2,1,192,512]{3,2,1,0:T(8,128)S(1)} %get-tuple-element.151), channel_id=1, source_target_pairs={{0,8},{4,12},{8,0},{12,4},{16,24},{20,28},{24,16},{28,20},{1,9},{5... | collective-permute-start | bytes 2359304 | tf_op jit(solution)/shard_map/ppermute | solution.py:432
  66.5 19.2 %collective-permute-start.11 = (f32[2,1,200,512]{3,2,1,0:T(8,128)S(1)}, f32[2,1,200,512]{3,2,1,0:T(8,128)S(1)}, u32[]{:S(2)}, u32[]{:S(2)}) collective-permute-start(f32[2,1,200,512]{3,2,1,0:T(8,128)S(1)} %get-tuple-element.152), channel_id=1, source_target_pairs={{0,16},{4,20},{8,24},{12,28},{16,0},{20,4},{24,8},{28,12},{1,17},{... | collective-permute-start | bytes 2457608 | tf_op jit(solution)/shard_map/ppermute | solution.py:432
  67.9 19.3 %collective-permute-start.12 = (f32[136,512]{1,0:T(8,128)S(1)}, f32[136,512]{1,0:T(8,128)S(1)}, u32[]{:S(2)}, u32[]{:S(2)}) collective-permute-start(f32[136,512]{1,0:T(8,128)S(1)} %maximum_bitcast_fusion), channel_id=1, source_target_pairs={{0,2},{1,3},{2,0},{3,1},{4,6},{5,7},{6,4},{7,5},{8,10},{9,11},{10,... | collective-permute-start | bytes 835592 | tf_op jit(solution)/shard_map/ppermute | solution.py:432
  87.8 13.0 %collective-permute-start.16 = (f32[1,1,192,512]{3,2,1,0:T(8,128)S(1)}, f32[1,1,192,512]{3,2,1,0:T(8,128)S(1)}, u32[]{:S(2)}, u32[]{:S(2)}) collective-permute-start(f32[1,1,192,512]{3,2,1,0:T(8,128)S(1)} %slice_add_fusion.1), channel_id=1, source_target_pairs={{0,16},{4,20},{8,24},{12,28},{16,0},{20,4},{24,8},{28,12},{1,17},{... | collective-permute-start | bytes 1179656 | tf_op jit(solution)/shard_map/ppermute | solution.py:432
  88.0 14.4 %collective-permute-start.17 = (f32[1,1,200,512]{3,2,1,0:T(8,128)S(1)}, f32[1,1,200,512]{3,2,1,0:T(8,128)S(1)}, u32[]{:S(2)}, u32[]{:S(2)}) collective-permute-start(f32[1,1,200,512]{3,2,1,0:T(8,128)S(1)} %slice_add_fusion), channel_id=1, source_target_pairs={{0,8},{4,12},{8,0},{12,4},{16,24},{20,28},{24,16},{28,20},{1,9},{5... | collective-permute-start | bytes 1228808 | tf_op jit(solution)/shard_map/ppermute | solution.py:432
  92.3 22.8 %collective-permute-start.15 = (f32[1,1,64,512]{3,2,1,0:T(8,128)S(1)}, f32[1,1,64,512]{3,2,1,0:T(8,128)S(1)}, u32[]{:S(2)}, u32[]{:S(2)}) collective-permute-start(f32[1,1,64,512]{3,2,1,0:T(8,128)S(1)} %slice_add_fusion.12), channel_id=1, source_target_pairs={{0,16},{4,20},{8,24},{12,28},{16,0},{20,4},{24,8},{28,12},{1,17},{... | collective-permute-start | bytes 393224 | tf_op jit(solution)/shard_map/ppermute | solution.py:432
  93.9 21.3 %collective-permute-start.19 = (f32[1,1,72,512]{3,2,1,0:T(8,128)S(1)}, f32[1,1,72,512]{3,2,1,0:T(8,128)S(1)}, u32[]{:S(2)}, u32[]{:S(2)}) collective-permute-start(f32[1,1,72,512]{3,2,1,0:T(8,128)S(1)} %slice_add_fusion.11), channel_id=1, source_target_pairs={{0,8},{4,12},{8,0},{12,4},{16,24},{20,28},{24,16},{28,20},{1,9},{5... | collective-permute-start | bytes 442376 | tf_op jit(solution)/shard_map/ppermute | solution.py:432
  95.2 21.7 %collective-permute-start.22 = (f32[2,1,64,1024]{3,2,1,0:T(8,128)S(1)}, f32[2,1,64,1024]{3,2,1,0:T(8,128)S(1)}, u32[]{:S(2)}, u32[]{:S(2)}) collective-permute-start(f32[2,1,64,1024]{3,2,1,0:T(8,128)S(1)} %get-tuple-element.175), channel_id=1, source_target_pairs={{0,8},{4,12},{8,0},{12,4},{16,24},{20,28},{24,16},{28,20},{1,9},{5... | collective-permute-start | bytes 1572872 | tf_op jit(solution)/shard_map/ppermute | solution.py:432
  100.8 16.1 %collective-permute-start.23 = (f32[2,1,64,1024]{3,2,1,0:T(8,128)S(1)}, f32[2,1,64,1024]{3,2,1,0:T(8,128)S(1)}, u32[]{:S(2)}, u32[]{:S(2)}) collective-permute-start(f32[2,1,64,1024]{3,2,1,0:T(8,128)S(1)} %get-tuple-element.177), channel_id=1, source_target_pairs={{0,16},{4,20},{8,24},{12,28},{16,0},{20,4},{24,8},{28,12},{1,17},{... | collective-permute-start | bytes 1572872 | tf_op jit(solution)/shard_map/ppermute | solution.py:432
  102.6 12.6 %collective-permute-start.18 = (f32[136,512]{1,0:T(8,128)S(1)}, f32[136,512]{1,0:T(8,128)S(1)}, u32[]{:S(2)}, u32[]{:S(2)}) collective-permute-start(f32[136,512]{1,0:T(8,128)S(1)} %maximum_bitcast_fusion.1), channel_id=1, source_target_pairs={{0,2},{1,3},{2,0},{3,1},{4,6},{5,7},{6,4},{7,5},{8,10},{9,11},{10,... | collective-permute-start | bytes 835592 | tf_op jit(solution)/shard_map/ppermute | solution.py:432
  118.5 23.4 %collective-permute-start.33 = (f32[128,1024]{1,0:T(8,128)S(1)}, f32[128,1024]{1,0:T(8,128)S(1)}, u32[]{:S(2)}, u32[]{:S(2)}) collective-permute-start(f32[128,1024]{1,0:T(8,128)S(1)} %bitcast.81), channel_id=1, source_target_pairs={{0,2},{1,3},{2,0},{3,1},{4,6},{5,7},{6,4},{7,5},{8,10},{9,11},{10,... | collective-permute-start | bytes 1572872 | tf_op jit(solution)/shard_map/ppermute | solution.py:432
  125.8 16.1 %collective-permute-start.27 = (f32[136,512]{1,0:T(8,128)S(1)}, f32[136,512]{1,0:T(8,128)S(1)}, u32[]{:S(2)}, u32[]{:S(2)}) collective-permute-start(f32[136,512]{1,0:T(8,128)S(1)} %get-tuple-element.237), channel_id=1, source_target_pairs={{0,16},{4,20},{8,24},{12,28},{16,0},{20,4},{24,8},{28,12},{1,17},{... | collective-permute-start | bytes 835592 | tf_op jit(solution)/shard_map/ppermute | solution.py:432
  127.1 14.8 %collective-permute-start.26 = (f32[136,512]{1,0:T(8,128)S(1)}, f32[136,512]{1,0:T(8,128)S(1)}, u32[]{:S(2)}, u32[]{:S(2)}) collective-permute-start(f32[136,512]{1,0:T(8,128)S(1)} %get-tuple-element.237), channel_id=1, source_target_pairs={{0,8},{4,12},{8,0},{12,4},{16,24},{20,28},{24,16},{28,20},{1,9},{5... | collective-permute-start | bytes 835592 | tf_op jit(solution)/shard_map/ppermute | solution.py:432
  134.4 10.9 %collective-permute-start.32 = (f32[544,512]{1,0:T(8,128)S(1)}, f32[544,512]{1,0:T(8,128)S(1)}, u32[]{:S(2)}, u32[]{:S(2)}) collective-permute-start(f32[544,512]{1,0:T(8,128)S(1)} %constant_dynamic-update-slice_fusion.2.refs_0_), channel_id=1, source_target_pairs={{0,4},{4,0},{8,12},{12,8},{16,20},{20,16},{24,28},{28,24},{1,5},{5... | collective-permute-start | bytes 3342344 | tf_op jit(solution)/shard_map/ppermute | solution.py:432
  142.1 15.2 %collective-permute-start.35 = (f32[128,1024]{1,0:T(8,128)S(1)}, f32[128,1024]{1,0:T(8,128)S(1)}, u32[]{:S(2)}, u32[]{:S(2)}) collective-permute-start(f32[128,1024]{1,0:T(8,128)S(1)} %pad_maximum_fusion), channel_id=1, source_target_pairs={{0,16},{4,20},{8,24},{12,28},{16,0},{20,4},{24,8},{28,12},{1,17},{... | collective-permute-start | bytes 1572872 | tf_op jit(solution)/shard_map/ppermute | solution.py:432
  142.4 14.9 %collective-permute-start.34 = (f32[128,1024]{1,0:T(8,128)S(1)}, f32[128,1024]{1,0:T(8,128)S(1)}, u32[]{:S(2)}, u32[]{:S(2)}) collective-permute-start(f32[128,1024]{1,0:T(8,128)S(1)} %pad_maximum_fusion), channel_id=1, source_target_pairs={{0,8},{4,12},{8,0},{12,4},{16,24},{20,28},{24,16},{28,20},{1,9},{5... | collective-permute-start | bytes 1572872 | tf_op jit(solution)/shard_map/ppermute | solution.py:432
  143.4 13.5 %collective-permute-start.28 = (f32[64,512]{1,0:T(8,128)S(1)}, f32[64,512]{1,0:T(8,128)S(1)}, u32[]{:S(2)}, u32[]{:S(2)}) collective-permute-start(f32[64,512]{1,0:T(8,128)S(1)} %get-tuple-element.235), channel_id=1, source_target_pairs={{0,16},{4,20},{8,24},{12,28},{16,0},{20,4},{24,8},{28,12},{1,17},{... | collective-permute-start | bytes 393224 | tf_op jit(solution)/shard_map/ppermute | solution.py:432
  144.8 12.5 %collective-permute-start.29 = (f32[72,512]{1,0:T(8,128)S(1)}, f32[72,512]{1,0:T(8,128)S(1)}, u32[]{:S(2)}, u32[]{:S(2)}) collective-permute-start(f32[72,512]{1,0:T(8,128)S(1)} %get-tuple-element.233), channel_id=1, source_target_pairs={{0,8},{4,12},{8,0},{12,4},{16,24},{20,28},{24,16},{28,20},{1,9},{5... | collective-permute-start | bytes 442376 | tf_op jit(solution)/shard_map/ppermute | solution.py:432
  160.2 10.2 %collective-permute-start.39 = (f32[384,1024]{1,0:T(8,128)S(1)}, f32[384,1024]{1,0:T(8,128)S(1)}, u32[]{:S(2)}, u32[]{:S(2)}) collective-permute-start(f32[384,1024]{1,0:T(8,128)S(1)} %slice_dynamic-update-slice_fusion.refs_0_), channel_id=1, source_target_pairs={{0,4},{4,0},{8,12},{12,8},{16,20},{20,16},{24,28},{28,24},{1,5},{5... | collective-permute-start | bytes 4718600 | tf_op jit(solution)/shard_map/ppermute | solution.py:432
  (21 other events, 132.8 us)

commit v14 on v12

--- a/solution.py
+++ b/solution.py
@@ -59,7 +59,7 @@
 
 def keep_row(parts, samples, expert):
     row, column = keep_place(expert, samples, parts[0].shape[1])
-    return jnp.concatenate([part[pl.ds(samples + row, 1), pl.ds(column, samples)] for part in parts], axis=1)
+    return jnp.concatenate([part[pl.ds(row, 1), pl.ds(column, samples)] for part in parts], axis=1)
 
 
 def weighted(rows, keeps):
@@ -127,19 +127,9 @@
     outs[output][position, number, here, :] = value
 
 
-def prepare_kernel(routes_ref, counts_ref, acts, out, routes, counts, keeps, sems):
-    samples, feat = acts.shape
+def prepare_kernel(routes, counts, out, samples, feat):
     experts = counts.shape[1]
-    copies = [
-        pltpu.make_async_copy(acts, out.at[pl.ds(0, samples), :], sems.at[0]),
-        pltpu.make_async_copy(routes_ref, routes, sems.at[1]),
-        pltpu.make_async_copy(counts_ref, counts, sems.at[2]),
-    ]
-    for copy in copies:
-        copy.start()
-    keeps[...] = jnp.zeros(keeps.shape, F32)
-    for copy in copies[1:]:
-        copy.wait()
+    out[...] = jnp.zeros(out.shape, F32)
     hits = []
     for expert in range(experts):
         same = [jnp.where(routes[k : k + 1, :] == expert, 1.0, 0.0) for k in range(routes.shape[0])]
@@ -153,22 +143,18 @@
         limit = counts[0, expert].astype(F32)
         keep = jnp.where(rank[expert : expert + 1, :] < limit, hits[expert], 0.0)
         row, column = expert // per_row, expert % per_row * samples
-        keeps[row : row + 1, column : column + samples] = keep
-    last = pltpu.make_async_copy(keeps, out.at[pl.ds(samples, keeps.shape[0]), :], sems.at[3])
-    last.start()
-    last.wait()
-    copies[0].wait()
+        out[row : row + 1, column : column + samples] = keep
 
 
 def act_kernel(turns, block, chips, seeded, samples, place, *refs):
-    parts, refs = refs[:2], refs[2:]
+    parts, kept, refs = refs[:2], refs[2:4], refs[4:]
     refs, (high, low, turned) = refs[:-3], refs[-3:]
     seeds, outs = (refs[: len(refs) // 2], refs[len(refs) // 2 :]) if seeded else ((), refs)
     feat = parts[0].shape[1]
     width = feat // 2 + TILE
     mine, expert = place[0], place[1]
     split_rows(parts, samples, high, low, feat)
-    keeps = [keep_row(parts, samples, expert ^ (2 * turn)) for turn in turns]
+    keeps = [keep_row(kept, samples, expert ^ (2 * turn)) for turn in turns]
     places = slots(chips)
     for k in range(chips):
         column, row = band_place(mine ^ (2 * k), block)
@@ -182,7 +168,7 @@
 
 
 def grad_kernel(turns, block, chips, seeded, samples, place, *refs):
-    grads, acts, refs = refs[:2], refs[2:4], refs[4:]
+    grads, acts, kept, refs = refs[:2], refs[2:4], refs[4:6], refs[6:]
     refs, (high, low, act_high, act_low, turned) = refs[:-5], refs[-5:]
     seeds, outs = (refs[: len(refs) // 2], refs[len(refs) // 2 :]) if seeded else ((), refs)
     feat = grads[0].shape[1]
@@ -190,7 +176,7 @@
     mine, expert = place[0], place[1]
     split_rows(grads, samples, high, low, feat)
     split_rows(acts, samples, act_high, act_low, feat)
-    keeps = [keep_row(acts, samples, expert ^ (2 * turn)) for turn in turns]
+    keeps = [keep_row(kept, samples, expert ^ (2 * turn)) for turn in turns]
     places = slots(chips)
     for k in range(chips):
         column, row = band_place(mine ^ (2 * k), block)
@@ -219,29 +205,23 @@
     return [pl.BlockSpec(memory_space=pltpu.VMEM)] * count
 
 
-def prepare(routes, counts, acts):
-    samples, feat = acts.shape
-    rows = samples + 8 * -(-counts.shape[1] * samples // (8 * feat))
+def prepare(routes, counts, feat):
+    samples = routes.shape[0]
+    rows = EXTRA * -(-counts.shape[1] * samples // (EXTRA * feat))
     return pl.pallas_call(
-        prepare_kernel,
+        functools.partial(prepare_kernel, samples=samples, feat=feat),
         out_shape=jax.ShapeDtypeStruct((rows, feat), F32),
-        in_specs=[pl.BlockSpec(memory_space=pltpu.HBM)] * 3,
-        out_specs=pl.BlockSpec(memory_space=pltpu.HBM),
-        scratch_shapes=[
-            pltpu.VMEM(routes.shape[::-1], jnp.int32),
-            pltpu.SMEM(counts.shape, jnp.int32),
-            pltpu.VMEM((rows - samples, feat), F32),
-            pltpu.SemaphoreType.DMA((4,)),
-        ],
+        in_specs=[pl.BlockSpec(memory_space=pltpu.VMEM), pl.BlockSpec(memory_space=pltpu.SMEM)],
+        out_specs=pl.BlockSpec(memory_space=pltpu.VMEM),
         compiler_params=pltpu.CompilerParams(vmem_limit_bytes=60 * MIB),
-    )(routes.T, counts, acts)
+    )(routes.T, counts)
 
 
 def bands(body, turns, groups, place, parts, seeds, samples, chips, block):
     feat = parts[0].shape[1]
     extended = pltpu.VMEM((2 * samples, feat + feat // 2), BF16)
     plain = pltpu.VMEM((2 * samples, feat), BF16)
-    scratch = [extended, extended] + ([plain, plain] if len(parts) > 2 else [])
+    scratch = [extended, extended] + ([plain, plain] if len(parts) > 4 else [])
     shapes = [
         jax.ShapeDtypeStruct((len(group), count, *piece_shape(kind, half, block, feat)), F32)
         for count, kind in groups
@@ -249,7 +229,7 @@
         for group in held_and_sent(chips, order)
     ]
     operands = (*parts, *seeds)
-    limit = 36 if len(parts) > 2 else 20
+    limit = 36 if len(parts) > 4 else 20
     return pl.pallas_call(
         functools.partial(body, range(turns), block, chips, bool(seeds), samples),
         out_shape=shapes,
@@ -509,9 +489,10 @@
     act_groups = ((turns, "factor"),)
     grad_groups = ((1, "factor"), (1, "mixed"), (turns - 1, "both"))
 
-    acts = prepare(routes, counts, acts)
     acts_far = swap(acts, "expert", 1)
-    near_acts = (acts, swap(acts, "dp", 1))
+    keep = prepare(routes, counts, feat)
+    keep_far = swap(keep, "expert", 1)
+    near_acts = (acts, swap(acts, "dp", 1), keep, swap(keep, "dp", 1))
     act_seeds = bands(act_kernel, turns, act_groups, place, near_acts, (), *size)
     grads_far = swap(grads_out, "expert", 1)
     grad_parts = (grads_out, swap(grads_out, "dp", 1)) + near_acts
@@ -520,7 +501,7 @@
     early = (act_seeds, grad_seeds, old_act, old_grad)
     acts_far, (act_seeds, grad_seeds, old_act, old_grad) = together(acts_far, early)
 
-    far_acts = (acts_far, swap(acts_far, "dp", 1))
+    far_acts = (acts_far, swap(acts_far, "dp", 1), keep_far, swap(keep_far, "dp", 1))
     act_sum = PlaneSum(bands(act_kernel, turns, act_groups, place, far_acts, act_seeds, *size), chips)
     act_sum.send()
     act_sum.add()

time: 209 us -> 177 us (0.85)
  Pallas kernels: 67 us -> 35 us
  waiting for transfers between devices: 89 us -> 83 us
  starting transfers between devices: 40.9 us -> 45.5 us
    pallas_call x1, Pallas kernels: 32.9 us -> 1.57 us  [prepare(): pl.pallas_call(functools.partial(prepare_kernel, samples=samples, feat=fe...]
    ppermute x41 -> x44, waiting for transfers between devices: 89 us -> 83 us  [swap(): return lax.ppermute(value, axis, [(i, i ^ step) for i in range(size)])]
    ppermute x41 -> x44, starting transfers between devices: 40.9 us -> 45.5 us  [swap(): return lax.ppermute(value, axis, [(i, i ^ step) for i in range(size)])]
  transfers between devices with their start and end apart: 41 -> 44, of which waited for: 22 -> 23; matrix products, arithmetic and copies ran while one was open for 5% -> 5% of each run, Pallas kernels for 14% -> 17%
where the time goes in v14:
time: 177 us; the launch traced here: 175 us
  waiting for transfers between devices  83 us (47%)
  starting transfers between devices  45.5 us (26%)
  Pallas kernels  35 us (20%)
  local copies, waits for them, and re-layouts  5.29 us (3%)
  other arithmetic  4.22 us (2%)
  between operations  1.84 us (1%)
    ppermute x44, waiting for transfers between devices, swap(): return lax.ppermute(value, axis, [(i, i ^ step) for i in range(size)])  83 us
    ppermute x44, starting transfers between devices, swap(): return lax.ppermute(value, axis, [(i, i ^ step) for i in range(size)])  45.5 us
    pallas_call x4, Pallas kernels, bands(): pl.pallas_call(functools.partial(body, range(turns), block, chips, bool(s...  21.7 us
    pallas_call x3, Pallas kernels, on_core(): pl.pallas_call(body, out_shape=shapes, in_specs=[pl.BlockSpec(memory_spac...  11.8 us
  transfers between devices with their start and end apart: 44, of which 23 were waited for; matrix products, arithmetic and copies ran while one was open for 5% of the time, Pallas kernels for 17%

profile of v14, /device:TPU:25, one launch (start us, length us, event | category | flops | bytes accessed | tf_op | source)
XLA Modules:
  0.0 174.8 jit_solution(13355751310731024471)
XLA Ops:
  7.0 1.9 %fusion = (f32[128,640]{1,0:T(8,128)S(1)}, f32[128,640]{1,0:T(8,128)}) fusion(s32[]{:T(128)S(6)} %select_n.36, f32[128,1024]{1,0:T(8,128)} %bitcast.78, f32[128,512]{1,0:T(8,128)} %slice.308, f32[128,512]{1,0:T(8,128)} %slice.302, f32[128,1024]{1,0:T(8,128)} %bitcast.80), kind=kLoop, calls=%fused_computation.10 | loop fusion | flops 163840 | bytes 2228228 | tf_op jit(solution)/shard_map/concatenate | solution.py:483
  11.2 3.7 %shard_map.112 = (f32[2,2,64,512]{3,2,1,0:T(8,128)S(1)}, f32[2,2,64,512]{3,2,1,0:T(8,128)S(1)}, f32[2,2,72,512]{3,2,1,0:T(8,128)S(1)}, f32[2,2,72,512]{3,2,1,0:T(8,128)S(1)}) custom-call(s32[2]{0:T(128)S(1)} %pad_add_fusion.place, f32[256,1024]{1,0:T(8,128)S(1)} %copy-done, f32[256,1024]{1,0:T(8,128)S(1)} %collective-permute-done.1.refs_1_.refs_3_, ...), custom_call_target="tpu_custom_call" | custom-call | tf_op jit(solution)/shard_map/pallas_call | solution.py:233
  14.9 7.0 %shard_map.113 = (f32[2,1,64,512]{3,2,1,0:T(8,128)S(1)}, f32[2,1,64,512]{3,2,1,0:T(8,128)S(1)}, f32[2,1,72,512]{3,2,1,0:T(8,128)S(1)}, f32[2,1,72,512]{3,2,1,0:T...) custom-call(s32[2]{0:T(128)S(1)} %pad_add_fusion.place, ...), custom_call_target="tpu_custom_call" | custom-call | tf_op jit(solution)/shard_map/pallas_call | solution.py:233
  21.9 4.4 %collective-permute-done.refs_0_.refs_2_ = f32[256,1024]{1,0:T(8,128)S(1)} collective-permute-done((f32[256,1024]{1,0:T(8,128)}, f32[256,1024]{1,0:T(8,128)S(1)}, u32[]{:S(2)}, u32[]{:S(2)}) %collective-permute-start) | collective-permute-done | bytes 1048608 | tf_op jit(solution)/shard_map/ppermute | solution.py:400
  32.2 3.8 %shard_map.114 = (f32[2,2,64,512]{3,2,1,0:T(8,128)S(1)}, f32[2,2,64,512]{3,2,1,0:T(8,128)S(1)}, f32[2,2,72,512]{3,2,1,0:T(8,128)S(1)}, f32[2,2,72,512]{3,2,1,0:T(8,128)S(1)}) custom-call(s32[2]{0:T(128)S(1)} %pad_add_fusion.place, f32[256,1024]{1,0:T(8,128)S(1)} %collective-permute-done.refs_0_.refs_2_, ...), custom_call_target="tpu_custom_call" | custom-call | tf_op jit(solution)/shard_map/pallas_call | solution.py:233
  38.5 10.7 %collective-permute-done.7 = f32[2,2,64,512]{3,2,1,0:T(8,128)S(1)} collective-permute-done((f32[2,2,64,512]{3,2,1,0:T(8,128)S(1)}, f32[2,2,64,512]{3,2,1,0:T(8,128)S(1)}, u32[]{:S(2)}, u32[]{:S(2)}) %collective-permute-start.7) | collective-permute-done | bytes 524320 | tf_op jit(solution)/shard_map/ppermute | solution.py:400
  49.3 2.2 %collective-permute-done.9 = f32[2,2,72,512]{3,2,1,0:T(8,128)S(1)} collective-permute-done((f32[2,2,72,512]{3,2,1,0:T(8,128)S(1)}, f32[2,2,72,512]{3,2,1,0:T(8,128)S(1)}, u32[]{:S(2)}, u32[]{:S(2)}) %collective-permute-start.9) | collective-permute-done | bytes 589856 | tf_op jit(solution)/shard_map/ppermute | solution.py:400
  55.9 7.2 %shard_map.115 = (f32[2,1,64,512]{3,2,1,0:T(8,128)S(1)}, f32[2,1,64,512]{3,2,1,0:T(8,128)S(1)}, f32[2,1,72,512]{3,2,1,0:T(8,128)S(1)}, f32[2,1,72,512]{3,2,1,0:T...) custom-call(s32[2]{0:T(128)S(1)} %pad_add_fusion.place, ...), custom_call_target="tpu_custom_call" | custom-call | tf_op jit(solution)/shard_map/pallas_call | solution.py:233
  65.8 15.9 %collective-permute-done.13 = f32[2,1,192,512]{3,2,1,0:T(8,128)S(1)} collective-permute-done((f32[2,1,192,512]{3,2,1,0:T(8,128)S(1)}, f32[2,1,192,512]{3,2,1,0:T(8,128)S(1)}, u32[]{:S(2)}, u32[]{:S(2)}) %collective-permute-start.13) | collective-permute-done | bytes 786464 | tf_op jit(solution)/shard_map/ppermute | solution.py:400
  87.6 2.0 %collective-permute-done.16 = f32[2,1,64,512]{3,2,1,0:T(8,128)S(1)} collective-permute-done((f32[2,1,64,512]{3,2,1,0:T(8,128)S(1)}, f32[2,1,64,512]{3,2,1,0:T(8,128)S(1)}, u32[]{:S(2)}, u32[]{:S(2)}) %collective-permute-start.16) | collective-permute-done | bytes 262176 | tf_op jit(solution)/shard_map/ppermute | solution.py:400
  93.1 5.3 %collective-permute-done.19 = f32[1,1,192,512]{3,2,1,0:T(8,128)S(1)} collective-permute-done((f32[1,1,192,512]{3,2,1,0:T(8,128)S(1)}, f32[1,1,192,512]{3,2,1,0:T(8,128)S(1)}, u32[]{:S(2)}, u32[]{:S(2)}) %collective-permute-start.19) | collective-permute-done | bytes 393248 | tf_op jit(solution)/shard_map/ppermute | solution.py:400
  100.5 9.6 %collective-permute-done.21 = f32[136,512]{1,0:T(8,128)S(1)} collective-permute-done((f32[136,512]{1,0:T(8,128)S(1)}, f32[136,512]{1,0:T(8,128)S(1)}, u32[]{:S(2)}, u32[]{:S(2)}) %collective-permute-start.21) | collective-permute-done | bytes 278560 | tf_op jit(solution)/shard_map/ppermute | solution.py:400
  114.8 3.0 %collective-permute-done.24 = f32[136,512]{1,0:T(8,128)S(1)} collective-permute-done((f32[136,512]{1,0:T(8,128)S(1)}, f32[136,512]{1,0:T(8,128)S(1)}, u32[]{:S(2)}, u32[]{:S(2)}) %collective-permute-start.24) | collective-permute-done | bytes 278560 | tf_op jit(solution)/shard_map/ppermute | solution.py:400
  117.7 4.4 %collective-permute-done.27 = f32[1,1,64,1024]{3,2,1,0:T(8,128)S(1)} collective-permute-done((f32[1,1,64,1024]{3,2,1,0:T(8,128)S(1)}, f32[1,1,64,1024]{3,2,1,0:T(8,128)S(1)}, u32[]{:S(2)}, u32[]{:S(2)}) %collective-permute-start.27) | collective-permute-done | bytes 262176 | tf_op jit(solution)/shard_map/ppermute | solution.py:400
  122.2 2.3 %collective-permute-start.30 = (f32[136,512]{1,0:T(8,128)S(1)}, f32[136,512]{1,0:T(8,128)S(1)}, u32[]{:S(2)}, u32[]{:S(2)}) collective-permute-start(f32[136,512]{1,0:T(8,128)S(1)} %get-tuple-element.237), channel_id=1, source_target_pairs={{0,16},{4,20},{8,24},{12,28},{16,0},{20,4},{24,8},{28,12},{1,17},{... | collective-permute-start | bytes 835592 | tf_op jit(solution)/shard_map/ppermute | solution.py:400
  126.2 4.8 %collective-permute-done.33 = f32[64,512]{1,0:T(8,128)S(1)} collective-permute-done((f32[64,512]{1,0:T(8,128)S(1)}, f32[64,512]{1,0:T(8,128)S(1)}, u32[]{:S(2)}, u32[]{:S(2)}) %collective-permute-start.33) | collective-permute-done | bytes 131104 | tf_op jit(solution)/shard_map/ppermute | solution.py:400
  131.8 5.9 %collective-permute-start.35 = (f32[544,512]{1,0:T(8,128)S(1)}, f32[544,512]{1,0:T(8,128)S(1)}, u32[]{:S(2)}, u32[]{:S(2)}) collective-permute-start(f32[544,512]{1,0:T(8,128)S(1)} %constant_dynamic-update-slice_fusion.2.refs_0_), channel_id=1, source_target_pairs={{0,4},{4,0},{8,12},{12,8},{16,20},{20,16},{24,28},{28,24},{1,5},{5... | collective-permute-start | bytes 3342344 | tf_op jit(solution)/shard_map/ppermute | solution.py:400
  139.5 1.7 collective-permute-start.37
  142.6 3.4 %shard_map.116 = (f32[128,1024]{1,0:T(8,128)}, f32[128,1024]{1,0:T(8,128)S(1)}) custom-call(s32[2]{0:T(128)S(1)} %pad_add_fusion.place, f32[544,512]{1,0:T(8,128)S(1)} %constant_dynamic-update-slice_fusion.2.refs_0_, f32[544,512]{1,0:T(8,128)S(1)} %collective-permute-done.35.refs_1_), custom_call_target="tpu_custom_call" | custom-call | tf_op jit(solution)/shard_map/pallas_call | solution.py:362
  146.1 6.5 %collective-permute-done.31 = f32[64,512]{1,0:T(8,128)S(1)} collective-permute-done((f32[64,512]{1,0:T(8,128)S(1)}, f32[64,512]{1,0:T(8,128)S(1)}, u32[]{:S(2)}, u32[]{:S(2)}) %collective-permute-start.31) | collective-permute-done | bytes 131104 | tf_op jit(solution)/shard_map/ppermute | solution.py:400
  154.2 3.2 %collective-permute-start.39 = (f32[544,512]{1,0:T(8,128)S(1)}, f32[544,512]{1,0:T(8,128)S(1)}, u32[]{:S(2)}, u32[]{:S(2)}) collective-permute-start(f32[544,512]{1,0:T(8,128)S(1)} %constant_dynamic-update-slice_fusion.8.refs_0_), channel_id=1, source_target_pairs={{0,4},{4,0},{8,12},{12,8},{16,20},{20,16},{24,28},{28,24},{1,5},{5... | collective-permute-start | bytes 3342344 | tf_op jit(solution)/shard_map/ppermute | solution.py:400
  160.3 2.7 %shard_map.117 = (f32[128,1024]{1,0:T(8,128)}, f32[8,128]{1,0:T(8,128)S(1)}, bf16[1024,1024]{1,0:T(8,128)(2,1)S(1)}, bf16[1024,1024]{1,0:T(8,128)(2,1)S(1)}) custom-call(s32[2]{0:T(128)S(1)} %pad_add_fusion.place, f32[544,512]{1,0:T(8,128)S(1)} %constant_dynamic-update-slice_fusion.8.refs_0_, f32[544,512]{1,0:T(8,128)S(1)} %collective-permute-done.39.refs_1_), custom_call_target="tpu_custom_call" | custom-call | tf_op jit(solution)/shard_map/pallas_call | solution.py:362
  163.0 2.1 %collective-permute-done.40 = f32[64,1024]{1,0:T(8,128)S(1)} collective-permute-done((f32[64,1024]{1,0:T(8,128)S(1)}, f32[64,1024]{1,0:T(8,128)S(1)}, u32[]{:S(2)}, u32[]{:S(2)}) %collective-permute-start.40) | collective-permute-done | bytes 262176 | tf_op jit(solution)/shard_map/ppermute | solution.py:400
  169.2 5.6 %shard_map.118 = (f32[128,1024]{1,0:T(8,128)}, f32[128,1024]{1,0:T(8,128)}) custom-call(s32[2]{0:T(128)S(1)} %pad_add_fusion.place, f32[384,1024]{1,0:T(8,128)S(1)} %slice_dynamic-update-slice_fusion.refs_0_, f32[128,1024]{1,0:T(8,128)S(1)} %constant_dynamic-update-slice_fusion.18.refs_1_, f32[384,1024]{1,0:T(8,128)S(1)} %collective-permute-done.42.refs_2_, ...), custom_call_target="tpu_custom_call" | custom-call | tf_op jit(solution)/shard_map/pallas_call | solution.py:362
  (146 shorter events, 53.7 us)
Async XLA Ops:
  0.6 10.5 %collective-permute-start.1 = (f32[256,1024]{1,0:T(8,128)}, f32[256,1024]{1,0:T(8,128)S(1)}, u32[]{:S(2)}, u32[]{:S(2)}) collective-permute-start(f32[256,1024]{1,0:T(8,128)} %refs_2_.1), channel_id=1, source_target_pairs={{0,4},{4,0},{8,12},{12,8},{16,20},{20,16},{24,28},{28,24},{1,5},{5... | collective-permute-start | bytes 3145736 | tf_op jit(solution)/shard_map/ppermute | solution.py:400
  1.4 24.9 %collective-permute-start = (f32[256,1024]{1,0:T(8,128)}, f32[256,1024]{1,0:T(8,128)S(1)}, u32[]{:S(2)}, u32[]{:S(2)}) collective-permute-start(f32[256,1024]{1,0:T(8,128)} %refs_2_.1), channel_id=1, source_target_pairs={{0,1},{1,0},{2,3},{3,2},{4,5},{5,4},{6,7},{7,6},{8,9},{9,8},{10,11... | collective-permute-start | bytes 3145736 | tf_op jit(solution)/shard_map/ppermute | solution.py:400
  3.5 11.4 %collective-permute-start.3 = (f32[256,1024]{1,0:T(8,128)}, f32[256,1024]{1,0:T(8,128)S(1)}, u32[]{:S(2)}, u32[]{:S(2)}) collective-permute-start(f32[256,1024]{1,0:T(8,128)} %refs_0_.3), channel_id=1, source_target_pairs={{0,4},{4,0},{8,12},{12,8},{16,20},{20,16},{24,28},{28,24},{1,5},{5... | collective-permute-start | bytes 3145736 | tf_op jit(solution)/shard_map/ppermute | solution.py:400
  27.3 25.3 %collective-permute-start.11 = (f32[256,1024]{1,0:T(8,128)S(1)}, f32[256,1024]{1,0:T(8,128)S(1)}, u32[]{:S(2)}, u32[]{:S(2)}) collective-permute-start(f32[256,1024]{1,0:T(8,128)S(1)} %copy-done.1), channel_id=1, source_target_pairs={{0,1},{1,0},{2,3},{3,2},{4,5},{5,4},{6,7},{7,6},{8,9},{9,8},{10,11... | collective-permute-start | bytes 3145736 | tf_op jit(solution)/shard_map/ppermute | solution.py:400
  36.0 13.3 %collective-permute-start.7 = (f32[2,2,64,512]{3,2,1,0:T(8,128)S(1)}, f32[2,2,64,512]{3,2,1,0:T(8,128)S(1)}, u32[]{:S(2)}, u32[]{:S(2)}) collective-permute-start(f32[2,2,64,512]{3,2,1,0:T(8,128)S(1)} %get-tuple-element.129), channel_id=1, source_target_pairs={{0,8},{4,12},{8,0},{12,4},{16,24},{20,28},{24,16},{28,20},{1,9},{5... | collective-permute-start | bytes 1572872 | tf_op jit(solution)/shard_map/ppermute | solution.py:400
  37.3 14.2 %collective-permute-start.9 = (f32[2,2,72,512]{3,2,1,0:T(8,128)S(1)}, f32[2,2,72,512]{3,2,1,0:T(8,128)S(1)}, u32[]{:S(2)}, u32[]{:S(2)}) collective-permute-start(f32[2,2,72,512]{3,2,1,0:T(8,128)S(1)} %get-tuple-element.131), channel_id=1, source_target_pairs={{0,16},{4,20},{8,24},{12,28},{16,0},{20,4},{24,8},{28,12},{1,17},{... | collective-permute-start | bytes 1769480 | tf_op jit(solution)/shard_map/ppermute | solution.py:400
  63.1 18.6 %collective-permute-start.13 = (f32[2,1,192,512]{3,2,1,0:T(8,128)S(1)}, f32[2,1,192,512]{3,2,1,0:T(8,128)S(1)}, u32[]{:S(2)}, u32[]{:S(2)}) collective-permute-start(f32[2,1,192,512]{3,2,1,0:T(8,128)S(1)} %get-tuple-element.151), channel_id=1, source_target_pairs={{0,8},{4,12},{8,0},{12,4},{16,24},{20,28},{24,16},{28,20},{1,9},{5... | collective-permute-start | bytes 2359304 | tf_op jit(solution)/shard_map/ppermute | solution.py:400
  64.2 19.1 %collective-permute-start.14 = (f32[2,1,200,512]{3,2,1,0:T(8,128)S(1)}, f32[2,1,200,512]{3,2,1,0:T(8,128)S(1)}, u32[]{:S(2)}, u32[]{:S(2)}) collective-permute-start(f32[2,1,200,512]{3,2,1,0:T(8,128)S(1)} %get-tuple-element.152), channel_id=1, source_target_pairs={{0,16},{4,20},{8,24},{12,28},{16,0},{20,4},{24,8},{28,12},{1,17},{... | collective-permute-start | bytes 2457608 | tf_op jit(solution)/shard_map/ppermute | solution.py:400
  65.7 19.3 %collective-permute-start.15 = (f32[136,512]{1,0:T(8,128)S(1)}, f32[136,512]{1,0:T(8,128)S(1)}, u32[]{:S(2)}, u32[]{:S(2)}) collective-permute-start(f32[136,512]{1,0:T(8,128)S(1)} %maximum_bitcast_fusion), channel_id=1, source_target_pairs={{0,2},{1,3},{2,0},{3,1},{4,6},{5,7},{6,4},{7,5},{8,10},{9,11},{10,... | collective-permute-start | bytes 835592 | tf_op jit(solution)/shard_map/ppermute | solution.py:400
  85.6 12.9 %collective-permute-start.19 = (f32[1,1,192,512]{3,2,1,0:T(8,128)S(1)}, f32[1,1,192,512]{3,2,1,0:T(8,128)S(1)}, u32[]{:S(2)}, u32[]{:S(2)}) collective-permute-start(f32[1,1,192,512]{3,2,1,0:T(8,128)S(1)} %slice_add_fusion.1), channel_id=1, source_target_pairs={{0,16},{4,20},{8,24},{12,28},{16,0},{20,4},{24,8},{28,12},{1,17},{... | collective-permute-start | bytes 1179656 | tf_op jit(solution)/shard_map/ppermute | solution.py:400
  85.7 14.4 %collective-permute-start.20 = (f32[1,1,200,512]{3,2,1,0:T(8,128)S(1)}, f32[1,1,200,512]{3,2,1,0:T(8,128)S(1)}, u32[]{:S(2)}, u32[]{:S(2)}) collective-permute-start(f32[1,1,200,512]{3,2,1,0:T(8,128)S(1)} %slice_add_fusion), channel_id=1, source_target_pairs={{0,8},{4,12},{8,0},{12,4},{16,24},{20,28},{24,16},{28,20},{1,9},{5... | collective-permute-start | bytes 1228808 | tf_op jit(solution)/shard_map/ppermute | solution.py:400
  90.0 20.0 %collective-permute-start.18 = (f32[1,1,64,512]{3,2,1,0:T(8,128)S(1)}, f32[1,1,64,512]{3,2,1,0:T(8,128)S(1)}, u32[]{:S(2)}, u32[]{:S(2)}) collective-permute-start(f32[1,1,64,512]{3,2,1,0:T(8,128)S(1)} %slice_add_fusion.12), channel_id=1, source_target_pairs={{0,16},{4,20},{8,24},{12,28},{16,0},{20,4},{24,8},{28,12},{1,17},{... | collective-permute-start | bytes 393224 | tf_op jit(solution)/shard_map/ppermute | solution.py:400
  91.7 18.5 %collective-permute-start.22 = (f32[1,1,72,512]{3,2,1,0:T(8,128)S(1)}, f32[1,1,72,512]{3,2,1,0:T(8,128)S(1)}, u32[]{:S(2)}, u32[]{:S(2)}) collective-permute-start(f32[1,1,72,512]{3,2,1,0:T(8,128)S(1)} %slice_add_fusion.11), channel_id=1, source_target_pairs={{0,8},{4,12},{8,0},{12,4},{16,24},{20,28},{24,16},{28,20},{1,9},{5... | collective-permute-start | bytes 442376 | tf_op jit(solution)/shard_map/ppermute | solution.py:400
  92.9 19.9 %collective-permute-start.25 = (f32[2,1,64,1024]{3,2,1,0:T(8,128)S(1)}, f32[2,1,64,1024]{3,2,1,0:T(8,128)S(1)}, u32[]{:S(2)}, u32[]{:S(2)}) collective-permute-start(f32[2,1,64,1024]{3,2,1,0:T(8,128)S(1)} %get-tuple-element.175), channel_id=1, source_target_pairs={{0,8},{4,12},{8,0},{12,4},{16,24},{20,28},{24,16},{28,20},{1,9},{5... | collective-permute-start | bytes 1572872 | tf_op jit(solution)/shard_map/ppermute | solution.py:400
  98.4 14.4 %collective-permute-start.26 = (f32[2,1,64,1024]{3,2,1,0:T(8,128)S(1)}, f32[2,1,64,1024]{3,2,1,0:T(8,128)S(1)}, u32[]{:S(2)}, u32[]{:S(2)}) collective-permute-start(f32[2,1,64,1024]{3,2,1,0:T(8,128)S(1)} %get-tuple-element.177), channel_id=1, source_target_pairs={{0,16},{4,20},{8,24},{12,28},{16,0},{20,4},{24,8},{28,12},{1,17},{... | collective-permute-start | bytes 1572872 | tf_op jit(solution)/shard_map/ppermute | solution.py:400
  114.6 24.0 %collective-permute-start.36 = (f32[128,1024]{1,0:T(8,128)S(1)}, f32[128,1024]{1,0:T(8,128)S(1)}, u32[]{:S(2)}, u32[]{:S(2)}) collective-permute-start(f32[128,1024]{1,0:T(8,128)S(1)} %bitcast.81), channel_id=1, source_target_pairs={{0,2},{1,3},{2,0},{3,1},{4,6},{5,7},{6,4},{7,5},{8,10},{9,11},{10,... | collective-permute-start | bytes 1572872 | tf_op jit(solution)/shard_map/ppermute | solution.py:400
  122.2 16.4 %collective-permute-start.30 = (f32[136,512]{1,0:T(8,128)S(1)}, f32[136,512]{1,0:T(8,128)S(1)}, u32[]{:S(2)}, u32[]{:S(2)}) collective-permute-start(f32[136,512]{1,0:T(8,128)S(1)} %get-tuple-element.237), channel_id=1, source_target_pairs={{0,16},{4,20},{8,24},{12,28},{16,0},{20,4},{24,8},{28,12},{1,17},{... | collective-permute-start | bytes 835592 | tf_op jit(solution)/shard_map/ppermute | solution.py:400
  124.5 14.1 %collective-permute-start.29 = (f32[136,512]{1,0:T(8,128)S(1)}, f32[136,512]{1,0:T(8,128)S(1)}, u32[]{:S(2)}, u32[]{:S(2)}) collective-permute-start(f32[136,512]{1,0:T(8,128)S(1)} %get-tuple-element.237), channel_id=1, source_target_pairs={{0,8},{4,12},{8,0},{12,4},{16,24},{20,28},{24,16},{28,20},{1,9},{5... | collective-permute-start | bytes 835592 | tf_op jit(solution)/shard_map/ppermute | solution.py:400
  131.8 10.9 %collective-permute-start.35 = (f32[544,512]{1,0:T(8,128)S(1)}, f32[544,512]{1,0:T(8,128)S(1)}, u32[]{:S(2)}, u32[]{:S(2)}) collective-permute-start(f32[544,512]{1,0:T(8,128)S(1)} %constant_dynamic-update-slice_fusion.2.refs_0_), channel_id=1, source_target_pairs={{0,4},{4,0},{8,12},{12,8},{16,20},{20,16},{24,28},{28,24},{1,5},{5... | collective-permute-start | bytes 3342344 | tf_op jit(solution)/shard_map/ppermute | solution.py:400
  138.8 15.3 %collective-permute-start.38 = (f32[128,1024]{1,0:T(8,128)S(1)}, f32[128,1024]{1,0:T(8,128)S(1)}, u32[]{:S(2)}, u32[]{:S(2)}) collective-permute-start(f32[128,1024]{1,0:T(8,128)S(1)} %pad_maximum_fusion), channel_id=1, source_target_pairs={{0,16},{4,20},{8,24},{12,28},{16,0},{20,4},{24,8},{28,12},{1,17},{... | collective-permute-start | bytes 1572872 | tf_op jit(solution)/shard_map/ppermute | solution.py:400
  139.5 14.6 %collective-permute-start.37 = (f32[128,1024]{1,0:T(8,128)S(1)}, f32[128,1024]{1,0:T(8,128)S(1)}, u32[]{:S(2)}, u32[]{:S(2)}) collective-permute-start(f32[128,1024]{1,0:T(8,128)S(1)} %pad_maximum_fusion), channel_id=1, source_target_pairs={{0,8},{4,12},{8,0},{12,4},{16,24},{20,28},{24,16},{28,20},{1,9},{5... | collective-permute-start | bytes 1572872 | tf_op jit(solution)/shard_map/ppermute | solution.py:400
  141.2 11.3 %collective-permute-start.31 = (f32[64,512]{1,0:T(8,128)S(1)}, f32[64,512]{1,0:T(8,128)S(1)}, u32[]{:S(2)}, u32[]{:S(2)}) collective-permute-start(f32[64,512]{1,0:T(8,128)S(1)} %get-tuple-element.235), channel_id=1, source_target_pairs={{0,16},{4,20},{8,24},{12,28},{16,0},{20,4},{24,8},{28,12},{1,17},{... | collective-permute-start | bytes 393224 | tf_op jit(solution)/shard_map/ppermute | solution.py:400
  142.5 11.6 %collective-permute-start.32 = (f32[72,512]{1,0:T(8,128)S(1)}, f32[72,512]{1,0:T(8,128)S(1)}, u32[]{:S(2)}, u32[]{:S(2)}) collective-permute-start(f32[72,512]{1,0:T(8,128)S(1)} %get-tuple-element.233), channel_id=1, source_target_pairs={{0,8},{4,12},{8,0},{12,4},{16,24},{20,28},{24,16},{28,20},{1,9},{5... | collective-permute-start | bytes 442376 | tf_op jit(solution)/shard_map/ppermute | solution.py:400
  157.5 10.2 %collective-permute-start.42 = (f32[384,1024]{1,0:T(8,128)S(1)}, f32[384,1024]{1,0:T(8,128)S(1)}, u32[]{:S(2)}, u32[]{:S(2)}) collective-permute-start(f32[384,1024]{1,0:T(8,128)S(1)} %slice_dynamic-update-slice_fusion.refs_0_), channel_id=1, source_target_pairs={{0,4},{4,0},{8,12},{12,8},{16,20},{20,16},{24,28},{28,24},{1,5},{5... | collective-permute-start | bytes 4718600 | tf_op jit(solution)/shard_map/ppermute | solution.py:400
  (25 other events, 157.4 us)

commit v15 on v14

--- a/solution.py
+++ b/solution.py
@@ -492,7 +492,8 @@
     acts_far = swap(acts, "expert", 1)
     keep = prepare(routes, counts, feat)
     keep_far = swap(keep, "expert", 1)
-    near_acts = (acts, swap(acts, "dp", 1), keep, swap(keep, "dp", 1))
+    later_acts, keep = together(acts, keep)
+    near_acts = (acts, swap(later_acts, "dp", 1), keep, swap(keep, "dp", 1))
     act_seeds = bands(act_kernel, turns, act_groups, place, near_acts, (), *size)
     grads_far = swap(grads_out, "expert", 1)
     grad_parts = (grads_out, swap(grads_out, "dp", 1)) + near_acts

time: 177 us -> 176 us (level)
  no operation moved by 1% of the time
where the time goes in v15:
time: 176 us; the launch traced here: 174 us
  waiting for transfers between devices  81.4 us (46%)
  starting transfers between devices  46.4 us (26%)
  Pallas kernels  35 us (20%)
  local copies, waits for them, and re-layouts  5.29 us (3%)
  other arithmetic  4.22 us (2%)
  between operations  1.83 us (1%)
    ppermute x44, waiting for transfers between devices, swap(): return lax.ppermute(value, axis, [(i, i ^ step) for i in range(size)])  81.4 us
    ppermute x44, starting transfers between devices, swap(): return lax.ppermute(value, axis, [(i, i ^ step) for i in range(size)])  46.4 us
    pallas_call x4, Pallas kernels, bands(): pl.pallas_call(functools.partial(body, range(turns), block, chips, bool(s...  21.7 us
    pallas_call x3, Pallas kernels, on_core(): pl.pallas_call(body, out_shape=shapes, in_specs=[pl.BlockSpec(memory_spac...  11.8 us
  transfers between devices with their start and end apart: 44, of which 23 were waited for; matrix products, arithmetic and copies ran while one was open for 5% of the time, Pallas kernels for 17%

profile of v15, /device:TPU:25, one launch (start us, length us, event | category | flops | bytes accessed | tf_op | source)
XLA Modules:
  0.0 174.1 jit_solution(8889574885894720904)
XLA Ops:
  3.9 1.7 slice.302
  7.2 1.9 %fusion = (f32[128,640]{1,0:T(8,128)S(1)}, f32[128,640]{1,0:T(8,128)}) fusion(s32[]{:T(128)S(6)} %select_n.36, f32[128,1024]{1,0:T(8,128)} %bitcast.78, f32[128,512]{1,0:T(8,128)} %slice.308, f32[128,512]{1,0:T(8,128)} %slice.302, f32[128,1024]{1,0:T(8,128)} %bitcast.80), kind=kLoop, calls=%fused_computation.10 | loop fusion | flops 163840 | bytes 2228228 | tf_op jit(solution)/shard_map/concatenate | solution.py:483
  11.4 3.7 %shard_map.112 = (f32[2,2,64,512]{3,2,1,0:T(8,128)S(1)}, f32[2,2,64,512]{3,2,1,0:T(8,128)S(1)}, f32[2,2,72,512]{3,2,1,0:T(8,128)S(1)}, f32[2,2,72,512]{3,2,1,0:T(8,128)S(1)}) custom-call(s32[2]{0:T(128)S(1)} %pad_add_fusion.place, f32[256,1024]{1,0:T(8,128)S(1)} %copy-done, f32[256,1024]{1,0:T(8,128)S(1)} %collective-permute-done.1.refs_1_.refs_3_, ...), custom_call_target="tpu_custom_call" | custom-call | tf_op jit(solution)/shard_map/pallas_call | solution.py:233
  15.2 7.0 %shard_map.113 = (f32[2,1,64,512]{3,2,1,0:T(8,128)S(1)}, f32[2,1,64,512]{3,2,1,0:T(8,128)S(1)}, f32[2,1,72,512]{3,2,1,0:T(8,128)S(1)}, f32[2,1,72,512]{3,2,1,0:T...) custom-call(s32[2]{0:T(128)S(1)} %pad_add_fusion.place, ...), custom_call_target="tpu_custom_call" | custom-call | tf_op jit(solution)/shard_map/pallas_call | solution.py:233
  22.2 2.7 %collective-permute-done.refs_0_.refs_2_ = f32[256,1024]{1,0:T(8,128)S(1)} collective-permute-done((f32[256,1024]{1,0:T(8,128)}, f32[256,1024]{1,0:T(8,128)S(1)}, u32[]{:S(2)}, u32[]{:S(2)}) %collective-permute-start) | collective-permute-done | bytes 1048608 | tf_op jit(solution)/shard_map/ppermute | solution.py:400
  31.5 3.8 %shard_map.114 = (f32[2,2,64,512]{3,2,1,0:T(8,128)S(1)}, f32[2,2,64,512]{3,2,1,0:T(8,128)S(1)}, f32[2,2,72,512]{3,2,1,0:T(8,128)S(1)}, f32[2,2,72,512]{3,2,1,0:T(8,128)S(1)}) custom-call(s32[2]{0:T(128)S(1)} %pad_add_fusion.place, f32[256,1024]{1,0:T(8,128)S(1)} %collective-permute-done.refs_0_.refs_2_, ...), custom_call_target="tpu_custom_call" | custom-call | tf_op jit(solution)/shard_map/pallas_call | solution.py:233
  37.8 10.7 %collective-permute-done.7 = f32[2,2,64,512]{3,2,1,0:T(8,128)S(1)} collective-permute-done((f32[2,2,64,512]{3,2,1,0:T(8,128)S(1)}, f32[2,2,64,512]{3,2,1,0:T(8,128)S(1)}, u32[]{:S(2)}, u32[]{:S(2)}) %collective-permute-start.7) | collective-permute-done | bytes 524320 | tf_op jit(solution)/shard_map/ppermute | solution.py:400
  48.6 2.2 %collective-permute-done.9 = f32[2,2,72,512]{3,2,1,0:T(8,128)S(1)} collective-permute-done((f32[2,2,72,512]{3,2,1,0:T(8,128)S(1)}, f32[2,2,72,512]{3,2,1,0:T(8,128)S(1)}, u32[]{:S(2)}, u32[]{:S(2)}) %collective-permute-start.9) | collective-permute-done | bytes 589856 | tf_op jit(solution)/shard_map/ppermute | solution.py:400
  55.2 7.2 %shard_map.115 = (f32[2,1,64,512]{3,2,1,0:T(8,128)S(1)}, f32[2,1,64,512]{3,2,1,0:T(8,128)S(1)}, f32[2,1,72,512]{3,2,1,0:T(8,128)S(1)}, f32[2,1,72,512]{3,2,1,0:T...) custom-call(s32[2]{0:T(128)S(1)} %pad_add_fusion.place, ...), custom_call_target="tpu_custom_call" | custom-call | tf_op jit(solution)/shard_map/pallas_call | solution.py:233
  65.1 15.9 %collective-permute-done.13 = f32[2,1,192,512]{3,2,1,0:T(8,128)S(1)} collective-permute-done((f32[2,1,192,512]{3,2,1,0:T(8,128)S(1)}, f32[2,1,192,512]{3,2,1,0:T(8,128)S(1)}, u32[]{:S(2)}, u32[]{:S(2)}) %collective-permute-start.13) | collective-permute-done | bytes 786464 | tf_op jit(solution)/shard_map/ppermute | solution.py:400
  86.9 2.0 %collective-permute-done.16 = f32[2,1,64,512]{3,2,1,0:T(8,128)S(1)} collective-permute-done((f32[2,1,64,512]{3,2,1,0:T(8,128)S(1)}, f32[2,1,64,512]{3,2,1,0:T(8,128)S(1)}, u32[]{:S(2)}, u32[]{:S(2)}) %collective-permute-start.16) | collective-permute-done | bytes 262176 | tf_op jit(solution)/shard_map/ppermute | solution.py:400
  92.4 5.3 %collective-permute-done.19 = f32[1,1,192,512]{3,2,1,0:T(8,128)S(1)} collective-permute-done((f32[1,1,192,512]{3,2,1,0:T(8,128)S(1)}, f32[1,1,192,512]{3,2,1,0:T(8,128)S(1)}, u32[]{:S(2)}, u32[]{:S(2)}) %collective-permute-start.19) | collective-permute-done | bytes 393248 | tf_op jit(solution)/shard_map/ppermute | solution.py:400
  99.8 9.6 %collective-permute-done.21 = f32[136,512]{1,0:T(8,128)S(1)} collective-permute-done((f32[136,512]{1,0:T(8,128)S(1)}, f32[136,512]{1,0:T(8,128)S(1)}, u32[]{:S(2)}, u32[]{:S(2)}) %collective-permute-start.21) | collective-permute-done | bytes 278560 | tf_op jit(solution)/shard_map/ppermute | solution.py:400
  114.1 3.0 %collective-permute-done.24 = f32[136,512]{1,0:T(8,128)S(1)} collective-permute-done((f32[136,512]{1,0:T(8,128)S(1)}, f32[136,512]{1,0:T(8,128)S(1)}, u32[]{:S(2)}, u32[]{:S(2)}) %collective-permute-start.24) | collective-permute-done | bytes 278560 | tf_op jit(solution)/shard_map/ppermute | solution.py:400
  117.1 4.4 %collective-permute-done.27 = f32[1,1,64,1024]{3,2,1,0:T(8,128)S(1)} collective-permute-done((f32[1,1,64,1024]{3,2,1,0:T(8,128)S(1)}, f32[1,1,64,1024]{3,2,1,0:T(8,128)S(1)}, u32[]{:S(2)}, u32[]{:S(2)}) %collective-permute-start.27) | collective-permute-done | bytes 262176 | tf_op jit(solution)/shard_map/ppermute | solution.py:400
  121.5 2.3 %collective-permute-start.30 = (f32[136,512]{1,0:T(8,128)S(1)}, f32[136,512]{1,0:T(8,128)S(1)}, u32[]{:S(2)}, u32[]{:S(2)}) collective-permute-start(f32[136,512]{1,0:T(8,128)S(1)} %get-tuple-element.241), channel_id=1, source_target_pairs={{0,16},{4,20},{8,24},{12,28},{16,0},{20,4},{24,8},{28,12},{1,17},{... | collective-permute-start | bytes 835592 | tf_op jit(solution)/shard_map/ppermute | solution.py:400
  125.6 4.8 %collective-permute-done.33 = f32[64,512]{1,0:T(8,128)S(1)} collective-permute-done((f32[64,512]{1,0:T(8,128)S(1)}, f32[64,512]{1,0:T(8,128)S(1)}, u32[]{:S(2)}, u32[]{:S(2)}) %collective-permute-start.33) | collective-permute-done | bytes 131104 | tf_op jit(solution)/shard_map/ppermute | solution.py:400
  131.1 5.9 %collective-permute-start.35 = (f32[544,512]{1,0:T(8,128)S(1)}, f32[544,512]{1,0:T(8,128)S(1)}, u32[]{:S(2)}, u32[]{:S(2)}) collective-permute-start(f32[544,512]{1,0:T(8,128)S(1)} %constant_dynamic-update-slice_fusion.2.refs_0_), channel_id=1, source_target_pairs={{0,4},{4,0},{8,12},{12,8},{16,20},{20,16},{24,28},{28,24},{1,5},{5... | collective-permute-start | bytes 3342344 | tf_op jit(solution)/shard_map/ppermute | solution.py:400
  141.9 3.4 %shard_map.116 = (f32[128,1024]{1,0:T(8,128)}, f32[128,1024]{1,0:T(8,128)S(1)}) custom-call(s32[2]{0:T(128)S(1)} %pad_add_fusion.place, f32[544,512]{1,0:T(8,128)S(1)} %constant_dynamic-update-slice_fusion.2.refs_0_, f32[544,512]{1,0:T(8,128)S(1)} %collective-permute-done.35.refs_1_), custom_call_target="tpu_custom_call" | custom-call | tf_op jit(solution)/shard_map/pallas_call | solution.py:362
  145.4 6.6 %collective-permute-done.31 = f32[64,512]{1,0:T(8,128)S(1)} collective-permute-done((f32[64,512]{1,0:T(8,128)S(1)}, f32[64,512]{1,0:T(8,128)S(1)}, u32[]{:S(2)}, u32[]{:S(2)}) %collective-permute-start.31) | collective-permute-done | bytes 131104 | tf_op jit(solution)/shard_map/ppermute | solution.py:400
  153.5 3.2 %collective-permute-start.39 = (f32[544,512]{1,0:T(8,128)S(1)}, f32[544,512]{1,0:T(8,128)S(1)}, u32[]{:S(2)}, u32[]{:S(2)}) collective-permute-start(f32[544,512]{1,0:T(8,128)S(1)} %constant_dynamic-update-slice_fusion.8.refs_0_), channel_id=1, source_target_pairs={{0,4},{4,0},{8,12},{12,8},{16,20},{20,16},{24,28},{28,24},{1,5},{5... | collective-permute-start | bytes 3342344 | tf_op jit(solution)/shard_map/ppermute | solution.py:400
  159.6 2.7 %shard_map.117 = (f32[128,1024]{1,0:T(8,128)}, f32[8,128]{1,0:T(8,128)S(1)}, bf16[1024,1024]{1,0:T(8,128)(2,1)S(1)}, bf16[1024,1024]{1,0:T(8,128)(2,1)S(1)}) custom-call(s32[2]{0:T(128)S(1)} %pad_add_fusion.place, f32[544,512]{1,0:T(8,128)S(1)} %constant_dynamic-update-slice_fusion.8.refs_0_, f32[544,512]{1,0:T(8,128)S(1)} %collective-permute-done.39.refs_1_), custom_call_target="tpu_custom_call" | custom-call | tf_op jit(solution)/shard_map/pallas_call | solution.py:362
  162.4 2.1 %collective-permute-done.40 = f32[64,1024]{1,0:T(8,128)S(1)} collective-permute-done((f32[64,1024]{1,0:T(8,128)S(1)}, f32[64,1024]{1,0:T(8,128)S(1)}, u32[]{:S(2)}, u32[]{:S(2)}) %collective-permute-start.40) | collective-permute-done | bytes 262176 | tf_op jit(solution)/shard_map/ppermute | solution.py:400
  168.5 5.6 %shard_map.118 = (f32[128,1024]{1,0:T(8,128)}, f32[128,1024]{1,0:T(8,128)}) custom-call(s32[2]{0:T(128)S(1)} %pad_add_fusion.place, f32[384,1024]{1,0:T(8,128)S(1)} %slice_dynamic-update-slice_fusion.refs_0_, f32[128,1024]{1,0:T(8,128)S(1)} %constant_dynamic-update-slice_fusion.18.refs_1_, f32[384,1024]{1,0:T(8,128)S(1)} %collective-permute-done.42.refs_2_, ...), custom_call_target="tpu_custom_call" | custom-call | tf_op jit(solution)/shard_map/pallas_call | solution.py:362
  (146 shorter events, 54.6 us)
Async XLA Ops:
  0.6 24.3 %collective-permute-start = (f32[256,1024]{1,0:T(8,128)}, f32[256,1024]{1,0:T(8,128)S(1)}, u32[]{:S(2)}, u32[]{:S(2)}) collective-permute-start(f32[256,1024]{1,0:T(8,128)} %refs_2_.1), channel_id=1, source_target_pairs={{0,1},{1,0},{2,3},{3,2},{4,5},{5,4},{6,7},{7,6},{8,9},{9,8},{10,11... | collective-permute-start | bytes 3145736 | tf_op jit(solution)/shard_map/ppermute | solution.py:400
  3.4 11.8 %collective-permute-start.3 = (f32[256,1024]{1,0:T(8,128)}, f32[256,1024]{1,0:T(8,128)S(1)}, u32[]{:S(2)}, u32[]{:S(2)}) collective-permute-start(f32[256,1024]{1,0:T(8,128)} %refs_0_.3), channel_id=1, source_target_pairs={{0,4},{4,0},{8,12},{12,8},{16,20},{20,16},{24,28},{28,24},{1,5},{5... | collective-permute-start | bytes 3145736 | tf_op jit(solution)/shard_map/ppermute | solution.py:400
  26.7 25.3 %collective-permute-start.11 = (f32[256,1024]{1,0:T(8,128)S(1)}, f32[256,1024]{1,0:T(8,128)S(1)}, u32[]{:S(2)}, u32[]{:S(2)}) collective-permute-start(f32[256,1024]{1,0:T(8,128)S(1)} %copy-done.1), channel_id=1, source_target_pairs={{0,1},{1,0},{2,3},{3,2},{4,5},{5,4},{6,7},{7,6},{8,9},{9,8},{10,11... | collective-permute-start | bytes 3145736 | tf_op jit(solution)/shard_map/ppermute | solution.py:400
  35.3 13.3 %collective-permute-start.7 = (f32[2,2,64,512]{3,2,1,0:T(8,128)S(1)}, f32[2,2,64,512]{3,2,1,0:T(8,128)S(1)}, u32[]{:S(2)}, u32[]{:S(2)}) collective-permute-start(f32[2,2,64,512]{3,2,1,0:T(8,128)S(1)} %get-tuple-element.133), channel_id=1, source_target_pairs={{0,8},{4,12},{8,0},{12,4},{16,24},{20,28},{24,16},{28,20},{1,9},{5... | collective-permute-start | bytes 1572872 | tf_op jit(solution)/shard_map/ppermute | solution.py:400
  36.6 14.2 %collective-permute-start.9 = (f32[2,2,72,512]{3,2,1,0:T(8,128)S(1)}, f32[2,2,72,512]{3,2,1,0:T(8,128)S(1)}, u32[]{:S(2)}, u32[]{:S(2)}) collective-permute-start(f32[2,2,72,512]{3,2,1,0:T(8,128)S(1)} %get-tuple-element.135), channel_id=1, source_target_pairs={{0,16},{4,20},{8,24},{12,28},{16,0},{20,4},{24,8},{28,12},{1,17},{... | collective-permute-start | bytes 1769480 | tf_op jit(solution)/shard_map/ppermute | solution.py:400
  62.4 18.6 %collective-permute-start.13 = (f32[2,1,192,512]{3,2,1,0:T(8,128)S(1)}, f32[2,1,192,512]{3,2,1,0:T(8,128)S(1)}, u32[]{:S(2)}, u32[]{:S(2)}) collective-permute-start(f32[2,1,192,512]{3,2,1,0:T(8,128)S(1)} %get-tuple-element.155), channel_id=1, source_target_pairs={{0,8},{4,12},{8,0},{12,4},{16,24},{20,28},{24,16},{28,20},{1,9},{5... | collective-permute-start | bytes 2359304 | tf_op jit(solution)/shard_map/ppermute | solution.py:400
  63.5 19.1 %collective-permute-start.14 = (f32[2,1,200,512]{3,2,1,0:T(8,128)S(1)}, f32[2,1,200,512]{3,2,1,0:T(8,128)S(1)}, u32[]{:S(2)}, u32[]{:S(2)}) collective-permute-start(f32[2,1,200,512]{3,2,1,0:T(8,128)S(1)} %get-tuple-element.156), channel_id=1, source_target_pairs={{0,16},{4,20},{8,24},{12,28},{16,0},{20,4},{24,8},{28,12},{1,17},{... | collective-permute-start | bytes 2457608 | tf_op jit(solution)/shard_map/ppermute | solution.py:400
  65.0 19.3 %collective-permute-start.15 = (f32[136,512]{1,0:T(8,128)S(1)}, f32[136,512]{1,0:T(8,128)S(1)}, u32[]{:S(2)}, u32[]{:S(2)}) collective-permute-start(f32[136,512]{1,0:T(8,128)S(1)} %maximum_bitcast_fusion), channel_id=1, source_target_pairs={{0,2},{1,3},{2,0},{3,1},{4,6},{5,7},{6,4},{7,5},{8,10},{9,11},{10,... | collective-permute-start | bytes 835592 | tf_op jit(solution)/shard_map/ppermute | solution.py:400
  84.9 12.9 %collective-permute-start.19 = (f32[1,1,192,512]{3,2,1,0:T(8,128)S(1)}, f32[1,1,192,512]{3,2,1,0:T(8,128)S(1)}, u32[]{:S(2)}, u32[]{:S(2)}) collective-permute-start(f32[1,1,192,512]{3,2,1,0:T(8,128)S(1)} %slice_add_fusion.1), channel_id=1, source_target_pairs={{0,16},{4,20},{8,24},{12,28},{16,0},{20,4},{24,8},{28,12},{1,17},{... | collective-permute-start | bytes 1179656 | tf_op jit(solution)/shard_map/ppermute | solution.py:400
  85.0 14.4 %collective-permute-start.20 = (f32[1,1,200,512]{3,2,1,0:T(8,128)S(1)}, f32[1,1,200,512]{3,2,1,0:T(8,128)S(1)}, u32[]{:S(2)}, u32[]{:S(2)}) collective-permute-start(f32[1,1,200,512]{3,2,1,0:T(8,128)S(1)} %slice_add_fusion), channel_id=1, source_target_pairs={{0,8},{4,12},{8,0},{12,4},{16,24},{20,28},{24,16},{28,20},{1,9},{5... | collective-permute-start | bytes 1228808 | tf_op jit(solution)/shard_map/ppermute | solution.py:400
  89.4 20.0 %collective-permute-start.18 = (f32[1,1,64,512]{3,2,1,0:T(8,128)S(1)}, f32[1,1,64,512]{3,2,1,0:T(8,128)S(1)}, u32[]{:S(2)}, u32[]{:S(2)}) collective-permute-start(f32[1,1,64,512]{3,2,1,0:T(8,128)S(1)} %slice_add_fusion.12), channel_id=1, source_target_pairs={{0,16},{4,20},{8,24},{12,28},{16,0},{20,4},{24,8},{28,12},{1,17},{... | collective-permute-start | bytes 393224 | tf_op jit(solution)/shard_map/ppermute | solution.py:400
  91.0 18.5 %collective-permute-start.22 = (f32[1,1,72,512]{3,2,1,0:T(8,128)S(1)}, f32[1,1,72,512]{3,2,1,0:T(8,128)S(1)}, u32[]{:S(2)}, u32[]{:S(2)}) collective-permute-start(f32[1,1,72,512]{3,2,1,0:T(8,128)S(1)} %slice_add_fusion.11), channel_id=1, source_target_pairs={{0,8},{4,12},{8,0},{12,4},{16,24},{20,28},{24,16},{28,20},{1,9},{5... | collective-permute-start | bytes 442376 | tf_op jit(solution)/shard_map/ppermute | solution.py:400
  92.2 20.0 %collective-permute-start.25 = (f32[2,1,64,1024]{3,2,1,0:T(8,128)S(1)}, f32[2,1,64,1024]{3,2,1,0:T(8,128)S(1)}, u32[]{:S(2)}, u32[]{:S(2)}) collective-permute-start(f32[2,1,64,1024]{3,2,1,0:T(8,128)S(1)} %get-tuple-element.179), channel_id=1, source_target_pairs={{0,8},{4,12},{8,0},{12,4},{16,24},{20,28},{24,16},{28,20},{1,9},{5... | collective-permute-start | bytes 1572872 | tf_op jit(solution)/shard_map/ppermute | solution.py:400
  97.8 14.4 %collective-permute-start.26 = (f32[2,1,64,1024]{3,2,1,0:T(8,128)S(1)}, f32[2,1,64,1024]{3,2,1,0:T(8,128)S(1)}, u32[]{:S(2)}, u32[]{:S(2)}) collective-permute-start(f32[2,1,64,1024]{3,2,1,0:T(8,128)S(1)} %get-tuple-element.181), channel_id=1, source_target_pairs={{0,16},{4,20},{8,24},{12,28},{16,0},{20,4},{24,8},{28,12},{1,17},{... | collective-permute-start | bytes 1572872 | tf_op jit(solution)/shard_map/ppermute | solution.py:400
  99.6 9.8 %collective-permute-start.21 = (f32[136,512]{1,0:T(8,128)S(1)}, f32[136,512]{1,0:T(8,128)S(1)}, u32[]{:S(2)}, u32[]{:S(2)}) collective-permute-start(f32[136,512]{1,0:T(8,128)S(1)} %maximum_bitcast_fusion.1), channel_id=1, source_target_pairs={{0,2},{1,3},{2,0},{3,1},{4,6},{5,7},{6,4},{7,5},{8,10},{9,11},{10,... | collective-permute-start | bytes 835592 | tf_op jit(solution)/shard_map/ppermute | solution.py:400
  113.9 24.1 %collective-permute-start.36 = (f32[128,1024]{1,0:T(8,128)S(1)}, f32[128,1024]{1,0:T(8,128)S(1)}, u32[]{:S(2)}, u32[]{:S(2)}) collective-permute-start(f32[128,1024]{1,0:T(8,128)S(1)} %bitcast.81), channel_id=1, source_target_pairs={{0,2},{1,3},{2,0},{3,1},{4,6},{5,7},{6,4},{7,5},{8,10},{9,11},{10,... | collective-permute-start | bytes 1572872 | tf_op jit(solution)/shard_map/ppermute | solution.py:400
  121.5 16.5 %collective-permute-start.30 = (f32[136,512]{1,0:T(8,128)S(1)}, f32[136,512]{1,0:T(8,128)S(1)}, u32[]{:S(2)}, u32[]{:S(2)}) collective-permute-start(f32[136,512]{1,0:T(8,128)S(1)} %get-tuple-element.241), channel_id=1, source_target_pairs={{0,16},{4,20},{8,24},{12,28},{16,0},{20,4},{24,8},{28,12},{1,17},{... | collective-permute-start | bytes 835592 | tf_op jit(solution)/shard_map/ppermute | solution.py:400
  123.8 14.2 %collective-permute-start.29 = (f32[136,512]{1,0:T(8,128)S(1)}, f32[136,512]{1,0:T(8,128)S(1)}, u32[]{:S(2)}, u32[]{:S(2)}) collective-permute-start(f32[136,512]{1,0:T(8,128)S(1)} %get-tuple-element.241), channel_id=1, source_target_pairs={{0,8},{4,12},{8,0},{12,4},{16,24},{20,28},{24,16},{28,20},{1,9},{5... | collective-permute-start | bytes 835592 | tf_op jit(solution)/shard_map/ppermute | solution.py:400
  131.1 10.9 %collective-permute-start.35 = (f32[544,512]{1,0:T(8,128)S(1)}, f32[544,512]{1,0:T(8,128)S(1)}, u32[]{:S(2)}, u32[]{:S(2)}) collective-permute-start(f32[544,512]{1,0:T(8,128)S(1)} %constant_dynamic-update-slice_fusion.2.refs_0_), channel_id=1, source_target_pairs={{0,4},{4,0},{8,12},{12,8},{16,20},{20,16},{24,28},{28,24},{1,5},{5... | collective-permute-start | bytes 3342344 | tf_op jit(solution)/shard_map/ppermute | solution.py:400
  138.2 15.2 %collective-permute-start.38 = (f32[128,1024]{1,0:T(8,128)S(1)}, f32[128,1024]{1,0:T(8,128)S(1)}, u32[]{:S(2)}, u32[]{:S(2)}) collective-permute-start(f32[128,1024]{1,0:T(8,128)S(1)} %pad_maximum_fusion), channel_id=1, source_target_pairs={{0,16},{4,20},{8,24},{12,28},{16,0},{20,4},{24,8},{28,12},{1,17},{... | collective-permute-start | bytes 1572872 | tf_op jit(solution)/shard_map/ppermute | solution.py:400
  138.9 14.5 %collective-permute-start.37 = (f32[128,1024]{1,0:T(8,128)S(1)}, f32[128,1024]{1,0:T(8,128)S(1)}, u32[]{:S(2)}, u32[]{:S(2)}) collective-permute-start(f32[128,1024]{1,0:T(8,128)S(1)} %pad_maximum_fusion), channel_id=1, source_target_pairs={{0,8},{4,12},{8,0},{12,4},{16,24},{20,28},{24,16},{28,20},{1,9},{5... | collective-permute-start | bytes 1572872 | tf_op jit(solution)/shard_map/ppermute | solution.py:400
  140.6 11.5 %collective-permute-start.31 = (f32[64,512]{1,0:T(8,128)S(1)}, f32[64,512]{1,0:T(8,128)S(1)}, u32[]{:S(2)}, u32[]{:S(2)}) collective-permute-start(f32[64,512]{1,0:T(8,128)S(1)} %get-tuple-element.239), channel_id=1, source_target_pairs={{0,16},{4,20},{8,24},{12,28},{16,0},{20,4},{24,8},{28,12},{1,17},{... | collective-permute-start | bytes 393224 | tf_op jit(solution)/shard_map/ppermute | solution.py:400
  141.8 11.6 %collective-permute-start.32 = (f32[72,512]{1,0:T(8,128)S(1)}, f32[72,512]{1,0:T(8,128)S(1)}, u32[]{:S(2)}, u32[]{:S(2)}) collective-permute-start(f32[72,512]{1,0:T(8,128)S(1)} %get-tuple-element.237), channel_id=1, source_target_pairs={{0,8},{4,12},{8,0},{12,4},{16,24},{20,28},{24,16},{28,20},{1,9},{5... | collective-permute-start | bytes 442376 | tf_op jit(solution)/shard_map/ppermute | solution.py:400
  156.8 10.2 %collective-permute-start.42 = (f32[384,1024]{1,0:T(8,128)S(1)}, f32[384,1024]{1,0:T(8,128)S(1)}, u32[]{:S(2)}, u32[]{:S(2)}) collective-permute-start(f32[384,1024]{1,0:T(8,128)S(1)} %slice_dynamic-update-slice_fusion.refs_0_), channel_id=1, source_target_pairs={{0,4},{4,0},{8,12},{12,8},{16,20},{20,16},{24,28},{28,24},{1,5},{5... | collective-permute-start | bytes 4718600 | tf_op jit(solution)/shard_map/ppermute | solution.py:400
  (25 other events, 157.4 us)
